TPU v7x, 32 devices: a whole 2x2x4 slice. The times are simulated.
32 devices in a mesh: member: 8 (over y, x, core), tile: 4 (over z).
Axes of the slice: x: 2, y: 2, z: 4, core: 2. Of those that a mesh axis runs over, the one named last changes fastest.
Arguments:
- member_concentration: float32 [16, 4, 128, 256], P('member', None, 'tile'), may hold values from -6 to 6
- courant_pairs: float32 [2, 4, 128, 256], P(None, None, 'tile'), may hold values from -0.4 to 0.4
- obs_cell: int32 [32768], replicated, may hold values from 0 to 131071, as said below
- obs_value: float32 [32768], replicated, may hold values from -6 to 6
- obs_error: float32 [32768], replicated, may hold values from 0.25 to 4
- obs_list: int32 [8, 16, 1024], P('tile', 'member'), may hold values from -1 to 32767, as said below
Outputs:
- analysis: float32 [16, 4, 128, 256], P('member', None, 'tile')
Inputs may be any that keep to these rules, and one draw needn't show every extreme that they name: `obs_cell`: observation g lies in rows r * 32 to r * 32 + 31 and columns c * 32 to c * 32 + 31, with r = (g // 1024) % (4) and c = (g // 1024) // 4. `obs_list`: filled slots come first in each list; each list has 1 to 1024 filled slots and some list has exactly 1024; a filled slot names an observation whose region (as for obs_cell) is the patch's own or one of the eight around it, columns wrapping around and rows not.
All inputs are finite; a program needn't handle non-finite values.
Results may differ from a plain program's by a relative error of at most 0.0013.
Values may be sent and summed in bfloat16 or wider, within the bound.
No kernel may reach another device: no remote copies, remote signals or barrier semaphores. Data moves between devices by JAX's collectives and lax.ppermute only.
A program may use at most 128 MiB of HBM per device.

v0:
```python
import jax
import jax.numpy as jnp
from jax import lax
from jax.sharding import PartitionSpec as P

PATCH = 16
LOC_LEN = 16


diffusion = 0.05
highest = lax.Precision.HIGHEST


def padded_2(array, sides, width, wrap):
    for axis, dim in sides:
        size, length = (lax.axis_size(axis), array.shape[dim])
        up = [(i, (i + 1) % size) for i in range(size if wrap else size - 1)]
        down = [(j, i) for i, j in up]
        last = lax.slice_in_dim(array, length - width, length, axis=dim)
        leading = lax.slice_in_dim(array, 0, width, axis=dim)
        before = lax.ppermute(last, axis, up)
        after = lax.ppermute(leading, axis, down)
        array = jnp.concatenate([before, array, after], axis=dim)
    return array


def update(current, north_rows, south_rows, east_cells, west_cells, courant_pairs):
    meridional = courant_pairs[0]
    zonal_flow = courant_pairs[1]
    advection = (
        jnp.maximum(zonal_flow, 0.0) * (current - west_cells)
        + jnp.minimum(zonal_flow, 0.0) * (east_cells - current)
        + jnp.maximum(meridional, 0.0) * (current - south_rows)
        + jnp.minimum(meridional, 0.0) * (north_rows - current)
    )
    return (
        current
        - advection
        + diffusion * (north_rows + south_rows + east_cells + west_cells - 4.0 * current)
    )


def transport_concentration(current, courant_pairs):
    padded = padded_2(current, (("tile", 2),), 1, False)
    north_rows = padded[:, :, 2:, :]
    south_rows = padded[:, :, :-2, :]
    east_cells = jnp.roll(current, -1, axis=3)
    west_cells = jnp.roll(current, 1, axis=3)
    return update(current, north_rows, south_rows, east_cells, west_cells, courant_pairs)


def localize(cells, patch_row, patch_column, variance, grid_height, grid_width):
    cell_row = cells // grid_width % grid_height
    column_of_cell = cells % grid_width
    row_gap = (cell_row - patch_row * PATCH - PATCH // 2).astype(jnp.float32) + 0.5
    column_gap = (
        (column_of_cell - patch_column * PATCH - PATCH // 2 + grid_width // 2) % grid_width
        - grid_width // 2
    ).astype(jnp.float32) + 0.5
    return (
        jnp.exp(-(row_gap * row_gap + column_gap * column_gap) / (2.0 * LOC_LEN * LOC_LEN))
        / variance
    )


def accumulate(spread, innovation, weight):
    scaled = spread * weight[:, :, None]
    system_terms = jnp.einsum("psm,psn->pmn", scaled, spread, precision=highest)
    forcing = jnp.einsum("psm,ps->pm", scaled, innovation, precision=highest)
    return (system_terms, forcing)


def solve_lower(factor):
    identity = jnp.eye(factor.shape[0], dtype=jnp.float32)
    return jax.scipy.linalg.solve_triangular(factor, identity, lower=True)


def transform(system_terms, forcing, ensemble_size):
    identity = jnp.eye(ensemble_size, dtype=jnp.float32)
    lower_factor = jnp.linalg.cholesky(system_terms + (ensemble_size - 1.0) * identity)
    inverse = jax.vmap(solve_lower)(lower_factor)
    inner = jnp.einsum("pij,pj->pi", inverse, forcing, precision=highest)
    mean_weight = jnp.einsum("pji,pj->pi", inverse, inner, precision=highest)
    spread_weight = jnp.sqrt(ensemble_size - 1.0) * jnp.swapaxes(inverse, 1, 2)
    return mean_weight[:, :, None] + spread_weight - identity


def shards(member_concentration, courant_pairs, obs_cell, obs_value, obs_error, obs_list):
    members_here = member_concentration.shape[0]
    levels_here = member_concentration.shape[1]
    region_side = member_concentration.shape[2]
    grid_width = member_concentration.shape[3]
    member_count = lax.axis_size("member")
    tile_count = lax.axis_size("tile")
    grid_height = region_side * tile_count
    column_block = lax.axis_index("member")
    row_block = lax.axis_index("tile")
    ensemble_size = members_here * member_count
    predicted_ensemble = member_concentration
    for repeat in range(2):
        predicted_ensemble = transport_concentration(predicted_ensemble, courant_pairs)
    common_arrays = predicted_ensemble.astype(jnp.bfloat16)
    pieces = common_arrays.reshape(
        members_here, levels_here, region_side, member_count, region_side
    )
    regional = lax.all_to_all(pieces, "member", split_axis=3, concat_axis=0, tiled=True)
    regional = regional.reshape(ensemble_size, levels_here, region_side, region_side)
    ensemble = regional.astype(jnp.float32)
    centred = ensemble - jnp.mean(ensemble, axis=0)
    beside_all = padded_2(regional, (("member", 3), ("tile", 2)), region_side, True)
    cell_major = beside_all.reshape(ensemble_size, levels_here * 9 * region_side * region_side).T
    patch_side = region_side // PATCH
    patch_count = patch_side * patch_side
    lists = obs_list.reshape(patch_count, obs_list.shape[2])
    patch_number = jnp.arange(patch_count, dtype=jnp.int32)
    patch_row = (row_block * patch_side + patch_number // patch_side)[:, None]
    patch_column = (column_block * patch_side + patch_number % patch_side)[:, None]
    valid = lists >= 0
    safe = jnp.where(valid, lists, 0)
    cells = obs_cell[safe]
    cell_level = cells // (grid_height * grid_width)
    cell_row = cells // grid_width % grid_height
    column_of_cell = cells % grid_width
    local_row = cell_row - (row_block - 1) * region_side
    local_column = (column_of_cell - (column_block - 1) * region_side + grid_width) % grid_width
    values = cell_major[
        (cell_level * 3 * region_side + local_row) * 3 * region_side + local_column
    ].astype(jnp.float32)
    obs_mean = jnp.mean(values, axis=2)
    spread = values - obs_mean[:, :, None]
    innovation = obs_value[safe] - obs_mean
    weight = jnp.where(
        valid,
        localize(obs_cell[safe], patch_row, patch_column, obs_error[safe], grid_height, grid_width),
        0.0,
    )
    system_terms, forcing = accumulate(spread, innovation, weight)
    trans = transform(system_terms, forcing, ensemble_size)
    trans_grid = trans.reshape(patch_side, patch_side, ensemble_size, ensemble_size)
    local = centred.reshape(ensemble_size, levels_here, patch_side, PATCH, patch_side, PATCH)
    change = jnp.einsum("abjk,jlaybx->klaybx", trans_grid, local, precision=highest).astype(
        jnp.bfloat16
    )
    change = change.reshape(ensemble_size, levels_here, region_side, 1, region_side)
    output_ensemble = lax.all_to_all(change, "member", split_axis=0, concat_axis=3, tiled=True)
    output_ensemble = output_ensemble.reshape(members_here, levels_here, region_side, grid_width)
    return predicted_ensemble + output_ensemble.astype(jnp.float32)


def solution(mesh):
    return jax.shard_map(
        shards,
        mesh=mesh,
        in_specs=(
            P("member", None, "tile", None),
            P(None, None, "tile", None),
            P(),
            P(),
            P(),
            P("tile", "member", None),
        ),
        out_specs=P("member", None, "tile", None),
        check_vma=False,
    )
```

profile of v0, /device:TPU:9, one launch (start us, length us, event | category | flops | bytes accessed | tf_op | source)
XLA Modules:
  0.0 206.3 jit_solution(13712333346911198139)
XLA Ops:
  0.9 1.9 collective-permute-start.1
  2.9 3.4 %collective-permute-start = (f32[2,4,1,256]{3,2,1,0:T(1,128)S(1)}, f32[2,4,1,256]{3,2,1,0:T(1,128)S(1)}, u32[]{:S(2)}, u32[]{:S(2)}) collective-permute-start(f32[2,4,1,256]{3,2,1,0:T(1,128)S(1)} %get-tuple-element.21), channel_id=1, source_target_pairs={{0,1},{1,2},{2,3},{4,5},{5,6},{6,7},{8,9},{9,10},{10,11},{12,13},{... | collective-permute-start | bytes 24584 | tf_op jit(solution)/shard_map/ppermute | solution.py:21
  10.0 23.0 %gather_fusion = s32[4096]{0:T(1024)S(1)} fusion(s32[32768]{0:T(1024)S(1)} %copy-done, s32[4096]{0:T(1024)S(1)} %bitcast_clamp_fusion.1), kind=kCustom, calls=%fused_computation | custom fusion | bytes 49152 | tf_op jit(solution)/shard_map/gather | solution.py:120
  33.9 23.0 %gather_fusion.2 = f32[4096]{0:T(1024)S(1)} fusion(f32[32768]{0:T(1024)S(1)} %copy-done.1, s32[4096]{0:T(1024)S(1)} %bitcast_clamp_fusion.1), kind=kCustom, calls=%fused_computation.2 | custom fusion | bytes 49152 | tf_op jit(solution)/shard_map/gather | solution.py:134
  58.2 1.9 collective-permute-start.3
  60.1 3.4 %collective-permute-start.2 = (f32[2,4,1,256]{3,2,1,0:T(1,128)S(1)}, f32[2,4,1,256]{3,2,1,0:T(1,128)S(1)}, u32[]{:S(2)}, u32[]{:S(2)}) collective-permute-start(f32[2,4,1,256]{3,2,1,0:T(1,128)S(1)} %get-tuple-element.11), channel_id=1, source_target_pairs={{0,1},{1,2},{2,3},{4,5},{5,6},{6,7},{8,9},{9,10},{10,11},{12,13},{... | collective-permute-start | bytes 24584 | tf_op jit(solution)/shard_map/ppermute | solution.py:21
  67.1 6.5 %all-to-all-start = ((bf16[8,2,4096]{2,1,0:T(2,128)(2,1)}), bf16[8,2,4096]{2,1,0:T(2,128)(2,1)S(1)}, u32[]{:S(2)}, u32[]{:S(2)}) async-start(bf16[8,2,4096]{2,1,0:T(2,128)(2,1)} %reshape.437), calls=%async_computation | async-start | bytes 262144 | tf_op jit(solution)/shard_map/all_to_all | solution.py:106
  74.8 23.0 %gather_fusion.3 = f32[4096]{0:T(1024)S(1)} fusion(f32[32768]{0:T(1024)S(1)} %copy-done.2, s32[4096]{0:T(1024)S(1)} %bitcast_clamp_fusion.1), kind=kCustom, calls=%fused_computation.3 | custom fusion | bytes 49152 | tf_op jit(solution)/shard_map/gather | solution.py:131
  99.4 1.7 collective-permute-start.4
  101.4 10.5 %collective-permute-done.5 = bf16[16,4,32,32]{3,2,1,0:T(8,128)(2,1)S(1)} collective-permute-done((bf16[16,4,32,32]{3,2,1,0:T(8,128)(2,1)S(1)}, bf16[16,4,32,32]{3,2,1,0:T(8,128)(2,1)S(1)}, u32[]{:S(2)}, u32[]{:S(2)}) %collective-permute-start.5) | collective-permute-done | bytes 131104 | tf_op jit(solution)/shard_map/ppermute | solution.py:22
  111.8 1.3 pad_maximum_fusion.1
  113.1 1.5 collective-permute-start.6
  114.6 2.5 %reshape.386 = f32[16,4,2,16,2,16]{5,4,3,2,1,0:T(2,128)} reshape(f32[8,2,4,32,1,32]{5,3,2,1,0,4:T(8,128)S(1)} %bitcast_convert_fusion) | data formatting | bytes 524288 | tf_op jit(solution)/shard_map/convert_element_type | solution.py:108
  117.3 2.1 broadcast_subtract_fusion
  119.3 4.0 %collective-permute-done.7 = bf16[16,4,32,96]{3,2,1,0:T(8,128)(2,1)} collective-permute-done((bf16[16,4,32,96]{3,2,1,0:T(8,128)(2,1)}, bf16[16,4,32,96]{3,2,1,0:T(8,128)(2,1)}, u32[]{:S(2)}, u32[]{:S(2)}) %collective-permute-start.7) | collective-permute-done | bytes 393248 | tf_op jit(solution)/shard_map/ppermute | solution.py:22
  123.3 13.4 %collective-permute-done.6 = bf16[16,4,32,96]{3,2,1,0:T(8,128)(2,1)} collective-permute-done((bf16[16,4,32,96]{3,2,1,0:T(8,128)(2,1)}, bf16[16,4,32,96]{3,2,1,0:T(8,128)(2,1)}, u32[]{:S(2)}, u32[]{:S(2)}) %collective-permute-start.6) | collective-permute-done | bytes 393248 | tf_op jit(solution)/shard_map/ppermute | solution.py:21
  136.7 3.1 %pad_maximum_fusion = bf16[16,4,96,96]{3,2,1,0:T(8,128)(2,1)} fusion(bf16[16,4,32,96]{3,2,1,0:T(8,128)(2,1)} %collective-permute-done.7, bf16[16,4,32,32]{3,2,1,0:T(8,128)(2,1)S(1)} %collective-permute-done.5, bf16[16,4,32,32]{3,2,1,0:T(8,128)(2,1)S(1)} %bitcast.106, bf16[16,4,32,32]{3,2,1,0:T(8,128)(2,1)S(1)} %copy-done.5, ...), kind=kLoop, calls=%fused_computation.6 | loop fusion | flops 5898240 | bytes 2359296 | tf_op jit(solution)/shard_map/concatenate | solution.py:23
  139.7 8.2 %copy.49 = bf16[16,4,96,96]{0,3,2,1:T(8,128)(2,1)} copy(bf16[16,4,96,96]{3,2,1,0:T(8,128)(2,1)} %pad_maximum_fusion) | data formatting | bytes 2359296 | tf_op jit(solution)/shard_map/concatenate | solution.py:23
  148.0 15.9 %gather_fusion.1 = bf16[4096,16]{1,0:T(8,128)(2,1)S(1)} fusion(bf16[36864,16]{1,0:T(8,128)(2,1)} %bitcast.102, s32[4096]{0:T(1024)S(1)} %copy-done.8), kind=kCustom, calls=%fused_computation.1 | custom fusion | bytes 278528 | tf_op jit(solution)/shard_map/gather | solution.py:126
  167.1 5.9 %custom-call.8 = f32[4,16,16]{2,1,0:T(8,128)S(1)} custom-call(f32[4,16,16]{2,1,0:T(8,128)S(1)} %fusion.47), custom_call_target="Cholesky" | custom-call | tf_op jit(solution)/shard_map/jit(cholesky)/cholesky | solution.py:80
  174.6 4.9 %custom-call.9 = f32[4,1,16,16]{2,3,1,0:T(8,128)S(1)} custom-call(f32[4,1,16,16]{3,2,1,0:T(8,128)S(1)} %select_bitcast_fusion), custom_call_target="InvertDiagBlocksLowerTriangular" | custom-call | tf_op jit(solution)/shard_map/vmap(jit(_solve_triangular))/triangular_solve | solution.py:75
  182.7 4.2 %fusion.5 = bf16[16,4,2,16,2,16]{0,5,3,1,4,2:T(8,128)(2,1)S(1)} fusion(f32[2,2,16,16,1,1]{2,3,5,4,1,0:T(8,128)S(1)} %bitcast.113, f32[16,4,2,16,2,16]{5,4,3,2,1,0:T(2,128)S(1)} %bitcast.108), kind=kOutput, calls=%fused_computation.8 | convolution fusion | flops 12648448 | bytes 397312 | tf_op jit(solution)/shard_map/abjk,jlaybx->klaybx/dot_general | solution.py:141
  186.9 1.9 copy.57
  189.9 14.3 %all_to_all.24 = bf16[8,2,4096]{2,1,0:T(2,128)(2,1)S(1)} all-to-all(bf16[8,2,4096]{2,1,0:T(2,128)(2,1)S(1)} %reshape.439), channel_id=1, replica_groups=mesh['member'=8,'tile'=4] {'member'}, dimensions={0} | all-to-all | bytes 262144 | tf_op jit(solution)/shard_map/all_to_all | solution.py:145
  (85 shorter events, 24.5 us)
Async XLA Ops:
  0.0 10.0 %copy-start = (s32[32768]{0:T(1024)S(1)}, s32[32768]{0:T(1024)}, u32[]{:S(2)}) copy-start(s32[32768]{0:T(1024)} %param.8) | copy-start | bytes 393220
  0.9 56.8 %collective-permute-start.1 = (f32[2,4,1,256]{3,2,1,0:T(1,128)S(1)}, f32[2,4,1,256]{3,2,1,0:T(1,128)S(1)}, u32[]{:S(2)}, u32[]{:S(2)}) collective-permute-start(f32[2,4,1,256]{3,2,1,0:T(1,128)S(1)} %get-tuple-element.22), channel_id=1, source_target_pairs={{1,0},{2,1},{3,2},{5,4},{6,5},{7,6},{9,8},{10,9},{11,10},{13,12},{... | collective-permute-start | bytes 24584 | tf_op jit(solution)/shard_map/ppermute | solution.py:22
  2.9 54.9 %collective-permute-start = (f32[2,4,1,256]{3,2,1,0:T(1,128)S(1)}, f32[2,4,1,256]{3,2,1,0:T(1,128)S(1)}, u32[]{:S(2)}, u32[]{:S(2)}) collective-permute-start(f32[2,4,1,256]{3,2,1,0:T(1,128)S(1)} %get-tuple-element.21), channel_id=1, source_target_pairs={{0,1},{1,2},{2,3},{4,5},{5,6},{6,7},{8,9},{9,10},{10,11},{12,13},{... | collective-permute-start | bytes 24584 | tf_op jit(solution)/shard_map/ppermute | solution.py:21
  10.0 23.1 %copy-start.7 = (f32[2,4,32,256]{3,2,1,0:T(8,128)S(1)}, f32[2,4,32,256]{3,2,1,0:T(8,128)}, u32[]{:S(2)}) copy-start(f32[2,4,32,256]{3,2,1,0:T(8,128)} %param.7) | copy-start | bytes 786436
  33.0 0.9 copy-start.1
  33.9 23.8 %copy-start.3 = (f32[2,4,32,256]{3,2,1,0:T(8,128)S(1)}, f32[2,4,32,256]{3,2,1,0:T(8,128)}, u32[]{:S(2)}) copy-start(f32[2,4,32,256]{3,2,1,0:T(8,128)} %param.6) | copy-start | bytes 786436
  58.2 5.4 %collective-permute-start.3 = (f32[2,4,1,256]{3,2,1,0:T(1,128)S(1)}, f32[2,4,1,256]{3,2,1,0:T(1,128)S(1)}, u32[]{:S(2)}, u32[]{:S(2)}) collective-permute-start(f32[2,4,1,256]{3,2,1,0:T(1,128)S(1)} %get-tuple-element.12), channel_id=1, source_target_pairs={{1,0},{2,1},{3,2},{5,4},{6,5},{7,6},{9,8},{10,9},{11,10},{13,12},{... | collective-permute-start | bytes 24584 | tf_op jit(solution)/shard_map/ppermute | solution.py:22
  60.1 4.5 %collective-permute-start.2 = (f32[2,4,1,256]{3,2,1,0:T(1,128)S(1)}, f32[2,4,1,256]{3,2,1,0:T(1,128)S(1)}, u32[]{:S(2)}, u32[]{:S(2)}) collective-permute-start(f32[2,4,1,256]{3,2,1,0:T(1,128)S(1)} %get-tuple-element.11), channel_id=1, source_target_pairs={{0,1},{1,2},{2,3},{4,5},{5,6},{6,7},{8,9},{9,10},{10,11},{12,13},{... | collective-permute-start | bytes 24584 | tf_op jit(solution)/shard_map/ppermute | solution.py:21
  64.6 10.2 %copy-start.2 = (f32[32768]{0:T(1024)S(1)}, f32[32768]{0:T(1024)}, u32[]{:S(2)}) copy-start(f32[32768]{0:T(1024)} %param.9) | copy-start | bytes 393220
  67.1 32.0 %all-to-all-start = ((bf16[8,2,4096]{2,1,0:T(2,128)(2,1)}), bf16[8,2,4096]{2,1,0:T(2,128)(2,1)S(1)}, u32[]{:S(2)}, u32[]{:S(2)}) async-start(bf16[8,2,4096]{2,1,0:T(2,128)(2,1)} %reshape.437), calls=%async_computation | async-start | bytes 262144 | tf_op jit(solution)/shard_map/all_to_all | solution.py:106
  99.3 12.5 %collective-permute-start.5 = (bf16[16,4,32,32]{3,2,1,0:T(8,128)(2,1)S(1)}, bf16[16,4,32,32]{3,2,1,0:T(8,128)(2,1)S(1)}, u32[]{:S(2)}, u32[]{:S(2)}) collective-permute-start(bf16[16,4,32,32]{3,2,1,0:T(8,128)(2,1)S(1)} %bitcast.103), channel_id=1, source_target_pairs={{4,0},{8,4},{12,8},{16,12},{20,16},{24,20},{28,24},{0,28},{5,1},{9... | collective-permute-start | bytes 393224 | tf_op jit(solution)/shard_map/ppermute | solution.py:22
  99.4 12.5 %collective-permute-start.4 = (bf16[16,4,32,32]{3,2,1,0:T(8,128)(2,1)S(1)}, bf16[16,4,32,32]{3,2,1,0:T(8,128)(2,1)S(1)}, u32[]{:S(2)}, u32[]{:S(2)}) collective-permute-start(bf16[16,4,32,32]{3,2,1,0:T(8,128)(2,1)S(1)} %bitcast.104), channel_id=1, source_target_pairs={{0,4},{4,8},{8,12},{12,16},{16,20},{20,24},{24,28},{28,0},{1,5},{5... | collective-permute-start | bytes 393224 | tf_op jit(solution)/shard_map/ppermute | solution.py:21
  111.8 5.3 %copy-start.4 = (bf16[16,4,32,32]{3,2,1,0:T(8,128)(2,1)}, bf16[16,4,32,32]{3,2,1,0:T(8,128)(2,1)S(1)}, u32[]{:S(2)}) copy-start(bf16[16,4,32,32]{3,2,1,0:T(8,128)(2,1)S(1)} %collective-permute-done.4) | copy-start | bytes 393220
  113.1 10.2 %collective-permute-start.7 = (bf16[16,4,32,96]{3,2,1,0:T(8,128)(2,1)}, bf16[16,4,32,96]{3,2,1,0:T(8,128)(2,1)}, u32[]{:S(2)}, u32[]{:S(2)}) collective-permute-start(bf16[16,4,32,96]{3,2,1,0:T(8,128)(2,1)} %pad_maximum_fusion.1), channel_id=1, source_target_pairs={{1,0},{2,1},{3,2},{0,3},{5,4},{6,5},{7,6},{4,7},{9,8},{10,9},{11,1... | collective-permute-start | bytes 1179656 | tf_op jit(solution)/shard_map/ppermute | solution.py:22
  113.1 23.5 %collective-permute-start.6 = (bf16[16,4,32,96]{3,2,1,0:T(8,128)(2,1)}, bf16[16,4,32,96]{3,2,1,0:T(8,128)(2,1)}, u32[]{:S(2)}, u32[]{:S(2)}) collective-permute-start(bf16[16,4,32,96]{3,2,1,0:T(8,128)(2,1)} %pad_maximum_fusion.1), channel_id=1, source_target_pairs={{0,1},{1,2},{2,3},{3,0},{4,5},{5,6},{6,7},{7,4},{8,9},{9,10},{10,1... | collective-permute-start | bytes 1179656 | tf_op jit(solution)/shard_map/ppermute | solution.py:21
  117.3 19.4 %copy-start.5 = (bf16[16,4,32,32]{3,2,1,0:T(8,128)(2,1)S(1)}, bf16[16,4,32,32]{3,2,1,0:T(8,128)(2,1)}, u32[]{:S(2)}) copy-start(bf16[16,4,32,32]{3,2,1,0:T(8,128)(2,1)} %copy-done.4) | copy-start | bytes 393220
  139.7 8.2 %copy-start.8 = (s32[4096]{0:T(1024)S(1)}, s32[4096]{0:T(1024)}, u32[]{:S(2)}) copy-start(s32[4096]{0:T(1024)} %bitcast_clamp_fusion) | copy-start | bytes 49156
  204.6 1.0 copy-start.6
where the time goes:
time: 209 us; the launch traced here: 206 us
  local copies, waits for them, and re-layouts  108 us (52%)
  waiting for transfers between devices  28.8 us (14%)
  other arithmetic  28.5 us (14%)
  starting transfers between devices  20.3 us (10%)
  blocking collectives  14.3 us (7%)
  matrix products  6.34 us (3%)
    gather x2, local copies, waits for them, and re-layouts, shards(): innovation = obs_value[safe] - obs_mean  23.6 us
    gather x3, local copies, waits for them, and re-layouts, shards(): cells = obs_cell[safe]  23.1 us
    gather x2, local copies, waits for them, and re-layouts, shards(): obs_error[safe]  23 us
    gather x1, local copies, waits for them, and re-layouts, shards(): cell_major[(cell_level * 3 * region_side + local_row) * 3 * region_side +...  15.9 us
    ppermute x4, waiting for transfers between devices, padded_2(): after = lax.ppermute(leading, axis, down)  14.5 us
    ppermute x4, waiting for transfers between devices, padded_2(): before = lax.ppermute(last, axis, up)  14.3 us
    all_to_all x1, blocking collectives, shards(): lax.all_to_all(change, 'member', split_axis=0, concat_axis=3, tiled=True)  14.3 us
    ppermute x4, starting transfers between devices, padded_2(): before = lax.ppermute(last, axis, up)  9.92 us
  transfers between devices with their start and end apart: 9, of which 4 were waited for; matrix products, arithmetic and copies ran while one was open for 40% of the time, Pallas kernels for 0%

commit v1 on v0

v1 whole, which is shorter than its diff:
```python
import functools

import jax
import jax.numpy as jnp
from jax import lax
from jax.experimental import pallas as pl
from jax.experimental.pallas import tpu as pltpu
from jax.sharding import PartitionSpec as P

PATCH = 16
LOC_LEN = 16
DIFFUSION = 0.05
LANES = 128
BLOCK = 8

f32 = jnp.float32
bf16 = jnp.bfloat16


def call(body, outs, scratch=(), flops=1_000_000, moved=1_000_000):
    return pl.pallas_call(
        body,
        out_shape=[jax.ShapeDtypeStruct(shape, kind) for shape, kind in outs],
        scratch_shapes=list(scratch),
        compiler_params=pltpu.CompilerParams(vmem_limit_bytes=48 * 1024 * 1024),
        cost_estimate=pl.CostEstimate(flops=flops, bytes_accessed=moved, transcendentals=0),
    )


def split(number, size):
    if size & (size - 1) == 0:
        return number >> (size.bit_length() - 1), number & (size - 1)
    quotient = number // size
    return quotient, number - quotient * size


def wrapped(number, size):
    if size & (size - 1) == 0:
        return number & (size - 1)
    return lax.rem(number + size, size)


def iota(shape, axis):
    return lax.broadcasted_iota(jnp.int32, shape, axis)


def pick_lanes(values, index):
    rows = [
        jnp.take_along_axis(values[r : r + BLOCK], index, axis=1, mode="promise_in_bounds")
        for r in range(0, values.shape[0], BLOCK)
    ]
    return rows[0] if len(rows) == 1 else jnp.concatenate(rows, axis=0)


def transpose_chunks(parts):
    lane = iota(parts[0].shape, 1)
    low = lane < 64
    even = (lane & 32) == 0
    parts = list(parts)
    for i in (0, 1):
        a, b = parts[i], parts[i + 2]
        parts[i] = jnp.where(low, a, pltpu.roll(b, 64, 1))
        parts[i + 2] = jnp.where(low, pltpu.roll(a, 64, 1), b)
    for i in (0, 2):
        a, b = parts[i], parts[i + 1]
        parts[i] = jnp.where(even, a, pltpu.roll(b, 32, 1))
        parts[i + 1] = jnp.where(even, pltpu.roll(a, 96, 1), b)
    return parts


def pack_edges(tracer, courant, lists, to_south, to_north):
    members, levels, side, width = tracer.shape
    for b in range(members):
        for l in range(levels):
            row = b * levels + l
            to_south[row : row + 1, :] = tracer[b, l, 0:1, :]
            to_south[8 + row : 9 + row, :] = tracer[b, l, 1:2, :]
            to_north[row : row + 1, :] = tracer[b, l, side - 1 : side, :]
            to_north[8 + row : 9 + row, :] = tracer[b, l, side - 2 : side - 1, :]
    for c in range(2):
        for l in range(levels):
            row = 16 + c * levels + l
            to_south[row : row + 1, :] = courant[c, l, 0:1, :]
            to_north[row : row + 1, :] = courant[c, l, side - 1 : side, :]
    row = 24
    for a in range(lists.shape[0]):
        for b in range(lists.shape[1]):
            for s in range(0, lists.shape[2], width):
                part = lists[a, b : b + 1, s : s + width].astype(f32)
                to_south[row : row + 1, :] = part
                to_north[row : row + 1, :] = part
                row += 1


def coefficients(meridional, zonal):
    return (
        (1.0 - 4.0 * DIFFUSION) - jnp.abs(zonal) - jnp.abs(meridional),
        DIFFUSION + jnp.maximum(zonal, 0.0),
        DIFFUSION - jnp.minimum(zonal, 0.0),
        DIFFUSION + jnp.maximum(meridional, 0.0),
        DIFFUSION - jnp.minimum(meridional, 0.0),
    )


def stencil(current, south, north, factors):
    width = current.shape[1]
    centre, from_west, from_east, from_south, from_north = factors
    west = pltpu.roll(current, 1, 1)
    east = pltpu.roll(current, width - 1, 1)
    return (
        centre * current
        + from_west * west
        + from_east * east
        + from_south * south
        + from_north * north
    )


def forecast_body(
    tracer, courant, own_south, own_north, south, north, cell, forecast, send, table, *, tiles, height
):
    members, levels, side, width = tracer.shape
    blocks = width // side
    tile = lax.axis_index("tile")
    planes = members * levels

    def edge(own, other):
        twice = lambda first: jnp.concatenate([other[first : first + levels, :]] * members, axis=0)
        return coefficients(twice(16), twice(16 + levels))

    below = stencil(
        south[0:planes, :], south[8 : 8 + planes, :], own_south[0:planes, :], edge(own_south, south)
    )
    above = stencil(
        north[0:planes, :], own_north[0:planes, :], north[8 : 8 + planes, :], edge(own_north, north)
    )
    below = jnp.where(tile == 0, 0.0, below)
    above = jnp.where(tile == tiles - 1, 0.0, above)
    row = iota((side, width), 0)
    for l in range(levels):
        factors = coefficients(courant[0, l], courant[1, l])
        for b in range(members):
            plane = b * levels + l
            current = tracer[b, l]
            for low, high in (
                (south[plane : plane + 1, :], north[plane : plane + 1, :]),
                (below[plane : plane + 1, :], above[plane : plane + 1, :]),
            ):
                lower = jnp.where(row == 0, low, pltpu.roll(current, 1, 0))
                upper = jnp.where(row == side - 1, high, pltpu.roll(current, side - 1, 0))
                current = stencil(current, lower, upper, factors)
            forecast[b, l] = current

    region_rows = planes * BLOCK
    for q in range(width // LANES):
        parts = [
            forecast[:, :, r : r + BLOCK, q * LANES : (q + 1) * LANES].reshape(region_rows, LANES)
            for r in range(0, side, BLOCK)
        ]
        for c, part in enumerate(transpose_chunks(parts)):
            rounded = part.astype(bf16)
            send[4 * q + c, 0:region_rows, :] = rounded
            table[4 * q + c] = rounded.astype(f32)

    hits = levels * BLOCK
    observed = []
    first = pl.multiple_of(tile * BLOCK, BLOCK)
    for c in range(blocks):
        cells = cell[c, pl.ds(first, BLOCK), :]
        above_row, column = split(cells, width)
        level, grid_row = split(above_row, height)
        _, local_row = split(grid_row, side)
        _, local_column = split(column, side)
        band, sub_row = split(local_row, BLOCK)
        high = level * BLOCK + sub_row
        low = band * side + local_column
        mine = [jnp.zeros((BLOCK, LANES), f32) for _ in range(members)]
        for h in range(hits):
            here = high == h
            for b in range(members):
                line = table[c, b * hits + h : b * hits + h + 1, :]
                line = jnp.broadcast_to(line, (BLOCK, LANES))
                mine[b] = jnp.where(here, pick_lanes(line, low), mine[b])
        observed.append(mine)
    for c in range(blocks):
        rows = [
            observed[(c + r - 1) % blocks][b] for b in range(members) for r in range(3)
        ]
        for i in range(0, len(rows), 2):
            at = region_rows + i * BLOCK
            send[c, at : at + 2 * BLOCK, :] = jnp.concatenate(rows[i : i + 2], axis=0).astype(bf16)


def weights_body(
    lists, south, north, cell, value, variance, weights, values, planes, *, tiles, blocks, height, width, side
):
    tile = lax.axis_index("tile")
    block = lax.axis_index("member")
    per_side = side // PATCH
    patches = per_side * per_side
    slots = lists.shape[2]
    sub = slots // LANES
    depth = 3 * BLOCK
    rows, columns, sizes = [], [], []
    for r in range(3):
        column_block = wrapped(block + (r - 1), blocks)
        first = pl.multiple_of((column_block * tiles + tile) * BLOCK, BLOCK)
        cells = cell[pl.ds(first, BLOCK), :]
        above_row, column = split(cells, width)
        _, grid_row = split(above_row, height)
        rows.append(grid_row)
        columns.append(column)
        sizes.append(variance[pl.ds(first, BLOCK), :])
        values[r * BLOCK : (r + 1) * BLOCK, :] = value[pl.ds(first, BLOCK), :]
    grid_row = jnp.concatenate(rows, axis=0)
    column = jnp.concatenate(columns, axis=0)
    size = jnp.concatenate(sizes, axis=0)

    def pieces(dt, p):
        if dt == 0:
            return [lists[p // per_side, p % per_side : p % per_side + 1, :]]
        source = south if dt < 0 else north
        each = slots // width
        return [
            source[24 + p * each + i : 25 + p * each + i, :].astype(jnp.int32) for i in range(each)
        ]

    index = 0
    for dt in (0, -1, 1):
        for p in range(patches):
            count = jnp.zeros((depth, LANES), f32)
            for part in pieces(dt, p):
                length = part.shape[1]
                region, within = split(part, BLOCK * LANES)
                region_column, region_row = split(region, tiles)
                line, lane = split(within, LANES)
                near = wrapped(region_column - block + 1, blocks)
                fits = (part >= 0) & (region_row == tile) & (near < 3)
                line = jnp.where(fits, near * BLOCK + line, -1)
                one = (iota((depth, length), 0) == line).astype(f32).astype(bf16)
                other = (iota((LANES, length), 0) == lane).astype(f32).astype(bf16)
                count += lax.dot_general(
                    one, other, (((1,), (1,)), ((), ())), preferred_element_type=f32
                )
            patch_row = (tile + dt) * per_side + p // per_side
            patch_column = block * per_side + p % per_side
            row_gap = (grid_row - patch_row * PATCH - PATCH // 2).astype(f32) + 0.5
            turned = column - patch_column * PATCH - PATCH // 2 + width // 2
            column_gap = (wrapped(turned, width) - width // 2).astype(f32) + 0.5
            near = jnp.exp(
                -(row_gap * row_gap + column_gap * column_gap) / (2.0 * LOC_LEN * LOC_LEN)
            )
            planes[index * depth : (index + 1) * depth, :] = count * (near / size)
            index += 1
    for extra in range(index, 16):
        planes[extra * depth : (extra + 1) * depth, :] = jnp.zeros((depth, LANES), f32)
    for i in range(depth):
        weights[:, i * LANES : (i + 1) * LANES] = planes[pl.ds(i, 16, stride=depth), :]


def halves(values):
    high = values.astype(bf16)
    return high, (values - high.astype(f32)).astype(bf16)


def dot_rows(left, right):
    return lax.dot_general(left, right, (((1,), (1,)), ((), ())), preferred_element_type=f32)


def systems_body(
    received, weights, values, own, to_south, to_north, planes, tall_high, tall_low, wide_high, wide_low, *, patches
):
    sources, all_rows, _ = received.shape
    depth = 3 * BLOCK
    region_rows = own_rows(received)
    members = (all_rows - region_rows) // depth
    ensemble = sources * members
    total = jnp.zeros((depth, LANES), f32)
    for s in range(sources):
        both = received[s, region_rows:all_rows, :].astype(f32)
        planes[s * members * depth : (s + 1) * members * depth, :] = both
        for b in range(members):
            total += both[b * depth : (b + 1) * depth, :]
    mean = total / ensemble
    for k in range(ensemble):
        planes[k * depth : (k + 1) * depth, :] -= mean
    planes[ensemble * depth : (ensemble + 1) * depth, :] = values[...] - mean
    for k in range(ensemble + 1, ensemble + 8):
        planes[k * depth : (k + 1) * depth, :] = jnp.zeros((depth, LANES), f32)
    for i in range(depth):
        at = slice(i * LANES, (i + 1) * LANES)
        tile = planes[pl.ds(i, ensemble + 8, stride=depth), :]
        high, low = halves(tile)
        wide_high[:, at] = high
        wide_low[:, at] = low
        spread = tile[0:ensemble, :]
        for p in range(3 * patches):
            high, low = halves(spread * weights[p : p + 1, at])
            tall_high[p * ensemble : (p + 1) * ensemble, at] = high
            tall_low[p * ensemble : (p + 1) * ensemble, at] = low
    result = (
        dot_rows(wide_high[...], tall_high[...])
        + dot_rows(wide_low[...], tall_high[...])
        + dot_rows(wide_high[...], tall_low[...])
    )
    count = patches * ensemble // 64
    for n in range(3 * count):
        target = (own, to_south, to_north)[n // count]
        at = n % count
        piece = result[:, n // 2 * LANES : (n // 2 + 1) * LANES] if n // 2 * LANES + LANES <= result.shape[1] else None
        if piece is None:
            piece = jnp.concatenate([result[:, n * 64 :], jnp.zeros((ensemble + 8, 64), f32)], axis=1)
        else:
            if n % 2:
                piece = pltpu.roll(piece, 64, 1)
            piece = jnp.where(iota(piece.shape, 1) < 64, piece, 0.0)
        target[:, at * LANES : (at + 1) * LANES] = piece


def own_rows(received):
    return 64


def analysis_body(received, own, south, north, send, centred, factors, *, patches):
    sources, all_rows, _ = received.shape
    region_rows = own_rows(received)
    members = send.shape[1] * sources // received.shape[0] // (region_rows // 2)
    ensemble = sources * members
    hits = region_rows // members
    total = jnp.zeros((hits, LANES), f32)
    for s in range(sources):
        part = received[s, 0:region_rows, :].astype(f32)
        for b in range(members):
            one = part[b * hits : (b + 1) * hits, :]
            centred[s * members + b] = one
            total += one
    mean = total / ensemble
    for k in range(ensemble):
        centred[k] -= mean

    count = patches * ensemble // 64
    group = 64 // ensemble
    row = iota((ensemble + 8, LANES), 0)
    lane = iota((ensemble + 8, LANES), 1)
    within = lane & (ensemble - 1)
    start = jnp.where(
        (row == within) & (row < ensemble), jnp.where(lane < 64, ensemble - 1.0, 1.0), 0.0
    )
    lane8 = iota((BLOCK, LANES), 1)
    group_start = (lane8 & 63) & ~(ensemble - 1)
    transforms = []
    for i in range(count):
        at = slice(i * LANES, (i + 1) * LANES)
        state = own[:, at] + south[:, at] + north[:, at] + start
        pivots = jnp.ones((ensemble, LANES), f32)
        for k in range(ensemble):
            column = pick_lanes(state, group_start + k)
            pivot = column[k : k + 1, :]
            scaled = state[k : k + 1, :] / pivot
            state = state - jnp.where(row > k, column, 0.0) * scaled
            pivots = jnp.where(row[0:ensemble] == k, pivot, pivots)
        inverse = state[0:ensemble, :] * lax.rsqrt(pivots)
        mean_weight = -state[ensemble : ensemble + 1, :]
        unit = jnp.where(row[0:ensemble] == within[0:ensemble], 1.0, 0.0)
        transforms.append(mean_weight + (ensemble - 1.0) ** 0.5 * inverse - unit)

    side_lanes = 32
    patch = (lane8 // (2 * side_lanes)) * 2 + (lane8 & (side_lanes - 1)) // PATCH
    inside = 64 + (patch & (group - 1)) * ensemble if group > 1 else 64 + 0 * patch
    which = patch // group
    for j in range(ensemble):
        chosen = pick_lanes(transforms[0], inside + j)
        for i in range(1, count):
            other = pick_lanes(transforms[i], inside + j)
            chosen = jnp.where(jnp.broadcast_to(which[0:1] == i, chosen.shape), other, chosen)
        factors[j] = chosen

    def one_destination(d, _):
        totals = [jnp.zeros((hits, LANES), f32) for _ in range(members)]
        for j in range(ensemble):
            block = centred[j]
            for b in range(members):
                totals[b] += factors[j, pl.ds(d * members + b, 1), :] * block
        send[d] = jnp.concatenate(totals, axis=0).astype(bf16)
        return 0

    lax.fori_loop(0, sources, one_destination, 0)


def output_body(forecast, received, analysis):
    members, levels, side, width = forecast.shape
    for q in range(width // LANES):
        parts = [received[4 * q + c].astype(f32) for c in range(4)]
        at = slice(q * LANES, (q + 1) * LANES)
        for r, part in enumerate(transpose_chunks(parts)):
            rows = slice(r * BLOCK, (r + 1) * BLOCK)
            analysis[:, :, rows, at] = forecast[:, :, rows, at] + part.reshape(
                members, levels, BLOCK, LANES
            )


def shards(member_concentration, courant_pairs, obs_cell, obs_value, obs_error, obs_list):
    members, levels, side, width = member_concentration.shape
    blocks = lax.axis_size("member")
    tiles = lax.axis_size("tile")
    height = side * tiles
    ensemble = members * blocks
    per_side = side // PATCH
    patches = per_side * per_side
    slots = obs_list.shape[2]
    region_rows = members * levels * BLOCK
    depth = 3 * BLOCK
    all_rows = region_rows + members * depth
    edge_rows = -(-(24 + patches * slots // width) // 8) * 8

    to_south, to_north = call(pack_edges, [((edge_rows, width), f32)] * 2)(
        member_concentration, courant_pairs, obs_list
    )
    up = [(i, i + 1) for i in range(tiles - 1)]
    down = [(i + 1, i) for i in range(tiles - 1)]
    south = lax.ppermute(to_north, "tile", up)
    north = lax.ppermute(to_south, "tile", down)

    flat = lambda array: array.reshape(-1, LANES)
    cell = flat(obs_cell)
    forecast, send = call(
        functools.partial(forecast_body, tiles=tiles, height=height),
        [(member_concentration.shape, f32), ((blocks, all_rows, LANES), bf16)],
        [pltpu.VMEM((blocks, region_rows, LANES), f32)],
    )(
        member_concentration,
        courant_pairs,
        to_south,
        to_north,
        south,
        north,
        cell.reshape(blocks, tiles * BLOCK, LANES),
    )
    received = lax.all_to_all(send, "member", split_axis=0, concat_axis=0, tiled=True)
    weights, values = call(
        functools.partial(
            weights_body, tiles=tiles, blocks=blocks, height=height, width=width, side=side
        ),
        [((16, depth * LANES), f32), ((depth, LANES), f32)],
        [pltpu.VMEM((16 * depth, LANES), f32)],
        flops=100_000_000,
    )(obs_list, south, north, cell, flat(obs_value), flat(obs_error))

    tall = 3 * patches * ensemble
    system_shape = (ensemble + 8, patches * ensemble // 64 * LANES)
    own, for_south, for_north = call(
        functools.partial(systems_body, patches=patches),
        [(system_shape, f32)] * 3,
        [
            pltpu.VMEM(((ensemble + 8) * depth, LANES), f32),
            pltpu.VMEM((tall, depth * LANES), bf16),
            pltpu.VMEM((tall, depth * LANES), bf16),
            pltpu.VMEM((ensemble + 8, depth * LANES), bf16),
            pltpu.VMEM((ensemble + 8, depth * LANES), bf16),
        ],
    )(received, weights, values)
    from_south = lax.ppermute(for_north, "tile", up)
    from_north = lax.ppermute(for_south, "tile", down)

    (change,) = call(
        functools.partial(analysis_body, patches=patches),
        [((blocks, region_rows, LANES), bf16)],
        [
            pltpu.VMEM((ensemble, levels * BLOCK, LANES), f32),
            pltpu.VMEM((ensemble, ensemble, LANES), f32),
        ],
    )(received, own, from_south, from_north)
    returned = lax.all_to_all(change, "member", split_axis=0, concat_axis=0, tiled=True)
    (analysis,) = call(output_body, [(forecast.shape, f32)])(forecast, returned)
    return analysis


def solution(mesh):
    return jax.shard_map(
        shards,
        mesh=mesh,
        in_specs=(
            P("member", None, "tile", None),
            P(None, None, "tile", None),
            P(),
            P(),
            P(),
            P("tile", "member", None),
        ),
        out_specs=P("member", None, "tile", None),
        check_vma=False,
    )
```

time: 209 us -> 47.8 us (0.23)
  the two profiles are of different devices: /device:TPU:9 before, /device:TPU:0 now
where the time goes in v1:
time: 47.8 us; the launch traced here: 47.3 us
  starting transfers between devices  15 us (31%)
  waiting for transfers between devices  14.2 us (30%)
  blocking collectives  7.92 us (17%)
  Pallas kernels  7.47 us (16%)
  local copies, waits for them, and re-layouts  2.63 us (6%)
    all_to_all x1, blocking collectives, shards(): lax.all_to_all(change, 'member', split_axis=0, concat_axis=0, tiled=True)  7.92 us
    all_to_all x1, waiting for transfers between devices, shards(): lax.all_to_all(send, 'member', split_axis=0, concat_axis=0, tiled=True)  5.36 us
    ppermute x1, starting transfers between devices, shards(): south = lax.ppermute(to_north, 'tile', up)  5.06 us
    ppermute x1, waiting for transfers between devices, shards(): north = lax.ppermute(to_south, 'tile', down)  4.24 us
    ppermute x1, waiting for transfers between devices, shards(): from_north = lax.ppermute(for_south, 'tile', down)  4.2 us
    all_to_all x1, starting transfers between devices, shards(): lax.all_to_all(send, 'member', split_axis=0, concat_axis=0, tiled=True)  3.85 us
    ppermute x1, starting transfers between devices, shards(): from_south = lax.ppermute(for_north, 'tile', up)  3.48 us
    unnamed x14, local copies, waits for them, and re-layouts  2.63 us
  transfers between devices with their start and end apart: 5, of which 5 were waited for; matrix products, arithmetic and copies ran while one was open for 0% of the time, Pallas kernels for 3%

profile of v1, /device:TPU:0, one launch (start us, length us, event | category | flops | bytes accessed | tf_op | source)
XLA Modules:
  0.0 47.3 jit_solution(9941153023158919827)
XLA Ops:
  0.0 0.0 copy-start
  0.0 0.9 %copy-done = f32[2,4,32,256]{3,2,1,0:T(8,128)S(1)} copy-done((f32[2,4,32,256]{3,2,1,0:T(8,128)S(1)}, f32[2,4,32,256]{3,2,1,0:T(8,128)}, u32[]{:S(2)}) %copy-start) | copy-done | bytes 262168
  1.0 0.9 %copy-done.1 = f32[2,4,32,256]{3,2,1,0:T(8,128)S(1)} copy-done((f32[2,4,32,256]{3,2,1,0:T(8,128)S(1)}, f32[2,4,32,256]{3,2,1,0:T(8,128)}, u32[]{:S(2)}) %copy-start.1) | copy-done | bytes 262168
  1.9 0.7 %copy-done.5 = s32[2,2,1024]{2,1,0:T(2,128)S(1)} copy-done((s32[2,2,1024]{2,1,0:T(2,128)S(1)}, s32[2,2,1024]{2,1,0:T(2,128)}, u32[]{:S(2)}) %copy-start.5) | copy-done | bytes 16408
  2.7 5.1 %collective-permute-start = (f32[40,256]{1,0:T(8,128)S(1)}, f32[40,256]{1,0:T(8,128)S(1)}, u32[]{:S(2)}, u32[]{:S(2)}) collective-permute-start(f32[40,256]{1,0:T(8,128)S(1)} %get-tuple-element.15.own_north), channel_id=1, source_target_pairs={{0,1},{1,2},{2,3},{4,5},{5,6},{6,7},{8,9},{9,10},{10,11},{12,13},{... | collective-permute-start | bytes 122888 | tf_op jit(solution)/shard_map/ppermute | solution.py:421
  7.7 1.3 %collective-permute-start.1 = (f32[40,256]{1,0:T(8,128)S(1)}, f32[40,256]{1,0:T(8,128)S(1)}, u32[]{:S(2)}, u32[]{:S(2)}) collective-permute-start(f32[40,256]{1,0:T(8,128)S(1)} %get-tuple-element.14.own_south), channel_id=1, source_target_pairs={{1,0},{2,1},{3,2},{5,4},{6,5},{7,6},{9,8},{10,9},{11,10},{13,12},{... | collective-permute-start | bytes 122888 | tf_op jit(solution)/shard_map/ppermute | solution.py:422
  9.0 0.4 collective-permute-done.south
  9.4 4.2 %collective-permute-done.1.north = f32[40,256]{1,0:T(8,128)S(1)} collective-permute-done((f32[40,256]{1,0:T(8,128)S(1)}, f32[40,256]{1,0:T(8,128)S(1)}, u32[]{:S(2)}, u32[]{:S(2)}) %collective-permute-start.1) | collective-permute-done | bytes 40992 | tf_op jit(solution)/shard_map/ppermute | solution.py:422
  13.6 0.0 copy-done.2
  13.6 2.1 %shard_map.65 = (f32[2,4,32,256]{3,2,1,0:T(8,128)S(1)}, bf16[8,112,128]{2,1,0:T(8,128)(2,1)}) custom-call(f32[2,4,32,256]{3,2,1,0:T(8,128)S(1)} %copy-done, f32[2,4,32,256]{3,2,1,0:T(8,128)S(1)} %copy-done.1, f32[40,256]{1,0:T(8,128)S(1)} %get-tuple-element.14.own_south, f32[40,256]{1,0:T(8,128)S(1)} %get-tuple-element.15.own_north, ...), custom_call_target="tpu_custom_call" | custom-call | flops 1000000 | bytes 1000000 | tf_op jit(solution)/shard_map/pallas_call | solution.py:426
  15.7 3.9 %all-to-all-start = ((bf16[8,112,128]{2,1,0:T(8,128)(2,1)}), bf16[8,112,128]{2,1,0:T(8,128)(2,1)S(1)}, u32[]{:S(2)}, u32[]{:S(2)}) async-start(bf16[8,112,128]{2,1,0:T(8,128)(2,1)} %get-tuple-element.17), calls=%async_computation | async-start | bytes 458752 | tf_op jit(solution)/shard_map/all_to_all | solution.py:439
  19.6 0.0 copy-done.3
  19.6 0.0 copy-done.4
  19.6 0.0 copy-done.6
  19.6 1.2 %shard_map.66 = (f32[16,3072]{1,0:T(8,128)S(1)}, f32[24,128]{1,0:T(8,128)S(1)}) custom-call(s32[2,2,1024]{2,1,0:T(2,128)S(1)} %copy-done.6, f32[40,256]{1,0:T(8,128)S(1)} %collective-permute-done.south, f32[40,256]{1,0:T(8,128)S(1)} %collective-permute-done.1.north, s32[256,128]{1,0:T(8,128)S(1)} %bitcast.5, f32[256,128]{1,0:T(8,128)S(1)} %bitcast.6, ...), custom_call_target="tpu_custom_call" | custom-call | flops 100000000 | bytes 1000000 | tf_op jit(solution)/shard_map/pallas_call | solution.py:440
  20.8 5.4 %all-to-all-done.received = bf16[8,112,128]{2,1,0:T(8,128)(2,1)S(1)} async-done(((bf16[8,112,128]{2,1,0:T(8,128)(2,1)}), bf16[8,112,128]{2,1,0:T(8,128)(2,1)S(1)}, u32[]{:S(2)}, u32[]{:S(2)}) %all-to-all-start) | async-done | bytes 229408 | tf_op jit(solution)/shard_map/all_to_all | solution.py:439
  26.2 1.4 %shard_map.67 = (f32[24,128]{1,0:T(8,128)S(1)}, f32[24,128]{1,0:T(8,128)S(1)}, f32[24,128]{1,0:T(8,128)S(1)}) custom-call(bf16[8,112,128]{2,1,0:T(8,128)(2,1)S(1)} %all-to-all-done.received, f32[16,3072]{1,0:T(8,128)S(1)} %get-tuple-element.18.weights, f32[24,128]{1,0:T(8,128)S(1)} %get-tuple-element.19.values), custom_call_target="tpu_custom_call" | custom-call | flops 1000000 | bytes 1000000 | tf_op jit(solution)/shard_map/pallas_call | solution.py:451
  27.6 3.5 %collective-permute-start.2 = (f32[24,128]{1,0:T(8,128)S(1)}, f32[24,128]{1,0:T(8,128)S(1)}, u32[]{:S(2)}, u32[]{:S(2)}) collective-permute-start(f32[24,128]{1,0:T(8,128)S(1)} %get-tuple-element.21), channel_id=1, source_target_pairs={{0,1},{1,2},{2,3},{4,5},{5,6},{6,7},{8,9},{9,10},{10,11},{12,13},{... | collective-permute-start | bytes 36872 | tf_op jit(solution)/shard_map/ppermute | solution.py:462
  31.1 1.3 %collective-permute-start.3 = (f32[24,128]{1,0:T(8,128)S(1)}, f32[24,128]{1,0:T(8,128)S(1)}, u32[]{:S(2)}, u32[]{:S(2)}) collective-permute-start(f32[24,128]{1,0:T(8,128)S(1)} %get-tuple-element.22), channel_id=1, source_target_pairs={{1,0},{2,1},{3,2},{5,4},{6,5},{7,6},{9,8},{10,9},{11,10},{13,12},{... | collective-permute-start | bytes 36872 | tf_op jit(solution)/shard_map/ppermute | solution.py:463
  32.4 0.1 collective-permute-done.2.south
  32.4 4.2 %collective-permute-done.3.north = f32[24,128]{1,0:T(8,128)S(1)} collective-permute-done((f32[24,128]{1,0:T(8,128)S(1)}, f32[24,128]{1,0:T(8,128)S(1)}, u32[]{:S(2)}, u32[]{:S(2)}) %collective-permute-start.3) | collective-permute-done | bytes 12320 | tf_op jit(solution)/shard_map/ppermute | solution.py:463
  36.6 1.9 %shard_map.68 = bf16[8,64,128]{2,1,0:T(8,128)(2,1)S(1)} custom-call(bf16[8,112,128]{2,1,0:T(8,128)(2,1)S(1)} %all-to-all-done.received, f32[24,128]{1,0:T(8,128)S(1)} %get-tuple-element.20.own, f32[24,128]{1,0:T(8,128)S(1)} %collective-permute-done.2.south, f32[24,128]{1,0:T(8,128)S(1)} %collective-permute-done.3.north), custom_call_target="tpu_custom_call" | custom-call | flops 1000000 | bytes 1000000 | tf_op jit(solution)/shard_map/pallas_call | solution.py:465
  38.5 7.9 %all_to_all.10.received = bf16[8,64,128]{2,1,0:T(8,128)(2,1)S(1)} all-to-all(bf16[8,64,128]{2,1,0:T(8,128)(2,1)S(1)} %shard_map.68), channel_id=1, replica_groups=mesh['member'=8,'tile'=4] {'member'}, dimensions={0} | all-to-all | bytes 262144 | tf_op jit(solution)/shard_map/all_to_all | solution.py:473
  46.4 0.9 %shard_map.69 = f32[2,4,32,256]{3,2,1,0:T(8,128)} custom-call(f32[2,4,32,256]{3,2,1,0:T(8,128)S(1)} %get-tuple-element.16.forecast, bf16[8,64,128]{2,1,0:T(8,128)(2,1)S(1)} %all_to_all.10.received), custom_call_target="tpu_custom_call" | custom-call | flops 1000000 | bytes 1000000 | tf_op jit(solution)/shard_map/pallas_call | solution.py:474
  (7 shorter events, 0.0 us)
Async XLA Ops:
  0.0 0.9 %copy-start = (f32[2,4,32,256]{3,2,1,0:T(8,128)S(1)}, f32[2,4,32,256]{3,2,1,0:T(8,128)}, u32[]{:S(2)}) copy-start(f32[2,4,32,256]{3,2,1,0:T(8,128)} %tracer.3) | copy-start | bytes 786436
  1.0 0.9 %copy-start.1 = (f32[2,4,32,256]{3,2,1,0:T(8,128)S(1)}, f32[2,4,32,256]{3,2,1,0:T(8,128)}, u32[]{:S(2)}) copy-start(f32[2,4,32,256]{3,2,1,0:T(8,128)} %courant.3) | copy-start | bytes 786436
  1.9 0.7 %copy-start.5 = (s32[2,2,1024]{2,1,0:T(2,128)S(1)}, s32[2,2,1024]{2,1,0:T(2,128)}, u32[]{:S(2)}) copy-start(s32[2,2,1024]{2,1,0:T(2,128)} %lists.3) | copy-start | bytes 49156
  2.6 11.0 %copy-start.2 = (s32[32768]{0:T(1024)S(1)}, s32[32768]{0:T(1024)}, u32[]{:S(2)}) copy-start(s32[32768]{0:T(1024)} %param.8) | copy-start | bytes 393220
  2.7 6.7 %collective-permute-start = (f32[40,256]{1,0:T(8,128)S(1)}, f32[40,256]{1,0:T(8,128)S(1)}, u32[]{:S(2)}, u32[]{:S(2)}) collective-permute-start(f32[40,256]{1,0:T(8,128)S(1)} %get-tuple-element.15.own_north), channel_id=1, source_target_pairs={{0,1},{1,2},{2,3},{4,5},{5,6},{6,7},{8,9},{9,10},{10,11},{12,13},{... | collective-permute-start | bytes 122888 | tf_op jit(solution)/shard_map/ppermute | solution.py:421
  7.7 5.9 %collective-permute-start.1 = (f32[40,256]{1,0:T(8,128)S(1)}, f32[40,256]{1,0:T(8,128)S(1)}, u32[]{:S(2)}, u32[]{:S(2)}) collective-permute-start(f32[40,256]{1,0:T(8,128)S(1)} %get-tuple-element.14.own_south), channel_id=1, source_target_pairs={{1,0},{2,1},{3,2},{5,4},{6,5},{7,6},{9,8},{10,9},{11,10},{13,12},{... | collective-permute-start | bytes 122888 | tf_op jit(solution)/shard_map/ppermute | solution.py:422
  15.7 3.9 %copy-start.3 = (f32[32768]{0:T(1024)S(1)}, f32[32768]{0:T(1024)}, u32[]{:S(2)}) copy-start(f32[32768]{0:T(1024)} %param.9) | copy-start | bytes 393220
  15.7 3.9 %copy-start.4 = (f32[32768]{0:T(1024)S(1)}, f32[32768]{0:T(1024)}, u32[]{:S(2)}) copy-start(f32[32768]{0:T(1024)} %param.10) | copy-start | bytes 393220
  15.7 3.9 %copy-start.6 = (s32[2,2,1024]{2,1,0:T(2,128)S(1)}, s32[2,2,1024]{2,1,0:T(2,128)}, u32[]{:S(2)}) copy-start(s32[2,2,1024]{2,1,0:T(2,128)} %lists.3) | copy-start | bytes 49156
  15.7 10.4 %all-to-all-start = ((bf16[8,112,128]{2,1,0:T(8,128)(2,1)}), bf16[8,112,128]{2,1,0:T(8,128)(2,1)S(1)}, u32[]{:S(2)}, u32[]{:S(2)}) async-start(bf16[8,112,128]{2,1,0:T(8,128)(2,1)} %get-tuple-element.17), calls=%async_computation | async-start | bytes 458752 | tf_op jit(solution)/shard_map/all_to_all | solution.py:439
  27.6 4.9 %collective-permute-start.2 = (f32[24,128]{1,0:T(8,128)S(1)}, f32[24,128]{1,0:T(8,128)S(1)}, u32[]{:S(2)}, u32[]{:S(2)}) collective-permute-start(f32[24,128]{1,0:T(8,128)S(1)} %get-tuple-element.21), channel_id=1, source_target_pairs={{0,1},{1,2},{2,3},{4,5},{5,6},{6,7},{8,9},{9,10},{10,11},{12,13},{... | collective-permute-start | bytes 36872 | tf_op jit(solution)/shard_map/ppermute | solution.py:462
  31.1 5.6 %collective-permute-start.3 = (f32[24,128]{1,0:T(8,128)S(1)}, f32[24,128]{1,0:T(8,128)S(1)}, u32[]{:S(2)}, u32[]{:S(2)}) collective-permute-start(f32[24,128]{1,0:T(8,128)S(1)} %get-tuple-element.22), channel_id=1, source_target_pairs={{1,0},{2,1},{3,2},{5,4},{6,5},{7,6},{9,8},{10,9},{11,10},{13,12},{... | collective-permute-start | bytes 36872 | tf_op jit(solution)/shard_map/ppermute | solution.py:463

commit v2 on v1

--- a/solution.py
+++ b/solution.py
@@ -17,9 +17,11 @@
 bf16 = jnp.bfloat16
 
 
-def call(body, outs, scratch=(), flops=1_000_000, moved=1_000_000):
+def call(body, outs, scratch=(), flops=1_000_000, moved=1_000_000, specs=None):
+    specs = {} if specs is None else {"in_specs": specs}
     return pl.pallas_call(
         body,
+        **specs,
         out_shape=[jax.ShapeDtypeStruct(shape, kind) for shape, kind in outs],
         scratch_shapes=list(scratch),
         compiler_params=pltpu.CompilerParams(vmem_limit_bytes=48 * 1024 * 1024),
@@ -68,27 +70,41 @@
     return parts
 
 
-def pack_edges(tracer, courant, lists, to_south, to_north):
+def pack_edges(tracer, courant, lists, edges, first, last, first_rates, last_rates, numbers, arrived):
     members, levels, side, width = tracer.shape
+    copies = [
+        pltpu.make_async_copy(source, target, arrived.at[i])
+        for i, (source, target) in enumerate(
+            (
+                (tracer.at[:, :, 0:BLOCK, :], first),
+                (tracer.at[:, :, side - BLOCK : side, :], last),
+                (courant.at[:, :, 0:BLOCK, :], first_rates),
+                (courant.at[:, :, side - BLOCK : side, :], last_rates),
+                (lists, numbers),
+            )
+        )
+    ]
+    for copy in copies:
+        copy.start()
+    for copy in copies:
+        copy.wait()
     for b in range(members):
         for l in range(levels):
             row = b * levels + l
-            to_south[row : row + 1, :] = tracer[b, l, 0:1, :]
-            to_south[8 + row : 9 + row, :] = tracer[b, l, 1:2, :]
-            to_north[row : row + 1, :] = tracer[b, l, side - 1 : side, :]
-            to_north[8 + row : 9 + row, :] = tracer[b, l, side - 2 : side - 1, :]
+            edges[row : row + 1, :] = first[b, l, 0:1, :]
+            edges[8 + row : 9 + row, :] = first[b, l, 1:2, :]
+            edges[24 + row : 25 + row, :] = last[b, l, BLOCK - 1 : BLOCK, :]
+            edges[32 + row : 33 + row, :] = last[b, l, BLOCK - 2 : BLOCK - 1, :]
     for c in range(2):
         for l in range(levels):
-            row = 16 + c * levels + l
-            to_south[row : row + 1, :] = courant[c, l, 0:1, :]
-            to_north[row : row + 1, :] = courant[c, l, side - 1 : side, :]
-    row = 24
-    for a in range(lists.shape[0]):
-        for b in range(lists.shape[1]):
-            for s in range(0, lists.shape[2], width):
-                part = lists[a, b : b + 1, s : s + width].astype(f32)
-                to_south[row : row + 1, :] = part
-                to_north[row : row + 1, :] = part
+            row = c * levels + l
+            edges[16 + row : 17 + row, :] = first_rates[c, l, 0:1, :]
+            edges[40 + row : 41 + row, :] = last_rates[c, l, BLOCK - 1 : BLOCK, :]
+    row = 48
+    for a in range(numbers.shape[0]):
+        for b in range(numbers.shape[1]):
+            for s in range(0, numbers.shape[2], width):
+                edges[row : row + 1, :] = numbers[a, b : b + 1, s : s + width].astype(f32)
                 row += 1
 
 
@@ -116,38 +132,43 @@
     )
 
 
-def forecast_body(
-    tracer, courant, own_south, own_north, south, north, cell, forecast, send, table, *, tiles, height
-):
+def beside(gathered, tile, tiles):
+    south = gathered.at[jnp.maximum(tile - 1, 0)]
+    north = gathered.at[jnp.minimum(tile + 1, tiles - 1)]
+    return south, north
+
+
+def forecast_body(tracer, courant, edges, cell, forecast, send, table, *, tiles, height):
     members, levels, side, width = tracer.shape
     blocks = width // side
     tile = lax.axis_index("tile")
     planes = members * levels
 
-    def edge(own, other):
-        twice = lambda first: jnp.concatenate([other[first : first + levels, :]] * members, axis=0)
-        return coefficients(twice(16), twice(16 + levels))
-
-    below = stencil(
-        south[0:planes, :], south[8 : 8 + planes, :], own_south[0:planes, :], edge(own_south, south)
-    )
-    above = stencil(
-        north[0:planes, :], own_north[0:planes, :], north[8 : 8 + planes, :], edge(own_north, north)
-    )
-    below = jnp.where(tile == 0, 0.0, below)
-    above = jnp.where(tile == tiles - 1, 0.0, above)
+    south, north = beside(edges, tile, tiles)
+    inside_south, inside_north = tile > 0, tile < tiles - 1
+    low = jnp.where(inside_south, south[24 : 24 + planes, :], 0.0)
+    lowest = south[32 : 32 + planes, :]
+    high = jnp.where(inside_north, north[0:planes, :], 0.0)
+    highest = north[8 : 8 + planes, :]
+
+    def edge(source, row):
+        twice = lambda first: jnp.concatenate([source[first : first + levels, :]] * members, axis=0)
+        return coefficients(twice(row), twice(row + levels))
+
+    below = stencil(low, lowest, edges[tile, 0:planes, :], edge(south, 40))
+    above = stencil(high, edges[tile, 24 : 24 + planes, :], highest, edge(north, 16))
+    below = jnp.where(inside_south, below, 0.0)
+    above = jnp.where(inside_north, above, 0.0)
     row = iota((side, width), 0)
     for l in range(levels):
         factors = coefficients(courant[0, l], courant[1, l])
         for b in range(members):
             plane = b * levels + l
             current = tracer[b, l]
-            for low, high in (
-                (south[plane : plane + 1, :], north[plane : plane + 1, :]),
-                (below[plane : plane + 1, :], above[plane : plane + 1, :]),
-            ):
-                lower = jnp.where(row == 0, low, pltpu.roll(current, 1, 0))
-                upper = jnp.where(row == side - 1, high, pltpu.roll(current, side - 1, 0))
+            for under, over in ((low, high), (below, above)):
+                under, over = under[plane : plane + 1, :], over[plane : plane + 1, :]
+                lower = jnp.where(row == 0, under, pltpu.roll(current, 1, 0))
+                upper = jnp.where(row == side - 1, over, pltpu.roll(current, side - 1, 0))
                 current = stencil(current, lower, upper, factors)
             forecast[b, l] = current
 
@@ -192,14 +213,14 @@
 
 
 def weights_body(
-    lists, south, north, cell, value, variance, weights, values, planes, *, tiles, blocks, height, width, side
+    lists, edges, cell, value, variance, weights, values, planes, *, tiles, blocks, height, width, side
 ):
     tile = lax.axis_index("tile")
     block = lax.axis_index("member")
+    south, north = beside(edges, tile, tiles)
     per_side = side // PATCH
     patches = per_side * per_side
     slots = lists.shape[2]
-    sub = slots // LANES
     depth = 3 * BLOCK
     rows, columns, sizes = [], [], []
     for r in range(3):
@@ -222,7 +243,7 @@
         source = south if dt < 0 else north
         each = slots // width
         return [
-            source[24 + p * each + i : 25 + p * each + i, :].astype(jnp.int32) for i in range(each)
+            source[48 + p * each + i : 49 + p * each + i, :].astype(jnp.int32) for i in range(each)
         ]
 
     index = 0
@@ -268,7 +289,7 @@
 
 
 def systems_body(
-    received, weights, values, own, to_south, to_north, planes, tall_high, tall_low, wide_high, wide_low, *, patches
+    received, weights, values, own, others, planes, tall_high, tall_low, wide_high, wide_low, *, patches
 ):
     sources, all_rows, _ = received.shape
     depth = 3 * BLOCK
@@ -305,7 +326,7 @@
     )
     count = patches * ensemble // 64
     for n in range(3 * count):
-        target = (own, to_south, to_north)[n // count]
+        target = (own, others.at[0], others.at[1])[n // count]
         at = n % count
         piece = result[:, n // 2 * LANES : (n // 2 + 1) * LANES] if n // 2 * LANES + LANES <= result.shape[1] else None
         if piece is None:
@@ -321,7 +342,7 @@
     return 64
 
 
-def analysis_body(received, own, south, north, send, centred, factors, *, patches):
+def analysis_body(received, own, others, send, centred, factors, *, patches, tiles):
     sources, all_rows, _ = received.shape
     region_rows = own_rows(received)
     members = send.shape[1] * sources // received.shape[0] // (region_rows // 2)
@@ -338,6 +359,10 @@
     for k in range(ensemble):
         centred[k] -= mean
 
+    tile = lax.axis_index("tile")
+    south, north = beside(others, tile, tiles)
+    south = jnp.where(tile > 0, south[1], 0.0)
+    north = jnp.where(tile < tiles - 1, north[0], 0.0)
     count = patches * ensemble // 64
     group = 64 // ensemble
     row = iota((ensemble + 8, LANES), 0)
@@ -411,15 +436,24 @@
     region_rows = members * levels * BLOCK
     depth = 3 * BLOCK
     all_rows = region_rows + members * depth
-    edge_rows = -(-(24 + patches * slots // width) // 8) * 8
-
-    to_south, to_north = call(pack_edges, [((edge_rows, width), f32)] * 2)(
-        member_concentration, courant_pairs, obs_list
-    )
-    up = [(i, i + 1) for i in range(tiles - 1)]
-    down = [(i + 1, i) for i in range(tiles - 1)]
-    south = lax.ppermute(to_north, "tile", up)
-    north = lax.ppermute(to_south, "tile", down)
+    edge_rows = -(-(48 + patches * slots // width) // 8) * 8
+    edge_shape = (members, levels, BLOCK, width)
+    rate_shape = (2, levels, BLOCK, width)
+
+    (own_edges,) = call(
+        pack_edges,
+        [((edge_rows, width), f32)],
+        [
+            pltpu.VMEM(edge_shape, f32),
+            pltpu.VMEM(edge_shape, f32),
+            pltpu.VMEM(rate_shape, f32),
+            pltpu.VMEM(rate_shape, f32),
+            pltpu.VMEM(obs_list.shape, jnp.int32),
+            pltpu.SemaphoreType.DMA((5,)),
+        ],
+        specs=[pl.BlockSpec(memory_space=pltpu.HBM)] * 3,
+    )(member_concentration, courant_pairs, obs_list)
+    edges = lax.all_gather(own_edges, "tile", axis=0, tiled=False)
 
     flat = lambda array: array.reshape(-1, LANES)
     cell = flat(obs_cell)
@@ -430,10 +464,7 @@
     )(
         member_concentration,
         courant_pairs,
-        to_south,
-        to_north,
-        south,
-        north,
+        edges,
         cell.reshape(blocks, tiles * BLOCK, LANES),
     )
     received = lax.all_to_all(send, "member", split_axis=0, concat_axis=0, tiled=True)
@@ -444,13 +475,13 @@
         [((16, depth * LANES), f32), ((depth, LANES), f32)],
         [pltpu.VMEM((16 * depth, LANES), f32)],
         flops=100_000_000,
-    )(obs_list, south, north, cell, flat(obs_value), flat(obs_error))
+    )(obs_list, edges, cell, flat(obs_value), flat(obs_error))
 
     tall = 3 * patches * ensemble
     system_shape = (ensemble + 8, patches * ensemble // 64 * LANES)
-    own, for_south, for_north = call(
+    own, for_others = call(
         functools.partial(systems_body, patches=patches),
-        [(system_shape, f32)] * 3,
+        [(system_shape, f32), ((2,) + system_shape, f32)],
         [
             pltpu.VMEM(((ensemble + 8) * depth, LANES), f32),
             pltpu.VMEM((tall, depth * LANES), bf16),
@@ -459,17 +490,16 @@
             pltpu.VMEM((ensemble + 8, depth * LANES), bf16),
         ],
     )(received, weights, values)
-    from_south = lax.ppermute(for_north, "tile", up)
-    from_north = lax.ppermute(for_south, "tile", down)
+    others = lax.all_gather(for_others, "tile", axis=0, tiled=False)
 
     (change,) = call(
-        functools.partial(analysis_body, patches=patches),
+        functools.partial(analysis_body, patches=patches, tiles=tiles),
         [((blocks, region_rows, LANES), bf16)],
         [
             pltpu.VMEM((ensemble, levels * BLOCK, LANES), f32),
             pltpu.VMEM((ensemble, ensemble, LANES), f32),
         ],
-    )(received, own, from_south, from_north)
+    )(received, own, others)
     returned = lax.all_to_all(change, "member", split_axis=0, concat_axis=0, tiled=True)
     (analysis,) = call(output_body, [(forecast.shape, f32)])(forecast, returned)
     return analysis

time: 47.8 us -> 56.9 us (1.19)
  blocking collectives: 7.92 us -> 37 us
  starting transfers between devices: 15 us -> 3.85 us
  waiting for transfers between devices: 14.2 us -> 5.36 us
    all_gather x0 -> x2, blocking collectives: none -> 29.1 us  [the longest x1 15.8 us: shards(): edges = lax.all_gather(own_edges, 'tile', axis=0, tiled=False)]
    ppermute x4 -> x0, starting transfers between devices: 11.1 us -> none  [the longest x1 5.06 us: shards(): south = lax.ppermute(to_north, 'tile', up)]
    ppermute x4 -> x0, waiting for transfers between devices: 8.88 us -> none  [the longest x1 4.24 us: shards(): north = lax.ppermute(to_south, 'tile', down)]
  transfers between devices with their start and end apart: 5 -> 1, of which waited for: 5 -> 1; matrix products, arithmetic and copies ran while one was open for 0% -> 0% of each run, Pallas kernels for 3% -> 2%
where the time goes in v2:
time: 56.9 us; the launch traced here: 56.5 us
  blocking collectives  37 us (65%)
  Pallas kernels  7.58 us (13%)
  waiting for transfers between devices  5.36 us (9%)
  starting transfers between devices  3.85 us (7%)
  local copies, waits for them, and re-layouts  2.63 us (5%)
    all_gather x1, blocking collectives, shards(): edges = lax.all_gather(own_edges, 'tile', axis=0, tiled=False)  15.8 us
    all_gather x1, blocking collectives, shards(): others = lax.all_gather(for_others, 'tile', axis=0, tiled=False)  13.3 us
    all_to_all x1, blocking collectives, shards(): lax.all_to_all(change, 'member', split_axis=0, concat_axis=0, tiled=True)  7.92 us
    all_to_all x1, waiting for transfers between devices, shards(): lax.all_to_all(send, 'member', split_axis=0, concat_axis=0, tiled=True)  5.36 us
    all_to_all x1, starting transfers between devices, shards(): lax.all_to_all(send, 'member', split_axis=0, concat_axis=0, tiled=True)  3.85 us
    unnamed x14, local copies, waits for them, and re-layouts  2.63 us
    pallas_call x1, Pallas kernels, shards(): call(functools.partial(forecast_body, tiles=tiles, height=height), [(memb...  2.08 us
    pallas_call x1, Pallas kernels, shards(): call(functools.partial(analysis_body, patches=patches, tiles=tiles), [((b...  1.85 us
  transfers between devices with their start and end apart: 1, of which 1 were waited for; matrix products, arithmetic and copies ran while one was open for 0% of the time, Pallas kernels for 2%

profile of v2, /device:TPU:0, one launch (start us, length us, event | category | flops | bytes accessed | tf_op | source)
XLA Modules:
  0.0 56.5 jit_solution(8354348470532125061)
XLA Ops:
  0.0 0.0 copy-start
  0.0 0.9 %copy-done = f32[2,4,32,256]{3,2,1,0:T(8,128)S(1)} copy-done((f32[2,4,32,256]{3,2,1,0:T(8,128)S(1)}, f32[2,4,32,256]{3,2,1,0:T(8,128)}, u32[]{:S(2)}) %copy-start) | copy-done | bytes 262168
  1.0 0.0 copy-start.1
  1.0 0.9 %copy-done.1 = f32[2,4,32,256]{3,2,1,0:T(8,128)S(1)} copy-done((f32[2,4,32,256]{3,2,1,0:T(8,128)S(1)}, f32[2,4,32,256]{3,2,1,0:T(8,128)}, u32[]{:S(2)}) %copy-start.1) | copy-done | bytes 262168
  1.9 0.0 copy-start.5
  1.9 0.7 %copy-done.5 = s32[2,2,1024]{2,1,0:T(2,128)S(1)} copy-done((s32[2,2,1024]{2,1,0:T(2,128)S(1)}, s32[2,2,1024]{2,1,0:T(2,128)}, u32[]{:S(2)}) %copy-start.5) | copy-done | bytes 16408
  2.6 0.1 shard_map.64
  2.8 0.0 copy-start.2
  2.8 15.8 %all-gather = f32[256,256]{1,0:T(8,128)S(1)} all-gather(f32[64,256]{1,0:T(8,128)S(1)} %shard_map.64), channel_id=2, replica_groups=mesh['member'=8,'tile'=4] {'tile'}, dimensions={0}, use_global_device_ids=true | all-gather | bytes 327680 | tf_op jit(solution)/shard_map/all_gather | solution.py:456
  18.5 0.0 copy-done.2
  18.6 2.1 %shard_map.65 = (f32[2,4,32,256]{3,2,1,0:T(8,128)S(1)}, bf16[8,112,128]{2,1,0:T(8,128)(2,1)}) custom-call(f32[2,4,32,256]{3,2,1,0:T(8,128)S(1)} %copy-done, f32[2,4,32,256]{3,2,1,0:T(8,128)S(1)} %copy-done.1, f32[4,64,256]{2,1,0:T(8,128)S(1)} %bitcast.6, s32[8,32,128]{2,1,0:T(8,128)S(1)} %bitcast.8), custom_call_target="tpu_custom_call" | custom-call | flops 1000000 | bytes 1000000 | tf_op jit(solution)/shard_map/pallas_call | solution.py:460
  20.6 0.0 copy-start.3
  20.6 0.0 copy-start.6
  20.6 3.9 %all-to-all-start = ((bf16[8,112,128]{2,1,0:T(8,128)(2,1)}), bf16[8,112,128]{2,1,0:T(8,128)(2,1)S(1)}, u32[]{:S(2)}, u32[]{:S(2)}) async-start(bf16[8,112,128]{2,1,0:T(8,128)(2,1)} %get-tuple-element.12), calls=%async_computation | async-start | bytes 458752 | tf_op jit(solution)/shard_map/all_to_all | solution.py:470
  24.5 0.0 copy-done.3
  24.5 0.0 copy-done.4
  24.5 0.0 copy-done.6
  24.5 1.2 %shard_map.66 = (f32[16,3072]{1,0:T(8,128)S(1)}, f32[24,128]{1,0:T(8,128)S(1)}) custom-call(s32[2,2,1024]{2,1,0:T(2,128)S(1)} %copy-done.6, f32[4,64,256]{2,1,0:T(8,128)S(1)} %bitcast.7, s32[256,128]{1,0:T(8,128)S(1)} %bitcast.9, f32[256,128]{1,0:T(8,128)S(1)} %bitcast.11, f32[256,128]{1,0:T(8,128)S(1)} %bitcast.12), custom_call_target="tpu_custom_call" | custom-call | flops 100000000 | bytes 1000000 | tf_op jit(solution)/shard_map/pallas_call | solution.py:471
  25.7 5.4 %all-to-all-done.received = bf16[8,112,128]{2,1,0:T(8,128)(2,1)S(1)} async-done(((bf16[8,112,128]{2,1,0:T(8,128)(2,1)}), bf16[8,112,128]{2,1,0:T(8,128)(2,1)S(1)}, u32[]{:S(2)}, u32[]{:S(2)}) %all-to-all-start) | async-done | bytes 229408 | tf_op jit(solution)/shard_map/all_to_all | solution.py:470
  31.1 1.4 %shard_map.67 = (f32[24,128]{1,0:T(8,128)S(1)}, f32[2,24,128]{2,1,0:T(8,128)S(1)}) custom-call(bf16[8,112,128]{2,1,0:T(8,128)(2,1)S(1)} %all-to-all-done.received, f32[16,3072]{1,0:T(8,128)S(1)} %get-tuple-element.13.weights, f32[24,128]{1,0:T(8,128)S(1)} %get-tuple-element.14.values), custom_call_target="tpu_custom_call" | custom-call | flops 1000000 | bytes 1000000 | tf_op jit(solution)/shard_map/pallas_call | solution.py:482
  32.5 13.3 %all-gather.1 = f32[8,24,128]{2,1,0:T(8,128)S(1)} all-gather(f32[2,24,128]{2,1,0:T(8,128)S(1)} %get-tuple-element.16), channel_id=3, replica_groups=mesh['member'=8,'tile'=4] {'tile'}, dimensions={0}, use_global_device_ids=true | all-gather | bytes 122880 | tf_op jit(solution)/shard_map/all_gather | solution.py:493
  45.8 1.9 %shard_map.68 = bf16[8,64,128]{2,1,0:T(8,128)(2,1)S(1)} custom-call(bf16[8,112,128]{2,1,0:T(8,128)(2,1)S(1)} %all-to-all-done.received, f32[24,128]{1,0:T(8,128)S(1)} %get-tuple-element.15.own, f32[4,2,24,128]{3,2,1,0:T(8,128)S(1)} %bitcast.10), custom_call_target="tpu_custom_call" | custom-call | flops 1000000 | bytes 1000000 | tf_op jit(solution)/shard_map/pallas_call | solution.py:495
  47.7 7.9 %all_to_all.10.received = bf16[8,64,128]{2,1,0:T(8,128)(2,1)S(1)} all-to-all(bf16[8,64,128]{2,1,0:T(8,128)(2,1)S(1)} %shard_map.68), channel_id=1, replica_groups=mesh['member'=8,'tile'=4] {'member'}, dimensions={0} | all-to-all | bytes 262144 | tf_op jit(solution)/shard_map/all_to_all | solution.py:503
  55.6 0.9 %shard_map.69 = f32[2,4,32,256]{3,2,1,0:T(8,128)} custom-call(f32[2,4,32,256]{3,2,1,0:T(8,128)S(1)} %get-tuple-element.11.forecast, bf16[8,64,128]{2,1,0:T(8,128)(2,1)S(1)} %all_to_all.10.received), custom_call_target="tpu_custom_call" | custom-call | flops 1000000 | bytes 1000000 | tf_op jit(solution)/shard_map/pallas_call | solution.py:504
  (1 shorter events, 0.0 us)
Async XLA Ops:
  0.0 0.9 %copy-start = (f32[2,4,32,256]{3,2,1,0:T(8,128)S(1)}, f32[2,4,32,256]{3,2,1,0:T(8,128)}, u32[]{:S(2)}) copy-start(f32[2,4,32,256]{3,2,1,0:T(8,128)} %tracer.3) | copy-start | bytes 786436
  1.0 0.9 %copy-start.1 = (f32[2,4,32,256]{3,2,1,0:T(8,128)S(1)}, f32[2,4,32,256]{3,2,1,0:T(8,128)}, u32[]{:S(2)}) copy-start(f32[2,4,32,256]{3,2,1,0:T(8,128)} %courant.3) | copy-start | bytes 786436
  1.9 0.7 %copy-start.5 = (s32[2,2,1024]{2,1,0:T(2,128)S(1)}, s32[2,2,1024]{2,1,0:T(2,128)}, u32[]{:S(2)}) copy-start(s32[2,2,1024]{2,1,0:T(2,128)} %lists.3) | copy-start | bytes 49156
  2.8 15.8 %copy-start.2 = (s32[32768]{0:T(1024)S(1)}, s32[32768]{0:T(1024)}, u32[]{:S(2)}) copy-start(s32[32768]{0:T(1024)} %param.8) | copy-start | bytes 393220
  20.6 3.9 %copy-start.3 = (f32[32768]{0:T(1024)S(1)}, f32[32768]{0:T(1024)}, u32[]{:S(2)}) copy-start(f32[32768]{0:T(1024)} %param.9) | copy-start | bytes 393220
  20.6 3.9 %copy-start.4 = (f32[32768]{0:T(1024)S(1)}, f32[32768]{0:T(1024)}, u32[]{:S(2)}) copy-start(f32[32768]{0:T(1024)} %param.10) | copy-start | bytes 393220
  20.6 3.9 %copy-start.6 = (s32[2,2,1024]{2,1,0:T(2,128)S(1)}, s32[2,2,1024]{2,1,0:T(2,128)}, u32[]{:S(2)}) copy-start(s32[2,2,1024]{2,1,0:T(2,128)} %lists.3) | copy-start | bytes 49156
  20.6 10.4 %all-to-all-start = ((bf16[8,112,128]{2,1,0:T(8,128)(2,1)}), bf16[8,112,128]{2,1,0:T(8,128)(2,1)S(1)}, u32[]{:S(2)}, u32[]{:S(2)}) async-start(bf16[8,112,128]{2,1,0:T(8,128)(2,1)} %get-tuple-element.12), calls=%async_computation | async-start | bytes 458752 | tf_op jit(solution)/shard_map/all_to_all | solution.py:470

commit v3 on v2

--- a/solution.py
+++ b/solution.py
@@ -17,14 +17,14 @@
 bf16 = jnp.bfloat16
 
 
-def call(body, outs, scratch=(), flops=1_000_000, moved=1_000_000, specs=None):
+def call(body, outs, scratch=(), flops=1_000_000, moved=1_000_000, specs=None, vmem=48):
     specs = {} if specs is None else {"in_specs": specs}
     return pl.pallas_call(
         body,
         **specs,
         out_shape=[jax.ShapeDtypeStruct(shape, kind) for shape, kind in outs],
         scratch_shapes=list(scratch),
-        compiler_params=pltpu.CompilerParams(vmem_limit_bytes=48 * 1024 * 1024),
+        compiler_params=pltpu.CompilerParams(vmem_limit_bytes=vmem * 1024 * 1024),
         cost_estimate=pl.CostEstimate(flops=flops, bytes_accessed=moved, transcendentals=0),
     )
 
@@ -70,7 +70,9 @@
     return parts
 
 
-def pack_edges(tracer, courant, lists, edges, first, last, first_rates, last_rates, numbers, arrived):
+def pack_edges(
+    tracer, courant, lists, to_first, to_second, first, last, first_rates, last_rates, numbers, arrived
+):
     members, levels, side, width = tracer.shape
     copies = [
         pltpu.make_async_copy(source, target, arrived.at[i])
@@ -88,23 +90,28 @@
         copy.start()
     for copy in copies:
         copy.wait()
+    even = lax.rem(lax.axis_index("tile"), 2) == 0
+
+    def put(row, low, high):
+        to_first[row : row + 1, :] = jnp.where(even, high, low)
+        to_second[row : row + 1, :] = jnp.where(even, low, high)
+
+    end = BLOCK - 1
     for b in range(members):
         for l in range(levels):
             row = b * levels + l
-            edges[row : row + 1, :] = first[b, l, 0:1, :]
-            edges[8 + row : 9 + row, :] = first[b, l, 1:2, :]
-            edges[24 + row : 25 + row, :] = last[b, l, BLOCK - 1 : BLOCK, :]
-            edges[32 + row : 33 + row, :] = last[b, l, BLOCK - 2 : BLOCK - 1, :]
+            put(row, first[b, l, 0:1, :], last[b, l, end : end + 1, :])
+            put(8 + row, first[b, l, 1:2, :], last[b, l, end - 1 : end, :])
     for c in range(2):
         for l in range(levels):
-            row = c * levels + l
-            edges[16 + row : 17 + row, :] = first_rates[c, l, 0:1, :]
-            edges[40 + row : 41 + row, :] = last_rates[c, l, BLOCK - 1 : BLOCK, :]
-    row = 48
+            put(16 + c * levels + l, first_rates[c, l, 0:1, :], last_rates[c, l, end : end + 1, :])
+    row = 24
     for a in range(numbers.shape[0]):
         for b in range(numbers.shape[1]):
             for s in range(0, numbers.shape[2], width):
-                edges[row : row + 1, :] = numbers[a, b : b + 1, s : s + width].astype(f32)
+                part = numbers[a, b : b + 1, s : s + width].astype(f32)
+                to_first[row : row + 1, :] = part
+                to_second[row : row + 1, :] = part
                 row += 1
 
 
@@ -132,31 +139,40 @@
     )
 
 
-def beside(gathered, tile, tiles):
-    south = gathered.at[jnp.maximum(tile - 1, 0)]
-    north = gathered.at[jnp.minimum(tile + 1, tiles - 1)]
-    return south, north
-
-
-def forecast_body(tracer, courant, edges, cell, forecast, send, table, *, tiles, height):
+def beside(first, second, tile):
+    even = lax.rem(tile, 2) == 0
+    return jnp.where(even, second, first), jnp.where(even, first, second)
+
+
+def swap(first, second, tiles):
+    pairs = lambda start: [
+        pair for i in range(start, tiles - 1, 2) for pair in ((i, i + 1), (i + 1, i))
+    ]
+    return lax.ppermute(first, "tile", pairs(0)), lax.ppermute(second, "tile", pairs(1))
+
+
+def forecast_body(
+    tracer, courant, first, second, cell, forecast, send, table, *, tiles, height
+):
     members, levels, side, width = tracer.shape
     blocks = width // side
     tile = lax.axis_index("tile")
     planes = members * levels
 
-    south, north = beside(edges, tile, tiles)
+    south, north = beside(first[0:24, :], second[0:24, :], tile)
+    own = lambda at: jnp.concatenate(
+        [tracer[b, l, at : at + 1, :] for b in range(members) for l in range(levels)], axis=0
+    )
     inside_south, inside_north = tile > 0, tile < tiles - 1
-    low = jnp.where(inside_south, south[24 : 24 + planes, :], 0.0)
-    lowest = south[32 : 32 + planes, :]
-    high = jnp.where(inside_north, north[0:planes, :], 0.0)
-    highest = north[8 : 8 + planes, :]
-
-    def edge(source, row):
-        twice = lambda first: jnp.concatenate([source[first : first + levels, :]] * members, axis=0)
-        return coefficients(twice(row), twice(row + levels))
-
-    below = stencil(low, lowest, edges[tile, 0:planes, :], edge(south, 40))
-    above = stencil(high, edges[tile, 24 : 24 + planes, :], highest, edge(north, 16))
+    low, lowest = south[0:planes], south[8 : 8 + planes]
+    high, highest = north[0:planes], north[8 : 8 + planes]
+
+    def edge(source):
+        twice = lambda at: jnp.concatenate([source[at : at + levels]] * members, axis=0)
+        return coefficients(twice(16), twice(16 + levels))
+
+    below = stencil(low, lowest, own(0), edge(south))
+    above = stencil(high, own(side - 1), highest, edge(north))
     below = jnp.where(inside_south, below, 0.0)
     above = jnp.where(inside_north, above, 0.0)
     row = iota((side, width), 0)
@@ -213,11 +229,12 @@
 
 
 def weights_body(
-    lists, edges, cell, value, variance, weights, values, planes, *, tiles, blocks, height, width, side
+    lists, first, second, cell, value, variance, weights, values, planes, *, tiles, blocks, height, width, side
 ):
     tile = lax.axis_index("tile")
     block = lax.axis_index("member")
-    south, north = beside(edges, tile, tiles)
+    own_lists = slice(24, 24 + lists.shape[0] * lists.shape[1] * lists.shape[2] // width)
+    south, north = beside(first[own_lists, :], second[own_lists, :], tile)
     per_side = side // PATCH
     patches = per_side * per_side
     slots = lists.shape[2]
@@ -243,7 +260,7 @@
         source = south if dt < 0 else north
         each = slots // width
         return [
-            source[48 + p * each + i : 49 + p * each + i, :].astype(jnp.int32) for i in range(each)
+            source[p * each + i : p * each + i + 1].astype(jnp.int32) for i in range(each)
         ]
 
     index = 0
@@ -289,7 +306,7 @@
 
 
 def systems_body(
-    received, weights, values, own, others, planes, tall_high, tall_low, wide_high, wide_low, *, patches
+    received, weights, values, own, to_first, to_second, planes, tall_high, tall_low, wide_high, wide_low, *, patches
 ):
     sources, all_rows, _ = received.shape
     depth = 3 * BLOCK
@@ -325,9 +342,9 @@
         + dot_rows(wide_high[...], tall_low[...])
     )
     count = patches * ensemble // 64
+    even = lax.rem(lax.axis_index("tile"), 2) == 0
+    found = []
     for n in range(3 * count):
-        target = (own, others.at[0], others.at[1])[n // count]
-        at = n % count
         piece = result[:, n // 2 * LANES : (n // 2 + 1) * LANES] if n // 2 * LANES + LANES <= result.shape[1] else None
         if piece is None:
             piece = jnp.concatenate([result[:, n * 64 :], jnp.zeros((ensemble + 8, 64), f32)], axis=1)
@@ -335,14 +352,20 @@
             if n % 2:
                 piece = pltpu.roll(piece, 64, 1)
             piece = jnp.where(iota(piece.shape, 1) < 64, piece, 0.0)
-        target[:, at * LANES : (at + 1) * LANES] = piece
+        found.append(piece)
+    for i in range(count):
+        at = slice(i * LANES, (i + 1) * LANES)
+        own[:, at] = found[i]
+        for_south, for_north = found[count + i], found[2 * count + i]
+        to_first[:, at] = jnp.where(even, for_north, for_south)
+        to_second[:, at] = jnp.where(even, for_south, for_north)
 
 
 def own_rows(received):
     return 64
 
 
-def analysis_body(received, own, others, send, centred, factors, *, patches, tiles):
+def analysis_body(received, own, first, second, send, centred, factors, *, patches):
     sources, all_rows, _ = received.shape
     region_rows = own_rows(received)
     members = send.shape[1] * sources // received.shape[0] // (region_rows // 2)
@@ -359,10 +382,6 @@
     for k in range(ensemble):
         centred[k] -= mean
 
-    tile = lax.axis_index("tile")
-    south, north = beside(others, tile, tiles)
-    south = jnp.where(tile > 0, south[1], 0.0)
-    north = jnp.where(tile < tiles - 1, north[0], 0.0)
     count = patches * ensemble // 64
     group = 64 // ensemble
     row = iota((ensemble + 8, LANES), 0)
@@ -376,7 +395,7 @@
     transforms = []
     for i in range(count):
         at = slice(i * LANES, (i + 1) * LANES)
-        state = own[:, at] + south[:, at] + north[:, at] + start
+        state = own[:, at] + first[:, at] + second[:, at] + start
         pivots = jnp.ones((ensemble, LANES), f32)
         for k in range(ensemble):
             column = pick_lanes(state, group_start + k)
@@ -436,13 +455,13 @@
     region_rows = members * levels * BLOCK
     depth = 3 * BLOCK
     all_rows = region_rows + members * depth
-    edge_rows = -(-(48 + patches * slots // width) // 8) * 8
+    edge_rows = -(-(24 + patches * slots // width) // 8) * 8
     edge_shape = (members, levels, BLOCK, width)
     rate_shape = (2, levels, BLOCK, width)
 
-    (own_edges,) = call(
+    to_first, to_second = call(
         pack_edges,
-        [((edge_rows, width), f32)],
+        [((edge_rows, width), f32)] * 2,
         [
             pltpu.VMEM(edge_shape, f32),
             pltpu.VMEM(edge_shape, f32),
@@ -452,8 +471,9 @@
             pltpu.SemaphoreType.DMA((5,)),
         ],
         specs=[pl.BlockSpec(memory_space=pltpu.HBM)] * 3,
+        vmem=63,
     )(member_concentration, courant_pairs, obs_list)
-    edges = lax.all_gather(own_edges, "tile", axis=0, tiled=False)
+    first, second = swap(to_first, to_second, tiles)
 
     flat = lambda array: array.reshape(-1, LANES)
     cell = flat(obs_cell)
@@ -464,7 +484,8 @@
     )(
         member_concentration,
         courant_pairs,
-        edges,
+        first,
+        second,
         cell.reshape(blocks, tiles * BLOCK, LANES),
     )
     received = lax.all_to_all(send, "member", split_axis=0, concat_axis=0, tiled=True)
@@ -475,13 +496,13 @@
         [((16, depth * LANES), f32), ((depth, LANES), f32)],
         [pltpu.VMEM((16 * depth, LANES), f32)],
         flops=100_000_000,
-    )(obs_list, edges, cell, flat(obs_value), flat(obs_error))
+    )(obs_list, first, second, cell, flat(obs_value), flat(obs_error))
 
     tall = 3 * patches * ensemble
     system_shape = (ensemble + 8, patches * ensemble // 64 * LANES)
-    own, for_others = call(
+    own, to_first, to_second = call(
         functools.partial(systems_body, patches=patches),
-        [(system_shape, f32), ((2,) + system_shape, f32)],
+        [(system_shape, f32)] * 3,
         [
             pltpu.VMEM(((ensemble + 8) * depth, LANES), f32),
             pltpu.VMEM((tall, depth * LANES), bf16),
@@ -490,16 +511,16 @@
             pltpu.VMEM((ensemble + 8, depth * LANES), bf16),
         ],
     )(received, weights, values)
-    others = lax.all_gather(for_others, "tile", axis=0, tiled=False)
+    first, second = swap(to_first, to_second, tiles)
 
     (change,) = call(
-        functools.partial(analysis_body, patches=patches, tiles=tiles),
+        functools.partial(analysis_body, patches=patches),
         [((blocks, region_rows, LANES), bf16)],
         [
             pltpu.VMEM((ensemble, levels * BLOCK, LANES), f32),
             pltpu.VMEM((ensemble, ensemble, LANES), f32),
         ],
-    )(received, own, others)
+    )(received, own, first, second)
     returned = lax.all_to_all(change, "member", split_axis=0, concat_axis=0, tiled=True)
     (analysis,) = call(output_body, [(forecast.shape, f32)])(forecast, returned)
     return analysis

time: 56.9 us -> 40.9 us (0.72)
  the two profiles are of different devices: /device:TPU:0 before, /device:TPU:16 now
where the time goes in v3:
time: 40.9 us; the launch traced here: 40.6 us
  waiting for transfers between devices  13.2 us (32%)
  starting transfers between devices  9.36 us (23%)
  Pallas kernels  9.12 us (22%)
  blocking collectives  7.92 us (19%)
  local copies, waits for them, and re-layouts  0.93 us (2%)
    all_to_all x1, blocking collectives, shards(): lax.all_to_all(change, 'member', split_axis=0, concat_axis=0, tiled=True)  7.92 us
    ppermute x2, waiting for transfers between devices, swap(): lax.ppermute(second, 'tile', pairs(1))  5.36 us
    all_to_all x1, waiting for transfers between devices, shards(): lax.all_to_all(send, 'member', split_axis=0, concat_axis=0, tiled=True)  5.36 us
    all_to_all x1, starting transfers between devices, shards(): lax.all_to_all(send, 'member', split_axis=0, concat_axis=0, tiled=True)  3.87 us
    ppermute x2, starting transfers between devices, swap(): lax.ppermute(second, 'tile', pairs(1))  3.83 us
    ppermute x2, waiting for transfers between devices, swap(): lax.ppermute(first, 'tile', pairs(0))  2.47 us
    pallas_call x1, Pallas kernels, shards(): call(functools.partial(forecast_body, tiles=tiles, height=height), [(memb...  2.08 us
    pallas_call x1, Pallas kernels, shards(): call(functools.partial(analysis_body, patches=patches), [((blocks, region...  1.85 us
  transfers between devices with their start and end apart: 5, of which 5 were waited for; matrix products, arithmetic and copies ran while one was open for 0% of the time, Pallas kernels for 3%

profile of v3, /device:TPU:16, one launch (start us, length us, event | category | flops | bytes accessed | tf_op | source)
XLA Modules:
  0.0 40.6 jit_solution(10830028287315869413)
XLA Ops:
  0.0 1.7 %shard_map.64 = (f32[40,256]{1,0:T(8,128)}, f32[40,256]{1,0:T(8,128)}) custom-call(f32[2,4,32,256]{3,2,1,0:T(8,128)} %tracer.3, f32[2,4,32,256]{3,2,1,0:T(8,128)} %courant.3, s32[2,2,1024]{2,1,0:T(2,128)} %lists.3), custom_call_target="tpu_custom_call" | custom-call | flops 1000000 | bytes 1000000 | tf_op jit(solution)/shard_map/pallas_call | solution.py:462
  1.7 1.6 %collective-permute-start = (f32[40,256]{1,0:T(8,128)}, f32[40,256]{1,0:T(8,128)S(1)}, u32[]{:S(2)}, u32[]{:S(2)}) collective-permute-start(f32[40,256]{1,0:T(8,128)} %get-tuple-element.14), channel_id=1, source_target_pairs={{0,1},{1,0},{2,3},{3,2},{4,5},{5,4},{6,7},{7,6},{8,9},{9,8},{10,11... | collective-permute-start | bytes 122888 | tf_op jit(solution)/shard_map/ppermute | solution.py:151
  3.4 1.9 %collective-permute-start.1 = (f32[40,256]{1,0:T(8,128)}, f32[40,256]{1,0:T(8,128)S(1)}, u32[]{:S(2)}, u32[]{:S(2)}) collective-permute-start(f32[40,256]{1,0:T(8,128)} %get-tuple-element.15), channel_id=1, source_target_pairs={{1,2},{2,1},{5,6},{6,5},{9,10},{10,9},{13,14},{14,13},{17,18},{18,... | collective-permute-start | bytes 122888 | tf_op jit(solution)/shard_map/ppermute | solution.py:151
  5.3 0.7 %collective-permute-done.first = f32[40,256]{1,0:T(8,128)S(1)} collective-permute-done((f32[40,256]{1,0:T(8,128)}, f32[40,256]{1,0:T(8,128)S(1)}, u32[]{:S(2)}, u32[]{:S(2)}) %collective-permute-start) | collective-permute-done | bytes 40992 | tf_op jit(solution)/shard_map/ppermute | solution.py:151
  6.0 3.5 %collective-permute-done.1.second = f32[40,256]{1,0:T(8,128)S(1)} collective-permute-done((f32[40,256]{1,0:T(8,128)}, f32[40,256]{1,0:T(8,128)S(1)}, u32[]{:S(2)}, u32[]{:S(2)}) %collective-permute-start.1) | collective-permute-done | bytes 40992 | tf_op jit(solution)/shard_map/ppermute | solution.py:151
  9.4 0.0 copy-done
  9.4 0.0 copy-done.1
  9.5 0.9 %copy-done.2 = s32[32768]{0:T(1024)S(1)} copy-done((s32[32768]{0:T(1024)S(1)}, s32[32768]{0:T(1024)}, u32[]{:S(2)}) %copy-start.2) | copy-done | bytes 131096
  10.4 2.1 %shard_map.65 = (f32[2,4,32,256]{3,2,1,0:T(8,128)S(1)}, bf16[8,112,128]{2,1,0:T(8,128)(2,1)}) custom-call(f32[2,4,32,256]{3,2,1,0:T(8,128)S(1)} %copy-done, f32[2,4,32,256]{3,2,1,0:T(8,128)S(1)} %copy-done.1, f32[40,256]{1,0:T(8,128)S(1)} %collective-permute-done.first, f32[40,256]{1,0:T(8,128)S(1)} %collective-permute-done.1.second, s32[8,32,128]{2,1,0:T(8,128)S(1)} %bitcast.4), custom_call_target="tpu_custom_call" | custom-call | flops 1000000 | bytes 1000000 | tf_op jit(solution)/shard_map/pallas_call | solution.py:480
  12.4 3.9 %all-to-all-start = ((bf16[8,112,128]{2,1,0:T(8,128)(2,1)}), bf16[8,112,128]{2,1,0:T(8,128)(2,1)S(1)}, u32[]{:S(2)}, u32[]{:S(2)}) async-start(bf16[8,112,128]{2,1,0:T(8,128)(2,1)} %get-tuple-element.17), calls=%async_computation | async-start | bytes 458752 | tf_op jit(solution)/shard_map/all_to_all | solution.py:491
  16.3 0.0 copy-done.3
  16.3 0.0 copy-done.4
  16.3 0.0 copy-done.5
  16.3 0.0 copy-done.6
  16.4 1.2 %shard_map.66 = (f32[16,3072]{1,0:T(8,128)S(1)}, f32[24,128]{1,0:T(8,128)S(1)}) custom-call(s32[2,2,1024]{2,1,0:T(2,128)S(1)} %copy-done.6, f32[40,256]{1,0:T(8,128)S(1)} %collective-permute-done.first, f32[40,256]{1,0:T(8,128)S(1)} %collective-permute-done.1.second, s32[256,128]{1,0:T(8,128)S(1)} %bitcast.5, f32[256,128]{1,0:T(8,128)S(1)} %bitcast.6, ...), custom_call_target="tpu_custom_call" | custom-call | flops 100000000 | bytes 1000000 | tf_op jit(solution)/shard_map/pallas_call | solution.py:492
  17.5 5.4 %all-to-all-done.received = bf16[8,112,128]{2,1,0:T(8,128)(2,1)S(1)} async-done(((bf16[8,112,128]{2,1,0:T(8,128)(2,1)}), bf16[8,112,128]{2,1,0:T(8,128)(2,1)S(1)}, u32[]{:S(2)}, u32[]{:S(2)}) %all-to-all-start) | async-done | bytes 229408 | tf_op jit(solution)/shard_map/all_to_all | solution.py:491
  22.9 1.4 %shard_map.67 = (f32[24,128]{1,0:T(8,128)S(1)}, f32[24,128]{1,0:T(8,128)S(1)}, f32[24,128]{1,0:T(8,128)S(1)}) custom-call(bf16[8,112,128]{2,1,0:T(8,128)(2,1)S(1)} %all-to-all-done.received, f32[16,3072]{1,0:T(8,128)S(1)} %get-tuple-element.18.weights, f32[24,128]{1,0:T(8,128)S(1)} %get-tuple-element.19.values), custom_call_target="tpu_custom_call" | custom-call | flops 1000000 | bytes 1000000 | tf_op jit(solution)/shard_map/pallas_call | solution.py:503
  24.3 0.0 collective-permute-start.2
  24.3 1.9 %collective-permute-start.3 = (f32[24,128]{1,0:T(8,128)S(1)}, f32[24,128]{1,0:T(8,128)S(1)}, u32[]{:S(2)}, u32[]{:S(2)}) collective-permute-start(f32[24,128]{1,0:T(8,128)S(1)} %get-tuple-element.22), channel_id=1, source_target_pairs={{1,2},{2,1},{5,6},{6,5},{9,10},{10,9},{13,14},{14,13},{17,18},{18,... | collective-permute-start | bytes 36872 | tf_op jit(solution)/shard_map/ppermute | solution.py:151
  26.3 1.8 %collective-permute-done.2.first = f32[24,128]{1,0:T(8,128)S(1)} collective-permute-done((f32[24,128]{1,0:T(8,128)S(1)}, f32[24,128]{1,0:T(8,128)S(1)}, u32[]{:S(2)}, u32[]{:S(2)}) %collective-permute-start.2) | collective-permute-done | bytes 12320 | tf_op jit(solution)/shard_map/ppermute | solution.py:151
  28.0 1.9 %collective-permute-done.3.second = f32[24,128]{1,0:T(8,128)S(1)} collective-permute-done((f32[24,128]{1,0:T(8,128)S(1)}, f32[24,128]{1,0:T(8,128)S(1)}, u32[]{:S(2)}, u32[]{:S(2)}) %collective-permute-start.3) | collective-permute-done | bytes 12320 | tf_op jit(solution)/shard_map/ppermute | solution.py:151
  29.9 1.9 %shard_map.68 = bf16[8,64,128]{2,1,0:T(8,128)(2,1)S(1)} custom-call(bf16[8,112,128]{2,1,0:T(8,128)(2,1)S(1)} %all-to-all-done.received, f32[24,128]{1,0:T(8,128)S(1)} %get-tuple-element.20.own, f32[24,128]{1,0:T(8,128)S(1)} %collective-permute-done.2.first, f32[24,128]{1,0:T(8,128)S(1)} %collective-permute-done.3.second), custom_call_target="tpu_custom_call" | custom-call | flops 1000000 | bytes 1000000 | tf_op jit(solution)/shard_map/pallas_call | solution.py:516
  31.8 7.9 %all_to_all.10.received = bf16[8,64,128]{2,1,0:T(8,128)(2,1)S(1)} all-to-all(bf16[8,64,128]{2,1,0:T(8,128)(2,1)S(1)} %shard_map.68), channel_id=1, replica_groups=mesh['member'=8,'tile'=4] {'member'}, dimensions={0} | all-to-all | bytes 262144 | tf_op jit(solution)/shard_map/all_to_all | solution.py:524
  39.7 0.9 %shard_map.69 = f32[2,4,32,256]{3,2,1,0:T(8,128)} custom-call(f32[2,4,32,256]{3,2,1,0:T(8,128)S(1)} %get-tuple-element.16.forecast, bf16[8,64,128]{2,1,0:T(8,128)(2,1)S(1)} %all_to_all.10.received), custom_call_target="tpu_custom_call" | custom-call | flops 1000000 | bytes 1000000 | tf_op jit(solution)/shard_map/pallas_call | solution.py:525
  (7 shorter events, 0.0 us)
Async XLA Ops:
  0.0 9.4 %copy-start = (f32[2,4,32,256]{3,2,1,0:T(8,128)S(1)}, f32[2,4,32,256]{3,2,1,0:T(8,128)}, u32[]{:S(2)}) copy-start(f32[2,4,32,256]{3,2,1,0:T(8,128)} %tracer.3) | copy-start | bytes 786436
  0.0 9.4 %copy-start.1 = (f32[2,4,32,256]{3,2,1,0:T(8,128)S(1)}, f32[2,4,32,256]{3,2,1,0:T(8,128)}, u32[]{:S(2)}) copy-start(f32[2,4,32,256]{3,2,1,0:T(8,128)} %courant.3) | copy-start | bytes 786436
  1.7 4.3 %collective-permute-start = (f32[40,256]{1,0:T(8,128)}, f32[40,256]{1,0:T(8,128)S(1)}, u32[]{:S(2)}, u32[]{:S(2)}) collective-permute-start(f32[40,256]{1,0:T(8,128)} %get-tuple-element.14), channel_id=1, source_target_pairs={{0,1},{1,0},{2,3},{3,2},{4,5},{5,4},{6,7},{7,6},{8,9},{9,8},{10,11... | collective-permute-start | bytes 122888 | tf_op jit(solution)/shard_map/ppermute | solution.py:151
  3.4 6.1 %collective-permute-start.1 = (f32[40,256]{1,0:T(8,128)}, f32[40,256]{1,0:T(8,128)S(1)}, u32[]{:S(2)}, u32[]{:S(2)}) collective-permute-start(f32[40,256]{1,0:T(8,128)} %get-tuple-element.15), channel_id=1, source_target_pairs={{1,2},{2,1},{5,6},{6,5},{9,10},{10,9},{13,14},{14,13},{17,18},{18,... | collective-permute-start | bytes 122888 | tf_op jit(solution)/shard_map/ppermute | solution.py:151
  9.5 0.9 %copy-start.2 = (s32[32768]{0:T(1024)S(1)}, s32[32768]{0:T(1024)}, u32[]{:S(2)}) copy-start(s32[32768]{0:T(1024)} %param.8) | copy-start | bytes 393220
  12.4 3.9 %copy-start.3 = (s32[32768]{0:T(1024)S(1)}, s32[32768]{0:T(1024)}, u32[]{:S(2)}) copy-start(s32[32768]{0:T(1024)} %param.8) | copy-start | bytes 393220
  12.4 3.9 %copy-start.4 = (f32[32768]{0:T(1024)S(1)}, f32[32768]{0:T(1024)}, u32[]{:S(2)}) copy-start(f32[32768]{0:T(1024)} %param.9) | copy-start | bytes 393220
  12.4 3.9 %copy-start.5 = (f32[32768]{0:T(1024)S(1)}, f32[32768]{0:T(1024)}, u32[]{:S(2)}) copy-start(f32[32768]{0:T(1024)} %param.10) | copy-start | bytes 393220
  12.4 3.9 %copy-start.6 = (s32[2,2,1024]{2,1,0:T(2,128)S(1)}, s32[2,2,1024]{2,1,0:T(2,128)}, u32[]{:S(2)}) copy-start(s32[2,2,1024]{2,1,0:T(2,128)} %lists.3) | copy-start | bytes 49156
  12.4 10.5 %all-to-all-start = ((bf16[8,112,128]{2,1,0:T(8,128)(2,1)}), bf16[8,112,128]{2,1,0:T(8,128)(2,1)S(1)}, u32[]{:S(2)}, u32[]{:S(2)}) async-start(bf16[8,112,128]{2,1,0:T(8,128)(2,1)} %get-tuple-element.17), calls=%async_computation | async-start | bytes 458752 | tf_op jit(solution)/shard_map/all_to_all | solution.py:491
  24.3 3.7 %collective-permute-start.2 = (f32[24,128]{1,0:T(8,128)S(1)}, f32[24,128]{1,0:T(8,128)S(1)}, u32[]{:S(2)}, u32[]{:S(2)}) collective-permute-start(f32[24,128]{1,0:T(8,128)S(1)} %get-tuple-element.21), channel_id=1, source_target_pairs={{0,1},{1,0},{2,3},{3,2},{4,5},{5,4},{6,7},{7,6},{8,9},{9,8},{10,11... | collective-permute-start | bytes 36872 | tf_op jit(solution)/shard_map/ppermute | solution.py:151
  24.3 5.6 %collective-permute-start.3 = (f32[24,128]{1,0:T(8,128)S(1)}, f32[24,128]{1,0:T(8,128)S(1)}, u32[]{:S(2)}, u32[]{:S(2)}) collective-permute-start(f32[24,128]{1,0:T(8,128)S(1)} %get-tuple-element.22), channel_id=1, source_target_pairs={{1,2},{2,1},{5,6},{6,5},{9,10},{10,9},{13,14},{14,13},{17,18},{18,... | collective-permute-start | bytes 36872 | tf_op jit(solution)/shard_map/ppermute | solution.py:151

commit v4 on v3

--- a/solution.py
+++ b/solution.py
@@ -151,9 +151,17 @@
     return lax.ppermute(first, "tile", pairs(0)), lax.ppermute(second, "tile", pairs(1))
 
 
+def exchange(chunks):
+    size = len(chunks)
+    swaps = lambda s: [(i, i ^ s) for i in range(size)]
+    received = {s: lax.ppermute(chunks[s], "member", swaps(s)) for s in range(size - 1, 0, -1)}
+    return [chunks[0]] + [received[s] for s in range(1, size)]
+
+
 def forecast_body(
-    tracer, courant, first, second, cell, forecast, send, table, *, tiles, height
+    tracer, courant, first, second, cell, forecast, *rest, tiles, height
 ):
+    *chunks, send, table = rest
     members, levels, side, width = tracer.shape
     blocks = width // side
     tile = lax.axis_index("tile")
@@ -201,9 +209,8 @@
 
     hits = levels * BLOCK
     observed = []
-    first = pl.multiple_of(tile * BLOCK, BLOCK)
     for c in range(blocks):
-        cells = cell[c, pl.ds(first, BLOCK), :]
+        cells = cell[c]
         above_row, column = split(cells, width)
         level, grid_row = split(above_row, height)
         _, local_row = split(grid_row, side)
@@ -226,6 +233,9 @@
         for i in range(0, len(rows), 2):
             at = region_rows + i * BLOCK
             send[c, at : at + 2 * BLOCK, :] = jnp.concatenate(rows[i : i + 2], axis=0).astype(bf16)
+    block = lax.axis_index("member")
+    for s, chunk in enumerate(chunks):
+        chunk[...] = send[block ^ s]
 
 
 def weights_body(
@@ -305,18 +315,18 @@
     return lax.dot_general(left, right, (((1,), (1,)), ((), ())), preferred_element_type=f32)
 
 
-def systems_body(
-    received, weights, values, own, to_first, to_second, planes, tall_high, tall_low, wide_high, wide_low, *, patches
-):
-    sources, all_rows, _ = received.shape
+def systems_body(*refs, patches, sources, members, region_rows):
+    received, rest = refs[:sources], refs[sources:]
+    weights, values, own, to_first, to_second, planes, tall_high, tall_low, wide_high, wide_low = rest
     depth = 3 * BLOCK
-    region_rows = own_rows(received)
-    members = (all_rows - region_rows) // depth
+    all_rows = received[0].shape[0]
+    block = lax.axis_index("member")
     ensemble = sources * members
     total = jnp.zeros((depth, LANES), f32)
     for s in range(sources):
-        both = received[s, region_rows:all_rows, :].astype(f32)
-        planes[s * members * depth : (s + 1) * members * depth, :] = both
+        both = received[s][region_rows:all_rows, :].astype(f32)
+        at = pl.multiple_of((block ^ s) * (members * depth), BLOCK)
+        planes[pl.ds(at, members * depth), :] = both
         for b in range(members):
             total += both[b * depth : (b + 1) * depth, :]
     mean = total / ensemble
@@ -361,22 +371,19 @@
         to_second[:, at] = jnp.where(even, for_south, for_north)
 
 
-def own_rows(received):
-    return 64
-
-
-def analysis_body(received, own, first, second, send, centred, factors, *, patches):
-    sources, all_rows, _ = received.shape
-    region_rows = own_rows(received)
-    members = send.shape[1] * sources // received.shape[0] // (region_rows // 2)
+def analysis_body(*refs, patches, sources, members, region_rows):
+    received, rest = refs[:sources], refs[sources:]
+    own, first, second = rest[:3]
+    chunks, (centred, factors) = rest[3:-2], rest[-2:]
+    block = lax.axis_index("member")
     ensemble = sources * members
     hits = region_rows // members
     total = jnp.zeros((hits, LANES), f32)
     for s in range(sources):
-        part = received[s, 0:region_rows, :].astype(f32)
+        part = received[s][0:region_rows, :].astype(f32)
         for b in range(members):
             one = part[b * hits : (b + 1) * hits, :]
-            centred[s * members + b] = one
+            centred[(block ^ s) * members + b] = one
             total += one
     mean = total / ensemble
     for k in range(ensemble):
@@ -419,22 +426,24 @@
             chosen = jnp.where(jnp.broadcast_to(which[0:1] == i, chosen.shape), other, chosen)
         factors[j] = chosen
 
-    def one_destination(d, _):
+    for s, chunk in enumerate(chunks):
+        target = block ^ s
         totals = [jnp.zeros((hits, LANES), f32) for _ in range(members)]
         for j in range(ensemble):
-            block = centred[j]
+            centred_j = centred[j]
             for b in range(members):
-                totals[b] += factors[j, pl.ds(d * members + b, 1), :] * block
-        send[d] = jnp.concatenate(totals, axis=0).astype(bf16)
-        return 0
-
-    lax.fori_loop(0, sources, one_destination, 0)
-
-
-def output_body(forecast, received, analysis):
+                totals[b] += factors[j, pl.ds(target * members + b, 1), :] * centred_j
+        chunk[...] = jnp.concatenate(totals, axis=0).astype(bf16)
+
+
+def output_body(forecast, *refs):
+    received, (analysis, ordered) = refs[:-2], refs[-2:]
     members, levels, side, width = forecast.shape
+    block = lax.axis_index("member")
+    for s, part in enumerate(received):
+        ordered[block ^ s] = part[...].astype(f32)
     for q in range(width // LANES):
-        parts = [received[4 * q + c].astype(f32) for c in range(4)]
+        parts = [ordered[4 * q + c] for c in range(4)]
         at = slice(q * LANES, (q + 1) * LANES)
         for r, part in enumerate(transpose_chunks(parts)):
             rows = slice(r * BLOCK, (r + 1) * BLOCK)
@@ -477,18 +486,24 @@
 
     flat = lambda array: array.reshape(-1, LANES)
     cell = flat(obs_cell)
-    forecast, send = call(
+    cell_row = lax.dynamic_index_in_dim(
+        cell.reshape(blocks, tiles, BLOCK, LANES), lax.axis_index("tile"), 1, False
+    )
+    forecast, *chunks = call(
         functools.partial(forecast_body, tiles=tiles, height=height),
-        [(member_concentration.shape, f32), ((blocks, all_rows, LANES), bf16)],
-        [pltpu.VMEM((blocks, region_rows, LANES), f32)],
+        [(member_concentration.shape, f32)] + [((all_rows, LANES), bf16)] * blocks,
+        [
+            pltpu.VMEM((blocks, all_rows, LANES), bf16),
+            pltpu.VMEM((blocks, region_rows, LANES), f32),
+        ],
     )(
         member_concentration,
         courant_pairs,
         first,
         second,
-        cell.reshape(blocks, tiles * BLOCK, LANES),
-    )
-    received = lax.all_to_all(send, "member", split_axis=0, concat_axis=0, tiled=True)
+        cell_row,
+    )
+    received = exchange(chunks)
     weights, values = call(
         functools.partial(
             weights_body, tiles=tiles, blocks=blocks, height=height, width=width, side=side
@@ -498,10 +513,11 @@
         flops=100_000_000,
     )(obs_list, first, second, cell, flat(obs_value), flat(obs_error))
 
+    sizes = dict(patches=patches, sources=blocks, members=members, region_rows=region_rows)
     tall = 3 * patches * ensemble
     system_shape = (ensemble + 8, patches * ensemble // 64 * LANES)
     own, to_first, to_second = call(
-        functools.partial(systems_body, patches=patches),
+        functools.partial(systems_body, **sizes),
         [(system_shape, f32)] * 3,
         [
             pltpu.VMEM(((ensemble + 8) * depth, LANES), f32),
@@ -510,19 +526,21 @@
             pltpu.VMEM((ensemble + 8, depth * LANES), bf16),
             pltpu.VMEM((ensemble + 8, depth * LANES), bf16),
         ],
-    )(received, weights, values)
+    )(*received, weights, values)
     first, second = swap(to_first, to_second, tiles)
 
-    (change,) = call(
-        functools.partial(analysis_body, patches=patches),
-        [((blocks, region_rows, LANES), bf16)],
+    changes = call(
+        functools.partial(analysis_body, **sizes),
+        [((region_rows, LANES), bf16)] * blocks,
         [
             pltpu.VMEM((ensemble, levels * BLOCK, LANES), f32),
             pltpu.VMEM((ensemble, ensemble, LANES), f32),
         ],
-    )(received, own, first, second)
-    returned = lax.all_to_all(change, "member", split_axis=0, concat_axis=0, tiled=True)
-    (analysis,) = call(output_body, [(forecast.shape, f32)])(forecast, returned)
+    )(*received, own, first, second)
+    returned = exchange(changes)
+    (analysis,) = call(
+        output_body, [(forecast.shape, f32)], [pltpu.VMEM((blocks, region_rows, LANES), f32)]
+    )(forecast, *returned)
     return analysis
 
 

time: 40.9 us -> 40.2 us (0.983)
  the two profiles are of different devices: /device:TPU:16 before, /device:TPU:9 now
where the time goes in v4:
time: 40.2 us; the launch traced here: 39.6 us
  starting transfers between devices  23.8 us (59%)
  Pallas kernels  8.5 us (21%)
  waiting for transfers between devices  6.36 us (16%)
  local copies, waits for them, and re-layouts  0.79 us (2%)
    ppermute x14, starting transfers between devices, exchange(): lax.ppermute(chunks[s], 'member', swaps(s))  15.5 us
    ppermute x2, starting transfers between devices, swap(): lax.ppermute(second, 'tile', pairs(1))  8.12 us
    ppermute x14, waiting for transfers between devices, exchange(): lax.ppermute(chunks[s], 'member', swaps(s))  4.5 us
    ppermute x2, waiting for transfers between devices, swap(): lax.ppermute(second, 'tile', pairs(1))  1.86 us
    pallas_call x1, Pallas kernels, shards(): call(functools.partial(analysis_body, **sizes), [((region_rows, LANES), b...  1.74 us
    pallas_call x1, Pallas kernels, shards(): call(pack_edges, [((edge_rows, width), f32)] * 2, [pltpu.VMEM(edge_shape,...  1.7 us
    pallas_call x1, Pallas kernels, shards(): call(functools.partial(systems_body, **sizes), [(system_shape, f32)] * 3,...  1.46 us
    pallas_call x1, Pallas kernels, shards(): call(functools.partial(forecast_body, tiles=tiles, height=height), [(memb...  1.41 us
  transfers between devices with their start and end apart: 18, of which 5 were waited for; matrix products, arithmetic and copies ran while one was open for 2% of the time, Pallas kernels for 3%

profile of v4, /device:TPU:9, one launch (start us, length us, event | category | flops | bytes accessed | tf_op | source)
XLA Modules:
  0.0 39.6 jit_solution(7066640789735184987)
XLA Ops:
  0.0 1.7 %shard_map.64 = (f32[40,256]{1,0:T(8,128)}, f32[40,256]{1,0:T(8,128)}) custom-call(f32[2,4,32,256]{3,2,1,0:T(8,128)} %tracer.3, f32[2,4,32,256]{3,2,1,0:T(8,128)} %courant.3, s32[2,2,1024]{2,1,0:T(2,128)} %lists.3), custom_call_target="tpu_custom_call" | custom-call | flops 1000000 | bytes 1000000 | tf_op jit(solution)/shard_map/pallas_call | solution.py:471
  1.8 4.5 %collective-permute-start.1 = (f32[40,256]{1,0:T(8,128)}, f32[40,256]{1,0:T(8,128)S(1)}, u32[]{:S(2)}, u32[]{:S(2)}) collective-permute-start(f32[40,256]{1,0:T(8,128)} %get-tuple-element.30), channel_id=1, source_target_pairs={{1,2},{2,1},{5,6},{6,5},{9,10},{10,9},{13,14},{14,13},{17,18},{18,... | collective-permute-start | bytes 122888 | tf_op jit(solution)/shard_map/ppermute | solution.py:151
  6.3 0.8 %dynamic-slice_bitcast_fusion.cell = s32[8,8,128]{2,1,0:T(8,128)S(1)} fusion(s32[8,4,8,128]{3,2,1,0:T(8,128)} %bitcast.6, s32[]{:T(128)S(6)} %select_n.4), kind=kLoop, calls=%fused_computation | loop fusion | bytes 65540 | tf_op jit(solution)/shard_map/jit(dynamic_index_in_dim)/squeeze | solution.py:489
  7.1 0.8 %collective-permute-done.1.second = f32[40,256]{1,0:T(8,128)S(1)} collective-permute-done((f32[40,256]{1,0:T(8,128)}, f32[40,256]{1,0:T(8,128)S(1)}, u32[]{:S(2)}, u32[]{:S(2)}) %collective-permute-start.1) | collective-permute-done | bytes 40992 | tf_op jit(solution)/shard_map/ppermute | solution.py:151
  7.9 1.4 %shard_map.65 = (f32[2,4,32,256]{3,2,1,0:T(8,128)S(1)}, bf16[112,128]{1,0:T(8,128)(2,1)S(1)}, bf16[112,128]{1,0:T(8,128)(2,1)S(1)}, bf16[112,128]{1,0:T(8,128)(2...) custom-call(f32[2,4,32,256]{3,2,1,0:T(8,128)S(1)} %copy-done, ...), custom_call_target="tpu_custom_call" | custom-call | flops 1000000 | bytes 1000000 | tf_op jit(solution)/shard_map/pallas_call | solution.py:492
  9.3 1.9 %collective-permute-start.2 = (bf16[112,128]{1,0:T(8,128)(2,1)S(1)}, bf16[112,128]{1,0:T(8,128)(2,1)S(1)}, u32[]{:S(2)}, u32[]{:S(2)}) collective-permute-start(bf16[112,128]{1,0:T(8,128)(2,1)S(1)} %get-tuple-element.33), channel_id=1, source_target_pairs={{0,4},{4,0},{8,12},{12,8},{16,20},{20,16},{24,28},{28,24},{1,5},{5... | collective-permute-start | bytes 86024 | tf_op jit(solution)/shard_map/ppermute | solution.py:157
  11.2 1.2 %collective-permute-start.3 = (bf16[112,128]{1,0:T(8,128)(2,1)S(1)}, bf16[112,128]{1,0:T(8,128)(2,1)S(1)}, u32[]{:S(2)}, u32[]{:S(2)}) collective-permute-start(bf16[112,128]{1,0:T(8,128)(2,1)S(1)} %get-tuple-element.34), channel_id=1, source_target_pairs={{0,8},{4,12},{8,0},{12,4},{16,24},{20,28},{24,16},{28,20},{1,9},{5... | collective-permute-start | bytes 86024 | tf_op jit(solution)/shard_map/ppermute | solution.py:157
  12.9 1.2 %collective-permute-start.5 = (bf16[112,128]{1,0:T(8,128)(2,1)S(1)}, bf16[112,128]{1,0:T(8,128)(2,1)S(1)}, u32[]{:S(2)}, u32[]{:S(2)}) collective-permute-start(bf16[112,128]{1,0:T(8,128)(2,1)S(1)} %get-tuple-element.36), channel_id=1, source_target_pairs={{0,16},{4,20},{8,24},{12,28},{16,0},{20,4},{24,8},{28,12},{1,17},{... | collective-permute-start | bytes 86024 | tf_op jit(solution)/shard_map/ppermute | solution.py:157
  14.7 2.2 %collective-permute-start.7 = (bf16[112,128]{1,0:T(8,128)(2,1)S(1)}, bf16[112,128]{1,0:T(8,128)(2,1)S(1)}, u32[]{:S(2)}, u32[]{:S(2)}) collective-permute-start(bf16[112,128]{1,0:T(8,128)(2,1)S(1)} %get-tuple-element.38), channel_id=1, source_target_pairs={{0,24},{4,28},{8,16},{12,20},{16,8},{20,12},{24,0},{28,4},{1,25},{... | collective-permute-start | bytes 86024 | tf_op jit(solution)/shard_map/ppermute | solution.py:157
  16.9 0.6 %collective-permute-start.8 = (bf16[112,128]{1,0:T(8,128)(2,1)S(1)}, bf16[112,128]{1,0:T(8,128)(2,1)S(1)}, u32[]{:S(2)}, u32[]{:S(2)}) collective-permute-start(bf16[112,128]{1,0:T(8,128)(2,1)S(1)} %get-tuple-element.39), channel_id=1, source_target_pairs={{0,28},{4,24},{8,20},{12,16},{16,12},{20,8},{24,4},{28,0},{1,29},{... | collective-permute-start | bytes 86024 | tf_op jit(solution)/shard_map/ppermute | solution.py:157
  17.5 1.2 %shard_map.66 = (f32[16,3072]{1,0:T(8,128)S(1)}, f32[24,128]{1,0:T(8,128)S(1)}) custom-call(s32[2,2,1024]{2,1,0:T(2,128)S(1)} %copy-done.5, f32[40,256]{1,0:T(8,128)S(1)} %collective-permute-done.first, f32[40,256]{1,0:T(8,128)S(1)} %collective-permute-done.1.second, s32[256,128]{1,0:T(8,128)S(1)} %bitcast.7, f32[256,128]{1,0:T(8,128)S(1)} %bitcast.8, ...), custom_call_target="tpu_custom_call" | custom-call | flops 100000000 | bytes 1000000 | tf_op jit(solution)/shard_map/pallas_call | solution.py:507
  18.7 2.4 %collective-permute-done.8.refs_7_ = bf16[112,128]{1,0:T(8,128)(2,1)S(1)} collective-permute-done((bf16[112,128]{1,0:T(8,128)(2,1)S(1)}, bf16[112,128]{1,0:T(8,128)(2,1)S(1)}, u32[]{:S(2)}, u32[]{:S(2)}) %collective-permute-start.8) | collective-permute-done | bytes 28704 | tf_op jit(solution)/shard_map/ppermute | solution.py:157
  21.1 1.5 %shard_map.67 = (f32[24,128]{1,0:T(8,128)S(1)}, f32[24,128]{1,0:T(8,128)S(1)}, f32[24,128]{1,0:T(8,128)S(1)}) custom-call(bf16[112,128]{1,0:T(8,128)(2,1)S(1)} %get-tuple-element.32.refs_0_, bf16[112,128]{1,0:T(8,128)(2,1)S(1)} %collective-permute-done.2.refs_1_, bf16[112,128]{1,0:T(8,128)(2,1)S(1)} %collective-permute-done.3.refs_2_, ...), custom_call_target="tpu_custom_call" | custom-call | flops 1000000 | bytes 1000000 | tf_op jit(solution)/shard_map/pallas_call | solution.py:519
  22.6 3.6 %collective-permute-start.10 = (f32[24,128]{1,0:T(8,128)S(1)}, f32[24,128]{1,0:T(8,128)S(1)}, u32[]{:S(2)}, u32[]{:S(2)}) collective-permute-start(f32[24,128]{1,0:T(8,128)S(1)} %get-tuple-element.44), channel_id=1, source_target_pairs={{1,2},{2,1},{5,6},{6,5},{9,10},{10,9},{13,14},{14,13},{17,18},{18,... | collective-permute-start | bytes 36872 | tf_op jit(solution)/shard_map/ppermute | solution.py:151
  26.2 1.1 %collective-permute-done.10.refs_10_ = f32[24,128]{1,0:T(8,128)S(1)} collective-permute-done((f32[24,128]{1,0:T(8,128)S(1)}, f32[24,128]{1,0:T(8,128)S(1)}, u32[]{:S(2)}, u32[]{:S(2)}) %collective-permute-start.10) | collective-permute-done | bytes 12320 | tf_op jit(solution)/shard_map/ppermute | solution.py:151
  27.3 1.7 %shard_map.68 = (bf16[64,128]{1,0:T(8,128)(2,1)S(1)}, bf16[64,128]{1,0:T(8,128)(2,1)S(1)}, bf16[64,128]{1,0:T(8,128)(2,1)S(1)}, bf16[64,128]{1,0:T(8,128)(2,1)S(...) custom-call(bf16[112,128]{1,0:T(8,128)(2,1)S(1)} %get-tuple-element., ...), custom_call_target="tpu_custom_call" | custom-call | flops 1000000 | bytes 1000000 | tf_op jit(solution)/shard_map/pallas_call | solution.py:532
  29.0 1.3 %collective-permute-start.11 = (bf16[64,128]{1,0:T(8,128)(2,1)S(1)}, bf16[64,128]{1,0:T(8,128)(2,1)S(1)}, u32[]{:S(2)}, u32[]{:S(2)}) collective-permute-start(bf16[64,128]{1,0:T(8,128)(2,1)S(1)} %get-tuple-element.46), channel_id=1, source_target_pairs={{0,4},{4,0},{8,12},{12,8},{16,20},{20,16},{24,28},{28,24},{1,5},{5... | collective-permute-start | bytes 49160 | tf_op jit(solution)/shard_map/ppermute | solution.py:157
  30.6 1.4 %collective-permute-start.13 = (bf16[64,128]{1,0:T(8,128)(2,1)S(1)}, bf16[64,128]{1,0:T(8,128)(2,1)S(1)}, u32[]{:S(2)}, u32[]{:S(2)}) collective-permute-start(bf16[64,128]{1,0:T(8,128)(2,1)S(1)} %get-tuple-element.48), channel_id=1, source_target_pairs={{0,12},{4,8},{8,4},{12,0},{16,28},{20,24},{24,20},{28,16},{1,13},{... | collective-permute-start | bytes 49160 | tf_op jit(solution)/shard_map/ppermute | solution.py:157
  32.2 1.6 %collective-permute-start.15 = (bf16[64,128]{1,0:T(8,128)(2,1)S(1)}, bf16[64,128]{1,0:T(8,128)(2,1)S(1)}, u32[]{:S(2)}, u32[]{:S(2)}) collective-permute-start(bf16[64,128]{1,0:T(8,128)(2,1)S(1)} %get-tuple-element.50), channel_id=1, source_target_pairs={{0,20},{4,16},{8,28},{12,24},{16,4},{20,0},{24,12},{28,8},{1,21},{... | collective-permute-start | bytes 49160 | tf_op jit(solution)/shard_map/ppermute | solution.py:157
  33.8 0.7 %collective-permute-start.16 = (bf16[64,128]{1,0:T(8,128)(2,1)S(1)}, bf16[64,128]{1,0:T(8,128)(2,1)S(1)}, u32[]{:S(2)}, u32[]{:S(2)}) collective-permute-start(bf16[64,128]{1,0:T(8,128)(2,1)S(1)} %get-tuple-element.51), channel_id=1, source_target_pairs={{0,24},{4,28},{8,16},{12,20},{16,8},{20,12},{24,0},{28,4},{1,25},{... | collective-permute-start | bytes 49160 | tf_op jit(solution)/shard_map/ppermute | solution.py:157
  34.5 1.9 %collective-permute-start.17 = (bf16[64,128]{1,0:T(8,128)(2,1)S(1)}, bf16[64,128]{1,0:T(8,128)(2,1)S(1)}, u32[]{:S(2)}, u32[]{:S(2)}) collective-permute-start(bf16[64,128]{1,0:T(8,128)(2,1)S(1)} %get-tuple-element.52), channel_id=1, source_target_pairs={{0,28},{4,24},{8,20},{12,16},{16,12},{20,8},{24,4},{28,0},{1,29},{... | collective-permute-start | bytes 49160 | tf_op jit(solution)/shard_map/ppermute | solution.py:157
  36.4 0.9 %collective-permute-done.16.refs_6_ = bf16[64,128]{1,0:T(8,128)(2,1)S(1)} collective-permute-done((bf16[64,128]{1,0:T(8,128)(2,1)S(1)}, bf16[64,128]{1,0:T(8,128)(2,1)S(1)}, u32[]{:S(2)}, u32[]{:S(2)}) %collective-permute-start.16) | collective-permute-done | bytes 16416 | tf_op jit(solution)/shard_map/ppermute | solution.py:157
  37.3 1.2 %collective-permute-done.17.refs_7_ = bf16[64,128]{1,0:T(8,128)(2,1)S(1)} collective-permute-done((bf16[64,128]{1,0:T(8,128)(2,1)S(1)}, bf16[64,128]{1,0:T(8,128)(2,1)S(1)}, u32[]{:S(2)}, u32[]{:S(2)}) %collective-permute-start.17) | collective-permute-done | bytes 16416 | tf_op jit(solution)/shard_map/ppermute | solution.py:157
  38.6 1.0 %shard_map.69 = f32[2,4,32,256]{3,2,1,0:T(8,128)} custom-call(f32[2,4,32,256]{3,2,1,0:T(8,128)S(1)} %get-tuple-element.31.forecast, bf16[64,128]{1,0:T(8,128)(2,1)S(1)} %get-tuple-element.45.refs_0_, bf16[64,128]{1,0:T(8,128)(2,1)S(1)} %collective-permute-done.11.refs_1_, bf16[64,128]{1,0:T(8,128)(2,1)S(1)} %collective-permute-done.12.refs_2_, ...), custom_call_target="tpu_custom_call" | custom-call | flops 1000000 | bytes 1000000 | tf_op jit(solution)/shard_map/pallas_call | solution.py:541
  (31 shorter events, 1.7 us)
Async XLA Ops:
  0.0 7.9 %copy-start = (f32[2,4,32,256]{3,2,1,0:T(8,128)S(1)}, f32[2,4,32,256]{3,2,1,0:T(8,128)}, u32[]{:S(2)}) copy-start(f32[2,4,32,256]{3,2,1,0:T(8,128)} %tracer.3) | copy-start | bytes 786436
  0.0 7.9 %copy-start.1 = (f32[2,4,32,256]{3,2,1,0:T(8,128)S(1)}, f32[2,4,32,256]{3,2,1,0:T(8,128)}, u32[]{:S(2)}) copy-start(f32[2,4,32,256]{3,2,1,0:T(8,128)} %courant.3) | copy-start | bytes 786436
  1.7 5.3 %collective-permute-start = (f32[40,256]{1,0:T(8,128)}, f32[40,256]{1,0:T(8,128)S(1)}, u32[]{:S(2)}, u32[]{:S(2)}) collective-permute-start(f32[40,256]{1,0:T(8,128)} %get-tuple-element.29), channel_id=1, source_target_pairs={{0,1},{1,0},{2,3},{3,2},{4,5},{5,4},{6,7},{7,6},{8,9},{9,8},{10,11... | collective-permute-start | bytes 122888 | tf_op jit(solution)/shard_map/ppermute | solution.py:151
  1.8 6.1 %collective-permute-start.1 = (f32[40,256]{1,0:T(8,128)}, f32[40,256]{1,0:T(8,128)S(1)}, u32[]{:S(2)}, u32[]{:S(2)}) collective-permute-start(f32[40,256]{1,0:T(8,128)} %get-tuple-element.30), channel_id=1, source_target_pairs={{1,2},{2,1},{5,6},{6,5},{9,10},{10,9},{13,14},{14,13},{17,18},{18,... | collective-permute-start | bytes 122888 | tf_op jit(solution)/shard_map/ppermute | solution.py:151
  7.0 10.4 %copy-start.2 = (s32[32768]{0:T(1024)S(1)}, s32[32768]{0:T(1024)}, u32[]{:S(2)}) copy-start(s32[32768]{0:T(1024)} %param.8) | copy-start | bytes 393220
  7.0 10.4 %copy-start.3 = (f32[32768]{0:T(1024)S(1)}, f32[32768]{0:T(1024)}, u32[]{:S(2)}) copy-start(f32[32768]{0:T(1024)} %param.9) | copy-start | bytes 393220
  7.0 10.4 %copy-start.4 = (f32[32768]{0:T(1024)S(1)}, f32[32768]{0:T(1024)}, u32[]{:S(2)}) copy-start(f32[32768]{0:T(1024)} %param.10) | copy-start | bytes 393220
  9.3 8.2 %copy-start.5 = (s32[2,2,1024]{2,1,0:T(2,128)S(1)}, s32[2,2,1024]{2,1,0:T(2,128)}, u32[]{:S(2)}) copy-start(s32[2,2,1024]{2,1,0:T(2,128)} %lists.3) | copy-start | bytes 49156
  9.3 5.4 %collective-permute-start.2 = (bf16[112,128]{1,0:T(8,128)(2,1)S(1)}, bf16[112,128]{1,0:T(8,128)(2,1)S(1)}, u32[]{:S(2)}, u32[]{:S(2)}) collective-permute-start(bf16[112,128]{1,0:T(8,128)(2,1)S(1)} %get-tuple-element.33), channel_id=1, source_target_pairs={{0,4},{4,0},{8,12},{12,8},{16,20},{20,16},{24,28},{28,24},{1,5},{5... | collective-permute-start | bytes 86024 | tf_op jit(solution)/shard_map/ppermute | solution.py:157
  11.2 5.7 %collective-permute-start.3 = (bf16[112,128]{1,0:T(8,128)(2,1)S(1)}, bf16[112,128]{1,0:T(8,128)(2,1)S(1)}, u32[]{:S(2)}, u32[]{:S(2)}) collective-permute-start(bf16[112,128]{1,0:T(8,128)(2,1)S(1)} %get-tuple-element.34), channel_id=1, source_target_pairs={{0,8},{4,12},{8,0},{12,4},{16,24},{20,28},{24,16},{28,20},{1,9},{5... | collective-permute-start | bytes 86024 | tf_op jit(solution)/shard_map/ppermute | solution.py:157
  12.4 6.3 %collective-permute-start.4 = (bf16[112,128]{1,0:T(8,128)(2,1)S(1)}, bf16[112,128]{1,0:T(8,128)(2,1)S(1)}, u32[]{:S(2)}, u32[]{:S(2)}) collective-permute-start(bf16[112,128]{1,0:T(8,128)(2,1)S(1)} %get-tuple-element.35), channel_id=1, source_target_pairs={{0,12},{4,8},{8,4},{12,0},{16,28},{20,24},{24,20},{28,16},{1,13},{... | collective-permute-start | bytes 86024 | tf_op jit(solution)/shard_map/ppermute | solution.py:157
  12.9 5.8 %collective-permute-start.5 = (bf16[112,128]{1,0:T(8,128)(2,1)S(1)}, bf16[112,128]{1,0:T(8,128)(2,1)S(1)}, u32[]{:S(2)}, u32[]{:S(2)}) collective-permute-start(bf16[112,128]{1,0:T(8,128)(2,1)S(1)} %get-tuple-element.36), channel_id=1, source_target_pairs={{0,16},{4,20},{8,24},{12,28},{16,0},{20,4},{24,8},{28,12},{1,17},{... | collective-permute-start | bytes 86024 | tf_op jit(solution)/shard_map/ppermute | solution.py:157
  14.1 4.5 %collective-permute-start.6 = (bf16[112,128]{1,0:T(8,128)(2,1)S(1)}, bf16[112,128]{1,0:T(8,128)(2,1)S(1)}, u32[]{:S(2)}, u32[]{:S(2)}) collective-permute-start(bf16[112,128]{1,0:T(8,128)(2,1)S(1)} %get-tuple-element.37), channel_id=1, source_target_pairs={{0,20},{4,16},{8,28},{12,24},{16,4},{20,0},{24,12},{28,8},{1,21},{... | collective-permute-start | bytes 86024 | tf_op jit(solution)/shard_map/ppermute | solution.py:157
  14.7 4.0 %collective-permute-start.7 = (bf16[112,128]{1,0:T(8,128)(2,1)S(1)}, bf16[112,128]{1,0:T(8,128)(2,1)S(1)}, u32[]{:S(2)}, u32[]{:S(2)}) collective-permute-start(bf16[112,128]{1,0:T(8,128)(2,1)S(1)} %get-tuple-element.38), channel_id=1, source_target_pairs={{0,24},{4,28},{8,16},{12,20},{16,8},{20,12},{24,0},{28,4},{1,25},{... | collective-permute-start | bytes 86024 | tf_op jit(solution)/shard_map/ppermute | solution.py:157
  16.9 4.2 %collective-permute-start.8 = (bf16[112,128]{1,0:T(8,128)(2,1)S(1)}, bf16[112,128]{1,0:T(8,128)(2,1)S(1)}, u32[]{:S(2)}, u32[]{:S(2)}) collective-permute-start(bf16[112,128]{1,0:T(8,128)(2,1)S(1)} %get-tuple-element.39), channel_id=1, source_target_pairs={{0,28},{4,24},{8,20},{12,16},{16,12},{20,8},{24,4},{28,0},{1,29},{... | collective-permute-start | bytes 86024 | tf_op jit(solution)/shard_map/ppermute | solution.py:157
  22.5 3.7 %collective-permute-start.9 = (f32[24,128]{1,0:T(8,128)S(1)}, f32[24,128]{1,0:T(8,128)S(1)}, u32[]{:S(2)}, u32[]{:S(2)}) collective-permute-start(f32[24,128]{1,0:T(8,128)S(1)} %get-tuple-element.43), channel_id=1, source_target_pairs={{0,1},{1,0},{2,3},{3,2},{4,5},{5,4},{6,7},{7,6},{8,9},{9,8},{10,11... | collective-permute-start | bytes 36872 | tf_op jit(solution)/shard_map/ppermute | solution.py:151
  22.6 4.7 %collective-permute-start.10 = (f32[24,128]{1,0:T(8,128)S(1)}, f32[24,128]{1,0:T(8,128)S(1)}, u32[]{:S(2)}, u32[]{:S(2)}) collective-permute-start(f32[24,128]{1,0:T(8,128)S(1)} %get-tuple-element.44), channel_id=1, source_target_pairs={{1,2},{2,1},{5,6},{6,5},{9,10},{10,9},{13,14},{14,13},{17,18},{18,... | collective-permute-start | bytes 36872 | tf_op jit(solution)/shard_map/ppermute | solution.py:151
  29.0 4.8 %collective-permute-start.11 = (bf16[64,128]{1,0:T(8,128)(2,1)S(1)}, bf16[64,128]{1,0:T(8,128)(2,1)S(1)}, u32[]{:S(2)}, u32[]{:S(2)}) collective-permute-start(bf16[64,128]{1,0:T(8,128)(2,1)S(1)} %get-tuple-element.46), channel_id=1, source_target_pairs={{0,4},{4,0},{8,12},{12,8},{16,20},{20,16},{24,28},{28,24},{1,5},{5... | collective-permute-start | bytes 49160 | tf_op jit(solution)/shard_map/ppermute | solution.py:157
  30.3 4.2 %collective-permute-start.12 = (bf16[64,128]{1,0:T(8,128)(2,1)S(1)}, bf16[64,128]{1,0:T(8,128)(2,1)S(1)}, u32[]{:S(2)}, u32[]{:S(2)}) collective-permute-start(bf16[64,128]{1,0:T(8,128)(2,1)S(1)} %get-tuple-element.47), channel_id=1, source_target_pairs={{0,8},{4,12},{8,0},{12,4},{16,24},{20,28},{24,16},{28,20},{1,9},{5... | collective-permute-start | bytes 49160 | tf_op jit(solution)/shard_map/ppermute | solution.py:157
  30.6 5.8 %collective-permute-start.13 = (bf16[64,128]{1,0:T(8,128)(2,1)S(1)}, bf16[64,128]{1,0:T(8,128)(2,1)S(1)}, u32[]{:S(2)}, u32[]{:S(2)}) collective-permute-start(bf16[64,128]{1,0:T(8,128)(2,1)S(1)} %get-tuple-element.48), channel_id=1, source_target_pairs={{0,12},{4,8},{8,4},{12,0},{16,28},{20,24},{24,20},{28,16},{1,13},{... | collective-permute-start | bytes 49160 | tf_op jit(solution)/shard_map/ppermute | solution.py:157
  32.0 4.4 %collective-permute-start.14 = (bf16[64,128]{1,0:T(8,128)(2,1)S(1)}, bf16[64,128]{1,0:T(8,128)(2,1)S(1)}, u32[]{:S(2)}, u32[]{:S(2)}) collective-permute-start(bf16[64,128]{1,0:T(8,128)(2,1)S(1)} %get-tuple-element.49), channel_id=1, source_target_pairs={{0,16},{4,20},{8,24},{12,28},{16,0},{20,4},{24,8},{28,12},{1,17},{... | collective-permute-start | bytes 49160 | tf_op jit(solution)/shard_map/ppermute | solution.py:157
  32.2 4.2 %collective-permute-start.15 = (bf16[64,128]{1,0:T(8,128)(2,1)S(1)}, bf16[64,128]{1,0:T(8,128)(2,1)S(1)}, u32[]{:S(2)}, u32[]{:S(2)}) collective-permute-start(bf16[64,128]{1,0:T(8,128)(2,1)S(1)} %get-tuple-element.50), channel_id=1, source_target_pairs={{0,20},{4,16},{8,28},{12,24},{16,4},{20,0},{24,12},{28,8},{1,21},{... | collective-permute-start | bytes 49160 | tf_op jit(solution)/shard_map/ppermute | solution.py:157
  33.8 3.5 %collective-permute-start.16 = (bf16[64,128]{1,0:T(8,128)(2,1)S(1)}, bf16[64,128]{1,0:T(8,128)(2,1)S(1)}, u32[]{:S(2)}, u32[]{:S(2)}) collective-permute-start(bf16[64,128]{1,0:T(8,128)(2,1)S(1)} %get-tuple-element.51), channel_id=1, source_target_pairs={{0,24},{4,28},{8,16},{12,20},{16,8},{20,12},{24,0},{28,4},{1,25},{... | collective-permute-start | bytes 49160 | tf_op jit(solution)/shard_map/ppermute | solution.py:157
  34.5 4.1 %collective-permute-start.17 = (bf16[64,128]{1,0:T(8,128)(2,1)S(1)}, bf16[64,128]{1,0:T(8,128)(2,1)S(1)}, u32[]{:S(2)}, u32[]{:S(2)}) collective-permute-start(bf16[64,128]{1,0:T(8,128)(2,1)S(1)} %get-tuple-element.52), channel_id=1, source_target_pairs={{0,28},{4,24},{8,20},{12,16},{16,12},{20,8},{24,4},{28,0},{1,29},{... | collective-permute-start | bytes 49160 | tf_op jit(solution)/shard_map/ppermute | solution.py:157

commit v5 on v4

--- a/solution.py
+++ b/solution.py
@@ -152,10 +152,42 @@
 
 
 def exchange(chunks):
-    size = len(chunks)
-    swaps = lambda s: [(i, i ^ s) for i in range(size)]
-    received = {s: lax.ppermute(chunks[s], "member", swaps(s)) for s in range(size - 1, 0, -1)}
-    return [chunks[0]] + [received[s] for s in range(1, size)]
+    chips = len(chunks)
+    device = lambda chip, core: 2 * chip + core
+    swaps = lambda s: [(device(i, c), device(i ^ s, c)) for i in range(chips) for c in (0, 1)]
+    received = {s: lax.ppermute(chunks[s], "member", swaps(s)) for s in range(chips - 1, 0, -1)}
+    return [chunks[0]] + [received[s] for s in range(1, chips)]
+
+
+def swap_cores(array):
+    return lax.ppermute(array, "member", [(i, i ^ 1) for i in range(lax.axis_size("member"))])
+
+
+def place():
+    block = lax.axis_index("member")
+    core = lax.rem(block, 2)
+    return block, (block - core) // 2, core
+
+
+def share_body(*refs, region_rows):
+    chunks, (own, other) = refs[:-2], refs[-2:]
+    _, _, core = place()
+    first = core == 0
+    each = own.shape[0] // len(chunks)
+    half = chunks[0].shape[0] - 2 * region_rows
+    lines = half // 2
+    for s, chunk in enumerate(chunks):
+        low, high = chunk[0:region_rows, :], chunk[region_rows : 2 * region_rows, :]
+        row = s * each
+        own[row : row + region_rows, :] = jnp.where(first, low, high)
+        other[row : row + region_rows, :] = jnp.where(first, high, low)
+        if each == region_rows:
+            continue
+        seen = chunk[2 * region_rows :, :].astype(f32)
+        west = jnp.concatenate([seen[0 : lines - 8], seen[lines : 2 * lines - 8]], axis=0)
+        east = jnp.concatenate([seen[8:lines], seen[lines + 8 : 2 * lines]], axis=0)
+        own[row + region_rows : row + each, :] = jnp.where(first, west, east).astype(bf16)
+        other[row + region_rows : row + each, :] = jnp.where(first, east, west).astype(bf16)
 
 
 def forecast_body(
@@ -202,10 +234,11 @@
             forecast[:, :, r : r + BLOCK, q * LANES : (q + 1) * LANES].reshape(region_rows, LANES)
             for r in range(0, side, BLOCK)
         ]
-        for c, part in enumerate(transpose_chunks(parts)):
+        for i, part in enumerate(transpose_chunks(parts)):
+            c = 4 * q + i
             rounded = part.astype(bf16)
-            send[4 * q + c, 0:region_rows, :] = rounded
-            table[4 * q + c] = rounded.astype(f32)
+            send[c // 2, c % 2 * region_rows : (c % 2 + 1) * region_rows, :] = rounded
+            table[c] = rounded.astype(f32)
 
     hits = levels * BLOCK
     observed = []
@@ -226,16 +259,18 @@
                 line = jnp.broadcast_to(line, (BLOCK, LANES))
                 mine[b] = jnp.where(here, pick_lanes(line, low), mine[b])
         observed.append(mine)
-    for c in range(blocks):
+    for chip in range(blocks // 2):
         rows = [
-            observed[(c + r - 1) % blocks][b] for b in range(members) for r in range(3)
+            observed[(2 * chip + r - 1) % blocks][b] for b in range(members) for r in range(4)
         ]
         for i in range(0, len(rows), 2):
-            at = region_rows + i * BLOCK
-            send[c, at : at + 2 * BLOCK, :] = jnp.concatenate(rows[i : i + 2], axis=0).astype(bf16)
-    block = lax.axis_index("member")
+            at = 2 * region_rows + i * BLOCK
+            send[chip, at : at + 2 * BLOCK, :] = jnp.concatenate(rows[i : i + 2], axis=0).astype(
+                bf16
+            )
+    _, chip, _ = place()
     for s, chunk in enumerate(chunks):
-        chunk[...] = send[block ^ s]
+        chunk[...] = send[chip ^ s]
 
 
 def weights_body(
@@ -316,16 +351,18 @@
 
 
 def systems_body(*refs, patches, sources, members, region_rows):
-    received, rest = refs[:sources], refs[sources:]
-    weights, values, own, to_first, to_second, planes, tall_high, tall_low, wide_high, wide_low = rest
+    mine, theirs, weights, values, own, to_first, to_second = refs[:7]
+    planes, tall_high, tall_low, wide_high, wide_low = refs[7:]
     depth = 3 * BLOCK
-    all_rows = received[0].shape[0]
-    block = lax.axis_index("member")
+    each = 2 * mine.shape[0] // sources
+    _, chip, core = place()
     ensemble = sources * members
     total = jnp.zeros((depth, LANES), f32)
     for s in range(sources):
-        both = received[s][region_rows:all_rows, :].astype(f32)
-        at = pl.multiple_of((block ^ s) * (members * depth), BLOCK)
+        source, row = (mine, theirs)[s % 2], s // 2 * each
+        both = source[row + region_rows : row + each, :].astype(f32)
+        device = 2 * (chip ^ (s // 2)) + (core ^ (s % 2))
+        at = pl.multiple_of(device * (members * depth), BLOCK)
         planes[pl.ds(at, members * depth), :] = both
         for b in range(members):
             total += both[b * depth : (b + 1) * depth, :]
@@ -372,18 +409,20 @@
 
 
 def analysis_body(*refs, patches, sources, members, region_rows):
-    received, rest = refs[:sources], refs[sources:]
-    own, first, second = rest[:3]
-    chunks, (centred, factors) = rest[3:-2], rest[-2:]
-    block = lax.axis_index("member")
+    mine, theirs, own, first, second = refs[:5]
+    chunks, (centred, factors) = refs[5:-2], refs[-2:]
+    each = 2 * mine.shape[0] // sources
+    _, chip, core = place()
     ensemble = sources * members
     hits = region_rows // members
     total = jnp.zeros((hits, LANES), f32)
     for s in range(sources):
-        part = received[s][0:region_rows, :].astype(f32)
+        source, row = (mine, theirs)[s % 2], s // 2 * each
+        device = 2 * (chip ^ (s // 2)) + (core ^ (s % 2))
+        part = source[row : row + region_rows, :].astype(f32)
         for b in range(members):
             one = part[b * hits : (b + 1) * hits, :]
-            centred[(block ^ s) * members + b] = one
+            centred[device * members + b] = one
             total += one
     mean = total / ensemble
     for k in range(ensemble):
@@ -427,21 +466,25 @@
         factors[j] = chosen
 
     for s, chunk in enumerate(chunks):
-        target = block ^ s
-        totals = [jnp.zeros((hits, LANES), f32) for _ in range(members)]
-        for j in range(ensemble):
-            centred_j = centred[j]
-            for b in range(members):
-                totals[b] += factors[j, pl.ds(target * members + b, 1), :] * centred_j
-        chunk[...] = jnp.concatenate(totals, axis=0).astype(bf16)
-
-
-def output_body(forecast, *refs):
-    received, (analysis, ordered) = refs[:-2], refs[-2:]
+        for c in (0, 1):
+            first_member = (2 * (chip ^ s) + c) * members
+            totals = [jnp.zeros((hits, LANES), f32) for _ in range(members)]
+            for j in range(ensemble):
+                centred_j = centred[j]
+                for b in range(members):
+                    totals[b] += factors[j, pl.ds(first_member + b, 1), :] * centred_j
+            at = slice(c * region_rows, (c + 1) * region_rows)
+            chunk[at, :] = jnp.concatenate(totals, axis=0).astype(bf16)
+
+
+def output_body(forecast, mine, theirs, analysis, ordered):
     members, levels, side, width = forecast.shape
-    block = lax.axis_index("member")
-    for s, part in enumerate(received):
-        ordered[block ^ s] = part[...].astype(f32)
+    _, chip, core = place()
+    rows = ordered.shape[1]
+    for s in range(mine.shape[0] // rows):
+        at = slice(s * rows, (s + 1) * rows)
+        ordered[2 * (chip ^ s) + core] = mine[at, :].astype(f32)
+        ordered[2 * (chip ^ s) + (core ^ 1)] = theirs[at, :].astype(f32)
     for q in range(width // LANES):
         parts = [ordered[4 * q + c] for c in range(4)]
         at = slice(q * LANES, (q + 1) * LANES)
@@ -464,6 +507,8 @@
     region_rows = members * levels * BLOCK
     depth = 3 * BLOCK
     all_rows = region_rows + members * depth
+    chips = blocks // 2
+    chip_rows = 2 * region_rows + members * 4 * BLOCK
     edge_rows = -(-(24 + patches * slots // width) // 8) * 8
     edge_shape = (members, levels, BLOCK, width)
     rate_shape = (2, levels, BLOCK, width)
@@ -491,9 +536,9 @@
     )
     forecast, *chunks = call(
         functools.partial(forecast_body, tiles=tiles, height=height),
-        [(member_concentration.shape, f32)] + [((all_rows, LANES), bf16)] * blocks,
+        [(member_concentration.shape, f32)] + [((chip_rows, LANES), bf16)] * chips,
         [
-            pltpu.VMEM((blocks, all_rows, LANES), bf16),
+            pltpu.VMEM((chips, chip_rows, LANES), bf16),
             pltpu.VMEM((blocks, region_rows, LANES), f32),
         ],
     )(
@@ -504,6 +549,9 @@
         cell_row,
     )
     received = exchange(chunks)
+    share = functools.partial(share_body, region_rows=region_rows)
+    mine, theirs = call(share, [((chips * all_rows, LANES), bf16)] * 2)(*received)
+    theirs = swap_cores(theirs)
     weights, values = call(
         functools.partial(
             weights_body, tiles=tiles, blocks=blocks, height=height, width=width, side=side
@@ -526,21 +574,23 @@
             pltpu.VMEM((ensemble + 8, depth * LANES), bf16),
             pltpu.VMEM((ensemble + 8, depth * LANES), bf16),
         ],
-    )(*received, weights, values)
+    )(mine, theirs, weights, values)
     first, second = swap(to_first, to_second, tiles)
 
     changes = call(
         functools.partial(analysis_body, **sizes),
-        [((region_rows, LANES), bf16)] * blocks,
+        [((2 * region_rows, LANES), bf16)] * chips,
         [
             pltpu.VMEM((ensemble, levels * BLOCK, LANES), f32),
             pltpu.VMEM((ensemble, ensemble, LANES), f32),
         ],
-    )(*received, own, first, second)
+    )(mine, theirs, own, first, second)
     returned = exchange(changes)
+    mine, theirs = call(share, [((chips * region_rows, LANES), bf16)] * 2)(*returned)
+    theirs = swap_cores(theirs)
     (analysis,) = call(
         output_body, [(forecast.shape, f32)], [pltpu.VMEM((blocks, region_rows, LANES), f32)]
-    )(forecast, *returned)
+    )(forecast, mine, theirs)
     return analysis
 
 

time: 40.2 us -> 38.6 us (0.960)
  starting transfers between devices: 23.8 us -> 20 us
  waiting for transfers between devices: 6.36 us -> 8.43 us
    ppermute x14 -> x6, starting transfers between devices: 15.5 us -> 5.43 us  [exchange(): lax.ppermute(chunks[s], 'member', swaps(s))]
    ppermute x0 -> x2, starting transfers between devices: none -> 6.32 us  [swap_cores(): lax.ppermute(array, 'member', [(i, i ^ 1) for i in range(lax.axis_size('m...]
    ppermute x14 -> x6, waiting for transfers between devices: 4.5 us -> 5.65 us  [exchange(): lax.ppermute(chunks[s], 'member', swaps(s))]
    ppermute x0 -> x2, waiting for transfers between devices: none -> 0.9 us  [swap_cores(): lax.ppermute(array, 'member', [(i, i ^ 1) for i in range(lax.axis_size('m...]
    pallas_call x1 -> x3, Pallas kernels: 1.74 us -> 1.8 us  [the longest x1 1.74 us: shards(): call(functools.partial(analysis_body, **sizes), [((2 * region_rows, LANES...]
  transfers between devices with their start and end apart: 18 -> 12, of which waited for: 5 -> 9; matrix products, arithmetic and copies ran while one was open for 2% -> 2% of each run, Pallas kernels for 3% -> 3%
where the time goes in v5:
time: 38.6 us; the launch traced here: 37.9 us
  starting transfers between devices  20 us (52%)
  Pallas kernels  8.53 us (22%)
  waiting for transfers between devices  8.43 us (22%)
  local copies, waits for them, and re-layouts  0.79 us (2%)
    ppermute x2, starting transfers between devices, swap(): lax.ppermute(second, 'tile', pairs(1))  8.12 us
    ppermute x2, starting transfers between devices, swap_cores(): lax.ppermute(array, 'member', [(i, i ^ 1) for i in range(lax.axis_size('m...  6.32 us
    ppermute x6, waiting for transfers between devices, exchange(): lax.ppermute(chunks[s], 'member', swaps(s))  5.65 us
    ppermute x6, starting transfers between devices, exchange(): lax.ppermute(chunks[s], 'member', swaps(s))  5.43 us
    ppermute x2, waiting for transfers between devices, swap(): lax.ppermute(second, 'tile', pairs(1))  1.87 us
    pallas_call x1, Pallas kernels, shards(): call(functools.partial(analysis_body, **sizes), [((2 * region_rows, LANES...  1.74 us
    pallas_call x1, Pallas kernels, shards(): call(pack_edges, [((edge_rows, width), f32)] * 2, [pltpu.VMEM(edge_shape,...  1.71 us
    pallas_call x1, Pallas kernels, shards(): call(functools.partial(systems_body, **sizes), [(system_shape, f32)] * 3,...  1.48 us
  transfers between devices with their start and end apart: 12, of which 9 were waited for; matrix products, arithmetic and copies ran while one was open for 2% of the time, Pallas kernels for 3%

profile of v5, /device:TPU:9, one launch (start us, length us, event | category | flops | bytes accessed | tf_op | source)
XLA Modules:
  0.0 37.9 jit_solution(9668081531920125292)
XLA Ops:
  0.0 1.7 %shard_map.64 = (f32[40,256]{1,0:T(8,128)}, f32[40,256]{1,0:T(8,128)}) custom-call(f32[2,4,32,256]{3,2,1,0:T(8,128)} %tracer.3, f32[2,4,32,256]{3,2,1,0:T(8,128)} %courant.3, s32[2,2,1024]{2,1,0:T(2,128)} %lists.3), custom_call_target="tpu_custom_call" | custom-call | flops 1000000 | bytes 1000000 | tf_op jit(solution)/shard_map/pallas_call | solution.py:516
  1.8 4.5 %collective-permute-start.1 = (f32[40,256]{1,0:T(8,128)}, f32[40,256]{1,0:T(8,128)S(1)}, u32[]{:S(2)}, u32[]{:S(2)}) collective-permute-start(f32[40,256]{1,0:T(8,128)} %get-tuple-element.26), channel_id=1, source_target_pairs={{1,2},{2,1},{5,6},{6,5},{9,10},{10,9},{13,14},{14,13},{17,18},{18,... | collective-permute-start | bytes 122888 | tf_op jit(solution)/shard_map/ppermute | solution.py:151
  6.3 0.8 %dynamic-slice_bitcast_fusion.cell = s32[8,8,128]{2,1,0:T(8,128)S(1)} fusion(s32[8,4,8,128]{3,2,1,0:T(8,128)} %bitcast.6, s32[]{:T(128)S(6)} %select_n.4), kind=kLoop, calls=%fused_computation | loop fusion | bytes 65540 | tf_op jit(solution)/shard_map/jit(dynamic_index_in_dim)/squeeze | solution.py:534
  7.1 0.8 %collective-permute-done.1.second = f32[40,256]{1,0:T(8,128)S(1)} collective-permute-done((f32[40,256]{1,0:T(8,128)}, f32[40,256]{1,0:T(8,128)S(1)}, u32[]{:S(2)}, u32[]{:S(2)}) %collective-permute-start.1) | collective-permute-done | bytes 40992 | tf_op jit(solution)/shard_map/ppermute | solution.py:151
  7.9 1.4 %shard_map.65 = (f32[2,4,32,256]{3,2,1,0:T(8,128)S(1)}, bf16[192,128]{1,0:T(8,128)(2,1)S(1)}, bf16[192,128]{1,0:T(8,128)(2,1)S(1)}, bf16[192,128]{1,0:T(8,128)(2,1)S(1)}, bf16[192,128]{1,0:T(8,128)(2,1)S(1)}) custom-call(f32[2,4,32,256]{3,2,1,0:T(8,128)S(1)} %copy-done, f32[2,4,32,256]{3,2,1,0:T(8,128)S(1)} %copy-done.1, ...), custom_call_target="tpu_custom_call" | custom-call | flops 1000000 | bytes 1000000 | tf_op jit(solution)/shard_map/pallas_call | solution.py:537
  9.3 1.3 %collective-permute-start.2 = (bf16[192,128]{1,0:T(8,128)(2,1)S(1)}, bf16[192,128]{1,0:T(8,128)(2,1)S(1)}, u32[]{:S(2)}, u32[]{:S(2)}) collective-permute-start(bf16[192,128]{1,0:T(8,128)(2,1)S(1)} %get-tuple-element.29), channel_id=1, source_target_pairs={{0,8},{4,12},{8,0},{12,4},{16,24},{20,28},{24,16},{28,20},{1,9},{5... | collective-permute-start | bytes 147464 | tf_op jit(solution)/shard_map/ppermute | solution.py:158
  10.6 1.2 %collective-permute-start.3 = (bf16[192,128]{1,0:T(8,128)(2,1)S(1)}, bf16[192,128]{1,0:T(8,128)(2,1)S(1)}, u32[]{:S(2)}, u32[]{:S(2)}) collective-permute-start(bf16[192,128]{1,0:T(8,128)(2,1)S(1)} %get-tuple-element.30), channel_id=1, source_target_pairs={{0,16},{4,20},{8,24},{12,28},{16,0},{20,4},{24,8},{28,12},{1,17},{... | collective-permute-start | bytes 147464 | tf_op jit(solution)/shard_map/ppermute | solution.py:158
  12.0 0.3 collective-permute-done.2.refs_1_
  12.3 1.2 %collective-permute-done.3.refs_2_ = bf16[192,128]{1,0:T(8,128)(2,1)S(1)} collective-permute-done((bf16[192,128]{1,0:T(8,128)(2,1)S(1)}, bf16[192,128]{1,0:T(8,128)(2,1)S(1)}, u32[]{:S(2)}, u32[]{:S(2)}) %collective-permute-start.3) | collective-permute-done | bytes 49184 | tf_op jit(solution)/shard_map/ppermute | solution.py:158
  13.5 2.7 %collective-permute-done.4.refs_3_ = bf16[192,128]{1,0:T(8,128)(2,1)S(1)} collective-permute-done((bf16[192,128]{1,0:T(8,128)(2,1)S(1)}, bf16[192,128]{1,0:T(8,128)(2,1)S(1)}, u32[]{:S(2)}, u32[]{:S(2)}) %collective-permute-start.4) | collective-permute-done | bytes 49184 | tf_op jit(solution)/shard_map/ppermute | solution.py:158
  16.2 3.1 %collective-permute-start.5 = (bf16[448,128]{1,0:T(8,128)(2,1)S(1)}, bf16[448,128]{1,0:T(8,128)(2,1)S(1)}, u32[]{:S(2)}, u32[]{:S(2)}) collective-permute-start(bf16[448,128]{1,0:T(8,128)(2,1)S(1)} %get-tuple-element.33), channel_id=1, source_target_pairs={{0,4},{4,0},{8,12},{12,8},{16,20},{20,16},{24,28},{28,24},{1,5},{5... | collective-permute-start | bytes 344072 | tf_op jit(solution)/shard_map/ppermute | solution.py:163
  19.3 1.2 %shard_map.67 = (f32[16,3072]{1,0:T(8,128)S(1)}, f32[24,128]{1,0:T(8,128)S(1)}) custom-call(s32[2,2,1024]{2,1,0:T(2,128)S(1)} %copy-done.5, f32[40,256]{1,0:T(8,128)S(1)} %collective-permute-done.first, f32[40,256]{1,0:T(8,128)S(1)} %collective-permute-done.1.second, s32[256,128]{1,0:T(8,128)S(1)} %bitcast.7, f32[256,128]{1,0:T(8,128)S(1)} %bitcast.8, ...), custom_call_target="tpu_custom_call" | custom-call | flops 100000000 | bytes 1000000 | tf_op jit(solution)/shard_map/pallas_call | solution.py:555
  20.5 1.5 %shard_map.68 = (f32[24,128]{1,0:T(8,128)S(1)}, f32[24,128]{1,0:T(8,128)S(1)}, f32[24,128]{1,0:T(8,128)S(1)}) custom-call(bf16[448,128]{1,0:T(8,128)(2,1)S(1)} %get-tuple-element.32.refs_0_, bf16[448,128]{1,0:T(8,128)(2,1)S(1)} %collective-permute-done.5.refs_1_, f32[16,3072]{1,0:T(8,128)S(1)} %get-tuple-element.34.refs_2_, ...), custom_call_target="tpu_custom_call" | custom-call | flops 1000000 | bytes 1000000 | tf_op jit(solution)/shard_map/pallas_call | solution.py:567
  22.1 3.6 %collective-permute-start.7 = (f32[24,128]{1,0:T(8,128)S(1)}, f32[24,128]{1,0:T(8,128)S(1)}, u32[]{:S(2)}, u32[]{:S(2)}) collective-permute-start(f32[24,128]{1,0:T(8,128)S(1)} %get-tuple-element.38), channel_id=1, source_target_pairs={{1,2},{2,1},{5,6},{6,5},{9,10},{10,9},{13,14},{14,13},{17,18},{18,... | collective-permute-start | bytes 36872 | tf_op jit(solution)/shard_map/ppermute | solution.py:151
  25.7 1.1 %collective-permute-done.7.refs_4_ = f32[24,128]{1,0:T(8,128)S(1)} collective-permute-done((f32[24,128]{1,0:T(8,128)S(1)}, f32[24,128]{1,0:T(8,128)S(1)}, u32[]{:S(2)}, u32[]{:S(2)}) %collective-permute-start.7) | collective-permute-done | bytes 12320 | tf_op jit(solution)/shard_map/ppermute | solution.py:151
  26.8 1.7 %shard_map.69 = (bf16[128,128]{1,0:T(8,128)(2,1)S(1)}, bf16[128,128]{1,0:T(8,128)(2,1)S(1)}, bf16[128,128]{1,0:T(8,128)(2,1)S(1)}, bf16[128,128]{1,0:T(8,128)(2,1)S(1)}) custom-call(bf16[448,128]{1,0:T(8,128)(2,1)S(1)} %get-tuple-element.32.refs_0_, bf16[448,128]{1,0:T(8,128)(2,1)S(1)} %collective-permute-done.5.refs_1_, ...), custom_call_target="tpu_custom_call" | custom-call | flops 1000000 | bytes 1000000 | tf_op jit(solution)/shard_map/pallas_call | solution.py:580
  28.5 0.3 collective-permute-start.8
  28.8 0.2 collective-permute-start.9
  29.1 2.2 %collective-permute-start.10 = (bf16[128,128]{1,0:T(8,128)(2,1)S(1)}, bf16[128,128]{1,0:T(8,128)(2,1)S(1)}, u32[]{:S(2)}, u32[]{:S(2)}) collective-permute-start(bf16[128,128]{1,0:T(8,128)(2,1)S(1)} %get-tuple-element.42), channel_id=1, source_target_pairs={{0,24},{4,28},{8,16},{12,20},{16,8},{20,12},{24,0},{28,4},{1,25},{... | collective-permute-start | bytes 98312 | tf_op jit(solution)/shard_map/ppermute | solution.py:158
  31.4 0.2 collective-permute-done.9.refs_2_
  31.6 1.1 %collective-permute-done.10.refs_3_ = bf16[128,128]{1,0:T(8,128)(2,1)S(1)} collective-permute-done((bf16[128,128]{1,0:T(8,128)(2,1)S(1)}, bf16[128,128]{1,0:T(8,128)(2,1)S(1)}, u32[]{:S(2)}, u32[]{:S(2)}) %collective-permute-start.10) | collective-permute-done | bytes 32800 | tf_op jit(solution)/shard_map/ppermute | solution.py:158
  32.8 3.2 %collective-permute-start.11 = (bf16[256,128]{1,0:T(8,128)(2,1)S(1)}, bf16[256,128]{1,0:T(8,128)(2,1)S(1)}, u32[]{:S(2)}, u32[]{:S(2)}) collective-permute-start(bf16[256,128]{1,0:T(8,128)(2,1)S(1)} %get-tuple-element.44), channel_id=1, source_target_pairs={{0,4},{4,0},{8,12},{12,8},{16,20},{20,16},{24,28},{28,24},{1,5},{5... | collective-permute-start | bytes 196616 | tf_op jit(solution)/shard_map/ppermute | solution.py:163
  36.0 0.9 %collective-permute-done.11.theirs = bf16[256,128]{1,0:T(8,128)(2,1)S(1)} collective-permute-done((bf16[256,128]{1,0:T(8,128)(2,1)S(1)}, bf16[256,128]{1,0:T(8,128)(2,1)S(1)}, u32[]{:S(2)}, u32[]{:S(2)}) %collective-permute-start.11) | collective-permute-done | bytes 65568 | tf_op jit(solution)/shard_map/ppermute | solution.py:163
  36.9 0.9 %shard_map.71 = f32[2,4,32,256]{3,2,1,0:T(8,128)} custom-call(f32[2,4,32,256]{3,2,1,0:T(8,128)S(1)} %get-tuple-element.27.forecast, bf16[256,128]{1,0:T(8,128)(2,1)S(1)} %get-tuple-element.43.mine, bf16[256,128]{1,0:T(8,128)(2,1)S(1)} %collective-permute-done.11.theirs), custom_call_target="tpu_custom_call" | custom-call | flops 1000000 | bytes 1000000 | tf_op jit(solution)/shard_map/pallas_call | solution.py:591
  (21 shorter events, 0.5 us)
Async XLA Ops:
  0.0 7.9 %copy-start = (f32[2,4,32,256]{3,2,1,0:T(8,128)S(1)}, f32[2,4,32,256]{3,2,1,0:T(8,128)}, u32[]{:S(2)}) copy-start(f32[2,4,32,256]{3,2,1,0:T(8,128)} %tracer.3) | copy-start | bytes 786436
  0.0 7.9 %copy-start.1 = (f32[2,4,32,256]{3,2,1,0:T(8,128)S(1)}, f32[2,4,32,256]{3,2,1,0:T(8,128)}, u32[]{:S(2)}) copy-start(f32[2,4,32,256]{3,2,1,0:T(8,128)} %courant.3) | copy-start | bytes 786436
  1.7 5.3 %collective-permute-start = (f32[40,256]{1,0:T(8,128)}, f32[40,256]{1,0:T(8,128)S(1)}, u32[]{:S(2)}, u32[]{:S(2)}) collective-permute-start(f32[40,256]{1,0:T(8,128)} %get-tuple-element.25), channel_id=1, source_target_pairs={{0,1},{1,0},{2,3},{3,2},{4,5},{5,4},{6,7},{7,6},{8,9},{9,8},{10,11... | collective-permute-start | bytes 122888 | tf_op jit(solution)/shard_map/ppermute | solution.py:151
  1.8 6.1 %collective-permute-start.1 = (f32[40,256]{1,0:T(8,128)}, f32[40,256]{1,0:T(8,128)S(1)}, u32[]{:S(2)}, u32[]{:S(2)}) collective-permute-start(f32[40,256]{1,0:T(8,128)} %get-tuple-element.26), channel_id=1, source_target_pairs={{1,2},{2,1},{5,6},{6,5},{9,10},{10,9},{13,14},{14,13},{17,18},{18,... | collective-permute-start | bytes 122888 | tf_op jit(solution)/shard_map/ppermute | solution.py:151
  7.9 11.4 %copy-start.3 = (f32[32768]{0:T(1024)S(1)}, f32[32768]{0:T(1024)}, u32[]{:S(2)}) copy-start(f32[32768]{0:T(1024)} %param.9) | copy-start | bytes 393220
  7.9 11.4 %copy-start.4 = (f32[32768]{0:T(1024)S(1)}, f32[32768]{0:T(1024)}, u32[]{:S(2)}) copy-start(f32[32768]{0:T(1024)} %param.10) | copy-start | bytes 393220
  9.3 10.0 %copy-start.2 = (s32[32768]{0:T(1024)S(1)}, s32[32768]{0:T(1024)}, u32[]{:S(2)}) copy-start(s32[32768]{0:T(1024)} %param.8) | copy-start | bytes 393220
  9.3 3.0 %collective-permute-start.2 = (bf16[192,128]{1,0:T(8,128)(2,1)S(1)}, bf16[192,128]{1,0:T(8,128)(2,1)S(1)}, u32[]{:S(2)}, u32[]{:S(2)}) collective-permute-start(bf16[192,128]{1,0:T(8,128)(2,1)S(1)} %get-tuple-element.29), channel_id=1, source_target_pairs={{0,8},{4,12},{8,0},{12,4},{16,24},{20,28},{24,16},{28,20},{1,9},{5... | collective-permute-start | bytes 147464 | tf_op jit(solution)/shard_map/ppermute | solution.py:158
  10.6 2.9 %collective-permute-start.3 = (bf16[192,128]{1,0:T(8,128)(2,1)S(1)}, bf16[192,128]{1,0:T(8,128)(2,1)S(1)}, u32[]{:S(2)}, u32[]{:S(2)}) collective-permute-start(bf16[192,128]{1,0:T(8,128)(2,1)S(1)} %get-tuple-element.30), channel_id=1, source_target_pairs={{0,16},{4,20},{8,24},{12,28},{16,0},{20,4},{24,8},{28,12},{1,17},{... | collective-permute-start | bytes 147464 | tf_op jit(solution)/shard_map/ppermute | solution.py:158
  11.8 4.4 %collective-permute-start.4 = (bf16[192,128]{1,0:T(8,128)(2,1)S(1)}, bf16[192,128]{1,0:T(8,128)(2,1)S(1)}, u32[]{:S(2)}, u32[]{:S(2)}) collective-permute-start(bf16[192,128]{1,0:T(8,128)(2,1)S(1)} %get-tuple-element.31), channel_id=1, source_target_pairs={{0,24},{4,28},{8,16},{12,20},{16,8},{20,12},{24,0},{28,4},{1,25},{... | collective-permute-start | bytes 147464 | tf_op jit(solution)/shard_map/ppermute | solution.py:158
  16.2 3.1 %copy-start.5 = (s32[2,2,1024]{2,1,0:T(2,128)S(1)}, s32[2,2,1024]{2,1,0:T(2,128)}, u32[]{:S(2)}) copy-start(s32[2,2,1024]{2,1,0:T(2,128)} %lists.3) | copy-start | bytes 49156
  16.2 4.3 %collective-permute-start.5 = (bf16[448,128]{1,0:T(8,128)(2,1)S(1)}, bf16[448,128]{1,0:T(8,128)(2,1)S(1)}, u32[]{:S(2)}, u32[]{:S(2)}) collective-permute-start(bf16[448,128]{1,0:T(8,128)(2,1)S(1)} %get-tuple-element.33), channel_id=1, source_target_pairs={{0,4},{4,0},{8,12},{12,8},{16,20},{20,16},{24,28},{28,24},{1,5},{5... | collective-permute-start | bytes 344072 | tf_op jit(solution)/shard_map/ppermute | solution.py:163
  22.0 3.7 %collective-permute-start.6 = (f32[24,128]{1,0:T(8,128)S(1)}, f32[24,128]{1,0:T(8,128)S(1)}, u32[]{:S(2)}, u32[]{:S(2)}) collective-permute-start(f32[24,128]{1,0:T(8,128)S(1)} %get-tuple-element.37), channel_id=1, source_target_pairs={{0,1},{1,0},{2,3},{3,2},{4,5},{5,4},{6,7},{7,6},{8,9},{9,8},{10,11... | collective-permute-start | bytes 36872 | tf_op jit(solution)/shard_map/ppermute | solution.py:151
  22.1 4.7 %collective-permute-start.7 = (f32[24,128]{1,0:T(8,128)S(1)}, f32[24,128]{1,0:T(8,128)S(1)}, u32[]{:S(2)}, u32[]{:S(2)}) collective-permute-start(f32[24,128]{1,0:T(8,128)S(1)} %get-tuple-element.38), channel_id=1, source_target_pairs={{1,2},{2,1},{5,6},{6,5},{9,10},{10,9},{13,14},{14,13},{17,18},{18,... | collective-permute-start | bytes 36872 | tf_op jit(solution)/shard_map/ppermute | solution.py:151
  28.5 2.8 %collective-permute-start.8 = (bf16[128,128]{1,0:T(8,128)(2,1)S(1)}, bf16[128,128]{1,0:T(8,128)(2,1)S(1)}, u32[]{:S(2)}, u32[]{:S(2)}) collective-permute-start(bf16[128,128]{1,0:T(8,128)(2,1)S(1)} %get-tuple-element.40), channel_id=1, source_target_pairs={{0,8},{4,12},{8,0},{12,4},{16,24},{20,28},{24,16},{28,20},{1,9},{5... | collective-permute-start | bytes 98312 | tf_op jit(solution)/shard_map/ppermute | solution.py:158
  28.8 2.8 %collective-permute-start.9 = (bf16[128,128]{1,0:T(8,128)(2,1)S(1)}, bf16[128,128]{1,0:T(8,128)(2,1)S(1)}, u32[]{:S(2)}, u32[]{:S(2)}) collective-permute-start(bf16[128,128]{1,0:T(8,128)(2,1)S(1)} %get-tuple-element.41), channel_id=1, source_target_pairs={{0,16},{4,20},{8,24},{12,28},{16,0},{20,4},{24,8},{28,12},{1,17},{... | collective-permute-start | bytes 98312 | tf_op jit(solution)/shard_map/ppermute | solution.py:158
  29.1 3.7 %collective-permute-start.10 = (bf16[128,128]{1,0:T(8,128)(2,1)S(1)}, bf16[128,128]{1,0:T(8,128)(2,1)S(1)}, u32[]{:S(2)}, u32[]{:S(2)}) collective-permute-start(bf16[128,128]{1,0:T(8,128)(2,1)S(1)} %get-tuple-element.42), channel_id=1, source_target_pairs={{0,24},{4,28},{8,16},{12,20},{16,8},{20,12},{24,0},{28,4},{1,25},{... | collective-permute-start | bytes 98312 | tf_op jit(solution)/shard_map/ppermute | solution.py:158
  32.8 4.1 %collective-permute-start.11 = (bf16[256,128]{1,0:T(8,128)(2,1)S(1)}, bf16[256,128]{1,0:T(8,128)(2,1)S(1)}, u32[]{:S(2)}, u32[]{:S(2)}) collective-permute-start(bf16[256,128]{1,0:T(8,128)(2,1)S(1)} %get-tuple-element.44), channel_id=1, source_target_pairs={{0,4},{4,0},{8,12},{12,8},{16,20},{20,16},{24,28},{28,24},{1,5},{5... | collective-permute-start | bytes 196616 | tf_op jit(solution)/shard_map/ppermute | solution.py:163

commit v6 on v5

--- a/solution.py
+++ b/solution.py
@@ -90,11 +90,11 @@
         copy.start()
     for copy in copies:
         copy.wait()
-    even = lax.rem(lax.axis_index("tile"), 2) == 0
+    odd = lax.rem(lax.axis_index("tile"), 2) == 1
 
     def put(row, low, high):
-        to_first[row : row + 1, :] = jnp.where(even, high, low)
-        to_second[row : row + 1, :] = jnp.where(even, low, high)
+        to_first[row : row + 1, :] = jnp.where(odd, high, low)
+        to_second[row : row + 1, :] = jnp.where(odd, low, high)
 
     end = BLOCK - 1
     for b in range(members):
@@ -140,15 +140,15 @@
 
 
 def beside(first, second, tile):
-    even = lax.rem(tile, 2) == 0
-    return jnp.where(even, second, first), jnp.where(even, first, second)
+    odd = lax.rem(tile, 2) == 1
+    return jnp.where(odd, second, first), jnp.where(odd, first, second)
 
 
 def swap(first, second, tiles):
     pairs = lambda start: [
         pair for i in range(start, tiles - 1, 2) for pair in ((i, i + 1), (i + 1, i))
     ]
-    return lax.ppermute(first, "tile", pairs(0)), lax.ppermute(second, "tile", pairs(1))
+    return lax.ppermute(first, "tile", pairs(1)), lax.ppermute(second, "tile", pairs(0))
 
 
 def exchange(chunks):
@@ -389,7 +389,7 @@
         + dot_rows(wide_high[...], tall_low[...])
     )
     count = patches * ensemble // 64
-    even = lax.rem(lax.axis_index("tile"), 2) == 0
+    odd = lax.rem(lax.axis_index("tile"), 2) == 1
     found = []
     for n in range(3 * count):
         piece = result[:, n // 2 * LANES : (n // 2 + 1) * LANES] if n // 2 * LANES + LANES <= result.shape[1] else None
@@ -404,8 +404,8 @@
         at = slice(i * LANES, (i + 1) * LANES)
         own[:, at] = found[i]
         for_south, for_north = found[count + i], found[2 * count + i]
-        to_first[:, at] = jnp.where(even, for_north, for_south)
-        to_second[:, at] = jnp.where(even, for_south, for_north)
+        to_first[:, at] = jnp.where(odd, for_north, for_south)
+        to_second[:, at] = jnp.where(odd, for_south, for_north)
 
 
 def analysis_body(*refs, patches, sources, members, region_rows):

time: 38.6 us -> 39.8 us (1.031)
  the two profiles are of different devices: /device:TPU:9 before, /device:TPU:0 now
where the time goes in v6:
time: 39.8 us; the launch traced here: 39.5 us
  starting transfers between devices  18.3 us (46%)
  waiting for transfers between devices  11.2 us (28%)
  Pallas kernels  8.53 us (21%)
  local copies, waits for them, and re-layouts  1.35 us (3%)
    ppermute x2, starting transfers between devices, swap(): lax.ppermute(second, 'tile', pairs(0))  9.69 us
    ppermute x6, starting transfers between devices, exchange(): lax.ppermute(chunks[s], 'member', swaps(s))  7.11 us
    ppermute x6, waiting for transfers between devices, exchange(): lax.ppermute(chunks[s], 'member', swaps(s))  6.88 us
    ppermute x2, waiting for transfers between devices, swap(): lax.ppermute(second, 'tile', pairs(0))  3.1 us
    pallas_call x1, Pallas kernels, shards(): call(functools.partial(analysis_body, **sizes), [((2 * region_rows, LANES...  1.74 us
    pallas_call x1, Pallas kernels, shards(): call(pack_edges, [((edge_rows, width), f32)] * 2, [pltpu.VMEM(edge_shape,...  1.71 us
    pallas_call x1, Pallas kernels, shards(): call(functools.partial(systems_body, **sizes), [(system_shape, f32)] * 3,...  1.48 us
    pallas_call x1, Pallas kernels, shards(): call(functools.partial(forecast_body, tiles=tiles, height=height), [(memb...  1.41 us
  transfers between devices with their start and end apart: 12, of which 9 were waited for; matrix products, arithmetic and copies ran while one was open for 2% of the time, Pallas kernels for 3%

profile of v6, /device:TPU:0, one launch (start us, length us, event | category | flops | bytes accessed | tf_op | source)
XLA Modules:
  0.0 39.5 jit_solution(7903838288963442342)
XLA Ops:
  0.0 1.7 %shard_map.64 = (f32[40,256]{1,0:T(8,128)}, f32[40,256]{1,0:T(8,128)}) custom-call(f32[2,4,32,256]{3,2,1,0:T(8,128)} %tracer.3, f32[2,4,32,256]{3,2,1,0:T(8,128)} %courant.3, s32[2,2,1024]{2,1,0:T(2,128)} %lists.3), custom_call_target="tpu_custom_call" | custom-call | flops 1000000 | bytes 1000000 | tf_op jit(solution)/shard_map/pallas_call | solution.py:516
  1.7 0.7 %collective-permute-start = (f32[40,256]{1,0:T(8,128)}, f32[40,256]{1,0:T(8,128)S(1)}, u32[]{:S(2)}, u32[]{:S(2)}) collective-permute-start(f32[40,256]{1,0:T(8,128)} %get-tuple-element.25), channel_id=1, source_target_pairs={{1,2},{2,1},{5,6},{6,5},{9,10},{10,9},{13,14},{14,13},{17,18},{18,... | collective-permute-start | bytes 122888 | tf_op jit(solution)/shard_map/ppermute | solution.py:151
  2.4 5.9 %collective-permute-start.1 = (f32[40,256]{1,0:T(8,128)}, f32[40,256]{1,0:T(8,128)S(1)}, u32[]{:S(2)}, u32[]{:S(2)}) collective-permute-start(f32[40,256]{1,0:T(8,128)} %get-tuple-element.26), channel_id=1, source_target_pairs={{0,1},{1,0},{2,3},{3,2},{4,5},{5,4},{6,7},{7,6},{8,9},{9,8},{10,11... | collective-permute-start | bytes 122888 | tf_op jit(solution)/shard_map/ppermute | solution.py:151
  8.3 0.8 %dynamic-slice_bitcast_fusion.cell = s32[8,8,128]{2,1,0:T(8,128)S(1)} fusion(s32[8,4,8,128]{3,2,1,0:T(8,128)} %bitcast.6, s32[]{:T(128)S(6)} %select_n.4), kind=kLoop, calls=%fused_computation | loop fusion | bytes 65540 | tf_op jit(solution)/shard_map/jit(dynamic_index_in_dim)/squeeze | solution.py:534
  9.1 1.4 %collective-permute-done.1.second = f32[40,256]{1,0:T(8,128)S(1)} collective-permute-done((f32[40,256]{1,0:T(8,128)}, f32[40,256]{1,0:T(8,128)S(1)}, u32[]{:S(2)}, u32[]{:S(2)}) %collective-permute-start.1) | collective-permute-done | bytes 40992 | tf_op jit(solution)/shard_map/ppermute | solution.py:151
  10.5 1.4 %shard_map.65 = (f32[2,4,32,256]{3,2,1,0:T(8,128)S(1)}, bf16[192,128]{1,0:T(8,128)(2,1)S(1)}, bf16[192,128]{1,0:T(8,128)(2,1)S(1)}, bf16[192,128]{1,0:T(8,128)(2,1)S(1)}, bf16[192,128]{1,0:T(8,128)(2,1)S(1)}) custom-call(f32[2,4,32,256]{3,2,1,0:T(8,128)S(1)} %copy-done, f32[2,4,32,256]{3,2,1,0:T(8,128)S(1)} %copy-done.1, ...), custom_call_target="tpu_custom_call" | custom-call | flops 1000000 | bytes 1000000 | tf_op jit(solution)/shard_map/pallas_call | solution.py:537
  11.9 1.6 %collective-permute-start.2 = (bf16[192,128]{1,0:T(8,128)(2,1)S(1)}, bf16[192,128]{1,0:T(8,128)(2,1)S(1)}, u32[]{:S(2)}, u32[]{:S(2)}) collective-permute-start(bf16[192,128]{1,0:T(8,128)(2,1)S(1)} %get-tuple-element.29), channel_id=1, source_target_pairs={{0,8},{4,12},{8,0},{12,4},{16,24},{20,28},{24,16},{28,20},{1,9},{5... | collective-permute-start | bytes 147464 | tf_op jit(solution)/shard_map/ppermute | solution.py:158
  13.5 1.5 %collective-permute-start.3 = (bf16[192,128]{1,0:T(8,128)(2,1)S(1)}, bf16[192,128]{1,0:T(8,128)(2,1)S(1)}, u32[]{:S(2)}, u32[]{:S(2)}) collective-permute-start(bf16[192,128]{1,0:T(8,128)(2,1)S(1)} %get-tuple-element.30), channel_id=1, source_target_pairs={{0,16},{4,20},{8,24},{12,28},{16,0},{20,4},{24,8},{28,12},{1,17},{... | collective-permute-start | bytes 147464 | tf_op jit(solution)/shard_map/ppermute | solution.py:158
  15.5 1.0 %collective-permute-done.2.refs_1_ = bf16[192,128]{1,0:T(8,128)(2,1)S(1)} collective-permute-done((bf16[192,128]{1,0:T(8,128)(2,1)S(1)}, bf16[192,128]{1,0:T(8,128)(2,1)S(1)}, u32[]{:S(2)}, u32[]{:S(2)}) %collective-permute-start.2) | collective-permute-done | bytes 49184 | tf_op jit(solution)/shard_map/ppermute | solution.py:158
  16.5 1.4 %collective-permute-done.3.refs_2_ = bf16[192,128]{1,0:T(8,128)(2,1)S(1)} collective-permute-done((bf16[192,128]{1,0:T(8,128)(2,1)S(1)}, bf16[192,128]{1,0:T(8,128)(2,1)S(1)}, u32[]{:S(2)}, u32[]{:S(2)}) %collective-permute-start.3) | collective-permute-done | bytes 49184 | tf_op jit(solution)/shard_map/ppermute | solution.py:158
  17.9 2.1 %collective-permute-done.4.refs_3_ = bf16[192,128]{1,0:T(8,128)(2,1)S(1)} collective-permute-done((bf16[192,128]{1,0:T(8,128)(2,1)S(1)}, bf16[192,128]{1,0:T(8,128)(2,1)S(1)}, u32[]{:S(2)}, u32[]{:S(2)}) %collective-permute-start.4) | collective-permute-done | bytes 49184 | tf_op jit(solution)/shard_map/ppermute | solution.py:158
  20.2 0.6 %copy-done.5 = s32[2,2,1024]{2,1,0:T(2,128)S(1)} copy-done((s32[2,2,1024]{2,1,0:T(2,128)S(1)}, s32[2,2,1024]{2,1,0:T(2,128)}, u32[]{:S(2)}) %copy-start.5) | copy-done | bytes 16408
  20.7 1.2 %shard_map.67 = (f32[16,3072]{1,0:T(8,128)S(1)}, f32[24,128]{1,0:T(8,128)S(1)}) custom-call(s32[2,2,1024]{2,1,0:T(2,128)S(1)} %copy-done.5, f32[40,256]{1,0:T(8,128)S(1)} %collective-permute-done.first, f32[40,256]{1,0:T(8,128)S(1)} %collective-permute-done.1.second, s32[256,128]{1,0:T(8,128)S(1)} %bitcast.7, f32[256,128]{1,0:T(8,128)S(1)} %bitcast.8, ...), custom_call_target="tpu_custom_call" | custom-call | flops 100000000 | bytes 1000000 | tf_op jit(solution)/shard_map/pallas_call | solution.py:555
  21.9 1.5 %shard_map.68 = (f32[24,128]{1,0:T(8,128)S(1)}, f32[24,128]{1,0:T(8,128)S(1)}, f32[24,128]{1,0:T(8,128)S(1)}) custom-call(bf16[448,128]{1,0:T(8,128)(2,1)S(1)} %get-tuple-element.32.refs_0_, bf16[448,128]{1,0:T(8,128)(2,1)S(1)} %collective-permute-done.5.refs_1_, f32[16,3072]{1,0:T(8,128)S(1)} %get-tuple-element.34.refs_2_, ...), custom_call_target="tpu_custom_call" | custom-call | flops 1000000 | bytes 1000000 | tf_op jit(solution)/shard_map/pallas_call | solution.py:567
  23.4 0.7 %collective-permute-start.6 = (f32[24,128]{1,0:T(8,128)S(1)}, f32[24,128]{1,0:T(8,128)S(1)}, u32[]{:S(2)}, u32[]{:S(2)}) collective-permute-start(f32[24,128]{1,0:T(8,128)S(1)} %get-tuple-element.37), channel_id=1, source_target_pairs={{1,2},{2,1},{5,6},{6,5},{9,10},{10,9},{13,14},{14,13},{17,18},{18,... | collective-permute-start | bytes 36872 | tf_op jit(solution)/shard_map/ppermute | solution.py:151
  24.1 3.8 %collective-permute-start.7 = (f32[24,128]{1,0:T(8,128)S(1)}, f32[24,128]{1,0:T(8,128)S(1)}, u32[]{:S(2)}, u32[]{:S(2)}) collective-permute-start(f32[24,128]{1,0:T(8,128)S(1)} %get-tuple-element.38), channel_id=1, source_target_pairs={{0,1},{1,0},{2,3},{3,2},{4,5},{5,4},{6,7},{7,6},{8,9},{9,8},{10,11... | collective-permute-start | bytes 36872 | tf_op jit(solution)/shard_map/ppermute | solution.py:151
  27.9 1.7 %collective-permute-done.7.refs_4_ = f32[24,128]{1,0:T(8,128)S(1)} collective-permute-done((f32[24,128]{1,0:T(8,128)S(1)}, f32[24,128]{1,0:T(8,128)S(1)}, u32[]{:S(2)}, u32[]{:S(2)}) %collective-permute-start.7) | collective-permute-done | bytes 12320 | tf_op jit(solution)/shard_map/ppermute | solution.py:151
  29.5 1.7 %shard_map.69 = (bf16[128,128]{1,0:T(8,128)(2,1)S(1)}, bf16[128,128]{1,0:T(8,128)(2,1)S(1)}, bf16[128,128]{1,0:T(8,128)(2,1)S(1)}, bf16[128,128]{1,0:T(8,128)(2,1)S(1)}) custom-call(bf16[448,128]{1,0:T(8,128)(2,1)S(1)} %get-tuple-element.32.refs_0_, bf16[448,128]{1,0:T(8,128)(2,1)S(1)} %collective-permute-done.5.refs_1_, ...), custom_call_target="tpu_custom_call" | custom-call | flops 1000000 | bytes 1000000 | tf_op jit(solution)/shard_map/pallas_call | solution.py:580
  31.3 0.6 %collective-permute-start.8 = (bf16[128,128]{1,0:T(8,128)(2,1)S(1)}, bf16[128,128]{1,0:T(8,128)(2,1)S(1)}, u32[]{:S(2)}, u32[]{:S(2)}) collective-permute-start(bf16[128,128]{1,0:T(8,128)(2,1)S(1)} %get-tuple-element.40), channel_id=1, source_target_pairs={{0,8},{4,12},{8,0},{12,4},{16,24},{20,28},{24,16},{28,20},{1,9},{5... | collective-permute-start | bytes 98312 | tf_op jit(solution)/shard_map/ppermute | solution.py:158
  32.4 2.4 %collective-permute-start.10 = (bf16[128,128]{1,0:T(8,128)(2,1)S(1)}, bf16[128,128]{1,0:T(8,128)(2,1)S(1)}, u32[]{:S(2)}, u32[]{:S(2)}) collective-permute-start(bf16[128,128]{1,0:T(8,128)(2,1)S(1)} %get-tuple-element.42), channel_id=1, source_target_pairs={{0,24},{4,28},{8,16},{12,20},{16,8},{20,12},{24,0},{28,4},{1,25},{... | collective-permute-start | bytes 98312 | tf_op jit(solution)/shard_map/ppermute | solution.py:158
  35.3 0.5 %collective-permute-done.9.refs_2_ = bf16[128,128]{1,0:T(8,128)(2,1)S(1)} collective-permute-done((bf16[128,128]{1,0:T(8,128)(2,1)S(1)}, bf16[128,128]{1,0:T(8,128)(2,1)S(1)}, u32[]{:S(2)}, u32[]{:S(2)}) %collective-permute-start.9) | collective-permute-done | bytes 32800 | tf_op jit(solution)/shard_map/ppermute | solution.py:158
  35.8 1.4 %collective-permute-done.10.refs_3_ = bf16[128,128]{1,0:T(8,128)(2,1)S(1)} collective-permute-done((bf16[128,128]{1,0:T(8,128)(2,1)S(1)}, bf16[128,128]{1,0:T(8,128)(2,1)S(1)}, u32[]{:S(2)}, u32[]{:S(2)}) %collective-permute-start.10) | collective-permute-done | bytes 32800 | tf_op jit(solution)/shard_map/ppermute | solution.py:158
  37.3 1.2 %collective-permute-done.11.theirs = bf16[256,128]{1,0:T(8,128)(2,1)S(1)} collective-permute-done((bf16[256,128]{1,0:T(8,128)(2,1)S(1)}, bf16[256,128]{1,0:T(8,128)(2,1)S(1)}, u32[]{:S(2)}, u32[]{:S(2)}) %collective-permute-start.11) | collective-permute-done | bytes 65568 | tf_op jit(solution)/shard_map/ppermute | solution.py:163
  38.6 0.9 %shard_map.71 = f32[2,4,32,256]{3,2,1,0:T(8,128)} custom-call(f32[2,4,32,256]{3,2,1,0:T(8,128)S(1)} %get-tuple-element.27.forecast, bf16[256,128]{1,0:T(8,128)(2,1)S(1)} %get-tuple-element.43.mine, bf16[256,128]{1,0:T(8,128)(2,1)S(1)} %collective-permute-done.11.theirs), custom_call_target="tpu_custom_call" | custom-call | flops 1000000 | bytes 1000000 | tf_op jit(solution)/shard_map/pallas_call | solution.py:591
  (21 shorter events, 1.6 us)
Async XLA Ops:
  0.0 10.5 %copy-start = (f32[2,4,32,256]{3,2,1,0:T(8,128)S(1)}, f32[2,4,32,256]{3,2,1,0:T(8,128)}, u32[]{:S(2)}) copy-start(f32[2,4,32,256]{3,2,1,0:T(8,128)} %tracer.3) | copy-start | bytes 786436
  0.0 10.5 %copy-start.1 = (f32[2,4,32,256]{3,2,1,0:T(8,128)S(1)}, f32[2,4,32,256]{3,2,1,0:T(8,128)}, u32[]{:S(2)}) copy-start(f32[2,4,32,256]{3,2,1,0:T(8,128)} %courant.3) | copy-start | bytes 786436
  1.7 7.3 %collective-permute-start = (f32[40,256]{1,0:T(8,128)}, f32[40,256]{1,0:T(8,128)S(1)}, u32[]{:S(2)}, u32[]{:S(2)}) collective-permute-start(f32[40,256]{1,0:T(8,128)} %get-tuple-element.25), channel_id=1, source_target_pairs={{1,2},{2,1},{5,6},{6,5},{9,10},{10,9},{13,14},{14,13},{17,18},{18,... | collective-permute-start | bytes 122888 | tf_op jit(solution)/shard_map/ppermute | solution.py:151
  2.4 8.1 %collective-permute-start.1 = (f32[40,256]{1,0:T(8,128)}, f32[40,256]{1,0:T(8,128)S(1)}, u32[]{:S(2)}, u32[]{:S(2)}) collective-permute-start(f32[40,256]{1,0:T(8,128)} %get-tuple-element.26), channel_id=1, source_target_pairs={{0,1},{1,0},{2,3},{3,2},{4,5},{5,4},{6,7},{7,6},{8,9},{9,8},{10,11... | collective-permute-start | bytes 122888 | tf_op jit(solution)/shard_map/ppermute | solution.py:151
  10.5 9.6 %copy-start.3 = (f32[32768]{0:T(1024)S(1)}, f32[32768]{0:T(1024)}, u32[]{:S(2)}) copy-start(f32[32768]{0:T(1024)} %param.9) | copy-start | bytes 393220
  10.5 9.6 %copy-start.4 = (f32[32768]{0:T(1024)S(1)}, f32[32768]{0:T(1024)}, u32[]{:S(2)}) copy-start(f32[32768]{0:T(1024)} %param.10) | copy-start | bytes 393220
  11.9 8.2 %copy-start.2 = (s32[32768]{0:T(1024)S(1)}, s32[32768]{0:T(1024)}, u32[]{:S(2)}) copy-start(s32[32768]{0:T(1024)} %param.8) | copy-start | bytes 393220
  11.9 4.6 %collective-permute-start.2 = (bf16[192,128]{1,0:T(8,128)(2,1)S(1)}, bf16[192,128]{1,0:T(8,128)(2,1)S(1)}, u32[]{:S(2)}, u32[]{:S(2)}) collective-permute-start(bf16[192,128]{1,0:T(8,128)(2,1)S(1)} %get-tuple-element.29), channel_id=1, source_target_pairs={{0,8},{4,12},{8,0},{12,4},{16,24},{20,28},{24,16},{28,20},{1,9},{5... | collective-permute-start | bytes 147464 | tf_op jit(solution)/shard_map/ppermute | solution.py:158
  13.5 4.4 %collective-permute-start.3 = (bf16[192,128]{1,0:T(8,128)(2,1)S(1)}, bf16[192,128]{1,0:T(8,128)(2,1)S(1)}, u32[]{:S(2)}, u32[]{:S(2)}) collective-permute-start(bf16[192,128]{1,0:T(8,128)(2,1)S(1)} %get-tuple-element.30), channel_id=1, source_target_pairs={{0,16},{4,20},{8,24},{12,28},{16,0},{20,4},{24,8},{28,12},{1,17},{... | collective-permute-start | bytes 147464 | tf_op jit(solution)/shard_map/ppermute | solution.py:158
  15.0 5.0 %collective-permute-start.4 = (bf16[192,128]{1,0:T(8,128)(2,1)S(1)}, bf16[192,128]{1,0:T(8,128)(2,1)S(1)}, u32[]{:S(2)}, u32[]{:S(2)}) collective-permute-start(bf16[192,128]{1,0:T(8,128)(2,1)S(1)} %get-tuple-element.31), channel_id=1, source_target_pairs={{0,24},{4,28},{8,16},{12,20},{16,8},{20,12},{24,0},{28,4},{1,25},{... | collective-permute-start | bytes 147464 | tf_op jit(solution)/shard_map/ppermute | solution.py:158
  20.0 0.7 %copy-start.5 = (s32[2,2,1024]{2,1,0:T(2,128)S(1)}, s32[2,2,1024]{2,1,0:T(2,128)}, u32[]{:S(2)}) copy-start(s32[2,2,1024]{2,1,0:T(2,128)} %lists.3) | copy-start | bytes 49156
  20.1 1.9 %collective-permute-start.5 = (bf16[448,128]{1,0:T(8,128)(2,1)S(1)}, bf16[448,128]{1,0:T(8,128)(2,1)S(1)}, u32[]{:S(2)}, u32[]{:S(2)}) collective-permute-start(bf16[448,128]{1,0:T(8,128)(2,1)S(1)} %get-tuple-element.33), channel_id=1, source_target_pairs={{0,4},{4,0},{8,12},{12,8},{16,20},{20,16},{24,28},{28,24},{1,5},{5... | collective-permute-start | bytes 344072 | tf_op jit(solution)/shard_map/ppermute | solution.py:163
  23.4 4.5 %collective-permute-start.6 = (f32[24,128]{1,0:T(8,128)S(1)}, f32[24,128]{1,0:T(8,128)S(1)}, u32[]{:S(2)}, u32[]{:S(2)}) collective-permute-start(f32[24,128]{1,0:T(8,128)S(1)} %get-tuple-element.37), channel_id=1, source_target_pairs={{1,2},{2,1},{5,6},{6,5},{9,10},{10,9},{13,14},{14,13},{17,18},{18,... | collective-permute-start | bytes 36872 | tf_op jit(solution)/shard_map/ppermute | solution.py:151
  24.1 5.5 %collective-permute-start.7 = (f32[24,128]{1,0:T(8,128)S(1)}, f32[24,128]{1,0:T(8,128)S(1)}, u32[]{:S(2)}, u32[]{:S(2)}) collective-permute-start(f32[24,128]{1,0:T(8,128)S(1)} %get-tuple-element.38), channel_id=1, source_target_pairs={{0,1},{1,0},{2,3},{3,2},{4,5},{5,4},{6,7},{7,6},{8,9},{9,8},{10,11... | collective-permute-start | bytes 36872 | tf_op jit(solution)/shard_map/ppermute | solution.py:151
  31.3 4.0 %collective-permute-start.8 = (bf16[128,128]{1,0:T(8,128)(2,1)S(1)}, bf16[128,128]{1,0:T(8,128)(2,1)S(1)}, u32[]{:S(2)}, u32[]{:S(2)}) collective-permute-start(bf16[128,128]{1,0:T(8,128)(2,1)S(1)} %get-tuple-element.40), channel_id=1, source_target_pairs={{0,8},{4,12},{8,0},{12,4},{16,24},{20,28},{24,16},{28,20},{1,9},{5... | collective-permute-start | bytes 98312 | tf_op jit(solution)/shard_map/ppermute | solution.py:158
  31.9 3.9 %collective-permute-start.9 = (bf16[128,128]{1,0:T(8,128)(2,1)S(1)}, bf16[128,128]{1,0:T(8,128)(2,1)S(1)}, u32[]{:S(2)}, u32[]{:S(2)}) collective-permute-start(bf16[128,128]{1,0:T(8,128)(2,1)S(1)} %get-tuple-element.41), channel_id=1, source_target_pairs={{0,16},{4,20},{8,24},{12,28},{16,0},{20,4},{24,8},{28,12},{1,17},{... | collective-permute-start | bytes 98312 | tf_op jit(solution)/shard_map/ppermute | solution.py:158
  32.4 4.8 %collective-permute-start.10 = (bf16[128,128]{1,0:T(8,128)(2,1)S(1)}, bf16[128,128]{1,0:T(8,128)(2,1)S(1)}, u32[]{:S(2)}, u32[]{:S(2)}) collective-permute-start(bf16[128,128]{1,0:T(8,128)(2,1)S(1)} %get-tuple-element.42), channel_id=1, source_target_pairs={{0,24},{4,28},{8,16},{12,20},{16,8},{20,12},{24,0},{28,4},{1,25},{... | collective-permute-start | bytes 98312 | tf_op jit(solution)/shard_map/ppermute | solution.py:158
  37.2 1.3 %collective-permute-start.11 = (bf16[256,128]{1,0:T(8,128)(2,1)S(1)}, bf16[256,128]{1,0:T(8,128)(2,1)S(1)}, u32[]{:S(2)}, u32[]{:S(2)}) collective-permute-start(bf16[256,128]{1,0:T(8,128)(2,1)S(1)} %get-tuple-element.44), channel_id=1, source_target_pairs={{0,4},{4,0},{8,12},{12,8},{16,20},{20,16},{24,28},{28,24},{1,5},{5... | collective-permute-start | bytes 196616 | tf_op jit(solution)/shard_map/ppermute | solution.py:163

commit v7 on v5

--- a/solution.py
+++ b/solution.py
@@ -152,11 +152,11 @@
 
 
 def exchange(chunks):
-    chips = len(chunks)
-    device = lambda chip, core: 2 * chip + core
-    swaps = lambda s: [(device(i, c), device(i ^ s, c)) for i in range(chips) for c in (0, 1)]
-    received = {s: lax.ppermute(chunks[s], "member", swaps(s)) for s in range(chips - 1, 0, -1)}
-    return [chunks[0]] + [received[s] for s in range(1, chips)]
+    chips = chunks.shape[0]
+    groups = [[2 * i + core for i in range(chips)] for core in (0, 1)]
+    return lax.all_to_all(
+        chunks, "member", split_axis=0, concat_axis=0, axis_index_groups=groups, tiled=True
+    )
 
 
 def swap_cores(array):
@@ -170,13 +170,15 @@
 
 
 def share_body(*refs, region_rows):
-    chunks, (own, other) = refs[:-2], refs[-2:]
+    chunks, (own, other) = refs[0], refs[-2:]
     _, _, core = place()
     first = core == 0
-    each = own.shape[0] // len(chunks)
-    half = chunks[0].shape[0] - 2 * region_rows
+    chips, chip_rows, _ = chunks.shape
+    each = own.shape[0] // chips
+    half = chip_rows - 2 * region_rows
     lines = half // 2
-    for s, chunk in enumerate(chunks):
+    for s in range(chips):
+        chunk = chunks.at[s]
         low, high = chunk[0:region_rows, :], chunk[region_rows : 2 * region_rows, :]
         row = s * each
         own[row : row + region_rows, :] = jnp.where(first, low, high)
@@ -193,7 +195,7 @@
 def forecast_body(
     tracer, courant, first, second, cell, forecast, *rest, tiles, height
 ):
-    *chunks, send, table = rest
+    send, table = rest
     members, levels, side, width = tracer.shape
     blocks = width // side
     tile = lax.axis_index("tile")
@@ -268,9 +270,6 @@
             send[chip, at : at + 2 * BLOCK, :] = jnp.concatenate(rows[i : i + 2], axis=0).astype(
                 bf16
             )
-    _, chip, _ = place()
-    for s, chunk in enumerate(chunks):
-        chunk[...] = send[chip ^ s]
 
 
 def weights_body(
@@ -355,13 +354,13 @@
     planes, tall_high, tall_low, wide_high, wide_low = refs[7:]
     depth = 3 * BLOCK
     each = 2 * mine.shape[0] // sources
-    _, chip, core = place()
+    _, _, core = place()
     ensemble = sources * members
     total = jnp.zeros((depth, LANES), f32)
     for s in range(sources):
         source, row = (mine, theirs)[s % 2], s // 2 * each
         both = source[row + region_rows : row + each, :].astype(f32)
-        device = 2 * (chip ^ (s // 2)) + (core ^ (s % 2))
+        device = 2 * (s // 2) + (core ^ (s % 2))
         at = pl.multiple_of(device * (members * depth), BLOCK)
         planes[pl.ds(at, members * depth), :] = both
         for b in range(members):
@@ -410,15 +409,15 @@
 
 def analysis_body(*refs, patches, sources, members, region_rows):
     mine, theirs, own, first, second = refs[:5]
-    chunks, (centred, factors) = refs[5:-2], refs[-2:]
+    send, centred, factors = refs[5:]
     each = 2 * mine.shape[0] // sources
-    _, chip, core = place()
+    _, _, core = place()
     ensemble = sources * members
     hits = region_rows // members
     total = jnp.zeros((hits, LANES), f32)
     for s in range(sources):
         source, row = (mine, theirs)[s % 2], s // 2 * each
-        device = 2 * (chip ^ (s // 2)) + (core ^ (s % 2))
+        device = 2 * (s // 2) + (core ^ (s % 2))
         part = source[row : row + region_rows, :].astype(f32)
         for b in range(members):
             one = part[b * hits : (b + 1) * hits, :]
@@ -465,26 +464,26 @@
             chosen = jnp.where(jnp.broadcast_to(which[0:1] == i, chosen.shape), other, chosen)
         factors[j] = chosen
 
-    for s, chunk in enumerate(chunks):
+    for s in range(send.shape[0]):
         for c in (0, 1):
-            first_member = (2 * (chip ^ s) + c) * members
+            first_member = (2 * s + c) * members
             totals = [jnp.zeros((hits, LANES), f32) for _ in range(members)]
             for j in range(ensemble):
                 centred_j = centred[j]
                 for b in range(members):
-                    totals[b] += factors[j, pl.ds(first_member + b, 1), :] * centred_j
+                    totals[b] += factors[j, first_member + b : first_member + b + 1, :] * centred_j
             at = slice(c * region_rows, (c + 1) * region_rows)
-            chunk[at, :] = jnp.concatenate(totals, axis=0).astype(bf16)
+            send[s, at, :] = jnp.concatenate(totals, axis=0).astype(bf16)
 
 
 def output_body(forecast, mine, theirs, analysis, ordered):
     members, levels, side, width = forecast.shape
-    _, chip, core = place()
+    _, _, core = place()
     rows = ordered.shape[1]
     for s in range(mine.shape[0] // rows):
         at = slice(s * rows, (s + 1) * rows)
-        ordered[2 * (chip ^ s) + core] = mine[at, :].astype(f32)
-        ordered[2 * (chip ^ s) + (core ^ 1)] = theirs[at, :].astype(f32)
+        ordered[2 * s + core] = mine[at, :].astype(f32)
+        ordered[2 * s + (core ^ 1)] = theirs[at, :].astype(f32)
     for q in range(width // LANES):
         parts = [ordered[4 * q + c] for c in range(4)]
         at = slice(q * LANES, (q + 1) * LANES)
@@ -534,11 +533,10 @@
     cell_row = lax.dynamic_index_in_dim(
         cell.reshape(blocks, tiles, BLOCK, LANES), lax.axis_index("tile"), 1, False
     )
-    forecast, *chunks = call(
+    forecast, chunks = call(
         functools.partial(forecast_body, tiles=tiles, height=height),
-        [(member_concentration.shape, f32)] + [((chip_rows, LANES), bf16)] * chips,
+        [(member_concentration.shape, f32), ((chips, chip_rows, LANES), bf16)],
         [
-            pltpu.VMEM((chips, chip_rows, LANES), bf16),
             pltpu.VMEM((blocks, region_rows, LANES), f32),
         ],
     )(
@@ -549,9 +547,6 @@
         cell_row,
     )
     received = exchange(chunks)
-    share = functools.partial(share_body, region_rows=region_rows)
-    mine, theirs = call(share, [((chips * all_rows, LANES), bf16)] * 2)(*received)
-    theirs = swap_cores(theirs)
     weights, values = call(
         functools.partial(
             weights_body, tiles=tiles, blocks=blocks, height=height, width=width, side=side
@@ -562,6 +557,10 @@
     )(obs_list, first, second, cell, flat(obs_value), flat(obs_error))
 
     sizes = dict(patches=patches, sources=blocks, members=members, region_rows=region_rows)
+    share = functools.partial(share_body, region_rows=region_rows)
+    mine, theirs = call(share, [((chips * all_rows, LANES), bf16)] * 2)(received, values)
+    theirs = swap_cores(theirs)
+
     tall = 3 * patches * ensemble
     system_shape = (ensemble + 8, patches * ensemble // 64 * LANES)
     own, to_first, to_second = call(
@@ -577,16 +576,16 @@
     )(mine, theirs, weights, values)
     first, second = swap(to_first, to_second, tiles)
 
-    changes = call(
+    (changes,) = call(
         functools.partial(analysis_body, **sizes),
-        [((2 * region_rows, LANES), bf16)] * chips,
+        [((chips, 2 * region_rows, LANES), bf16)],
         [
             pltpu.VMEM((ensemble, levels * BLOCK, LANES), f32),
             pltpu.VMEM((ensemble, ensemble, LANES), f32),
         ],
     )(mine, theirs, own, first, second)
     returned = exchange(changes)
-    mine, theirs = call(share, [((chips * region_rows, LANES), bf16)] * 2)(*returned)
+    mine, theirs = call(share, [((chips * region_rows, LANES), bf16)] * 2)(returned, forecast)
     theirs = swap_cores(theirs)
     (analysis,) = call(
         output_body, [(forecast.shape, f32)], [pltpu.VMEM((blocks, region_rows, LANES), f32)]

time: 38.6 us -> 41.3 us (1.070)
  blocking collectives: 0 us -> 6.26 us
  starting transfers between devices: 20 us -> 17.6 us
  waiting for transfers between devices: 8.43 us -> 6.58 us
  Pallas kernels: 8.53 us -> 9.22 us
    all_to_all x0 -> x1, blocking collectives: none -> 6.26 us  [exchange(): lax.all_to_all(chunks, 'member', split_axis=0, concat_axis=0, axis_index_...]
    ppermute x6 -> x0, waiting for transfers between devices: 5.65 us -> none  [exchange(): lax.ppermute(chunks[s], 'member', swaps(s))]
    ppermute x6 -> x0, starting transfers between devices: 5.43 us -> none  [exchange(): lax.ppermute(chunks[s], 'member', swaps(s))]
    all_to_all x0 -> x1, starting transfers between devices: none -> 3.57 us  [exchange(): lax.all_to_all(chunks, 'member', split_axis=0, concat_axis=0, axis_index_...]
    all_to_all x0 -> x1, waiting for transfers between devices: none -> 2.84 us  [exchange(): lax.all_to_all(chunks, 'member', split_axis=0, concat_axis=0, axis_index_...]
    ppermute x2, waiting for transfers between devices: 0.9 us -> 1.87 us  [swap_cores(): lax.ppermute(array, 'member', [(i, i ^ 1) for i in range(lax.axis_size('m...]
    pallas_call x1, Pallas kernels: 1.41 us -> 2.08 us  [shards(): call(functools.partial(forecast_body, tiles=tiles, height=height), [(memb...]
    ppermute x2, starting transfers between devices: 6.32 us -> 5.76 us  [swap_cores(): lax.ppermute(array, 'member', [(i, i ^ 1) for i in range(lax.axis_size('m...]
  transfers between devices with their start and end apart: 12 -> 7, of which waited for: 9 -> 5; matrix products, arithmetic and copies ran while one was open for 2% -> 2% of each run, Pallas kernels for 3% -> 3%
where the time goes in v7:
time: 41.3 us; the launch traced here: 40.5 us
  starting transfers between devices  17.6 us (43%)
  Pallas kernels  9.22 us (22%)
  waiting for transfers between devices  6.58 us (16%)
  blocking collectives  6.26 us (15%)
  local copies, waits for them, and re-layouts  0.79 us (2%)
    ppermute x2, starting transfers between devices, swap(): lax.ppermute(second, 'tile', pairs(1))  8.12 us
    all_to_all x1, blocking collectives, exchange(): lax.all_to_all(chunks, 'member', split_axis=0, concat_axis=0, axis_index_...  6.26 us
    ppermute x2, starting transfers between devices, swap_cores(): lax.ppermute(array, 'member', [(i, i ^ 1) for i in range(lax.axis_size('m...  5.76 us
    all_to_all x1, starting transfers between devices, exchange(): lax.all_to_all(chunks, 'member', split_axis=0, concat_axis=0, axis_index_...  3.57 us
    all_to_all x1, waiting for transfers between devices, exchange(): lax.all_to_all(chunks, 'member', split_axis=0, concat_axis=0, axis_index_...  2.84 us
    pallas_call x1, Pallas kernels, shards(): call(functools.partial(forecast_body, tiles=tiles, height=height), [(memb...  2.08 us
    ppermute x2, waiting for transfers between devices, swap(): lax.ppermute(second, 'tile', pairs(1))  1.87 us
    ppermute x2, waiting for transfers between devices, swap_cores(): lax.ppermute(array, 'member', [(i, i ^ 1) for i in range(lax.axis_size('m...  1.87 us
  transfers between devices with their start and end apart: 7, of which 5 were waited for; matrix products, arithmetic and copies ran while one was open for 2% of the time, Pallas kernels for 3%

profile of v7, /device:TPU:9, one launch (start us, length us, event | category | flops | bytes accessed | tf_op | source)
XLA Modules:
  0.0 40.5 jit_solution(411844307836511283)
XLA Ops:
  0.0 1.7 %shard_map.64 = (f32[40,256]{1,0:T(8,128)}, f32[40,256]{1,0:T(8,128)}) custom-call(f32[2,4,32,256]{3,2,1,0:T(8,128)} %tracer.3, f32[2,4,32,256]{3,2,1,0:T(8,128)} %courant.3, s32[2,2,1024]{2,1,0:T(2,128)} %lists.3), custom_call_target="tpu_custom_call" | custom-call | flops 1000000 | bytes 1000000 | tf_op jit(solution)/shard_map/pallas_call | solution.py:515
  1.7 0.1 collective-permute-start
  1.8 4.5 %collective-permute-start.1 = (f32[40,256]{1,0:T(8,128)}, f32[40,256]{1,0:T(8,128)S(1)}, u32[]{:S(2)}, u32[]{:S(2)}) collective-permute-start(f32[40,256]{1,0:T(8,128)} %get-tuple-element.19), channel_id=1, source_target_pairs={{1,2},{2,1},{5,6},{6,5},{9,10},{10,9},{13,14},{14,13},{17,18},{18,... | collective-permute-start | bytes 122888 | tf_op jit(solution)/shard_map/ppermute | solution.py:151
  6.3 0.8 %dynamic-slice_bitcast_fusion.cell = s32[8,8,128]{2,1,0:T(8,128)S(1)} fusion(s32[8,4,8,128]{3,2,1,0:T(8,128)} %bitcast.6, s32[]{:T(128)S(6)} %select_n.4), kind=kLoop, calls=%fused_computation | loop fusion | bytes 65540 | tf_op jit(solution)/shard_map/jit(dynamic_index_in_dim)/squeeze | solution.py:533
  7.0 0.0 collective-permute-done.first
  7.0 0.8 %collective-permute-done.1.second = f32[40,256]{1,0:T(8,128)S(1)} collective-permute-done((f32[40,256]{1,0:T(8,128)}, f32[40,256]{1,0:T(8,128)S(1)}, u32[]{:S(2)}, u32[]{:S(2)}) %collective-permute-start.1) | collective-permute-done | bytes 40992 | tf_op jit(solution)/shard_map/ppermute | solution.py:151
  7.9 0.0 copy-done
  7.9 2.1 %shard_map.65 = (f32[2,4,32,256]{3,2,1,0:T(8,128)S(1)}, bf16[4,192,128]{2,1,0:T(8,128)(2,1)}) custom-call(f32[2,4,32,256]{3,2,1,0:T(8,128)S(1)} %copy-done, f32[2,4,32,256]{3,2,1,0:T(8,128)S(1)} %copy-done.1, f32[40,256]{1,0:T(8,128)S(1)} %collective-permute-done.first, f32[40,256]{1,0:T(8,128)S(1)} %collective-permute-done.1.second, ...), custom_call_target="tpu_custom_call" | custom-call | flops 1000000 | bytes 1000000 | tf_op jit(solution)/shard_map/pallas_call | solution.py:536
  10.0 3.6 %all-to-all-start = ((bf16[4,192,128]{2,1,0:T(8,128)(2,1)}), bf16[4,192,128]{2,1,0:T(8,128)(2,1)S(1)}, u32[]{:S(2)}, u32[]{:S(2)}) async-start(bf16[4,192,128]{2,1,0:T(8,128)(2,1)} %get-tuple-element.21), calls=%async_computation | async-start | bytes 393216 | tf_op jit(solution)/shard_map/all_to_all | solution.py:157
  13.5 0.0 copy-done.2
  13.5 1.2 %shard_map.66 = (f32[16,3072]{1,0:T(8,128)S(1)}, f32[24,128]{1,0:T(8,128)S(1)}) custom-call(s32[2,2,1024]{2,1,0:T(2,128)S(1)} %copy-done.5, f32[40,256]{1,0:T(8,128)S(1)} %collective-permute-done.first, f32[40,256]{1,0:T(8,128)S(1)} %collective-permute-done.1.second, s32[256,128]{1,0:T(8,128)S(1)} %bitcast.7, f32[256,128]{1,0:T(8,128)S(1)} %bitcast.8, ...), custom_call_target="tpu_custom_call" | custom-call | flops 100000000 | bytes 1000000 | tf_op jit(solution)/shard_map/pallas_call | solution.py:550
  14.7 2.8 %all-to-all-done.refs_0_ = bf16[4,192,128]{2,1,0:T(8,128)(2,1)S(1)} async-done(((bf16[4,192,128]{2,1,0:T(8,128)(2,1)}), bf16[4,192,128]{2,1,0:T(8,128)(2,1)S(1)}, u32[]{:S(2)}, u32[]{:S(2)}) %all-to-all-start) | async-done | bytes 196640 | tf_op jit(solution)/shard_map/all_to_all | solution.py:157
  17.6 3.3 %collective-permute-start.2 = (bf16[448,128]{1,0:T(8,128)(2,1)S(1)}, bf16[448,128]{1,0:T(8,128)(2,1)S(1)}, u32[]{:S(2)}, u32[]{:S(2)}) collective-permute-start(bf16[448,128]{1,0:T(8,128)(2,1)S(1)} %get-tuple-element.24), channel_id=1, source_target_pairs={{0,4},{4,0},{8,12},{12,8},{16,20},{20,16},{24,28},{28,24},{1,5},{5... | collective-permute-start | bytes 344072 | tf_op jit(solution)/shard_map/ppermute | solution.py:163
  20.9 1.0 %collective-permute-done.2.refs_1_ = bf16[448,128]{1,0:T(8,128)(2,1)S(1)} collective-permute-done((bf16[448,128]{1,0:T(8,128)(2,1)S(1)}, bf16[448,128]{1,0:T(8,128)(2,1)S(1)}, u32[]{:S(2)}, u32[]{:S(2)}) %collective-permute-start.2) | collective-permute-done | bytes 114720 | tf_op jit(solution)/shard_map/ppermute | solution.py:163
  21.9 1.5 %shard_map.68 = (f32[24,128]{1,0:T(8,128)S(1)}, f32[24,128]{1,0:T(8,128)S(1)}, f32[24,128]{1,0:T(8,128)S(1)}) custom-call(bf16[448,128]{1,0:T(8,128)(2,1)S(1)} %get-tuple-element.23.refs_0_, bf16[448,128]{1,0:T(8,128)(2,1)S(1)} %collective-permute-done.2.refs_1_, f32[16,3072]{1,0:T(8,128)S(1)} %get-tuple-element.25.refs_2_, ...), custom_call_target="tpu_custom_call" | custom-call | flops 1000000 | bytes 1000000 | tf_op jit(solution)/shard_map/pallas_call | solution.py:566
  23.4 0.0 collective-permute-start.3
  23.4 3.6 %collective-permute-start.4 = (f32[24,128]{1,0:T(8,128)S(1)}, f32[24,128]{1,0:T(8,128)S(1)}, u32[]{:S(2)}, u32[]{:S(2)}) collective-permute-start(f32[24,128]{1,0:T(8,128)S(1)} %get-tuple-element.28), channel_id=1, source_target_pairs={{1,2},{2,1},{5,6},{6,5},{9,10},{10,9},{13,14},{14,13},{17,18},{18,... | collective-permute-start | bytes 36872 | tf_op jit(solution)/shard_map/ppermute | solution.py:151
  27.1 0.0 collective-permute-done.3.refs_3_
  27.1 1.1 %collective-permute-done.4.refs_4_ = f32[24,128]{1,0:T(8,128)S(1)} collective-permute-done((f32[24,128]{1,0:T(8,128)S(1)}, f32[24,128]{1,0:T(8,128)S(1)}, u32[]{:S(2)}, u32[]{:S(2)}) %collective-permute-start.4) | collective-permute-done | bytes 12320 | tf_op jit(solution)/shard_map/ppermute | solution.py:151
  28.1 1.7 %shard_map.69 = bf16[4,128,128]{2,1,0:T(8,128)(2,1)S(1)} custom-call(bf16[448,128]{1,0:T(8,128)(2,1)S(1)} %get-tuple-element.23.refs_0_, bf16[448,128]{1,0:T(8,128)(2,1)S(1)} %collective-permute-done.2.refs_1_, f32[24,128]{1,0:T(8,128)S(1)} %get-tuple-element.26.refs_2_, f32[24,128]{1,0:T(8,128)S(1)} %collective-permute-done.3.refs_3_, ...), custom_call_target="tpu_custom_call" | custom-call | flops 1000000 | bytes 1000000 | tf_op jit(solution)/shard_map/pallas_call | solution.py:579
  29.9 6.3 %all_to_all.10.refs_0_ = bf16[4,128,128]{2,1,0:T(8,128)(2,1)S(1)} all-to-all(bf16[4,128,128]{2,1,0:T(8,128)(2,1)S(1)} %shard_map.69), channel_id=1, replica_groups={{0,8,16,24},{4,12,20,28},{1,9,17,25},{5,13,21,29},{2,10,18,26},{6,14,22..., dimensions={0} | all-to-all | bytes 262144 | tf_op jit(solution)/shard_map/all_to_all | solution.py:157
  36.2 2.4 %collective-permute-start.5 = (bf16[256,128]{1,0:T(8,128)(2,1)S(1)}, bf16[256,128]{1,0:T(8,128)(2,1)S(1)}, u32[]{:S(2)}, u32[]{:S(2)}) collective-permute-start(bf16[256,128]{1,0:T(8,128)(2,1)S(1)} %get-tuple-element.30), channel_id=1, source_target_pairs={{0,4},{4,0},{8,12},{12,8},{16,20},{20,16},{24,28},{28,24},{1,5},{5... | collective-permute-start | bytes 196616 | tf_op jit(solution)/shard_map/ppermute | solution.py:163
  38.6 0.9 %collective-permute-done.5.theirs = bf16[256,128]{1,0:T(8,128)(2,1)S(1)} collective-permute-done((bf16[256,128]{1,0:T(8,128)(2,1)S(1)}, bf16[256,128]{1,0:T(8,128)(2,1)S(1)}, u32[]{:S(2)}, u32[]{:S(2)}) %collective-permute-start.5) | collective-permute-done | bytes 65568 | tf_op jit(solution)/shard_map/ppermute | solution.py:163
  39.5 1.0 %shard_map.71 = f32[2,4,32,256]{3,2,1,0:T(8,128)} custom-call(f32[2,4,32,256]{3,2,1,0:T(8,128)S(1)} %get-tuple-element.20.refs_1_.forecast, bf16[256,128]{1,0:T(8,128)(2,1)S(1)} %get-tuple-element.29.mine, bf16[256,128]{1,0:T(8,128)(2,1)S(1)} %collective-permute-done.5.theirs), custom_call_target="tpu_custom_call" | custom-call | flops 1000000 | bytes 1000000 | tf_op jit(solution)/shard_map/pallas_call | solution.py:590
  (12 shorter events, 0.1 us)
Async XLA Ops:
  0.0 7.9 %copy-start.1 = (f32[2,4,32,256]{3,2,1,0:T(8,128)S(1)}, f32[2,4,32,256]{3,2,1,0:T(8,128)}, u32[]{:S(2)}) copy-start(f32[2,4,32,256]{3,2,1,0:T(8,128)} %courant.3) | copy-start | bytes 786436
  0.0 7.9 %copy-start = (f32[2,4,32,256]{3,2,1,0:T(8,128)S(1)}, f32[2,4,32,256]{3,2,1,0:T(8,128)}, u32[]{:S(2)}) copy-start(f32[2,4,32,256]{3,2,1,0:T(8,128)} %tracer.3) | copy-start | bytes 786436
  1.7 5.3 %collective-permute-start = (f32[40,256]{1,0:T(8,128)}, f32[40,256]{1,0:T(8,128)S(1)}, u32[]{:S(2)}, u32[]{:S(2)}) collective-permute-start(f32[40,256]{1,0:T(8,128)} %get-tuple-element.18), channel_id=1, source_target_pairs={{0,1},{1,0},{2,3},{3,2},{4,5},{5,4},{6,7},{7,6},{8,9},{9,8},{10,11... | collective-permute-start | bytes 122888 | tf_op jit(solution)/shard_map/ppermute | solution.py:151
  1.8 6.1 %collective-permute-start.1 = (f32[40,256]{1,0:T(8,128)}, f32[40,256]{1,0:T(8,128)S(1)}, u32[]{:S(2)}, u32[]{:S(2)}) collective-permute-start(f32[40,256]{1,0:T(8,128)} %get-tuple-element.19), channel_id=1, source_target_pairs={{1,2},{2,1},{5,6},{6,5},{9,10},{10,9},{13,14},{14,13},{17,18},{18,... | collective-permute-start | bytes 122888 | tf_op jit(solution)/shard_map/ppermute | solution.py:151
  7.9 5.7 %copy-start.5 = (s32[2,2,1024]{2,1,0:T(2,128)S(1)}, s32[2,2,1024]{2,1,0:T(2,128)}, u32[]{:S(2)}) copy-start(s32[2,2,1024]{2,1,0:T(2,128)} %lists.3) | copy-start | bytes 49156
  9.9 3.6 %copy-start.2 = (s32[32768]{0:T(1024)S(1)}, s32[32768]{0:T(1024)}, u32[]{:S(2)}) copy-start(s32[32768]{0:T(1024)} %param.8) | copy-start | bytes 393220
  10.0 3.6 %copy-start.3 = (f32[32768]{0:T(1024)S(1)}, f32[32768]{0:T(1024)}, u32[]{:S(2)}) copy-start(f32[32768]{0:T(1024)} %param.9) | copy-start | bytes 393220
  10.0 3.6 %copy-start.4 = (f32[32768]{0:T(1024)S(1)}, f32[32768]{0:T(1024)}, u32[]{:S(2)}) copy-start(f32[32768]{0:T(1024)} %param.10) | copy-start | bytes 393220
  10.0 7.6 %all-to-all-start = ((bf16[4,192,128]{2,1,0:T(8,128)(2,1)}), bf16[4,192,128]{2,1,0:T(8,128)(2,1)S(1)}, u32[]{:S(2)}, u32[]{:S(2)}) async-start(bf16[4,192,128]{2,1,0:T(8,128)(2,1)} %get-tuple-element.21), calls=%async_computation | async-start | bytes 393216 | tf_op jit(solution)/shard_map/all_to_all | solution.py:157
  17.6 4.3 %collective-permute-start.2 = (bf16[448,128]{1,0:T(8,128)(2,1)S(1)}, bf16[448,128]{1,0:T(8,128)(2,1)S(1)}, u32[]{:S(2)}, u32[]{:S(2)}) collective-permute-start(bf16[448,128]{1,0:T(8,128)(2,1)S(1)} %get-tuple-element.24), channel_id=1, source_target_pairs={{0,4},{4,0},{8,12},{12,8},{16,20},{20,16},{24,28},{28,24},{1,5},{5... | collective-permute-start | bytes 344072 | tf_op jit(solution)/shard_map/ppermute | solution.py:163
  23.4 3.7 %collective-permute-start.3 = (f32[24,128]{1,0:T(8,128)S(1)}, f32[24,128]{1,0:T(8,128)S(1)}, u32[]{:S(2)}, u32[]{:S(2)}) collective-permute-start(f32[24,128]{1,0:T(8,128)S(1)} %get-tuple-element.27), channel_id=1, source_target_pairs={{0,1},{1,0},{2,3},{3,2},{4,5},{5,4},{6,7},{7,6},{8,9},{9,8},{10,11... | collective-permute-start | bytes 36872 | tf_op jit(solution)/shard_map/ppermute | solution.py:151
  23.4 4.7 %collective-permute-start.4 = (f32[24,128]{1,0:T(8,128)S(1)}, f32[24,128]{1,0:T(8,128)S(1)}, u32[]{:S(2)}, u32[]{:S(2)}) collective-permute-start(f32[24,128]{1,0:T(8,128)S(1)} %get-tuple-element.28), channel_id=1, source_target_pairs={{1,2},{2,1},{5,6},{6,5},{9,10},{10,9},{13,14},{14,13},{17,18},{18,... | collective-permute-start | bytes 36872 | tf_op jit(solution)/shard_map/ppermute | solution.py:151
  36.2 3.3 %collective-permute-start.5 = (bf16[256,128]{1,0:T(8,128)(2,1)S(1)}, bf16[256,128]{1,0:T(8,128)(2,1)S(1)}, u32[]{:S(2)}, u32[]{:S(2)}) collective-permute-start(bf16[256,128]{1,0:T(8,128)(2,1)S(1)} %get-tuple-element.30), channel_id=1, source_target_pairs={{0,4},{4,0},{8,12},{12,8},{16,20},{20,16},{24,28},{28,24},{1,5},{5... | collective-permute-start | bytes 196616 | tf_op jit(solution)/shard_map/ppermute | solution.py:163

commit v8 on v5

--- a/solution.py
+++ b/solution.py
@@ -170,7 +170,7 @@
 
 
 def share_body(*refs, region_rows):
-    chunks, (own, other) = refs[:-2], refs[-2:]
+    chunks, (own, other) = refs[:-3], refs[-2:]
     _, _, core = place()
     first = core == 0
     each = own.shape[0] // len(chunks)
@@ -442,12 +442,14 @@
     for i in range(count):
         at = slice(i * LANES, (i + 1) * LANES)
         state = own[:, at] + first[:, at] + second[:, at] + start
+        columns = [pick_lanes(state, group_start + k) for k in range(ensemble)]
         pivots = jnp.ones((ensemble, LANES), f32)
         for k in range(ensemble):
-            column = pick_lanes(state, group_start + k)
-            pivot = column[k : k + 1, :]
-            scaled = state[k : k + 1, :] / pivot
-            state = state - jnp.where(row > k, column, 0.0) * scaled
+            pivot = columns[k][k : k + 1, :]
+            factor = jnp.where(row > k, columns[k], 0.0) / pivot
+            for j in range(k + 1, ensemble):
+                columns[j] = columns[j] - factor * columns[j][k : k + 1, :]
+            state = state - factor * state[k : k + 1, :]
             pivots = jnp.where(row[0:ensemble] == k, pivot, pivots)
         inverse = state[0:ensemble, :] * lax.rsqrt(pivots)
         mean_weight = -state[ensemble : ensemble + 1, :]
@@ -549,9 +551,6 @@
         cell_row,
     )
     received = exchange(chunks)
-    share = functools.partial(share_body, region_rows=region_rows)
-    mine, theirs = call(share, [((chips * all_rows, LANES), bf16)] * 2)(*received)
-    theirs = swap_cores(theirs)
     weights, values = call(
         functools.partial(
             weights_body, tiles=tiles, blocks=blocks, height=height, width=width, side=side
@@ -562,6 +561,10 @@
     )(obs_list, first, second, cell, flat(obs_value), flat(obs_error))
 
     sizes = dict(patches=patches, sources=blocks, members=members, region_rows=region_rows)
+    share = functools.partial(share_body, region_rows=region_rows)
+    mine, theirs = call(share, [((chips * all_rows, LANES), bf16)] * 2)(*received, values)
+    theirs = swap_cores(theirs)
+
     tall = 3 * patches * ensemble
     system_shape = (ensemble + 8, patches * ensemble // 64 * LANES)
     own, to_first, to_second = call(
@@ -586,7 +589,7 @@
         ],
     )(mine, theirs, own, first, second)
     returned = exchange(changes)
-    mine, theirs = call(share, [((chips * region_rows, LANES), bf16)] * 2)(*returned)
+    mine, theirs = call(share, [((chips * region_rows, LANES), bf16)] * 2)(*returned, forecast)
     theirs = swap_cores(theirs)
     (analysis,) = call(
         output_body, [(forecast.shape, f32)], [pltpu.VMEM((blocks, region_rows, LANES), f32)]

time: 38.6 us -> 36.9 us (0.956)
  Pallas kernels: 8.53 us -> 7.47 us
  starting transfers between devices: 20 us -> 19.6 us
    ppermute x6, waiting for transfers between devices: 5.65 us -> 4.54 us  [exchange(): lax.ppermute(chunks[s], 'member', swaps(s))]
    pallas_call x1, Pallas kernels: 1.74 us -> 0.69 us  [shards(): call(functools.partial(analysis_body, **sizes), [((2 * region_rows, LANES...]
    ppermute x2, waiting for transfers between devices: 0.9 us -> 1.87 us  [swap_cores(): lax.ppermute(array, 'member', [(i, i ^ 1) for i in range(lax.axis_size('m...]
where the time goes in v8:
time: 36.9 us; the launch traced here: 36.3 us
  starting transfers between devices  19.6 us (53%)
  waiting for transfers between devices  8.27 us (22%)
  Pallas kernels  7.47 us (20%)
  local copies, waits for them, and re-layouts  0.79 us (2%)
    ppermute x2, starting transfers between devices, swap(): lax.ppermute(second, 'tile', pairs(1))  8.12 us
    ppermute x2, starting transfers between devices, swap_cores(): lax.ppermute(array, 'member', [(i, i ^ 1) for i in range(lax.axis_size('m...  5.98 us
    ppermute x6, starting transfers between devices, exchange(): lax.ppermute(chunks[s], 'member', swaps(s))  5.43 us
    ppermute x6, waiting for transfers between devices, exchange(): lax.ppermute(chunks[s], 'member', swaps(s))  4.54 us
    ppermute x2, waiting for transfers between devices, swap_cores(): lax.ppermute(array, 'member', [(i, i ^ 1) for i in range(lax.axis_size('m...  1.87 us
    ppermute x2, waiting for transfers between devices, swap(): lax.ppermute(second, 'tile', pairs(1))  1.86 us
    pallas_call x1, Pallas kernels, shards(): call(pack_edges, [((edge_rows, width), f32)] * 2, [pltpu.VMEM(edge_shape,...  1.71 us
    pallas_call x1, Pallas kernels, shards(): call(functools.partial(systems_body, **sizes), [(system_shape, f32)] * 3,...  1.47 us
  transfers between devices with their start and end apart: 12, of which 9 were waited for; matrix products, arithmetic and copies ran while one was open for 2% of the time, Pallas kernels for 3%

profile of v8, /device:TPU:9, one launch (start us, length us, event | category | flops | bytes accessed | tf_op | source)
XLA Modules:
  0.0 36.3 jit_solution(10102218408667953680)
XLA Ops:
  0.0 1.7 %shard_map.64 = (f32[40,256]{1,0:T(8,128)}, f32[40,256]{1,0:T(8,128)}) custom-call(f32[2,4,32,256]{3,2,1,0:T(8,128)} %tracer.3, f32[2,4,32,256]{3,2,1,0:T(8,128)} %courant.3, s32[2,2,1024]{2,1,0:T(2,128)} %lists.3), custom_call_target="tpu_custom_call" | custom-call | flops 1000000 | bytes 1000000 | tf_op jit(solution)/shard_map/pallas_call | solution.py:518
  1.8 4.5 %collective-permute-start.1 = (f32[40,256]{1,0:T(8,128)}, f32[40,256]{1,0:T(8,128)S(1)}, u32[]{:S(2)}, u32[]{:S(2)}) collective-permute-start(f32[40,256]{1,0:T(8,128)} %get-tuple-element.26), channel_id=1, source_target_pairs={{1,2},{2,1},{5,6},{6,5},{9,10},{10,9},{13,14},{14,13},{17,18},{18,... | collective-permute-start | bytes 122888 | tf_op jit(solution)/shard_map/ppermute | solution.py:151
  6.3 0.8 %dynamic-slice_bitcast_fusion.cell = s32[8,8,128]{2,1,0:T(8,128)S(1)} fusion(s32[8,4,8,128]{3,2,1,0:T(8,128)} %bitcast.6, s32[]{:T(128)S(6)} %select_n.4), kind=kLoop, calls=%fused_computation | loop fusion | bytes 65540 | tf_op jit(solution)/shard_map/jit(dynamic_index_in_dim)/squeeze | solution.py:536
  7.1 0.8 %collective-permute-done.1.second = f32[40,256]{1,0:T(8,128)S(1)} collective-permute-done((f32[40,256]{1,0:T(8,128)}, f32[40,256]{1,0:T(8,128)S(1)}, u32[]{:S(2)}, u32[]{:S(2)}) %collective-permute-start.1) | collective-permute-done | bytes 40992 | tf_op jit(solution)/shard_map/ppermute | solution.py:151
  7.9 1.4 %shard_map.65 = (f32[2,4,32,256]{3,2,1,0:T(8,128)S(1)}, bf16[192,128]{1,0:T(8,128)(2,1)S(1)}, bf16[192,128]{1,0:T(8,128)(2,1)S(1)}, bf16[192,128]{1,0:T(8,128)(2,1)S(1)}, bf16[192,128]{1,0:T(8,128)(2,1)S(1)}) custom-call(f32[2,4,32,256]{3,2,1,0:T(8,128)S(1)} %copy-done, f32[2,4,32,256]{3,2,1,0:T(8,128)S(1)} %copy-done.1, ...), custom_call_target="tpu_custom_call" | custom-call | flops 1000000 | bytes 1000000 | tf_op jit(solution)/shard_map/pallas_call | solution.py:539
  9.3 1.3 %collective-permute-start.2 = (bf16[192,128]{1,0:T(8,128)(2,1)S(1)}, bf16[192,128]{1,0:T(8,128)(2,1)S(1)}, u32[]{:S(2)}, u32[]{:S(2)}) collective-permute-start(bf16[192,128]{1,0:T(8,128)(2,1)S(1)} %get-tuple-element.29), channel_id=1, source_target_pairs={{0,8},{4,12},{8,0},{12,4},{16,24},{20,28},{24,16},{28,20},{1,9},{5... | collective-permute-start | bytes 147464 | tf_op jit(solution)/shard_map/ppermute | solution.py:158
  10.6 1.2 %collective-permute-start.3 = (bf16[192,128]{1,0:T(8,128)(2,1)S(1)}, bf16[192,128]{1,0:T(8,128)(2,1)S(1)}, u32[]{:S(2)}, u32[]{:S(2)}) collective-permute-start(bf16[192,128]{1,0:T(8,128)(2,1)S(1)} %get-tuple-element.30), channel_id=1, source_target_pairs={{0,16},{4,20},{8,24},{12,28},{16,0},{20,4},{24,8},{28,12},{1,17},{... | collective-permute-start | bytes 147464 | tf_op jit(solution)/shard_map/ppermute | solution.py:158
  12.0 1.2 %shard_map.66 = (f32[16,3072]{1,0:T(8,128)S(1)}, f32[24,128]{1,0:T(8,128)S(1)}) custom-call(s32[2,2,1024]{2,1,0:T(2,128)S(1)} %copy-done.5, f32[40,256]{1,0:T(8,128)S(1)} %collective-permute-done.first, f32[40,256]{1,0:T(8,128)S(1)} %collective-permute-done.1.second, s32[256,128]{1,0:T(8,128)S(1)} %bitcast.7, f32[256,128]{1,0:T(8,128)S(1)} %bitcast.8, ...), custom_call_target="tpu_custom_call" | custom-call | flops 100000000 | bytes 1000000 | tf_op jit(solution)/shard_map/pallas_call | solution.py:554
  13.2 0.3 collective-permute-done.3.refs_2_
  13.5 2.7 %collective-permute-done.4.refs_3_ = bf16[192,128]{1,0:T(8,128)(2,1)S(1)} collective-permute-done((bf16[192,128]{1,0:T(8,128)(2,1)S(1)}, bf16[192,128]{1,0:T(8,128)(2,1)S(1)}, u32[]{:S(2)}, u32[]{:S(2)}) %collective-permute-start.4) | collective-permute-done | bytes 49184 | tf_op jit(solution)/shard_map/ppermute | solution.py:158
  16.2 3.1 %collective-permute-start.5 = (bf16[448,128]{1,0:T(8,128)(2,1)S(1)}, bf16[448,128]{1,0:T(8,128)(2,1)S(1)}, u32[]{:S(2)}, u32[]{:S(2)}) collective-permute-start(bf16[448,128]{1,0:T(8,128)(2,1)S(1)} %get-tuple-element.34), channel_id=1, source_target_pairs={{0,4},{4,0},{8,12},{12,8},{16,20},{20,16},{24,28},{28,24},{1,5},{5... | collective-permute-start | bytes 344072 | tf_op jit(solution)/shard_map/ppermute | solution.py:163
  19.3 1.0 %collective-permute-done.5.refs_1_ = bf16[448,128]{1,0:T(8,128)(2,1)S(1)} collective-permute-done((bf16[448,128]{1,0:T(8,128)(2,1)S(1)}, bf16[448,128]{1,0:T(8,128)(2,1)S(1)}, u32[]{:S(2)}, u32[]{:S(2)}) %collective-permute-start.5) | collective-permute-done | bytes 114720 | tf_op jit(solution)/shard_map/ppermute | solution.py:163
  20.3 1.5 %shard_map.68 = (f32[24,128]{1,0:T(8,128)S(1)}, f32[24,128]{1,0:T(8,128)S(1)}, f32[24,128]{1,0:T(8,128)S(1)}) custom-call(bf16[448,128]{1,0:T(8,128)(2,1)S(1)} %get-tuple-element.33.refs_0_, bf16[448,128]{1,0:T(8,128)(2,1)S(1)} %collective-permute-done.5.refs_1_, f32[16,3072]{1,0:T(8,128)S(1)} %get-tuple-element.35.refs_2_, ...), custom_call_target="tpu_custom_call" | custom-call | flops 1000000 | bytes 1000000 | tf_op jit(solution)/shard_map/pallas_call | solution.py:570
  21.8 3.6 %collective-permute-start.7 = (f32[24,128]{1,0:T(8,128)S(1)}, f32[24,128]{1,0:T(8,128)S(1)}, u32[]{:S(2)}, u32[]{:S(2)}) collective-permute-start(f32[24,128]{1,0:T(8,128)S(1)} %get-tuple-element.38), channel_id=1, source_target_pairs={{1,2},{2,1},{5,6},{6,5},{9,10},{10,9},{13,14},{14,13},{17,18},{18,... | collective-permute-start | bytes 36872 | tf_op jit(solution)/shard_map/ppermute | solution.py:151
  25.4 1.1 %collective-permute-done.7.refs_4_ = f32[24,128]{1,0:T(8,128)S(1)} collective-permute-done((f32[24,128]{1,0:T(8,128)S(1)}, f32[24,128]{1,0:T(8,128)S(1)}, u32[]{:S(2)}, u32[]{:S(2)}) %collective-permute-start.7) | collective-permute-done | bytes 12320 | tf_op jit(solution)/shard_map/ppermute | solution.py:151
  26.5 0.7 %shard_map.69 = (bf16[128,128]{1,0:T(8,128)(2,1)S(1)}, bf16[128,128]{1,0:T(8,128)(2,1)S(1)}, bf16[128,128]{1,0:T(8,128)(2,1)S(1)}, bf16[128,128]{1,0:T(8,128)(2,1)S(1)}) custom-call(bf16[448,128]{1,0:T(8,128)(2,1)S(1)} %get-tuple-element.33.refs_0_, bf16[448,128]{1,0:T(8,128)(2,1)S(1)} %collective-permute-done.5.refs_1_, ...), custom_call_target="tpu_custom_call" | custom-call | flops 1000000 | bytes 1000000 | tf_op jit(solution)/shard_map/pallas_call | solution.py:583
  27.2 0.3 collective-permute-start.8
  27.5 0.2 collective-permute-start.9
  27.7 2.2 %collective-permute-start.10 = (bf16[128,128]{1,0:T(8,128)(2,1)S(1)}, bf16[128,128]{1,0:T(8,128)(2,1)S(1)}, u32[]{:S(2)}, u32[]{:S(2)}) collective-permute-start(bf16[128,128]{1,0:T(8,128)(2,1)S(1)} %get-tuple-element.42), channel_id=1, source_target_pairs={{0,24},{4,28},{8,16},{12,20},{16,8},{20,12},{24,0},{28,4},{1,25},{... | collective-permute-start | bytes 98312 | tf_op jit(solution)/shard_map/ppermute | solution.py:158
  30.0 0.3 collective-permute-done.9.refs_2_
  30.3 1.2 %collective-permute-done.10.refs_3_ = bf16[128,128]{1,0:T(8,128)(2,1)S(1)} collective-permute-done((bf16[128,128]{1,0:T(8,128)(2,1)S(1)}, bf16[128,128]{1,0:T(8,128)(2,1)S(1)}, u32[]{:S(2)}, u32[]{:S(2)}) %collective-permute-start.10) | collective-permute-done | bytes 32800 | tf_op jit(solution)/shard_map/ppermute | solution.py:158
  31.5 2.9 %collective-permute-start.11 = (bf16[256,128]{1,0:T(8,128)(2,1)S(1)}, bf16[256,128]{1,0:T(8,128)(2,1)S(1)}, u32[]{:S(2)}, u32[]{:S(2)}) collective-permute-start(bf16[256,128]{1,0:T(8,128)(2,1)S(1)} %get-tuple-element.44), channel_id=1, source_target_pairs={{0,4},{4,0},{8,12},{12,8},{16,20},{20,16},{24,28},{28,24},{1,5},{5... | collective-permute-start | bytes 196616 | tf_op jit(solution)/shard_map/ppermute | solution.py:163
  34.4 0.9 %collective-permute-done.11.theirs = bf16[256,128]{1,0:T(8,128)(2,1)S(1)} collective-permute-done((bf16[256,128]{1,0:T(8,128)(2,1)S(1)}, bf16[256,128]{1,0:T(8,128)(2,1)S(1)}, u32[]{:S(2)}, u32[]{:S(2)}) %collective-permute-start.11) | collective-permute-done | bytes 65568 | tf_op jit(solution)/shard_map/ppermute | solution.py:163
  35.3 0.9 %shard_map.71 = f32[2,4,32,256]{3,2,1,0:T(8,128)} custom-call(f32[2,4,32,256]{3,2,1,0:T(8,128)S(1)} %get-tuple-element.27.refs_4_.forecast, bf16[256,128]{1,0:T(8,128)(2,1)S(1)} %get-tuple-element.43.mine, bf16[256,128]{1,0:T(8,128)(2,1)S(1)} %collective-permute-done.11.theirs), custom_call_target="tpu_custom_call" | custom-call | flops 1000000 | bytes 1000000 | tf_op jit(solution)/shard_map/pallas_call | solution.py:594
  (21 shorter events, 0.5 us)
Async XLA Ops:
  0.0 7.9 %copy-start.1 = (f32[2,4,32,256]{3,2,1,0:T(8,128)S(1)}, f32[2,4,32,256]{3,2,1,0:T(8,128)}, u32[]{:S(2)}) copy-start(f32[2,4,32,256]{3,2,1,0:T(8,128)} %courant.3) | copy-start | bytes 786436
  0.0 7.9 %copy-start = (f32[2,4,32,256]{3,2,1,0:T(8,128)S(1)}, f32[2,4,32,256]{3,2,1,0:T(8,128)}, u32[]{:S(2)}) copy-start(f32[2,4,32,256]{3,2,1,0:T(8,128)} %tracer.3) | copy-start | bytes 786436
  1.7 5.3 %collective-permute-start = (f32[40,256]{1,0:T(8,128)}, f32[40,256]{1,0:T(8,128)S(1)}, u32[]{:S(2)}, u32[]{:S(2)}) collective-permute-start(f32[40,256]{1,0:T(8,128)} %get-tuple-element.25), channel_id=1, source_target_pairs={{0,1},{1,0},{2,3},{3,2},{4,5},{5,4},{6,7},{7,6},{8,9},{9,8},{10,11... | collective-permute-start | bytes 122888 | tf_op jit(solution)/shard_map/ppermute | solution.py:151
  1.8 6.1 %collective-permute-start.1 = (f32[40,256]{1,0:T(8,128)}, f32[40,256]{1,0:T(8,128)S(1)}, u32[]{:S(2)}, u32[]{:S(2)}) collective-permute-start(f32[40,256]{1,0:T(8,128)} %get-tuple-element.26), channel_id=1, source_target_pairs={{1,2},{2,1},{5,6},{6,5},{9,10},{10,9},{13,14},{14,13},{17,18},{18,... | collective-permute-start | bytes 122888 | tf_op jit(solution)/shard_map/ppermute | solution.py:151
  7.1 5.0 %copy-start.2 = (s32[32768]{0:T(1024)S(1)}, s32[32768]{0:T(1024)}, u32[]{:S(2)}) copy-start(s32[32768]{0:T(1024)} %param.8) | copy-start | bytes 393220
  7.1 5.0 %copy-start.3 = (f32[32768]{0:T(1024)S(1)}, f32[32768]{0:T(1024)}, u32[]{:S(2)}) copy-start(f32[32768]{0:T(1024)} %param.9) | copy-start | bytes 393220
  7.1 5.0 %copy-start.4 = (f32[32768]{0:T(1024)S(1)}, f32[32768]{0:T(1024)}, u32[]{:S(2)}) copy-start(f32[32768]{0:T(1024)} %param.10) | copy-start | bytes 393220
  7.9 4.1 %copy-start.5 = (s32[2,2,1024]{2,1,0:T(2,128)S(1)}, s32[2,2,1024]{2,1,0:T(2,128)}, u32[]{:S(2)}) copy-start(s32[2,2,1024]{2,1,0:T(2,128)} %lists.3) | copy-start | bytes 49156
  9.3 3.9 %collective-permute-start.2 = (bf16[192,128]{1,0:T(8,128)(2,1)S(1)}, bf16[192,128]{1,0:T(8,128)(2,1)S(1)}, u32[]{:S(2)}, u32[]{:S(2)}) collective-permute-start(bf16[192,128]{1,0:T(8,128)(2,1)S(1)} %get-tuple-element.29), channel_id=1, source_target_pairs={{0,8},{4,12},{8,0},{12,4},{16,24},{20,28},{24,16},{28,20},{1,9},{5... | collective-permute-start | bytes 147464 | tf_op jit(solution)/shard_map/ppermute | solution.py:158
  10.6 2.9 %collective-permute-start.3 = (bf16[192,128]{1,0:T(8,128)(2,1)S(1)}, bf16[192,128]{1,0:T(8,128)(2,1)S(1)}, u32[]{:S(2)}, u32[]{:S(2)}) collective-permute-start(bf16[192,128]{1,0:T(8,128)(2,1)S(1)} %get-tuple-element.30), channel_id=1, source_target_pairs={{0,16},{4,20},{8,24},{12,28},{16,0},{20,4},{24,8},{28,12},{1,17},{... | collective-permute-start | bytes 147464 | tf_op jit(solution)/shard_map/ppermute | solution.py:158
  11.8 4.4 %collective-permute-start.4 = (bf16[192,128]{1,0:T(8,128)(2,1)S(1)}, bf16[192,128]{1,0:T(8,128)(2,1)S(1)}, u32[]{:S(2)}, u32[]{:S(2)}) collective-permute-start(bf16[192,128]{1,0:T(8,128)(2,1)S(1)} %get-tuple-element.31), channel_id=1, source_target_pairs={{0,24},{4,28},{8,16},{12,20},{16,8},{20,12},{24,0},{28,4},{1,25},{... | collective-permute-start | bytes 147464 | tf_op jit(solution)/shard_map/ppermute | solution.py:158
  16.2 4.0 %collective-permute-start.5 = (bf16[448,128]{1,0:T(8,128)(2,1)S(1)}, bf16[448,128]{1,0:T(8,128)(2,1)S(1)}, u32[]{:S(2)}, u32[]{:S(2)}) collective-permute-start(bf16[448,128]{1,0:T(8,128)(2,1)S(1)} %get-tuple-element.34), channel_id=1, source_target_pairs={{0,4},{4,0},{8,12},{12,8},{16,20},{20,16},{24,28},{28,24},{1,5},{5... | collective-permute-start | bytes 344072 | tf_op jit(solution)/shard_map/ppermute | solution.py:163
  21.7 3.7 %collective-permute-start.6 = (f32[24,128]{1,0:T(8,128)S(1)}, f32[24,128]{1,0:T(8,128)S(1)}, u32[]{:S(2)}, u32[]{:S(2)}) collective-permute-start(f32[24,128]{1,0:T(8,128)S(1)} %get-tuple-element.37), channel_id=1, source_target_pairs={{0,1},{1,0},{2,3},{3,2},{4,5},{5,4},{6,7},{7,6},{8,9},{9,8},{10,11... | collective-permute-start | bytes 36872 | tf_op jit(solution)/shard_map/ppermute | solution.py:151
  21.8 4.7 %collective-permute-start.7 = (f32[24,128]{1,0:T(8,128)S(1)}, f32[24,128]{1,0:T(8,128)S(1)}, u32[]{:S(2)}, u32[]{:S(2)}) collective-permute-start(f32[24,128]{1,0:T(8,128)S(1)} %get-tuple-element.38), channel_id=1, source_target_pairs={{1,2},{2,1},{5,6},{6,5},{9,10},{10,9},{13,14},{14,13},{17,18},{18,... | collective-permute-start | bytes 36872 | tf_op jit(solution)/shard_map/ppermute | solution.py:151
  27.2 2.8 %collective-permute-start.8 = (bf16[128,128]{1,0:T(8,128)(2,1)S(1)}, bf16[128,128]{1,0:T(8,128)(2,1)S(1)}, u32[]{:S(2)}, u32[]{:S(2)}) collective-permute-start(bf16[128,128]{1,0:T(8,128)(2,1)S(1)} %get-tuple-element.40), channel_id=1, source_target_pairs={{0,8},{4,12},{8,0},{12,4},{16,24},{20,28},{24,16},{28,20},{1,9},{5... | collective-permute-start | bytes 98312 | tf_op jit(solution)/shard_map/ppermute | solution.py:158
  27.5 2.8 %collective-permute-start.9 = (bf16[128,128]{1,0:T(8,128)(2,1)S(1)}, bf16[128,128]{1,0:T(8,128)(2,1)S(1)}, u32[]{:S(2)}, u32[]{:S(2)}) collective-permute-start(bf16[128,128]{1,0:T(8,128)(2,1)S(1)} %get-tuple-element.41), channel_id=1, source_target_pairs={{0,16},{4,20},{8,24},{12,28},{16,0},{20,4},{24,8},{28,12},{1,17},{... | collective-permute-start | bytes 98312 | tf_op jit(solution)/shard_map/ppermute | solution.py:158
  27.7 3.8 %collective-permute-start.10 = (bf16[128,128]{1,0:T(8,128)(2,1)S(1)}, bf16[128,128]{1,0:T(8,128)(2,1)S(1)}, u32[]{:S(2)}, u32[]{:S(2)}) collective-permute-start(bf16[128,128]{1,0:T(8,128)(2,1)S(1)} %get-tuple-element.42), channel_id=1, source_target_pairs={{0,24},{4,28},{8,16},{12,20},{16,8},{20,12},{24,0},{28,4},{1,25},{... | collective-permute-start | bytes 98312 | tf_op jit(solution)/shard_map/ppermute | solution.py:158
  31.5 3.8 %collective-permute-start.11 = (bf16[256,128]{1,0:T(8,128)(2,1)S(1)}, bf16[256,128]{1,0:T(8,128)(2,1)S(1)}, u32[]{:S(2)}, u32[]{:S(2)}) collective-permute-start(bf16[256,128]{1,0:T(8,128)(2,1)S(1)} %get-tuple-element.44), channel_id=1, source_target_pairs={{0,4},{4,0},{8,12},{12,8},{16,20},{20,16},{24,28},{28,24},{1,5},{5... | collective-permute-start | bytes 196616 | tf_op jit(solution)/shard_map/ppermute | solution.py:163

commit v9 on v8

--- a/solution.py
+++ b/solution.py
@@ -151,12 +151,17 @@
     return lax.ppermute(first, "tile", pairs(0)), lax.ppermute(second, "tile", pairs(1))
 
 
+def turn(s, chips):
+    return (chips - s) % chips
+
+
 def exchange(chunks):
     chips = len(chunks)
     device = lambda chip, core: 2 * chip + core
-    swaps = lambda s: [(device(i, c), device(i ^ s, c)) for i in range(chips) for c in (0, 1)]
-    received = {s: lax.ppermute(chunks[s], "member", swaps(s)) for s in range(chips - 1, 0, -1)}
-    return [chunks[0]] + [received[s] for s in range(1, chips)]
+    swaps = lambda s: [
+        (device(i, c), device(i ^ turn(s, chips), c)) for i in range(chips) for c in (0, 1)
+    ]
+    return [chunks[0]] + [lax.ppermute(chunks[s], "member", swaps(s)) for s in range(1, chips)]
 
 
 def swap_cores(array):
@@ -270,7 +275,7 @@
             )
     _, chip, _ = place()
     for s, chunk in enumerate(chunks):
-        chunk[...] = send[chip ^ s]
+        chunk[...] = send[chip ^ turn(s, len(chunks))]
 
 
 def weights_body(
@@ -350,9 +355,33 @@
     return lax.dot_general(left, right, (((1,), (1,)), ((), ())), preferred_element_type=f32)
 
 
-def systems_body(*refs, patches, sources, members, region_rows):
-    mine, theirs, weights, values, own, to_first, to_second = refs[:7]
-    planes, tall_high, tall_low, wide_high, wide_low = refs[7:]
+def scale(spread, weights, tall_high, tall_low, at, first):
+    ensemble = spread.shape[0]
+    for p in range(tall_high.shape[0] // ensemble):
+        high, low = halves(spread * weights[first + p : first + p + 1, at])
+        tall_high[p * ensemble : (p + 1) * ensemble, at] = high
+        tall_low[p * ensemble : (p + 1) * ensemble, at] = low
+
+
+def products(wide, tall_high, tall_low):
+    rows = wide.shape[0] // 2
+    both = dot_rows(wide[...], tall_high[...])
+    result = both[0:rows] + both[rows:] + dot_rows(wide[0:rows, :], tall_low[...])
+    count = result.shape[1] // 64
+    if count % 2:
+        result = jnp.concatenate([result, jnp.zeros((rows, 64), f32)], axis=1)
+    found = []
+    for n in range(count):
+        piece = result[:, n // 2 * LANES : (n // 2 + 1) * LANES]
+        if n % 2:
+            piece = pltpu.roll(piece, 64, 1)
+        found.append(jnp.where(iota(piece.shape, 1) < 64, piece, 0.0))
+    return found
+
+
+def neighbours_body(
+    mine, theirs, weights, values, to_first, to_second, wide, planes, tall_high, tall_low, *, sources, members, region_rows
+):
     depth = 3 * BLOCK
     each = 2 * mine.shape[0] // sources
     _, chip, core = place()
@@ -361,7 +390,7 @@
     for s in range(sources):
         source, row = (mine, theirs)[s % 2], s // 2 * each
         both = source[row + region_rows : row + each, :].astype(f32)
-        device = 2 * (chip ^ (s // 2)) + (core ^ (s % 2))
+        device = 2 * (chip ^ turn(s // 2, sources // 2)) + (core ^ (s % 2))
         at = pl.multiple_of(device * (members * depth), BLOCK)
         planes[pl.ds(at, members * depth), :] = both
         for b in range(members):
@@ -372,53 +401,36 @@
     planes[ensemble * depth : (ensemble + 1) * depth, :] = values[...] - mean
     for k in range(ensemble + 1, ensemble + 8):
         planes[k * depth : (k + 1) * depth, :] = jnp.zeros((depth, LANES), f32)
+    rows = ensemble + 8
+    patches = tall_high.shape[0] // (2 * ensemble)
     for i in range(depth):
         at = slice(i * LANES, (i + 1) * LANES)
-        tile = planes[pl.ds(i, ensemble + 8, stride=depth), :]
+        tile = planes[pl.ds(i, rows, stride=depth), :]
         high, low = halves(tile)
-        wide_high[:, at] = high
-        wide_low[:, at] = low
-        spread = tile[0:ensemble, :]
-        for p in range(3 * patches):
-            high, low = halves(spread * weights[p : p + 1, at])
-            tall_high[p * ensemble : (p + 1) * ensemble, at] = high
-            tall_low[p * ensemble : (p + 1) * ensemble, at] = low
-    result = (
-        dot_rows(wide_high[...], tall_high[...])
-        + dot_rows(wide_low[...], tall_high[...])
-        + dot_rows(wide_high[...], tall_low[...])
-    )
-    count = patches * ensemble // 64
-    even = lax.rem(lax.axis_index("tile"), 2) == 0
-    found = []
-    for n in range(3 * count):
-        piece = result[:, n // 2 * LANES : (n // 2 + 1) * LANES] if n // 2 * LANES + LANES <= result.shape[1] else None
-        if piece is None:
-            piece = jnp.concatenate([result[:, n * 64 :], jnp.zeros((ensemble + 8, 64), f32)], axis=1)
-        else:
-            if n % 2:
-                piece = pltpu.roll(piece, 64, 1)
-            piece = jnp.where(iota(piece.shape, 1) < 64, piece, 0.0)
-        found.append(piece)
+        wide[0:rows, at] = high
+        wide[rows : 2 * rows, at] = low
+        scale(tile[0:ensemble, :], weights, tall_high, tall_low, at, patches)
+    found = products(wide, tall_high, tall_low)
+    odd = lax.rem(lax.axis_index("tile"), 2) == 1
+    count = len(found) // 2
     for i in range(count):
         at = slice(i * LANES, (i + 1) * LANES)
-        own[:, at] = found[i]
-        for_south, for_north = found[count + i], found[2 * count + i]
-        to_first[:, at] = jnp.where(even, for_north, for_south)
-        to_second[:, at] = jnp.where(even, for_south, for_north)
-
-
-def analysis_body(*refs, patches, sources, members, region_rows):
-    mine, theirs, own, first, second = refs[:5]
-    chunks, (centred, factors) = refs[5:-2], refs[-2:]
+        for_south, for_north = found[i], found[count + i]
+        to_first[:, at] = jnp.where(odd, for_south, for_north)
+        to_second[:, at] = jnp.where(odd, for_north, for_south)
+
+
+def own_body(
+    mine, theirs, weights, wide, own, centred, tall_high, tall_low, *, sources, members, region_rows
+):
+    _, chip, core = place()
     each = 2 * mine.shape[0] // sources
-    _, chip, core = place()
     ensemble = sources * members
     hits = region_rows // members
     total = jnp.zeros((hits, LANES), f32)
     for s in range(sources):
         source, row = (mine, theirs)[s % 2], s // 2 * each
-        device = 2 * (chip ^ (s // 2)) + (core ^ (s % 2))
+        device = 2 * (chip ^ turn(s // 2, sources // 2)) + (core ^ (s % 2))
         part = source[row : row + region_rows, :].astype(f32)
         for b in range(members):
             one = part[b * hits : (b + 1) * hits, :]
@@ -427,7 +439,20 @@
     mean = total / ensemble
     for k in range(ensemble):
         centred[k] -= mean
-
+    rows = ensemble + 8
+    for i in range(0, wide.shape[1], LANES):
+        at = slice(i, i + LANES)
+        spread = wide[0:ensemble, at].astype(f32) + wide[rows : rows + ensemble, at].astype(f32)
+        scale(spread, weights, tall_high, tall_low, at, 0)
+    for i, piece in enumerate(products(wide, tall_high, tall_low)):
+        own[:, i * LANES : (i + 1) * LANES] = piece
+
+
+def analysis_body(own, first, second, centred, *refs, patches, sources, members, region_rows):
+    chunks, factors = refs[:-1], refs[-1]
+    _, chip, _ = place()
+    ensemble = sources * members
+    hits = region_rows // members
     count = patches * ensemble // 64
     group = 64 // ensemble
     row = iota((ensemble + 8, LANES), 0)
@@ -469,7 +494,7 @@
 
     for s, chunk in enumerate(chunks):
         for c in (0, 1):
-            first_member = (2 * (chip ^ s) + c) * members
+            first_member = (2 * (chip ^ turn(s, len(chunks))) + c) * members
             totals = [jnp.zeros((hits, LANES), f32) for _ in range(members)]
             for j in range(ensemble):
                 centred_j = centred[j]
@@ -483,10 +508,12 @@
     members, levels, side, width = forecast.shape
     _, chip, core = place()
     rows = ordered.shape[1]
-    for s in range(mine.shape[0] // rows):
+    chips = mine.shape[0] // rows
+    for s in range(chips):
         at = slice(s * rows, (s + 1) * rows)
-        ordered[2 * (chip ^ s) + core] = mine[at, :].astype(f32)
-        ordered[2 * (chip ^ s) + (core ^ 1)] = theirs[at, :].astype(f32)
+        source = 2 * (chip ^ turn(s, chips))
+        ordered[source + core] = mine[at, :].astype(f32)
+        ordered[source + (core ^ 1)] = theirs[at, :].astype(f32)
     for q in range(width // LANES):
         parts = [ordered[4 * q + c] for c in range(4)]
         at = slice(q * LANES, (q + 1) * LANES)
@@ -560,34 +587,37 @@
         flops=100_000_000,
     )(obs_list, first, second, cell, flat(obs_value), flat(obs_error))
 
-    sizes = dict(patches=patches, sources=blocks, members=members, region_rows=region_rows)
+    sizes = dict(sources=blocks, members=members, region_rows=region_rows)
+    tall = patches * ensemble
+    length = depth * LANES
+    system_shape = (ensemble + 8, tall // 64 * LANES)
+    wide_shape = (2 * (ensemble + 8), length)
+    centred_shape = (ensemble, levels * BLOCK, LANES)
     share = functools.partial(share_body, region_rows=region_rows)
     mine, theirs = call(share, [((chips * all_rows, LANES), bf16)] * 2)(*received, values)
     theirs = swap_cores(theirs)
-
-    tall = 3 * patches * ensemble
-    system_shape = (ensemble + 8, patches * ensemble // 64 * LANES)
-    own, to_first, to_second = call(
-        functools.partial(systems_body, **sizes),
-        [(system_shape, f32)] * 3,
+    to_first, to_second, wide = call(
+        functools.partial(neighbours_body, **sizes),
+        [(system_shape, f32), (system_shape, f32), (wide_shape, bf16)],
         [
             pltpu.VMEM(((ensemble + 8) * depth, LANES), f32),
-            pltpu.VMEM((tall, depth * LANES), bf16),
-            pltpu.VMEM((tall, depth * LANES), bf16),
-            pltpu.VMEM((ensemble + 8, depth * LANES), bf16),
-            pltpu.VMEM((ensemble + 8, depth * LANES), bf16),
+            pltpu.VMEM((2 * tall, length), bf16),
+            pltpu.VMEM((2 * tall, length), bf16),
         ],
     )(mine, theirs, weights, values)
     first, second = swap(to_first, to_second, tiles)
+    own, centred = call(
+        functools.partial(own_body, **sizes),
+        [(system_shape, f32), (centred_shape, f32)],
+        [pltpu.VMEM((tall, length), bf16), pltpu.VMEM((tall, length), bf16)],
+        flops=50_000_000,
+    )(mine, theirs, weights, wide)
 
     changes = call(
-        functools.partial(analysis_body, **sizes),
+        functools.partial(analysis_body, patches=patches, **sizes),
         [((2 * region_rows, LANES), bf16)] * chips,
-        [
-            pltpu.VMEM((ensemble, levels * BLOCK, LANES), f32),
-            pltpu.VMEM((ensemble, ensemble, LANES), f32),
-        ],
-    )(mine, theirs, own, first, second)
+        [pltpu.VMEM((ensemble, ensemble, LANES), f32)],
+    )(own, first, second, centred)
     returned = exchange(changes)
     mine, theirs = call(share, [((chips * region_rows, LANES), bf16)] * 2)(*returned, forecast)
     theirs = swap_cores(theirs)

time: 36.9 us -> 35.3 us (0.957)
  waiting for transfers between devices: 8.27 us -> 6.26 us
  starting transfers between devices: 19.6 us -> 20.2 us
    ppermute x6, waiting for transfers between devices: 4.54 us -> 3.02 us  [exchange(): lax.ppermute(chunks[s], 'member', swaps(s))]
    ppermute x2, starting transfers between devices: 5.98 us -> 6.6 us  [swap_cores(): lax.ppermute(array, 'member', [(i, i ^ 1) for i in range(lax.axis_size('m...]
    ppermute x2, waiting for transfers between devices: 1.86 us -> 1.37 us  [swap(): lax.ppermute(second, 'tile', pairs(1))]
    pallas_call x2 -> x3, Pallas kernels: 2.16 us -> 1.96 us  [the longest x1 0.79 us: shards(): call(functools.partial(neighbours_body, **sizes), [(system_shape, f32), (...]
  transfers between devices with their start and end apart: 12 -> 12, of which waited for: 9 -> 9; matrix products, arithmetic and copies ran while one was open for 2% -> 2% of each run, Pallas kernels for 3% -> 5%
where the time goes in v9:
time: 35.3 us; the launch traced here: 34.7 us
  starting transfers between devices  20.2 us (57%)
  Pallas kernels  7.27 us (21%)
  waiting for transfers between devices  6.26 us (18%)
  local copies, waits for them, and re-layouts  0.79 us (2%)
    ppermute x2, starting transfers between devices, swap(): lax.ppermute(second, 'tile', pairs(1))  8.12 us
    ppermute x2, starting transfers between devices, swap_cores(): lax.ppermute(array, 'member', [(i, i ^ 1) for i in range(lax.axis_size('m...  6.6 us
    ppermute x6, starting transfers between devices, exchange(): lax.ppermute(chunks[s], 'member', swaps(s))  5.43 us
    ppermute x6, waiting for transfers between devices, exchange(): lax.ppermute(chunks[s], 'member', swaps(s))  3.02 us
    ppermute x2, waiting for transfers between devices, swap_cores(): lax.ppermute(array, 'member', [(i, i ^ 1) for i in range(lax.axis_size('m...  1.87 us
    pallas_call x1, Pallas kernels, shards(): call(pack_edges, [((edge_rows, width), f32)] * 2, [pltpu.VMEM(edge_shape,...  1.71 us
    pallas_call x1, Pallas kernels, shards(): call(functools.partial(forecast_body, tiles=tiles, height=height), [(memb...  1.41 us
    ppermute x2, waiting for transfers between devices, swap(): lax.ppermute(second, 'tile', pairs(1))  1.37 us
  transfers between devices with their start and end apart: 12, of which 9 were waited for; matrix products, arithmetic and copies ran while one was open for 2% of the time, Pallas kernels for 5%

profile of v9, /device:TPU:9, one launch (start us, length us, event | category | flops | bytes accessed | tf_op | source)
XLA Modules:
  0.0 34.7 jit_solution(17638183364652146055)
XLA Ops:
  0.0 1.7 %shard_map.64 = (f32[40,256]{1,0:T(8,128)}, f32[40,256]{1,0:T(8,128)}) custom-call(f32[2,4,32,256]{3,2,1,0:T(8,128)} %tracer.3, f32[2,4,32,256]{3,2,1,0:T(8,128)} %courant.3, s32[2,2,1024]{2,1,0:T(2,128)} %lists.3), custom_call_target="tpu_custom_call" | custom-call | flops 1000000 | bytes 1000000 | tf_op jit(solution)/shard_map/pallas_call | solution.py:545
  1.8 4.5 %collective-permute-start.1 = (f32[40,256]{1,0:T(8,128)}, f32[40,256]{1,0:T(8,128)S(1)}, u32[]{:S(2)}, u32[]{:S(2)}) collective-permute-start(f32[40,256]{1,0:T(8,128)} %get-tuple-element.28), channel_id=1, source_target_pairs={{1,2},{2,1},{5,6},{6,5},{9,10},{10,9},{13,14},{14,13},{17,18},{18,... | collective-permute-start | bytes 122888 | tf_op jit(solution)/shard_map/ppermute | solution.py:151
  6.3 0.8 %dynamic-slice_bitcast_fusion.cell = s32[8,8,128]{2,1,0:T(8,128)S(1)} fusion(s32[8,4,8,128]{3,2,1,0:T(8,128)} %bitcast.6, s32[]{:T(128)S(6)} %select_n.4), kind=kLoop, calls=%fused_computation | loop fusion | bytes 65540 | tf_op jit(solution)/shard_map/jit(dynamic_index_in_dim)/squeeze | solution.py:563
  7.1 0.8 %collective-permute-done.1.second = f32[40,256]{1,0:T(8,128)S(1)} collective-permute-done((f32[40,256]{1,0:T(8,128)}, f32[40,256]{1,0:T(8,128)S(1)}, u32[]{:S(2)}, u32[]{:S(2)}) %collective-permute-start.1) | collective-permute-done | bytes 40992 | tf_op jit(solution)/shard_map/ppermute | solution.py:151
  7.9 1.4 %shard_map.65 = (f32[2,4,32,256]{3,2,1,0:T(8,128)S(1)}, bf16[192,128]{1,0:T(8,128)(2,1)S(1)}, bf16[192,128]{1,0:T(8,128)(2,1)S(1)}, bf16[192,128]{1,0:T(8,128)(2,1)S(1)}, bf16[192,128]{1,0:T(8,128)(2,1)S(1)}) custom-call(f32[2,4,32,256]{3,2,1,0:T(8,128)S(1)} %copy-done, f32[2,4,32,256]{3,2,1,0:T(8,128)S(1)} %copy-done.1, ...), custom_call_target="tpu_custom_call" | custom-call | flops 1000000 | bytes 1000000 | tf_op jit(solution)/shard_map/pallas_call | solution.py:566
  9.3 2.2 %collective-permute-start.2 = (bf16[192,128]{1,0:T(8,128)(2,1)S(1)}, bf16[192,128]{1,0:T(8,128)(2,1)S(1)}, u32[]{:S(2)}, u32[]{:S(2)}) collective-permute-start(bf16[192,128]{1,0:T(8,128)(2,1)S(1)} %get-tuple-element.31), channel_id=1, source_target_pairs={{0,24},{4,28},{8,16},{12,20},{16,8},{20,12},{24,0},{28,4},{1,25},{... | collective-permute-start | bytes 147464 | tf_op jit(solution)/shard_map/ppermute | solution.py:164
  11.7 0.3 collective-permute-start.4
  12.0 1.2 %shard_map.66 = (f32[16,3072]{1,0:T(8,128)S(1)}, f32[24,128]{1,0:T(8,128)S(1)}) custom-call(s32[2,2,1024]{2,1,0:T(2,128)S(1)} %copy-done.5, f32[40,256]{1,0:T(8,128)S(1)} %collective-permute-done.first, f32[40,256]{1,0:T(8,128)S(1)} %collective-permute-done.1.second, s32[256,128]{1,0:T(8,128)S(1)} %bitcast.7, f32[256,128]{1,0:T(8,128)S(1)} %bitcast.8, ...), custom_call_target="tpu_custom_call" | custom-call | flops 100000000 | bytes 1000000 | tf_op jit(solution)/shard_map/pallas_call | solution.py:581
  13.2 1.2 %collective-permute-done.3.refs_2_ = bf16[192,128]{1,0:T(8,128)(2,1)S(1)} collective-permute-done((bf16[192,128]{1,0:T(8,128)(2,1)S(1)}, bf16[192,128]{1,0:T(8,128)(2,1)S(1)}, u32[]{:S(2)}, u32[]{:S(2)}) %collective-permute-start.3) | collective-permute-done | bytes 49184 | tf_op jit(solution)/shard_map/ppermute | solution.py:164
  14.7 3.6 %collective-permute-start.5 = (bf16[448,128]{1,0:T(8,128)(2,1)S(1)}, bf16[448,128]{1,0:T(8,128)(2,1)S(1)}, u32[]{:S(2)}, u32[]{:S(2)}) collective-permute-start(bf16[448,128]{1,0:T(8,128)(2,1)S(1)} %get-tuple-element.36), channel_id=1, source_target_pairs={{0,4},{4,0},{8,12},{12,8},{16,20},{20,16},{24,28},{28,24},{1,5},{5... | collective-permute-start | bytes 344072 | tf_op jit(solution)/shard_map/ppermute | solution.py:168
  18.3 1.0 %collective-permute-done.5.theirs = bf16[448,128]{1,0:T(8,128)(2,1)S(1)} collective-permute-done((bf16[448,128]{1,0:T(8,128)(2,1)S(1)}, bf16[448,128]{1,0:T(8,128)(2,1)S(1)}, u32[]{:S(2)}, u32[]{:S(2)}) %collective-permute-start.5) | collective-permute-done | bytes 114720 | tf_op jit(solution)/shard_map/ppermute | solution.py:168
  19.3 0.8 %shard_map.68 = (f32[24,128]{1,0:T(8,128)S(1)}, f32[24,128]{1,0:T(8,128)S(1)}, bf16[48,3072]{1,0:T(8,128)(2,1)S(1)}) custom-call(bf16[448,128]{1,0:T(8,128)(2,1)S(1)} %get-tuple-element.35.mine, bf16[448,128]{1,0:T(8,128)(2,1)S(1)} %collective-permute-done.5.theirs, f32[16,3072]{1,0:T(8,128)S(1)} %get-tuple-element.37.weights, ...), custom_call_target="tpu_custom_call" | custom-call | flops 1000000 | bytes 1000000 | tf_op jit(solution)/shard_map/pallas_call | solution.py:599
  20.1 3.6 %collective-permute-start.7 = (f32[24,128]{1,0:T(8,128)S(1)}, f32[24,128]{1,0:T(8,128)S(1)}, u32[]{:S(2)}, u32[]{:S(2)}) collective-permute-start(f32[24,128]{1,0:T(8,128)S(1)} %get-tuple-element.41), channel_id=1, source_target_pairs={{1,2},{2,1},{5,6},{6,5},{9,10},{10,9},{13,14},{14,13},{17,18},{18,... | collective-permute-start | bytes 36872 | tf_op jit(solution)/shard_map/ppermute | solution.py:151
  23.8 0.5 %shard_map.69 = (f32[24,128]{1,0:T(8,128)S(1)}, f32[16,32,128]{2,1,0:T(8,128)S(1)}) custom-call(bf16[448,128]{1,0:T(8,128)(2,1)S(1)} %get-tuple-element.35.mine, bf16[448,128]{1,0:T(8,128)(2,1)S(1)} %collective-permute-done.5.theirs, f32[16,3072]{1,0:T(8,128)S(1)} %get-tuple-element.37.weights, bf16[48,3072]{1,0:T(8,128)(2,1)S(1)} %get-tuple-element.38.wide), custom_call_target="tpu_custom_call" | custom-call | flops 50000000 | bytes 1000000 | tf_op jit(solution)/shard_map/pallas_call | solution.py:609
  24.3 0.6 %collective-permute-done.7.second = f32[24,128]{1,0:T(8,128)S(1)} collective-permute-done((f32[24,128]{1,0:T(8,128)S(1)}, f32[24,128]{1,0:T(8,128)S(1)}, u32[]{:S(2)}, u32[]{:S(2)}) %collective-permute-start.7) | collective-permute-done | bytes 12320 | tf_op jit(solution)/shard_map/ppermute | solution.py:151
  24.8 0.7 %shard_map.70 = (bf16[128,128]{1,0:T(8,128)(2,1)S(1)}, bf16[128,128]{1,0:T(8,128)(2,1)S(1)}, bf16[128,128]{1,0:T(8,128)(2,1)S(1)}, bf16[128,128]{1,0:T(8,128)(2,1)S(1)}) custom-call(f32[24,128]{1,0:T(8,128)S(1)} %get-tuple-element.39.own, f32[24,128]{1,0:T(8,128)S(1)} %collective-permute-done.6.first, f32[24,128]{1,0:T(8,128)S(1)} %collective-permute-done.7.second, ...), custom_call_target="tpu_custom_call" | custom-call | flops 1000000 | bytes 1000000 | tf_op jit(solution)/shard_map/pallas_call | solution.py:616
  25.5 1.3 %collective-permute-start.8 = (bf16[128,128]{1,0:T(8,128)(2,1)S(1)}, bf16[128,128]{1,0:T(8,128)(2,1)S(1)}, u32[]{:S(2)}, u32[]{:S(2)}) collective-permute-start(bf16[128,128]{1,0:T(8,128)(2,1)S(1)} %get-tuple-element.44), channel_id=1, source_target_pairs={{0,24},{4,28},{8,16},{12,20},{16,8},{20,12},{24,0},{28,4},{1,25},{... | collective-permute-start | bytes 98312 | tf_op jit(solution)/shard_map/ppermute | solution.py:164
  26.8 0.2 collective-permute-start.9
  27.0 1.2 %collective-permute-start.10 = (bf16[128,128]{1,0:T(8,128)(2,1)S(1)}, bf16[128,128]{1,0:T(8,128)(2,1)S(1)}, u32[]{:S(2)}, u32[]{:S(2)}) collective-permute-start(bf16[128,128]{1,0:T(8,128)(2,1)S(1)} %get-tuple-element.46), channel_id=1, source_target_pairs={{0,8},{4,12},{8,0},{12,4},{16,24},{20,28},{24,16},{28,20},{1,9},{5... | collective-permute-start | bytes 98312 | tf_op jit(solution)/shard_map/ppermute | solution.py:164
  28.2 1.0 %collective-permute-done.8.refs_1_ = bf16[128,128]{1,0:T(8,128)(2,1)S(1)} collective-permute-done((bf16[128,128]{1,0:T(8,128)(2,1)S(1)}, bf16[128,128]{1,0:T(8,128)(2,1)S(1)}, u32[]{:S(2)}, u32[]{:S(2)}) %collective-permute-start.8) | collective-permute-done | bytes 32800 | tf_op jit(solution)/shard_map/ppermute | solution.py:164
  29.3 0.4 %collective-permute-done.9.refs_2_ = bf16[128,128]{1,0:T(8,128)(2,1)S(1)} collective-permute-done((bf16[128,128]{1,0:T(8,128)(2,1)S(1)}, bf16[128,128]{1,0:T(8,128)(2,1)S(1)}, u32[]{:S(2)}, u32[]{:S(2)}) %collective-permute-start.9) | collective-permute-done | bytes 32800 | tf_op jit(solution)/shard_map/ppermute | solution.py:164
  29.8 3.0 %collective-permute-start.11 = (bf16[256,128]{1,0:T(8,128)(2,1)S(1)}, bf16[256,128]{1,0:T(8,128)(2,1)S(1)}, u32[]{:S(2)}, u32[]{:S(2)}) collective-permute-start(bf16[256,128]{1,0:T(8,128)(2,1)S(1)} %get-tuple-element.48), channel_id=1, source_target_pairs={{0,4},{4,0},{8,12},{12,8},{16,20},{20,16},{24,28},{28,24},{1,5},{5... | collective-permute-start | bytes 196616 | tf_op jit(solution)/shard_map/ppermute | solution.py:168
  32.8 0.9 %collective-permute-done.11.theirs = bf16[256,128]{1,0:T(8,128)(2,1)S(1)} collective-permute-done((bf16[256,128]{1,0:T(8,128)(2,1)S(1)}, bf16[256,128]{1,0:T(8,128)(2,1)S(1)}, u32[]{:S(2)}, u32[]{:S(2)}) %collective-permute-start.11) | collective-permute-done | bytes 65568 | tf_op jit(solution)/shard_map/ppermute | solution.py:168
  33.7 0.9 %shard_map.72 = f32[2,4,32,256]{3,2,1,0:T(8,128)} custom-call(f32[2,4,32,256]{3,2,1,0:T(8,128)S(1)} %get-tuple-element.29.refs_4_.forecast, bf16[256,128]{1,0:T(8,128)(2,1)S(1)} %get-tuple-element.47.mine, bf16[256,128]{1,0:T(8,128)(2,1)S(1)} %collective-permute-done.11.theirs), custom_call_target="tpu_custom_call" | custom-call | flops 1000000 | bytes 1000000 | tf_op jit(solution)/shard_map/pallas_call | solution.py:624
  (22 shorter events, 0.8 us)
Async XLA Ops:
  0.0 7.9 %copy-start.1 = (f32[2,4,32,256]{3,2,1,0:T(8,128)S(1)}, f32[2,4,32,256]{3,2,1,0:T(8,128)}, u32[]{:S(2)}) copy-start(f32[2,4,32,256]{3,2,1,0:T(8,128)} %courant.3) | copy-start | bytes 786436
  0.0 7.9 %copy-start = (f32[2,4,32,256]{3,2,1,0:T(8,128)S(1)}, f32[2,4,32,256]{3,2,1,0:T(8,128)}, u32[]{:S(2)}) copy-start(f32[2,4,32,256]{3,2,1,0:T(8,128)} %tracer.3) | copy-start | bytes 786436
  1.7 5.3 %collective-permute-start = (f32[40,256]{1,0:T(8,128)}, f32[40,256]{1,0:T(8,128)S(1)}, u32[]{:S(2)}, u32[]{:S(2)}) collective-permute-start(f32[40,256]{1,0:T(8,128)} %get-tuple-element.27), channel_id=1, source_target_pairs={{0,1},{1,0},{2,3},{3,2},{4,5},{5,4},{6,7},{7,6},{8,9},{9,8},{10,11... | collective-permute-start | bytes 122888 | tf_op jit(solution)/shard_map/ppermute | solution.py:151
  1.8 6.1 %collective-permute-start.1 = (f32[40,256]{1,0:T(8,128)}, f32[40,256]{1,0:T(8,128)S(1)}, u32[]{:S(2)}, u32[]{:S(2)}) collective-permute-start(f32[40,256]{1,0:T(8,128)} %get-tuple-element.28), channel_id=1, source_target_pairs={{1,2},{2,1},{5,6},{6,5},{9,10},{10,9},{13,14},{14,13},{17,18},{18,... | collective-permute-start | bytes 122888 | tf_op jit(solution)/shard_map/ppermute | solution.py:151
  7.0 5.0 %copy-start.2 = (s32[32768]{0:T(1024)S(1)}, s32[32768]{0:T(1024)}, u32[]{:S(2)}) copy-start(s32[32768]{0:T(1024)} %param.8) | copy-start | bytes 393220
  7.1 5.0 %copy-start.3 = (f32[32768]{0:T(1024)S(1)}, f32[32768]{0:T(1024)}, u32[]{:S(2)}) copy-start(f32[32768]{0:T(1024)} %param.9) | copy-start | bytes 393220
  7.1 5.0 %copy-start.4 = (f32[32768]{0:T(1024)S(1)}, f32[32768]{0:T(1024)}, u32[]{:S(2)}) copy-start(f32[32768]{0:T(1024)} %param.10) | copy-start | bytes 393220
  7.9 4.1 %copy-start.5 = (s32[2,2,1024]{2,1,0:T(2,128)S(1)}, s32[2,2,1024]{2,1,0:T(2,128)}, u32[]{:S(2)}) copy-start(s32[2,2,1024]{2,1,0:T(2,128)} %lists.3) | copy-start | bytes 49156
  9.3 3.9 %collective-permute-start.2 = (bf16[192,128]{1,0:T(8,128)(2,1)S(1)}, bf16[192,128]{1,0:T(8,128)(2,1)S(1)}, u32[]{:S(2)}, u32[]{:S(2)}) collective-permute-start(bf16[192,128]{1,0:T(8,128)(2,1)S(1)} %get-tuple-element.31), channel_id=1, source_target_pairs={{0,24},{4,28},{8,16},{12,20},{16,8},{20,12},{24,0},{28,4},{1,25},{... | collective-permute-start | bytes 147464 | tf_op jit(solution)/shard_map/ppermute | solution.py:164
  11.5 2.9 %collective-permute-start.3 = (bf16[192,128]{1,0:T(8,128)(2,1)S(1)}, bf16[192,128]{1,0:T(8,128)(2,1)S(1)}, u32[]{:S(2)}, u32[]{:S(2)}) collective-permute-start(bf16[192,128]{1,0:T(8,128)(2,1)S(1)} %get-tuple-element.32), channel_id=1, source_target_pairs={{0,16},{4,20},{8,24},{12,28},{16,0},{20,4},{24,8},{28,12},{1,17},{... | collective-permute-start | bytes 147464 | tf_op jit(solution)/shard_map/ppermute | solution.py:164
  11.7 2.9 %collective-permute-start.4 = (bf16[192,128]{1,0:T(8,128)(2,1)S(1)}, bf16[192,128]{1,0:T(8,128)(2,1)S(1)}, u32[]{:S(2)}, u32[]{:S(2)}) collective-permute-start(bf16[192,128]{1,0:T(8,128)(2,1)S(1)} %get-tuple-element.33), channel_id=1, source_target_pairs={{0,8},{4,12},{8,0},{12,4},{16,24},{20,28},{24,16},{28,20},{1,9},{5... | collective-permute-start | bytes 147464 | tf_op jit(solution)/shard_map/ppermute | solution.py:164
  14.7 4.6 %collective-permute-start.5 = (bf16[448,128]{1,0:T(8,128)(2,1)S(1)}, bf16[448,128]{1,0:T(8,128)(2,1)S(1)}, u32[]{:S(2)}, u32[]{:S(2)}) collective-permute-start(bf16[448,128]{1,0:T(8,128)(2,1)S(1)} %get-tuple-element.36), channel_id=1, source_target_pairs={{0,4},{4,0},{8,12},{12,8},{16,20},{20,16},{24,28},{28,24},{1,5},{5... | collective-permute-start | bytes 344072 | tf_op jit(solution)/shard_map/ppermute | solution.py:168
  20.1 4.2 %collective-permute-start.6 = (f32[24,128]{1,0:T(8,128)S(1)}, f32[24,128]{1,0:T(8,128)S(1)}, u32[]{:S(2)}, u32[]{:S(2)}) collective-permute-start(f32[24,128]{1,0:T(8,128)S(1)} %get-tuple-element.40), channel_id=1, source_target_pairs={{0,1},{1,0},{2,3},{3,2},{4,5},{5,4},{6,7},{7,6},{8,9},{9,8},{10,11... | collective-permute-start | bytes 36872 | tf_op jit(solution)/shard_map/ppermute | solution.py:151
  20.1 4.7 %collective-permute-start.7 = (f32[24,128]{1,0:T(8,128)S(1)}, f32[24,128]{1,0:T(8,128)S(1)}, u32[]{:S(2)}, u32[]{:S(2)}) collective-permute-start(f32[24,128]{1,0:T(8,128)S(1)} %get-tuple-element.41), channel_id=1, source_target_pairs={{1,2},{2,1},{5,6},{6,5},{9,10},{10,9},{13,14},{14,13},{17,18},{18,... | collective-permute-start | bytes 36872 | tf_op jit(solution)/shard_map/ppermute | solution.py:151
  25.5 3.7 %collective-permute-start.8 = (bf16[128,128]{1,0:T(8,128)(2,1)S(1)}, bf16[128,128]{1,0:T(8,128)(2,1)S(1)}, u32[]{:S(2)}, u32[]{:S(2)}) collective-permute-start(bf16[128,128]{1,0:T(8,128)(2,1)S(1)} %get-tuple-element.44), channel_id=1, source_target_pairs={{0,24},{4,28},{8,16},{12,20},{16,8},{20,12},{24,0},{28,4},{1,25},{... | collective-permute-start | bytes 98312 | tf_op jit(solution)/shard_map/ppermute | solution.py:164
  26.8 2.8 %collective-permute-start.9 = (bf16[128,128]{1,0:T(8,128)(2,1)S(1)}, bf16[128,128]{1,0:T(8,128)(2,1)S(1)}, u32[]{:S(2)}, u32[]{:S(2)}) collective-permute-start(bf16[128,128]{1,0:T(8,128)(2,1)S(1)} %get-tuple-element.45), channel_id=1, source_target_pairs={{0,16},{4,20},{8,24},{12,28},{16,0},{20,4},{24,8},{28,12},{1,17},{... | collective-permute-start | bytes 98312 | tf_op jit(solution)/shard_map/ppermute | solution.py:164
  27.0 2.8 %collective-permute-start.10 = (bf16[128,128]{1,0:T(8,128)(2,1)S(1)}, bf16[128,128]{1,0:T(8,128)(2,1)S(1)}, u32[]{:S(2)}, u32[]{:S(2)}) collective-permute-start(bf16[128,128]{1,0:T(8,128)(2,1)S(1)} %get-tuple-element.46), channel_id=1, source_target_pairs={{0,8},{4,12},{8,0},{12,4},{16,24},{20,28},{24,16},{28,20},{1,9},{5... | collective-permute-start | bytes 98312 | tf_op jit(solution)/shard_map/ppermute | solution.py:164
  29.8 3.9 %collective-permute-start.11 = (bf16[256,128]{1,0:T(8,128)(2,1)S(1)}, bf16[256,128]{1,0:T(8,128)(2,1)S(1)}, u32[]{:S(2)}, u32[]{:S(2)}) collective-permute-start(bf16[256,128]{1,0:T(8,128)(2,1)S(1)} %get-tuple-element.48), channel_id=1, source_target_pairs={{0,4},{4,0},{8,12},{12,8},{16,20},{20,16},{24,28},{28,24},{1,5},{5... | collective-permute-start | bytes 196616 | tf_op jit(solution)/shard_map/ppermute | solution.py:168

commit v10 on v9

--- a/solution.py
+++ b/solution.py
@@ -195,82 +195,115 @@
         other[row + region_rows : row + each, :] = jnp.where(first, east, west).astype(bf16)
 
 
+def pack(forecast):
+    members, levels, side, width = forecast.shape
+    for q in range(width // LANES):
+        parts = [
+            forecast[:, :, r : r + BLOCK, q * LANES : (q + 1) * LANES].reshape(-1, LANES)
+            for r in range(0, side, BLOCK)
+        ]
+        for i, part in enumerate(transpose_chunks(parts)):
+            yield 4 * q + i, part.astype(bf16)
+
+
+def observe(cell, table, observed, rows, levels, side, width, height):
+    members = len(observed[0])
+    hits = levels * BLOCK
+    for c in range(cell.shape[0]):
+        above_row, column = split(cell[c], width)
+        level, grid_row = split(above_row, height)
+        _, local_row = split(grid_row, side)
+        _, local_column = split(column, side)
+        band, sub_row = split(local_row, BLOCK)
+        high = level * BLOCK + sub_row
+        low = band * side + local_column
+        for h in [l * BLOCK + r for l in range(levels) for r in rows]:
+            here = high == h
+            for b in range(members):
+                line = table[c, b * hits + h : b * hits + h + 1, :]
+                line = jnp.broadcast_to(line, (BLOCK, LANES))
+                observed[c][b] = jnp.where(here, pick_lanes(line, low), observed[c][b])
+
+
+def draft_body(tracer, courant, cell, _, forecast, seen, table, *, height):
+    members, levels, side, width = tracer.shape
+    for l in range(levels):
+        factors = coefficients(courant[0, l], courant[1, l])
+        for b in range(members):
+            current = tracer[b, l]
+            for step in range(2):
+                lower = pltpu.roll(current, 1, 0)
+                upper = pltpu.roll(current, side - 1, 0)
+                current = stencil(current, lower, upper, factors)
+            forecast[b, l] = current
+    for c, rounded in pack(forecast):
+        table[c] = rounded.astype(f32)
+    blocks = cell.shape[0]
+    observed = [[jnp.zeros((BLOCK, LANES), f32) for _ in range(members)] for _ in range(blocks)]
+    observe(cell, table, observed, range(BLOCK), levels, side, width, height)
+    for c in range(blocks):
+        for b in range(members):
+            seen[c, b] = observed[c][b]
+
+
 def forecast_body(
-    tracer, courant, first, second, cell, forecast, *rest, tiles, height
+    tracer, courant, draft, seen, first, second, cell, forecast, *rest, tiles, height
 ):
     *chunks, send, table = rest
     members, levels, side, width = tracer.shape
     blocks = width // side
     tile = lax.axis_index("tile")
     planes = members * levels
-
+    region_rows = planes * BLOCK
     south, north = beside(first[0:24, :], second[0:24, :], tile)
     own = lambda at: jnp.concatenate(
         [tracer[b, l, at : at + 1, :] for b in range(members) for l in range(levels)], axis=0
     )
-    inside_south, inside_north = tile > 0, tile < tiles - 1
-    low, lowest = south[0:planes], south[8 : 8 + planes]
-    high, highest = north[0:planes], north[8 : 8 + planes]
-
-    def edge(source):
+    rates = lambda part, at: jnp.concatenate(
+        [courant[part, l, at : at + 1, :] for l in range(levels)] * members, axis=0
+    )
+    here = lambda at: coefficients(rates(0, at), rates(1, at))
+
+    def there(source):
         twice = lambda at: jnp.concatenate([source[at : at + levels]] * members, axis=0)
         return coefficients(twice(16), twice(16 + levels))
 
-    below = stencil(low, lowest, own(0), edge(south))
-    above = stencil(high, own(side - 1), highest, edge(north))
-    below = jnp.where(inside_south, below, 0.0)
-    above = jnp.where(inside_north, above, 0.0)
-    row = iota((side, width), 0)
-    for l in range(levels):
-        factors = coefficients(courant[0, l], courant[1, l])
-        for b in range(members):
-            plane = b * levels + l
-            current = tracer[b, l]
-            for under, over in ((low, high), (below, above)):
-                under, over = under[plane : plane + 1, :], over[plane : plane + 1, :]
-                lower = jnp.where(row == 0, under, pltpu.roll(current, 1, 0))
-                upper = jnp.where(row == side - 1, over, pltpu.roll(current, side - 1, 0))
-                current = stencil(current, lower, upper, factors)
-            forecast[b, l] = current
-
-    region_rows = planes * BLOCK
-    for q in range(width // LANES):
-        parts = [
-            forecast[:, :, r : r + BLOCK, q * LANES : (q + 1) * LANES].reshape(region_rows, LANES)
-            for r in range(0, side, BLOCK)
-        ]
-        for i, part in enumerate(transpose_chunks(parts)):
-            c = 4 * q + i
-            rounded = part.astype(bf16)
-            send[c // 2, c % 2 * region_rows : (c % 2 + 1) * region_rows, :] = rounded
-            table[c] = rounded.astype(f32)
-
-    hits = levels * BLOCK
-    observed = []
-    for c in range(blocks):
-        cells = cell[c]
-        above_row, column = split(cells, width)
-        level, grid_row = split(above_row, height)
-        _, local_row = split(grid_row, side)
-        _, local_column = split(column, side)
-        band, sub_row = split(local_row, BLOCK)
-        high = level * BLOCK + sub_row
-        low = band * side + local_column
-        mine = [jnp.zeros((BLOCK, LANES), f32) for _ in range(members)]
-        for h in range(hits):
-            here = high == h
+    forecast[...] = draft[...]
+    for other, inside, at, toward in (
+        (south, tile > 0, 0, 1),
+        (north, tile < tiles - 1, side - 1, -1),
+    ):
+        order = lambda outer, inner: (outer, inner) if toward == 1 else (inner, outer)
+        rows = [own(at + toward * i) for i in range(4)]
+        factors = [here(at + toward * i) for i in range(3)]
+        near, far = other[0:planes], other[8 : 8 + planes]
+        outside = jnp.where(inside, stencil(near, *order(far, rows[0]), there(other)), 0.0)
+        outer = [near, rows[0], rows[1]]
+        once = [stencil(rows[i], *order(outer[i], rows[i + 1]), factors[i]) for i in range(3)]
+        final = (
+            stencil(once[0], *order(outside, once[1]), factors[0]),
+            stencil(once[1], *order(once[0], once[2]), factors[1]),
+        )
+        for i, values in enumerate(final):
+            row = at + toward * i
             for b in range(members):
-                line = table[c, b * hits + h : b * hits + h + 1, :]
-                line = jnp.broadcast_to(line, (BLOCK, LANES))
-                mine[b] = jnp.where(here, pick_lanes(line, low), mine[b])
-        observed.append(mine)
+                for l in range(levels):
+                    plane = b * levels + l
+                    forecast[b, l, row : row + 1, :] = values[plane : plane + 1, :]
+
+    for c, rounded in pack(forecast):
+        send[c // 2, c % 2 * region_rows : (c % 2 + 1) * region_rows, :] = rounded
+        table[c] = rounded.astype(f32)
+    observed = [[seen[c, b] for b in range(members)] for c in range(blocks)]
+    edge = (0, 1, BLOCK - 2, BLOCK - 1)
+    observe(cell, table, observed, edge, levels, side, width, height)
     for chip in range(blocks // 2):
-        rows = [
+        lines = [
             observed[(2 * chip + r - 1) % blocks][b] for b in range(members) for r in range(4)
         ]
-        for i in range(0, len(rows), 2):
+        for i in range(0, len(lines), 2):
             at = 2 * region_rows + i * BLOCK
-            send[chip, at : at + 2 * BLOCK, :] = jnp.concatenate(rows[i : i + 2], axis=0).astype(
+            send[chip, at : at + 2 * BLOCK, :] = jnp.concatenate(lines[i : i + 2], axis=0).astype(
                 bf16
             )
     _, chip, _ = place()
@@ -558,11 +591,19 @@
     )(member_concentration, courant_pairs, obs_list)
     first, second = swap(to_first, to_second, tiles)
 
+    whole = pl.BlockSpec(memory_space=pltpu.VMEM)
     flat = lambda array: array.reshape(-1, LANES)
     cell = flat(obs_cell)
     cell_row = lax.dynamic_index_in_dim(
         cell.reshape(blocks, tiles, BLOCK, LANES), lax.axis_index("tile"), 1, False
     )
+    draft, seen = call(
+        functools.partial(draft_body, height=height),
+        [(member_concentration.shape, f32), ((blocks, members, BLOCK, LANES), f32)],
+        [pltpu.VMEM((blocks, region_rows, LANES), f32)],
+        flops=50_000_000,
+        specs=[whole, whole, whole, pl.BlockSpec(memory_space=pltpu.HBM)],
+    )(member_concentration, courant_pairs, cell_row, to_second)
     forecast, *chunks = call(
         functools.partial(forecast_body, tiles=tiles, height=height),
         [(member_concentration.shape, f32)] + [((chip_rows, LANES), bf16)] * chips,
@@ -573,6 +614,8 @@
     )(
         member_concentration,
         courant_pairs,
+        draft,
+        seen,
         first,
         second,
         cell_row,

time: 35.3 us -> 34.5 us (0.977)
  starting transfers between devices: 20.2 us -> 19.1 us
  Pallas kernels: 7.27 us -> 8.06 us
    pallas_call x0 -> x1, Pallas kernels: none -> 1.63 us  [shards(): call(functools.partial(draft_body, height=height), [(member_concentration...]
    pallas_call x1, Pallas kernels: 1.41 us -> 0.56 us  [shards(): call(functools.partial(forecast_body, tiles=tiles, height=height), [(memb...]
    ppermute x2, starting transfers between devices: 6.6 us -> 5.79 us  [swap_cores(): lax.ppermute(array, 'member', [(i, i ^ 1) for i in range(lax.axis_size('m...]
    ppermute x2, waiting for transfers between devices: 1.37 us -> 0.58 us  [swap(): lax.ppermute(second, 'tile', pairs(1))]
    ppermute x6, waiting for transfers between devices: 3.02 us -> 3.52 us  [exchange(): lax.ppermute(chunks[s], 'member', swaps(s))]
  transfers between devices with their start and end apart: 12 -> 12, of which waited for: 9 -> 8; matrix products, arithmetic and copies ran while one was open for 2% -> 2% of each run, Pallas kernels for 5% -> 10%
where the time goes in v10:
time: 34.5 us; the launch traced here: 34.2 us
  starting transfers between devices  19.1 us (55%)
  Pallas kernels  8.06 us (23%)
  waiting for transfers between devices  5.97 us (17%)
  local copies, waits for them, and re-layouts  0.8 us (2%)
    ppermute x2, starting transfers between devices, swap(): lax.ppermute(second, 'tile', pairs(1))  7.83 us
    ppermute x2, starting transfers between devices, swap_cores(): lax.ppermute(array, 'member', [(i, i ^ 1) for i in range(lax.axis_size('m...  5.79 us
    ppermute x6, starting transfers between devices, exchange(): lax.ppermute(chunks[s], 'member', swaps(s))  5.43 us
    ppermute x6, waiting for transfers between devices, exchange(): lax.ppermute(chunks[s], 'member', swaps(s))  3.52 us
    ppermute x2, waiting for transfers between devices, swap_cores(): lax.ppermute(array, 'member', [(i, i ^ 1) for i in range(lax.axis_size('m...  1.87 us
    pallas_call x1, Pallas kernels, shards(): call(pack_edges, [((edge_rows, width), f32)] * 2, [pltpu.VMEM(edge_shape,...  1.7 us
    pallas_call x1, Pallas kernels, shards(): call(functools.partial(draft_body, height=height), [(member_concentration...  1.63 us
    pallas_call x1, Pallas kernels, shards(): call(functools.partial(weights_body, tiles=tiles, blocks=blocks, height=h...  1.19 us
  transfers between devices with their start and end apart: 12, of which 8 were waited for; matrix products, arithmetic and copies ran while one was open for 2% of the time, Pallas kernels for 10%

profile of v10, /device:TPU:9, one launch (start us, length us, event | category | flops | bytes accessed | tf_op | source)
XLA Modules:
  0.0 34.2 jit_solution(17490044613324472791)
XLA Ops:
  0.0 1.7 %shard_map.64 = (f32[40,256]{1,0:T(8,128)}, f32[40,256]{1,0:T(8,128)}) custom-call(f32[2,4,32,256]{3,2,1,0:T(8,128)} %tracer.5, f32[2,4,32,256]{3,2,1,0:T(8,128)} %courant.5, s32[2,2,1024]{2,1,0:T(2,128)} %lists.3), custom_call_target="tpu_custom_call" | custom-call | flops 1000000 | bytes 1000000 | tf_op jit(solution)/shard_map/pallas_call | solution.py:578
  1.8 4.5 %collective-permute-start.1 = (f32[40,256]{1,0:T(8,128)}, f32[40,256]{1,0:T(8,128)S(1)}, u32[]{:S(2)}, u32[]{:S(2)}) collective-permute-start(f32[40,256]{1,0:T(8,128)} %get-tuple-element.29._), channel_id=1, source_target_pairs={{1,2},{2,1},{5,6},{6,5},{9,10},{10,9},{13,14},{14,13},{17,18},{18,... | collective-permute-start | bytes 122888 | tf_op jit(solution)/shard_map/ppermute | solution.py:151
  6.3 0.8 %dynamic-slice_bitcast_fusion.cell = s32[8,8,128]{2,1,0:T(8,128)S(1)} fusion(s32[8,4,8,128]{3,2,1,0:T(8,128)} %bitcast.6, s32[]{:T(128)S(6)} %select_n.4), kind=kLoop, calls=%fused_computation | loop fusion | bytes 65540 | tf_op jit(solution)/shard_map/jit(dynamic_index_in_dim)/squeeze | solution.py:597
  7.1 1.6 %shard_map.65 = (f32[2,4,32,256]{3,2,1,0:T(8,128)S(1)}, f32[8,2,8,128]{3,2,1,0:T(8,128)S(1)}) custom-call(f32[2,4,32,256]{3,2,1,0:T(8,128)S(1)} %copy-done, f32[2,4,32,256]{3,2,1,0:T(8,128)S(1)} %copy-done.1, s32[8,8,128]{2,1,0:T(8,128)S(1)} %dynamic-slice_bitcast_fusion.cell, f32[40,256]{1,0:T(8,128)S(1)} %copy-done.6), custom_call_target="tpu_custom_call" | custom-call | flops 50000000 | bytes 1000000 | tf_op jit(solution)/shard_map/pallas_call | solution.py:600
  8.8 0.6 %shard_map.66 = (f32[2,4,32,256]{3,2,1,0:T(8,128)S(1)}, bf16[192,128]{1,0:T(8,128)(2,1)S(1)}, bf16[192,128]{1,0:T(8,128)(2,1)S(1)}, bf16[192,128]{1,0:T(8,128)(2,1)S(1)}, bf16[192,128]{1,0:T(8,128)(2,1)S(1)}) custom-call(f32[2,4,32,256]{3,2,1,0:T(8,128)S(1)} %copy-done, f32[2,4,32,256]{3,2,1,0:T(8,128)S(1)} %copy-done.1, ...), custom_call_target="tpu_custom_call" | custom-call | flops 1000000 | bytes 1000000 | tf_op jit(solution)/shard_map/pallas_call | solution.py:607
  9.3 2.2 %collective-permute-start.2 = (bf16[192,128]{1,0:T(8,128)(2,1)S(1)}, bf16[192,128]{1,0:T(8,128)(2,1)S(1)}, u32[]{:S(2)}, u32[]{:S(2)}) collective-permute-start(bf16[192,128]{1,0:T(8,128)(2,1)S(1)} %get-tuple-element.35), channel_id=1, source_target_pairs={{0,24},{4,28},{8,16},{12,20},{16,8},{20,12},{24,0},{28,4},{1,25},{... | collective-permute-start | bytes 147464 | tf_op jit(solution)/shard_map/ppermute | solution.py:164
  11.8 0.3 collective-permute-start.4
  12.1 1.2 %shard_map.67 = (f32[16,3072]{1,0:T(8,128)S(1)}, f32[24,128]{1,0:T(8,128)S(1)}) custom-call(s32[2,2,1024]{2,1,0:T(2,128)S(1)} %copy-done.5, f32[40,256]{1,0:T(8,128)S(1)} %collective-permute-done.first, f32[40,256]{1,0:T(8,128)S(1)} %collective-permute-done.1.second, s32[256,128]{1,0:T(8,128)S(1)} %bitcast.7, f32[256,128]{1,0:T(8,128)S(1)} %bitcast.8, ...), custom_call_target="tpu_custom_call" | custom-call | flops 100000000 | bytes 1000000 | tf_op jit(solution)/shard_map/pallas_call | solution.py:624
  13.3 1.5 %collective-permute-done.3.refs_2_ = bf16[192,128]{1,0:T(8,128)(2,1)S(1)} collective-permute-done((bf16[192,128]{1,0:T(8,128)(2,1)S(1)}, bf16[192,128]{1,0:T(8,128)(2,1)S(1)}, u32[]{:S(2)}, u32[]{:S(2)}) %collective-permute-start.3) | collective-permute-done | bytes 49184 | tf_op jit(solution)/shard_map/ppermute | solution.py:164
  14.8 0.4 %collective-permute-done.4.refs_3_ = bf16[192,128]{1,0:T(8,128)(2,1)S(1)} collective-permute-done((bf16[192,128]{1,0:T(8,128)(2,1)S(1)}, bf16[192,128]{1,0:T(8,128)(2,1)S(1)}, u32[]{:S(2)}, u32[]{:S(2)}) %collective-permute-start.4) | collective-permute-done | bytes 49184 | tf_op jit(solution)/shard_map/ppermute | solution.py:164
  15.3 2.5 %collective-permute-start.5 = (bf16[448,128]{1,0:T(8,128)(2,1)S(1)}, bf16[448,128]{1,0:T(8,128)(2,1)S(1)}, u32[]{:S(2)}, u32[]{:S(2)}) collective-permute-start(bf16[448,128]{1,0:T(8,128)(2,1)S(1)} %get-tuple-element.40), channel_id=1, source_target_pairs={{0,4},{4,0},{8,12},{12,8},{16,20},{20,16},{24,28},{28,24},{1,5},{5... | collective-permute-start | bytes 344072 | tf_op jit(solution)/shard_map/ppermute | solution.py:168
  17.8 1.0 %collective-permute-done.5.theirs = bf16[448,128]{1,0:T(8,128)(2,1)S(1)} collective-permute-done((bf16[448,128]{1,0:T(8,128)(2,1)S(1)}, bf16[448,128]{1,0:T(8,128)(2,1)S(1)}, u32[]{:S(2)}, u32[]{:S(2)}) %collective-permute-start.5) | collective-permute-done | bytes 114720 | tf_op jit(solution)/shard_map/ppermute | solution.py:168
  18.7 0.8 %shard_map.69 = (f32[24,128]{1,0:T(8,128)S(1)}, f32[24,128]{1,0:T(8,128)S(1)}, bf16[48,3072]{1,0:T(8,128)(2,1)S(1)}) custom-call(bf16[448,128]{1,0:T(8,128)(2,1)S(1)} %get-tuple-element.39.mine, bf16[448,128]{1,0:T(8,128)(2,1)S(1)} %collective-permute-done.5.theirs, f32[16,3072]{1,0:T(8,128)S(1)} %get-tuple-element.41.weights, ...), custom_call_target="tpu_custom_call" | custom-call | flops 1000000 | bytes 1000000 | tf_op jit(solution)/shard_map/pallas_call | solution.py:642
  19.6 3.4 %collective-permute-start.7 = (f32[24,128]{1,0:T(8,128)S(1)}, f32[24,128]{1,0:T(8,128)S(1)}, u32[]{:S(2)}, u32[]{:S(2)}) collective-permute-start(f32[24,128]{1,0:T(8,128)S(1)} %get-tuple-element.45), channel_id=1, source_target_pairs={{1,2},{2,1},{5,6},{6,5},{9,10},{10,9},{13,14},{14,13},{17,18},{18,... | collective-permute-start | bytes 36872 | tf_op jit(solution)/shard_map/ppermute | solution.py:151
  22.9 0.5 %shard_map.70 = (f32[24,128]{1,0:T(8,128)S(1)}, f32[16,32,128]{2,1,0:T(8,128)S(1)}) custom-call(bf16[448,128]{1,0:T(8,128)(2,1)S(1)} %get-tuple-element.39.mine, bf16[448,128]{1,0:T(8,128)(2,1)S(1)} %collective-permute-done.5.theirs, f32[16,3072]{1,0:T(8,128)S(1)} %get-tuple-element.41.weights, bf16[48,3072]{1,0:T(8,128)(2,1)S(1)} %get-tuple-element.42.wide), custom_call_target="tpu_custom_call" | custom-call | flops 50000000 | bytes 1000000 | tf_op jit(solution)/shard_map/pallas_call | solution.py:652
  23.4 0.6 %collective-permute-done.7.second = f32[24,128]{1,0:T(8,128)S(1)} collective-permute-done((f32[24,128]{1,0:T(8,128)S(1)}, f32[24,128]{1,0:T(8,128)S(1)}, u32[]{:S(2)}, u32[]{:S(2)}) %collective-permute-start.7) | collective-permute-done | bytes 12320 | tf_op jit(solution)/shard_map/ppermute | solution.py:151
  24.0 0.7 %shard_map.71 = (bf16[128,128]{1,0:T(8,128)(2,1)S(1)}, bf16[128,128]{1,0:T(8,128)(2,1)S(1)}, bf16[128,128]{1,0:T(8,128)(2,1)S(1)}, bf16[128,128]{1,0:T(8,128)(2,1)S(1)}) custom-call(f32[24,128]{1,0:T(8,128)S(1)} %get-tuple-element.43.own, f32[24,128]{1,0:T(8,128)S(1)} %collective-permute-done.6.first, f32[24,128]{1,0:T(8,128)S(1)} %collective-permute-done.7.second, ...), custom_call_target="tpu_custom_call" | custom-call | flops 1000000 | bytes 1000000 | tf_op jit(solution)/shard_map/pallas_call | solution.py:659
  24.7 1.3 %collective-permute-start.8 = (bf16[128,128]{1,0:T(8,128)(2,1)S(1)}, bf16[128,128]{1,0:T(8,128)(2,1)S(1)}, u32[]{:S(2)}, u32[]{:S(2)}) collective-permute-start(bf16[128,128]{1,0:T(8,128)(2,1)S(1)} %get-tuple-element.48), channel_id=1, source_target_pairs={{0,24},{4,28},{8,16},{12,20},{16,8},{20,12},{24,0},{28,4},{1,25},{... | collective-permute-start | bytes 98312 | tf_op jit(solution)/shard_map/ppermute | solution.py:164
  26.2 1.2 %collective-permute-start.10 = (bf16[128,128]{1,0:T(8,128)(2,1)S(1)}, bf16[128,128]{1,0:T(8,128)(2,1)S(1)}, u32[]{:S(2)}, u32[]{:S(2)}) collective-permute-start(bf16[128,128]{1,0:T(8,128)(2,1)S(1)} %get-tuple-element.50), channel_id=1, source_target_pairs={{0,8},{4,12},{8,0},{12,4},{16,24},{20,28},{24,16},{28,20},{1,9},{5... | collective-permute-start | bytes 98312 | tf_op jit(solution)/shard_map/ppermute | solution.py:164
  27.4 1.0 %collective-permute-done.8.refs_1_ = bf16[128,128]{1,0:T(8,128)(2,1)S(1)} collective-permute-done((bf16[128,128]{1,0:T(8,128)(2,1)S(1)}, bf16[128,128]{1,0:T(8,128)(2,1)S(1)}, u32[]{:S(2)}, u32[]{:S(2)}) %collective-permute-start.8) | collective-permute-done | bytes 32800 | tf_op jit(solution)/shard_map/ppermute | solution.py:164
  28.4 0.4 %collective-permute-done.9.refs_2_ = bf16[128,128]{1,0:T(8,128)(2,1)S(1)} collective-permute-done((bf16[128,128]{1,0:T(8,128)(2,1)S(1)}, bf16[128,128]{1,0:T(8,128)(2,1)S(1)}, u32[]{:S(2)}, u32[]{:S(2)}) %collective-permute-start.9) | collective-permute-done | bytes 32800 | tf_op jit(solution)/shard_map/ppermute | solution.py:164
  29.0 3.3 %collective-permute-start.11 = (bf16[256,128]{1,0:T(8,128)(2,1)S(1)}, bf16[256,128]{1,0:T(8,128)(2,1)S(1)}, u32[]{:S(2)}, u32[]{:S(2)}) collective-permute-start(bf16[256,128]{1,0:T(8,128)(2,1)S(1)} %get-tuple-element.52), channel_id=1, source_target_pairs={{0,4},{4,0},{8,12},{12,8},{16,20},{20,16},{24,28},{28,24},{1,5},{5... | collective-permute-start | bytes 196616 | tf_op jit(solution)/shard_map/ppermute | solution.py:168
  32.3 0.9 %collective-permute-done.11.theirs = bf16[256,128]{1,0:T(8,128)(2,1)S(1)} collective-permute-done((bf16[256,128]{1,0:T(8,128)(2,1)S(1)}, bf16[256,128]{1,0:T(8,128)(2,1)S(1)}, u32[]{:S(2)}, u32[]{:S(2)}) %collective-permute-start.11) | collective-permute-done | bytes 65568 | tf_op jit(solution)/shard_map/ppermute | solution.py:168
  33.2 0.9 %shard_map.73 = f32[2,4,32,256]{3,2,1,0:T(8,128)} custom-call(f32[2,4,32,256]{3,2,1,0:T(8,128)S(1)} %get-tuple-element.33.refs_4_.forecast, bf16[256,128]{1,0:T(8,128)(2,1)S(1)} %get-tuple-element.51.mine, bf16[256,128]{1,0:T(8,128)(2,1)S(1)} %collective-permute-done.11.theirs), custom_call_target="tpu_custom_call" | custom-call | flops 1000000 | bytes 1000000 | tf_op jit(solution)/shard_map/pallas_call | solution.py:667
  (25 shorter events, 0.8 us)
Async XLA Ops:
  0.0 7.1 %copy-start.1 = (f32[2,4,32,256]{3,2,1,0:T(8,128)S(1)}, f32[2,4,32,256]{3,2,1,0:T(8,128)}, u32[]{:S(2)}) copy-start(f32[2,4,32,256]{3,2,1,0:T(8,128)} %courant.5) | copy-start | bytes 786436
  0.0 7.1 %copy-start = (f32[2,4,32,256]{3,2,1,0:T(8,128)S(1)}, f32[2,4,32,256]{3,2,1,0:T(8,128)}, u32[]{:S(2)}) copy-start(f32[2,4,32,256]{3,2,1,0:T(8,128)} %tracer.5) | copy-start | bytes 786436
  1.7 5.3 %copy-start.6 = (f32[40,256]{1,0:T(8,128)S(1)}, f32[40,256]{1,0:T(8,128)}, u32[]{:S(2)}) copy-start(f32[40,256]{1,0:T(8,128)} %get-tuple-element.29._) | copy-start | bytes 122884
  1.7 7.0 %collective-permute-start = (f32[40,256]{1,0:T(8,128)}, f32[40,256]{1,0:T(8,128)S(1)}, u32[]{:S(2)}, u32[]{:S(2)}) collective-permute-start(f32[40,256]{1,0:T(8,128)} %get-tuple-element.32), channel_id=1, source_target_pairs={{0,1},{1,0},{2,3},{3,2},{4,5},{5,4},{6,7},{7,6},{8,9},{9,8},{10,11... | collective-permute-start | bytes 122888 | tf_op jit(solution)/shard_map/ppermute | solution.py:151
  1.8 6.9 %collective-permute-start.1 = (f32[40,256]{1,0:T(8,128)}, f32[40,256]{1,0:T(8,128)S(1)}, u32[]{:S(2)}, u32[]{:S(2)}) collective-permute-start(f32[40,256]{1,0:T(8,128)} %get-tuple-element.29._), channel_id=1, source_target_pairs={{1,2},{2,1},{5,6},{6,5},{9,10},{10,9},{13,14},{14,13},{17,18},{18,... | collective-permute-start | bytes 122888 | tf_op jit(solution)/shard_map/ppermute | solution.py:151
  8.7 3.3 %copy-start.2 = (s32[32768]{0:T(1024)S(1)}, s32[32768]{0:T(1024)}, u32[]{:S(2)}) copy-start(s32[32768]{0:T(1024)} %param.8) | copy-start | bytes 393220
  8.7 3.3 %copy-start.3 = (f32[32768]{0:T(1024)S(1)}, f32[32768]{0:T(1024)}, u32[]{:S(2)}) copy-start(f32[32768]{0:T(1024)} %param.9) | copy-start | bytes 393220
  8.7 3.3 %copy-start.4 = (f32[32768]{0:T(1024)S(1)}, f32[32768]{0:T(1024)}, u32[]{:S(2)}) copy-start(f32[32768]{0:T(1024)} %param.10) | copy-start | bytes 393220
  8.7 3.3 %copy-start.5 = (s32[2,2,1024]{2,1,0:T(2,128)S(1)}, s32[2,2,1024]{2,1,0:T(2,128)}, u32[]{:S(2)}) copy-start(s32[2,2,1024]{2,1,0:T(2,128)} %lists.3) | copy-start | bytes 49156
  9.3 3.9 %collective-permute-start.2 = (bf16[192,128]{1,0:T(8,128)(2,1)S(1)}, bf16[192,128]{1,0:T(8,128)(2,1)S(1)}, u32[]{:S(2)}, u32[]{:S(2)}) collective-permute-start(bf16[192,128]{1,0:T(8,128)(2,1)S(1)} %get-tuple-element.35), channel_id=1, source_target_pairs={{0,24},{4,28},{8,16},{12,20},{16,8},{20,12},{24,0},{28,4},{1,25},{... | collective-permute-start | bytes 147464 | tf_op jit(solution)/shard_map/ppermute | solution.py:164
  11.6 3.2 %collective-permute-start.3 = (bf16[192,128]{1,0:T(8,128)(2,1)S(1)}, bf16[192,128]{1,0:T(8,128)(2,1)S(1)}, u32[]{:S(2)}, u32[]{:S(2)}) collective-permute-start(bf16[192,128]{1,0:T(8,128)(2,1)S(1)} %get-tuple-element.36), channel_id=1, source_target_pairs={{0,16},{4,20},{8,24},{12,28},{16,0},{20,4},{24,8},{28,12},{1,17},{... | collective-permute-start | bytes 147464 | tf_op jit(solution)/shard_map/ppermute | solution.py:164
  11.8 3.4 %collective-permute-start.4 = (bf16[192,128]{1,0:T(8,128)(2,1)S(1)}, bf16[192,128]{1,0:T(8,128)(2,1)S(1)}, u32[]{:S(2)}, u32[]{:S(2)}) collective-permute-start(bf16[192,128]{1,0:T(8,128)(2,1)S(1)} %get-tuple-element.37), channel_id=1, source_target_pairs={{0,8},{4,12},{8,0},{12,4},{16,24},{20,28},{24,16},{28,20},{1,9},{5... | collective-permute-start | bytes 147464 | tf_op jit(solution)/shard_map/ppermute | solution.py:164
  15.3 3.5 %collective-permute-start.5 = (bf16[448,128]{1,0:T(8,128)(2,1)S(1)}, bf16[448,128]{1,0:T(8,128)(2,1)S(1)}, u32[]{:S(2)}, u32[]{:S(2)}) collective-permute-start(bf16[448,128]{1,0:T(8,128)(2,1)S(1)} %get-tuple-element.40), channel_id=1, source_target_pairs={{0,4},{4,0},{8,12},{12,8},{16,20},{20,16},{24,28},{28,24},{1,5},{5... | collective-permute-start | bytes 344072 | tf_op jit(solution)/shard_map/ppermute | solution.py:168
  19.5 3.9 %collective-permute-start.6 = (f32[24,128]{1,0:T(8,128)S(1)}, f32[24,128]{1,0:T(8,128)S(1)}, u32[]{:S(2)}, u32[]{:S(2)}) collective-permute-start(f32[24,128]{1,0:T(8,128)S(1)} %get-tuple-element.44), channel_id=1, source_target_pairs={{0,1},{1,0},{2,3},{3,2},{4,5},{5,4},{6,7},{7,6},{8,9},{9,8},{10,11... | collective-permute-start | bytes 36872 | tf_op jit(solution)/shard_map/ppermute | solution.py:151
  19.6 4.4 %collective-permute-start.7 = (f32[24,128]{1,0:T(8,128)S(1)}, f32[24,128]{1,0:T(8,128)S(1)}, u32[]{:S(2)}, u32[]{:S(2)}) collective-permute-start(f32[24,128]{1,0:T(8,128)S(1)} %get-tuple-element.45), channel_id=1, source_target_pairs={{1,2},{2,1},{5,6},{6,5},{9,10},{10,9},{13,14},{14,13},{17,18},{18,... | collective-permute-start | bytes 36872 | tf_op jit(solution)/shard_map/ppermute | solution.py:151
  24.7 3.7 %collective-permute-start.8 = (bf16[128,128]{1,0:T(8,128)(2,1)S(1)}, bf16[128,128]{1,0:T(8,128)(2,1)S(1)}, u32[]{:S(2)}, u32[]{:S(2)}) collective-permute-start(bf16[128,128]{1,0:T(8,128)(2,1)S(1)} %get-tuple-element.48), channel_id=1, source_target_pairs={{0,24},{4,28},{8,16},{12,20},{16,8},{20,12},{24,0},{28,4},{1,25},{... | collective-permute-start | bytes 98312 | tf_op jit(solution)/shard_map/ppermute | solution.py:164
  26.0 2.8 %collective-permute-start.9 = (bf16[128,128]{1,0:T(8,128)(2,1)S(1)}, bf16[128,128]{1,0:T(8,128)(2,1)S(1)}, u32[]{:S(2)}, u32[]{:S(2)}) collective-permute-start(bf16[128,128]{1,0:T(8,128)(2,1)S(1)} %get-tuple-element.49), channel_id=1, source_target_pairs={{0,16},{4,20},{8,24},{12,28},{16,0},{20,4},{24,8},{28,12},{1,17},{... | collective-permute-start | bytes 98312 | tf_op jit(solution)/shard_map/ppermute | solution.py:164
  26.2 2.8 %collective-permute-start.10 = (bf16[128,128]{1,0:T(8,128)(2,1)S(1)}, bf16[128,128]{1,0:T(8,128)(2,1)S(1)}, u32[]{:S(2)}, u32[]{:S(2)}) collective-permute-start(bf16[128,128]{1,0:T(8,128)(2,1)S(1)} %get-tuple-element.50), channel_id=1, source_target_pairs={{0,8},{4,12},{8,0},{12,4},{16,24},{20,28},{24,16},{28,20},{1,9},{5... | collective-permute-start | bytes 98312 | tf_op jit(solution)/shard_map/ppermute | solution.py:164
  29.0 4.2 %collective-permute-start.11 = (bf16[256,128]{1,0:T(8,128)(2,1)S(1)}, bf16[256,128]{1,0:T(8,128)(2,1)S(1)}, u32[]{:S(2)}, u32[]{:S(2)}) collective-permute-start(bf16[256,128]{1,0:T(8,128)(2,1)S(1)} %get-tuple-element.52), channel_id=1, source_target_pairs={{0,4},{4,0},{8,12},{12,8},{16,20},{20,16},{24,28},{28,24},{1,5},{5... | collective-permute-start | bytes 196616 | tf_op jit(solution)/shard_map/ppermute | solution.py:168

commit v11 on v10

--- a/solution.py
+++ b/solution.py
@@ -90,11 +90,11 @@
         copy.start()
     for copy in copies:
         copy.wait()
-    even = lax.rem(lax.axis_index("tile"), 2) == 0
+    odd = lax.rem(lax.axis_index("tile"), 2) == 1
 
     def put(row, low, high):
-        to_first[row : row + 1, :] = jnp.where(even, high, low)
-        to_second[row : row + 1, :] = jnp.where(even, low, high)
+        to_first[row : row + 1, :] = jnp.where(odd, high, low)
+        to_second[row : row + 1, :] = jnp.where(odd, low, high)
 
     end = BLOCK - 1
     for b in range(members):
@@ -140,15 +140,18 @@
 
 
 def beside(first, second, tile):
-    even = lax.rem(tile, 2) == 0
-    return jnp.where(even, second, first), jnp.where(even, first, second)
-
-
-def swap(first, second, tiles):
+    odd = lax.rem(tile, 2) == 1
+    return jnp.where(odd, second, first), jnp.where(odd, first, second)
+
+
+def swap(first, second, tiles, lead):
     pairs = lambda start: [
         pair for i in range(start, tiles - 1, 2) for pair in ((i, i + 1), (i + 1, i))
     ]
-    return lax.ppermute(first, "tile", pairs(0)), lax.ppermute(second, "tile", pairs(1))
+    return (
+        lax.ppermute(first, "tile", pairs(lead)),
+        lax.ppermute(second, "tile", pairs(1 - lead)),
+    )
 
 
 def turn(s, chips):
@@ -589,7 +592,7 @@
         specs=[pl.BlockSpec(memory_space=pltpu.HBM)] * 3,
         vmem=63,
     )(member_concentration, courant_pairs, obs_list)
-    first, second = swap(to_first, to_second, tiles)
+    first, second = swap(to_first, to_second, tiles, 1)
 
     whole = pl.BlockSpec(memory_space=pltpu.VMEM)
     flat = lambda array: array.reshape(-1, LANES)
@@ -648,7 +651,7 @@
             pltpu.VMEM((2 * tall, length), bf16),
         ],
     )(mine, theirs, weights, values)
-    first, second = swap(to_first, to_second, tiles)
+    first, second = swap(to_first, to_second, tiles, 0)
     own, centred = call(
         functools.partial(own_body, **sizes),
         [(system_shape, f32), (centred_shape, f32)],

time: 34.5 us -> 34.8 us (level)
  waiting for transfers between devices: 5.97 us -> 7.43 us
  starting transfers between devices: 19.1 us -> 18.2 us
    ppermute x4, starting transfers between devices: 7.92 us -> 5.37 us  [the longest x2 3.22 us: swap(): lax.ppermute(first, 'tile', pairs(lead))]
    ppermute x4, waiting for transfers between devices: 0.58 us -> 2.54 us  [the longest x2 2.53 us: swap(): lax.ppermute(second, 'tile', pairs(1 - lead))]
    ppermute x2, starting transfers between devices: 5.79 us -> 7.36 us  [swap_cores(): lax.ppermute(array, 'member', [(i, i ^ 1) for i in range(lax.axis_size('m...]
    ppermute x6, waiting for transfers between devices: 3.52 us -> 3.02 us  [exchange(): lax.ppermute(chunks[s], 'member', swaps(s))]
  transfers between devices with their start and end apart: 12 -> 12, of which waited for: 8 -> 9; matrix products, arithmetic and copies ran while one was open for 2% -> 2% of each run, Pallas kernels for 10% -> 10%
where the time goes in v11:
time: 34.8 us; the launch traced here: 34.6 us
  starting transfers between devices  18.2 us (52%)
  Pallas kernels  8.06 us (23%)
  waiting for transfers between devices  7.43 us (21%)
  local copies, waits for them, and re-layouts  0.79 us (2%)
    ppermute x2, starting transfers between devices, swap_cores(): lax.ppermute(array, 'member', [(i, i ^ 1) for i in range(lax.axis_size('m...  7.36 us
    ppermute x6, starting transfers between devices, exchange(): lax.ppermute(chunks[s], 'member', swaps(s))  5.43 us
    ppermute x2, starting transfers between devices, swap(): lax.ppermute(first, 'tile', pairs(lead))  3.22 us
    ppermute x6, waiting for transfers between devices, exchange(): lax.ppermute(chunks[s], 'member', swaps(s))  3.02 us
    ppermute x2, waiting for transfers between devices, swap(): lax.ppermute(second, 'tile', pairs(1 - lead))  2.53 us
    ppermute x2, starting transfers between devices, swap(): lax.ppermute(second, 'tile', pairs(1 - lead))  2.15 us
    ppermute x2, waiting for transfers between devices, swap_cores(): lax.ppermute(array, 'member', [(i, i ^ 1) for i in range(lax.axis_size('m...  1.87 us
    pallas_call x1, Pallas kernels, shards(): call(pack_edges, [((edge_rows, width), f32)] * 2, [pltpu.VMEM(edge_shape,...  1.7 us
  transfers between devices with their start and end apart: 12, of which 9 were waited for; matrix products, arithmetic and copies ran while one was open for 2% of the time, Pallas kernels for 10%

profile of v11, /device:TPU:9, one launch (start us, length us, event | category | flops | bytes accessed | tf_op | source)
XLA Modules:
  0.0 34.6 jit_solution(17949057936956062856)
XLA Ops:
  0.0 1.7 %shard_map.64 = (f32[40,256]{1,0:T(8,128)}, f32[40,256]{1,0:T(8,128)}) custom-call(f32[2,4,32,256]{3,2,1,0:T(8,128)} %tracer.5, f32[2,4,32,256]{3,2,1,0:T(8,128)} %courant.5, s32[2,2,1024]{2,1,0:T(2,128)} %lists.3), custom_call_target="tpu_custom_call" | custom-call | flops 1000000 | bytes 1000000 | tf_op jit(solution)/shard_map/pallas_call | solution.py:581
  1.7 3.2 %collective-permute-start = (f32[40,256]{1,0:T(8,128)}, f32[40,256]{1,0:T(8,128)S(1)}, u32[]{:S(2)}, u32[]{:S(2)}) collective-permute-start(f32[40,256]{1,0:T(8,128)} %get-tuple-element.32), channel_id=1, source_target_pairs={{1,2},{2,1},{5,6},{6,5},{9,10},{10,9},{13,14},{14,13},{17,18},{18,... | collective-permute-start | bytes 122888 | tf_op jit(solution)/shard_map/ppermute | solution.py:152
  5.0 0.8 %dynamic-slice_bitcast_fusion.cell = s32[8,8,128]{2,1,0:T(8,128)S(1)} fusion(s32[8,4,8,128]{3,2,1,0:T(8,128)} %bitcast.6, s32[]{:T(128)S(6)} %select_n.4), kind=kLoop, calls=%fused_computation | loop fusion | bytes 65540 | tf_op jit(solution)/shard_map/jit(dynamic_index_in_dim)/squeeze | solution.py:600
  5.8 1.6 %shard_map.65 = (f32[2,4,32,256]{3,2,1,0:T(8,128)S(1)}, f32[8,2,8,128]{3,2,1,0:T(8,128)S(1)}) custom-call(f32[2,4,32,256]{3,2,1,0:T(8,128)S(1)} %copy-done, f32[2,4,32,256]{3,2,1,0:T(8,128)S(1)} %copy-done.1, s32[8,8,128]{2,1,0:T(8,128)S(1)} %dynamic-slice_bitcast_fusion.cell, f32[40,256]{1,0:T(8,128)S(1)} %copy-done.6), custom_call_target="tpu_custom_call" | custom-call | flops 50000000 | bytes 1000000 | tf_op jit(solution)/shard_map/pallas_call | solution.py:603
  7.4 0.7 %collective-permute-done.1.second = f32[40,256]{1,0:T(8,128)S(1)} collective-permute-done((f32[40,256]{1,0:T(8,128)}, f32[40,256]{1,0:T(8,128)S(1)}, u32[]{:S(2)}, u32[]{:S(2)}) %collective-permute-start.1) | collective-permute-done | bytes 40992 | tf_op jit(solution)/shard_map/ppermute | solution.py:153
  8.1 0.6 %shard_map.66 = (f32[2,4,32,256]{3,2,1,0:T(8,128)S(1)}, bf16[192,128]{1,0:T(8,128)(2,1)S(1)}, bf16[192,128]{1,0:T(8,128)(2,1)S(1)}, bf16[192,128]{1,0:T(8,128)(2,1)S(1)}, bf16[192,128]{1,0:T(8,128)(2,1)S(1)}) custom-call(f32[2,4,32,256]{3,2,1,0:T(8,128)S(1)} %copy-done, f32[2,4,32,256]{3,2,1,0:T(8,128)S(1)} %copy-done.1, ...), custom_call_target="tpu_custom_call" | custom-call | flops 1000000 | bytes 1000000 | tf_op jit(solution)/shard_map/pallas_call | solution.py:610
  8.7 2.2 %collective-permute-start.2 = (bf16[192,128]{1,0:T(8,128)(2,1)S(1)}, bf16[192,128]{1,0:T(8,128)(2,1)S(1)}, u32[]{:S(2)}, u32[]{:S(2)}) collective-permute-start(bf16[192,128]{1,0:T(8,128)(2,1)S(1)} %get-tuple-element.35), channel_id=1, source_target_pairs={{0,24},{4,28},{8,16},{12,20},{16,8},{20,12},{24,0},{28,4},{1,25},{... | collective-permute-start | bytes 147464 | tf_op jit(solution)/shard_map/ppermute | solution.py:167
  11.1 0.3 collective-permute-start.4
  11.4 1.2 %shard_map.67 = (f32[16,3072]{1,0:T(8,128)S(1)}, f32[24,128]{1,0:T(8,128)S(1)}) custom-call(s32[2,2,1024]{2,1,0:T(2,128)S(1)} %copy-done.5, f32[40,256]{1,0:T(8,128)S(1)} %collective-permute-done.first, f32[40,256]{1,0:T(8,128)S(1)} %collective-permute-done.1.second, s32[256,128]{1,0:T(8,128)S(1)} %bitcast.7, f32[256,128]{1,0:T(8,128)S(1)} %bitcast.8, ...), custom_call_target="tpu_custom_call" | custom-call | flops 100000000 | bytes 1000000 | tf_op jit(solution)/shard_map/pallas_call | solution.py:627
  12.6 1.2 %collective-permute-done.3.refs_2_ = bf16[192,128]{1,0:T(8,128)(2,1)S(1)} collective-permute-done((bf16[192,128]{1,0:T(8,128)(2,1)S(1)}, bf16[192,128]{1,0:T(8,128)(2,1)S(1)}, u32[]{:S(2)}, u32[]{:S(2)}) %collective-permute-start.3) | collective-permute-done | bytes 49184 | tf_op jit(solution)/shard_map/ppermute | solution.py:167
  14.1 3.8 %collective-permute-start.5 = (bf16[448,128]{1,0:T(8,128)(2,1)S(1)}, bf16[448,128]{1,0:T(8,128)(2,1)S(1)}, u32[]{:S(2)}, u32[]{:S(2)}) collective-permute-start(bf16[448,128]{1,0:T(8,128)(2,1)S(1)} %get-tuple-element.40), channel_id=1, source_target_pairs={{0,4},{4,0},{8,12},{12,8},{16,20},{20,16},{24,28},{28,24},{1,5},{5... | collective-permute-start | bytes 344072 | tf_op jit(solution)/shard_map/ppermute | solution.py:171
  18.0 1.0 %collective-permute-done.5.theirs = bf16[448,128]{1,0:T(8,128)(2,1)S(1)} collective-permute-done((bf16[448,128]{1,0:T(8,128)(2,1)S(1)}, bf16[448,128]{1,0:T(8,128)(2,1)S(1)}, u32[]{:S(2)}, u32[]{:S(2)}) %collective-permute-start.5) | collective-permute-done | bytes 114720 | tf_op jit(solution)/shard_map/ppermute | solution.py:171
  18.9 0.8 %shard_map.69 = (f32[24,128]{1,0:T(8,128)S(1)}, f32[24,128]{1,0:T(8,128)S(1)}, bf16[48,3072]{1,0:T(8,128)(2,1)S(1)}) custom-call(bf16[448,128]{1,0:T(8,128)(2,1)S(1)} %get-tuple-element.39.mine, bf16[448,128]{1,0:T(8,128)(2,1)S(1)} %collective-permute-done.5.theirs, f32[16,3072]{1,0:T(8,128)S(1)} %get-tuple-element.41.weights, ...), custom_call_target="tpu_custom_call" | custom-call | flops 1000000 | bytes 1000000 | tf_op jit(solution)/shard_map/pallas_call | solution.py:645
  19.8 2.1 %collective-permute-start.7 = (f32[24,128]{1,0:T(8,128)S(1)}, f32[24,128]{1,0:T(8,128)S(1)}, u32[]{:S(2)}, u32[]{:S(2)}) collective-permute-start(f32[24,128]{1,0:T(8,128)S(1)} %get-tuple-element.45), channel_id=1, source_target_pairs={{1,2},{2,1},{5,6},{6,5},{9,10},{10,9},{13,14},{14,13},{17,18},{18,... | collective-permute-start | bytes 36872 | tf_op jit(solution)/shard_map/ppermute | solution.py:153
  21.8 0.5 %shard_map.70 = (f32[24,128]{1,0:T(8,128)S(1)}, f32[16,32,128]{2,1,0:T(8,128)S(1)}) custom-call(bf16[448,128]{1,0:T(8,128)(2,1)S(1)} %get-tuple-element.39.mine, bf16[448,128]{1,0:T(8,128)(2,1)S(1)} %collective-permute-done.5.theirs, f32[16,3072]{1,0:T(8,128)S(1)} %get-tuple-element.41.weights, bf16[48,3072]{1,0:T(8,128)(2,1)S(1)} %get-tuple-element.42.wide), custom_call_target="tpu_custom_call" | custom-call | flops 50000000 | bytes 1000000 | tf_op jit(solution)/shard_map/pallas_call | solution.py:655
  22.3 1.9 %collective-permute-done.7.second = f32[24,128]{1,0:T(8,128)S(1)} collective-permute-done((f32[24,128]{1,0:T(8,128)S(1)}, f32[24,128]{1,0:T(8,128)S(1)}, u32[]{:S(2)}, u32[]{:S(2)}) %collective-permute-start.7) | collective-permute-done | bytes 12320 | tf_op jit(solution)/shard_map/ppermute | solution.py:153
  24.2 0.7 %shard_map.71 = (bf16[128,128]{1,0:T(8,128)(2,1)S(1)}, bf16[128,128]{1,0:T(8,128)(2,1)S(1)}, bf16[128,128]{1,0:T(8,128)(2,1)S(1)}, bf16[128,128]{1,0:T(8,128)(2,1)S(1)}) custom-call(f32[24,128]{1,0:T(8,128)S(1)} %get-tuple-element.43.own, f32[24,128]{1,0:T(8,128)S(1)} %collective-permute-done.6.first, f32[24,128]{1,0:T(8,128)S(1)} %collective-permute-done.7.second, ...), custom_call_target="tpu_custom_call" | custom-call | flops 1000000 | bytes 1000000 | tf_op jit(solution)/shard_map/pallas_call | solution.py:662
  24.9 1.3 %collective-permute-start.8 = (bf16[128,128]{1,0:T(8,128)(2,1)S(1)}, bf16[128,128]{1,0:T(8,128)(2,1)S(1)}, u32[]{:S(2)}, u32[]{:S(2)}) collective-permute-start(bf16[128,128]{1,0:T(8,128)(2,1)S(1)} %get-tuple-element.48), channel_id=1, source_target_pairs={{0,24},{4,28},{8,16},{12,20},{16,8},{20,12},{24,0},{28,4},{1,25},{... | collective-permute-start | bytes 98312 | tf_op jit(solution)/shard_map/ppermute | solution.py:167
  26.4 1.2 %collective-permute-start.10 = (bf16[128,128]{1,0:T(8,128)(2,1)S(1)}, bf16[128,128]{1,0:T(8,128)(2,1)S(1)}, u32[]{:S(2)}, u32[]{:S(2)}) collective-permute-start(bf16[128,128]{1,0:T(8,128)(2,1)S(1)} %get-tuple-element.50), channel_id=1, source_target_pairs={{0,8},{4,12},{8,0},{12,4},{16,24},{20,28},{24,16},{28,20},{1,9},{5... | collective-permute-start | bytes 98312 | tf_op jit(solution)/shard_map/ppermute | solution.py:167
  27.6 1.0 %collective-permute-done.8.refs_1_ = bf16[128,128]{1,0:T(8,128)(2,1)S(1)} collective-permute-done((bf16[128,128]{1,0:T(8,128)(2,1)S(1)}, bf16[128,128]{1,0:T(8,128)(2,1)S(1)}, u32[]{:S(2)}, u32[]{:S(2)}) %collective-permute-start.8) | collective-permute-done | bytes 32800 | tf_op jit(solution)/shard_map/ppermute | solution.py:167
  28.6 0.4 %collective-permute-done.9.refs_2_ = bf16[128,128]{1,0:T(8,128)(2,1)S(1)} collective-permute-done((bf16[128,128]{1,0:T(8,128)(2,1)S(1)}, bf16[128,128]{1,0:T(8,128)(2,1)S(1)}, u32[]{:S(2)}, u32[]{:S(2)}) %collective-permute-start.9) | collective-permute-done | bytes 32800 | tf_op jit(solution)/shard_map/ppermute | solution.py:167
  29.2 3.5 %collective-permute-start.11 = (bf16[256,128]{1,0:T(8,128)(2,1)S(1)}, bf16[256,128]{1,0:T(8,128)(2,1)S(1)}, u32[]{:S(2)}, u32[]{:S(2)}) collective-permute-start(bf16[256,128]{1,0:T(8,128)(2,1)S(1)} %get-tuple-element.52), channel_id=1, source_target_pairs={{0,4},{4,0},{8,12},{12,8},{16,20},{20,16},{24,28},{28,24},{1,5},{5... | collective-permute-start | bytes 196616 | tf_op jit(solution)/shard_map/ppermute | solution.py:171
  32.7 0.9 %collective-permute-done.11.theirs = bf16[256,128]{1,0:T(8,128)(2,1)S(1)} collective-permute-done((bf16[256,128]{1,0:T(8,128)(2,1)S(1)}, bf16[256,128]{1,0:T(8,128)(2,1)S(1)}, u32[]{:S(2)}, u32[]{:S(2)}) %collective-permute-start.11) | collective-permute-done | bytes 65568 | tf_op jit(solution)/shard_map/ppermute | solution.py:171
  33.6 0.9 %shard_map.73 = f32[2,4,32,256]{3,2,1,0:T(8,128)} custom-call(f32[2,4,32,256]{3,2,1,0:T(8,128)S(1)} %get-tuple-element.33.refs_4_.forecast, bf16[256,128]{1,0:T(8,128)(2,1)S(1)} %get-tuple-element.51.mine, bf16[256,128]{1,0:T(8,128)(2,1)S(1)} %collective-permute-done.11.theirs), custom_call_target="tpu_custom_call" | custom-call | flops 1000000 | bytes 1000000 | tf_op jit(solution)/shard_map/pallas_call | solution.py:670
  (25 shorter events, 1.1 us)
Async XLA Ops:
  0.0 5.8 %copy-start.1 = (f32[2,4,32,256]{3,2,1,0:T(8,128)S(1)}, f32[2,4,32,256]{3,2,1,0:T(8,128)}, u32[]{:S(2)}) copy-start(f32[2,4,32,256]{3,2,1,0:T(8,128)} %courant.5) | copy-start | bytes 786436
  0.0 5.8 %copy-start = (f32[2,4,32,256]{3,2,1,0:T(8,128)S(1)}, f32[2,4,32,256]{3,2,1,0:T(8,128)}, u32[]{:S(2)}) copy-start(f32[2,4,32,256]{3,2,1,0:T(8,128)} %tracer.5) | copy-start | bytes 786436
  1.7 4.1 %copy-start.6 = (f32[40,256]{1,0:T(8,128)S(1)}, f32[40,256]{1,0:T(8,128)}, u32[]{:S(2)}) copy-start(f32[40,256]{1,0:T(8,128)} %get-tuple-element.29._) | copy-start | bytes 122884
  1.7 5.7 %collective-permute-start = (f32[40,256]{1,0:T(8,128)}, f32[40,256]{1,0:T(8,128)S(1)}, u32[]{:S(2)}, u32[]{:S(2)}) collective-permute-start(f32[40,256]{1,0:T(8,128)} %get-tuple-element.32), channel_id=1, source_target_pairs={{1,2},{2,1},{5,6},{6,5},{9,10},{10,9},{13,14},{14,13},{17,18},{18,... | collective-permute-start | bytes 122888 | tf_op jit(solution)/shard_map/ppermute | solution.py:152
  4.9 3.2 %collective-permute-start.1 = (f32[40,256]{1,0:T(8,128)}, f32[40,256]{1,0:T(8,128)S(1)}, u32[]{:S(2)}, u32[]{:S(2)}) collective-permute-start(f32[40,256]{1,0:T(8,128)} %get-tuple-element.29._), channel_id=1, source_target_pairs={{0,1},{1,0},{2,3},{3,2},{4,5},{5,4},{6,7},{7,6},{8,9},{9,8},{10,11... | collective-permute-start | bytes 122888 | tf_op jit(solution)/shard_map/ppermute | solution.py:153
  8.1 3.3 %copy-start.2 = (s32[32768]{0:T(1024)S(1)}, s32[32768]{0:T(1024)}, u32[]{:S(2)}) copy-start(s32[32768]{0:T(1024)} %param.8) | copy-start | bytes 393220
  8.1 3.3 %copy-start.3 = (f32[32768]{0:T(1024)S(1)}, f32[32768]{0:T(1024)}, u32[]{:S(2)}) copy-start(f32[32768]{0:T(1024)} %param.9) | copy-start | bytes 393220
  8.1 3.3 %copy-start.4 = (f32[32768]{0:T(1024)S(1)}, f32[32768]{0:T(1024)}, u32[]{:S(2)}) copy-start(f32[32768]{0:T(1024)} %param.10) | copy-start | bytes 393220
  8.1 3.3 %copy-start.5 = (s32[2,2,1024]{2,1,0:T(2,128)S(1)}, s32[2,2,1024]{2,1,0:T(2,128)}, u32[]{:S(2)}) copy-start(s32[2,2,1024]{2,1,0:T(2,128)} %lists.3) | copy-start | bytes 49156
  8.7 3.9 %collective-permute-start.2 = (bf16[192,128]{1,0:T(8,128)(2,1)S(1)}, bf16[192,128]{1,0:T(8,128)(2,1)S(1)}, u32[]{:S(2)}, u32[]{:S(2)}) collective-permute-start(bf16[192,128]{1,0:T(8,128)(2,1)S(1)} %get-tuple-element.35), channel_id=1, source_target_pairs={{0,24},{4,28},{8,16},{12,20},{16,8},{20,12},{24,0},{28,4},{1,25},{... | collective-permute-start | bytes 147464 | tf_op jit(solution)/shard_map/ppermute | solution.py:167
  10.9 2.9 %collective-permute-start.3 = (bf16[192,128]{1,0:T(8,128)(2,1)S(1)}, bf16[192,128]{1,0:T(8,128)(2,1)S(1)}, u32[]{:S(2)}, u32[]{:S(2)}) collective-permute-start(bf16[192,128]{1,0:T(8,128)(2,1)S(1)} %get-tuple-element.36), channel_id=1, source_target_pairs={{0,16},{4,20},{8,24},{12,28},{16,0},{20,4},{24,8},{28,12},{1,17},{... | collective-permute-start | bytes 147464 | tf_op jit(solution)/shard_map/ppermute | solution.py:167
  11.1 2.9 %collective-permute-start.4 = (bf16[192,128]{1,0:T(8,128)(2,1)S(1)}, bf16[192,128]{1,0:T(8,128)(2,1)S(1)}, u32[]{:S(2)}, u32[]{:S(2)}) collective-permute-start(bf16[192,128]{1,0:T(8,128)(2,1)S(1)} %get-tuple-element.37), channel_id=1, source_target_pairs={{0,8},{4,12},{8,0},{12,4},{16,24},{20,28},{24,16},{28,20},{1,9},{5... | collective-permute-start | bytes 147464 | tf_op jit(solution)/shard_map/ppermute | solution.py:167
  14.1 4.8 %collective-permute-start.5 = (bf16[448,128]{1,0:T(8,128)(2,1)S(1)}, bf16[448,128]{1,0:T(8,128)(2,1)S(1)}, u32[]{:S(2)}, u32[]{:S(2)}) collective-permute-start(bf16[448,128]{1,0:T(8,128)(2,1)S(1)} %get-tuple-element.40), channel_id=1, source_target_pairs={{0,4},{4,0},{8,12},{12,8},{16,20},{20,16},{24,28},{28,24},{1,5},{5... | collective-permute-start | bytes 344072 | tf_op jit(solution)/shard_map/ppermute | solution.py:171
  19.7 2.6 %collective-permute-start.6 = (f32[24,128]{1,0:T(8,128)S(1)}, f32[24,128]{1,0:T(8,128)S(1)}, u32[]{:S(2)}, u32[]{:S(2)}) collective-permute-start(f32[24,128]{1,0:T(8,128)S(1)} %get-tuple-element.44), channel_id=1, source_target_pairs={{0,1},{1,0},{2,3},{3,2},{4,5},{5,4},{6,7},{7,6},{8,9},{9,8},{10,11... | collective-permute-start | bytes 36872 | tf_op jit(solution)/shard_map/ppermute | solution.py:152
  19.8 4.4 %collective-permute-start.7 = (f32[24,128]{1,0:T(8,128)S(1)}, f32[24,128]{1,0:T(8,128)S(1)}, u32[]{:S(2)}, u32[]{:S(2)}) collective-permute-start(f32[24,128]{1,0:T(8,128)S(1)} %get-tuple-element.45), channel_id=1, source_target_pairs={{1,2},{2,1},{5,6},{6,5},{9,10},{10,9},{13,14},{14,13},{17,18},{18,... | collective-permute-start | bytes 36872 | tf_op jit(solution)/shard_map/ppermute | solution.py:153
  24.9 3.7 %collective-permute-start.8 = (bf16[128,128]{1,0:T(8,128)(2,1)S(1)}, bf16[128,128]{1,0:T(8,128)(2,1)S(1)}, u32[]{:S(2)}, u32[]{:S(2)}) collective-permute-start(bf16[128,128]{1,0:T(8,128)(2,1)S(1)} %get-tuple-element.48), channel_id=1, source_target_pairs={{0,24},{4,28},{8,16},{12,20},{16,8},{20,12},{24,0},{28,4},{1,25},{... | collective-permute-start | bytes 98312 | tf_op jit(solution)/shard_map/ppermute | solution.py:167
  26.2 2.8 %collective-permute-start.9 = (bf16[128,128]{1,0:T(8,128)(2,1)S(1)}, bf16[128,128]{1,0:T(8,128)(2,1)S(1)}, u32[]{:S(2)}, u32[]{:S(2)}) collective-permute-start(bf16[128,128]{1,0:T(8,128)(2,1)S(1)} %get-tuple-element.49), channel_id=1, source_target_pairs={{0,16},{4,20},{8,24},{12,28},{16,0},{20,4},{24,8},{28,12},{1,17},{... | collective-permute-start | bytes 98312 | tf_op jit(solution)/shard_map/ppermute | solution.py:167
  26.4 2.8 %collective-permute-start.10 = (bf16[128,128]{1,0:T(8,128)(2,1)S(1)}, bf16[128,128]{1,0:T(8,128)(2,1)S(1)}, u32[]{:S(2)}, u32[]{:S(2)}) collective-permute-start(bf16[128,128]{1,0:T(8,128)(2,1)S(1)} %get-tuple-element.50), channel_id=1, source_target_pairs={{0,8},{4,12},{8,0},{12,4},{16,24},{20,28},{24,16},{28,20},{1,9},{5... | collective-permute-start | bytes 98312 | tf_op jit(solution)/shard_map/ppermute | solution.py:167
  29.2 4.4 %collective-permute-start.11 = (bf16[256,128]{1,0:T(8,128)(2,1)S(1)}, bf16[256,128]{1,0:T(8,128)(2,1)S(1)}, u32[]{:S(2)}, u32[]{:S(2)}) collective-permute-start(bf16[256,128]{1,0:T(8,128)(2,1)S(1)} %get-tuple-element.52), channel_id=1, source_target_pairs={{0,4},{4,0},{8,12},{12,8},{16,20},{20,16},{24,28},{28,24},{1,5},{5... | collective-permute-start | bytes 196616 | tf_op jit(solution)/shard_map/ppermute | solution.py:171

commit v12 on v10

--- a/solution.py
+++ b/solution.py
@@ -162,6 +162,44 @@
         (device(i, c), device(i ^ turn(s, chips), c)) for i in range(chips) for c in (0, 1)
     ]
     return [chunks[0]] + [lax.ppermute(chunks[s], "member", swaps(s)) for s in range(1, chips)]
+
+
+def gather_body(*refs, places, outputs):
+    inputs, targets = refs[:-outputs], refs[-outputs:]
+    for target, parts in zip(targets, places):
+        rows = target.shape[0] // len(parts)
+        for i, (source, at) in enumerate(parts):
+            target[i * rows : (i + 1) * rows, :] = inputs[source][at * rows : (at + 1) * rows, :]
+
+
+def regroup(slots, groups):
+    arrays = []
+    for group in groups:
+        for array, _ in (slots[d] for d in group):
+            if not any(array is other for other in arrays):
+                arrays.append(array)
+    find = lambda array: [array is other for other in arrays].index(True)
+    places = [[(find(slots[d][0]), slots[d][1]) for d in group] for group in groups]
+    rows = slots[0][0].shape[0]
+    return call(
+        functools.partial(gather_body, places=places, outputs=len(groups)),
+        [((rows * len(group), LANES), bf16) for group in groups],
+    )(*arrays)
+
+
+def exchange_by_bits(chunks):
+    chips = len(chunks)
+    slots = {turn(s, chips): (chunk, 0) for s, chunk in enumerate(chunks)}
+    bit = 1
+    while bit < chips:
+        moving = [d for d in range(chips) if d & bit]
+        (packed,) = regroup(slots, [moving])
+        pairs = [(i, i ^ (2 * bit)) for i in range(2 * chips)]
+        arrived = lax.ppermute(packed, "member", pairs)
+        for i, d in enumerate(moving):
+            slots[d] = (arrived, i)
+        bit *= 2
+    return regroup(slots, [[turn(s, chips)] for s in range(chips)])
 
 
 def swap_cores(array):
@@ -661,7 +699,7 @@
         [((2 * region_rows, LANES), bf16)] * chips,
         [pltpu.VMEM((ensemble, ensemble, LANES), f32)],
     )(own, first, second, centred)
-    returned = exchange(changes)
+    returned = exchange_by_bits(changes)
     mine, theirs = call(share, [((chips * region_rows, LANES), bf16)] * 2)(*returned, forecast)
     theirs = swap_cores(theirs)
     (analysis,) = call(

time: 34.5 us -> 37.2 us (1.078)
  waiting for transfers between devices: 5.97 us -> 9.14 us
  starting transfers between devices: 19.1 us -> 18.6 us
    ppermute x0 -> x2, waiting for transfers between devices: none -> 4.73 us  [exchange_by_bits(): arrived = lax.ppermute(packed, 'member', pairs)]
    ppermute x6 -> x3, starting transfers between devices: 5.43 us -> 2.71 us  [exchange(): lax.ppermute(chunks[s], 'member', swaps(s))]
    ppermute x0 -> x2, starting transfers between devices: none -> 1.57 us  [exchange_by_bits(): arrived = lax.ppermute(packed, 'member', pairs)]
    ppermute x6 -> x3, waiting for transfers between devices: 3.52 us -> 1.96 us  [exchange(): lax.ppermute(chunks[s], 'member', swaps(s))]
    ppermute x2, starting transfers between devices: 5.79 us -> 6.39 us  [swap_cores(): lax.ppermute(array, 'member', [(i, i ^ 1) for i in range(lax.axis_size('m...]
  transfers between devices with their start and end apart: 12 -> 11, of which waited for: 8 -> 7; matrix products, arithmetic and copies ran while one was open for 2% -> 2% of each run, Pallas kernels for 10% -> 9%
where the time goes in v12:
time: 37.2 us; the launch traced here: 36.8 us
  starting transfers between devices  18.6 us (50%)
  waiting for transfers between devices  9.14 us (25%)
  Pallas kernels  8.09 us (22%)
  local copies, waits for them, and re-layouts  0.8 us (2%)
    ppermute x2, starting transfers between devices, swap(): lax.ppermute(second, 'tile', pairs(1))  7.83 us
    ppermute x2, starting transfers between devices, swap_cores(): lax.ppermute(array, 'member', [(i, i ^ 1) for i in range(lax.axis_size('m...  6.39 us
    ppermute x2, waiting for transfers between devices, exchange_by_bits(): arrived = lax.ppermute(packed, 'member', pairs)  4.73 us
    ppermute x3, starting transfers between devices, exchange(): lax.ppermute(chunks[s], 'member', swaps(s))  2.71 us
    ppermute x3, waiting for transfers between devices, exchange(): lax.ppermute(chunks[s], 'member', swaps(s))  1.96 us
    ppermute x2, waiting for transfers between devices, swap_cores(): lax.ppermute(array, 'member', [(i, i ^ 1) for i in range(lax.axis_size('m...  1.87 us
    pallas_call x1, Pallas kernels, shards(): call(pack_edges, [((edge_rows, width), f32)] * 2, [pltpu.VMEM(edge_shape,...  1.7 us
    pallas_call x1, Pallas kernels, shards(): call(functools.partial(draft_body, height=height), [(member_concentration...  1.63 us
  transfers between devices with their start and end apart: 11, of which 7 were waited for; matrix products, arithmetic and copies ran while one was open for 2% of the time, Pallas kernels for 9%

profile of v12, /device:TPU:9, one launch (start us, length us, event | category | flops | bytes accessed | tf_op | source)
XLA Modules:
  0.0 36.8 jit_solution(15784482520192798785)
XLA Ops:
  0.0 1.7 %shard_map.64 = (f32[40,256]{1,0:T(8,128)}, f32[40,256]{1,0:T(8,128)}) custom-call(f32[2,4,32,256]{3,2,1,0:T(8,128)} %tracer.5, f32[2,4,32,256]{3,2,1,0:T(8,128)} %courant.5, s32[2,2,1024]{2,1,0:T(2,128)} %lists.3), custom_call_target="tpu_custom_call" | custom-call | flops 1000000 | bytes 1000000 | tf_op jit(solution)/shard_map/pallas_call | solution.py:616
  1.8 4.5 %collective-permute-start.1 = (f32[40,256]{1,0:T(8,128)}, f32[40,256]{1,0:T(8,128)S(1)}, u32[]{:S(2)}, u32[]{:S(2)}) collective-permute-start(f32[40,256]{1,0:T(8,128)} %get-tuple-element.33._), channel_id=1, source_target_pairs={{1,2},{2,1},{5,6},{6,5},{9,10},{10,9},{13,14},{14,13},{17,18},{18,... | collective-permute-start | bytes 122888 | tf_op jit(solution)/shard_map/ppermute | solution.py:151
  6.3 0.8 %dynamic-slice_bitcast_fusion.cell = s32[8,8,128]{2,1,0:T(8,128)S(1)} fusion(s32[8,4,8,128]{3,2,1,0:T(8,128)} %bitcast.6, s32[]{:T(128)S(6)} %select_n.4), kind=kLoop, calls=%fused_computation | loop fusion | bytes 65540 | tf_op jit(solution)/shard_map/jit(dynamic_index_in_dim)/squeeze | solution.py:635
  7.1 1.6 %shard_map.65 = (f32[2,4,32,256]{3,2,1,0:T(8,128)S(1)}, f32[8,2,8,128]{3,2,1,0:T(8,128)S(1)}) custom-call(f32[2,4,32,256]{3,2,1,0:T(8,128)S(1)} %copy-done, f32[2,4,32,256]{3,2,1,0:T(8,128)S(1)} %copy-done.1, s32[8,8,128]{2,1,0:T(8,128)S(1)} %dynamic-slice_bitcast_fusion.cell, f32[40,256]{1,0:T(8,128)S(1)} %copy-done.6), custom_call_target="tpu_custom_call" | custom-call | flops 50000000 | bytes 1000000 | tf_op jit(solution)/shard_map/pallas_call | solution.py:638
  8.8 0.6 %shard_map.66 = (f32[2,4,32,256]{3,2,1,0:T(8,128)S(1)}, bf16[192,128]{1,0:T(8,128)(2,1)S(1)}, bf16[192,128]{1,0:T(8,128)(2,1)S(1)}, bf16[192,128]{1,0:T(8,128)(2,1)S(1)}, bf16[192,128]{1,0:T(8,128)(2,1)S(1)}) custom-call(f32[2,4,32,256]{3,2,1,0:T(8,128)S(1)} %copy-done, f32[2,4,32,256]{3,2,1,0:T(8,128)S(1)} %copy-done.1, ...), custom_call_target="tpu_custom_call" | custom-call | flops 1000000 | bytes 1000000 | tf_op jit(solution)/shard_map/pallas_call | solution.py:645
  9.3 2.2 %collective-permute-start.2 = (bf16[192,128]{1,0:T(8,128)(2,1)S(1)}, bf16[192,128]{1,0:T(8,128)(2,1)S(1)}, u32[]{:S(2)}, u32[]{:S(2)}) collective-permute-start(bf16[192,128]{1,0:T(8,128)(2,1)S(1)} %get-tuple-element.39), channel_id=1, source_target_pairs={{0,24},{4,28},{8,16},{12,20},{16,8},{20,12},{24,0},{28,4},{1,25},{... | collective-permute-start | bytes 147464 | tf_op jit(solution)/shard_map/ppermute | solution.py:164
  11.8 0.3 collective-permute-start.4
  12.1 1.2 %shard_map.67 = (f32[16,3072]{1,0:T(8,128)S(1)}, f32[24,128]{1,0:T(8,128)S(1)}) custom-call(s32[2,2,1024]{2,1,0:T(2,128)S(1)} %copy-done.5, f32[40,256]{1,0:T(8,128)S(1)} %collective-permute-done.first, f32[40,256]{1,0:T(8,128)S(1)} %collective-permute-done.1.second, s32[256,128]{1,0:T(8,128)S(1)} %bitcast.7, f32[256,128]{1,0:T(8,128)S(1)} %bitcast.8, ...), custom_call_target="tpu_custom_call" | custom-call | flops 100000000 | bytes 1000000 | tf_op jit(solution)/shard_map/pallas_call | solution.py:662
  13.3 1.5 %collective-permute-done.3.refs_2_ = bf16[192,128]{1,0:T(8,128)(2,1)S(1)} collective-permute-done((bf16[192,128]{1,0:T(8,128)(2,1)S(1)}, bf16[192,128]{1,0:T(8,128)(2,1)S(1)}, u32[]{:S(2)}, u32[]{:S(2)}) %collective-permute-start.3) | collective-permute-done | bytes 49184 | tf_op jit(solution)/shard_map/ppermute | solution.py:164
  14.8 0.4 %collective-permute-done.4.refs_3_ = bf16[192,128]{1,0:T(8,128)(2,1)S(1)} collective-permute-done((bf16[192,128]{1,0:T(8,128)(2,1)S(1)}, bf16[192,128]{1,0:T(8,128)(2,1)S(1)}, u32[]{:S(2)}, u32[]{:S(2)}) %collective-permute-start.4) | collective-permute-done | bytes 49184 | tf_op jit(solution)/shard_map/ppermute | solution.py:164
  15.3 2.5 %collective-permute-start.5 = (bf16[448,128]{1,0:T(8,128)(2,1)S(1)}, bf16[448,128]{1,0:T(8,128)(2,1)S(1)}, u32[]{:S(2)}, u32[]{:S(2)}) collective-permute-start(bf16[448,128]{1,0:T(8,128)(2,1)S(1)} %get-tuple-element.44), channel_id=1, source_target_pairs={{0,4},{4,0},{8,12},{12,8},{16,20},{20,16},{24,28},{28,24},{1,5},{5... | collective-permute-start | bytes 344072 | tf_op jit(solution)/shard_map/ppermute | solution.py:206
  17.8 1.0 %collective-permute-done.5.theirs = bf16[448,128]{1,0:T(8,128)(2,1)S(1)} collective-permute-done((bf16[448,128]{1,0:T(8,128)(2,1)S(1)}, bf16[448,128]{1,0:T(8,128)(2,1)S(1)}, u32[]{:S(2)}, u32[]{:S(2)}) %collective-permute-start.5) | collective-permute-done | bytes 114720 | tf_op jit(solution)/shard_map/ppermute | solution.py:206
  18.7 0.8 %shard_map.69 = (f32[24,128]{1,0:T(8,128)S(1)}, f32[24,128]{1,0:T(8,128)S(1)}, bf16[48,3072]{1,0:T(8,128)(2,1)S(1)}) custom-call(bf16[448,128]{1,0:T(8,128)(2,1)S(1)} %get-tuple-element.43.mine, bf16[448,128]{1,0:T(8,128)(2,1)S(1)} %collective-permute-done.5.theirs, f32[16,3072]{1,0:T(8,128)S(1)} %get-tuple-element.45.weights, ...), custom_call_target="tpu_custom_call" | custom-call | flops 1000000 | bytes 1000000 | tf_op jit(solution)/shard_map/pallas_call | solution.py:680
  19.6 3.4 %collective-permute-start.7 = (f32[24,128]{1,0:T(8,128)S(1)}, f32[24,128]{1,0:T(8,128)S(1)}, u32[]{:S(2)}, u32[]{:S(2)}) collective-permute-start(f32[24,128]{1,0:T(8,128)S(1)} %get-tuple-element.49), channel_id=1, source_target_pairs={{1,2},{2,1},{5,6},{6,5},{9,10},{10,9},{13,14},{14,13},{17,18},{18,... | collective-permute-start | bytes 36872 | tf_op jit(solution)/shard_map/ppermute | solution.py:151
  22.9 0.5 %shard_map.70 = (f32[24,128]{1,0:T(8,128)S(1)}, f32[16,32,128]{2,1,0:T(8,128)S(1)}) custom-call(bf16[448,128]{1,0:T(8,128)(2,1)S(1)} %get-tuple-element.43.mine, bf16[448,128]{1,0:T(8,128)(2,1)S(1)} %collective-permute-done.5.theirs, f32[16,3072]{1,0:T(8,128)S(1)} %get-tuple-element.45.weights, bf16[48,3072]{1,0:T(8,128)(2,1)S(1)} %get-tuple-element.46.wide), custom_call_target="tpu_custom_call" | custom-call | flops 50000000 | bytes 1000000 | tf_op jit(solution)/shard_map/pallas_call | solution.py:690
  23.4 0.6 %collective-permute-done.7.second = f32[24,128]{1,0:T(8,128)S(1)} collective-permute-done((f32[24,128]{1,0:T(8,128)S(1)}, f32[24,128]{1,0:T(8,128)S(1)}, u32[]{:S(2)}, u32[]{:S(2)}) %collective-permute-start.7) | collective-permute-done | bytes 12320 | tf_op jit(solution)/shard_map/ppermute | solution.py:151
  24.0 0.7 %shard_map.71 = (bf16[128,128]{1,0:T(8,128)(2,1)S(1)}, bf16[128,128]{1,0:T(8,128)(2,1)S(1)}, bf16[128,128]{1,0:T(8,128)(2,1)S(1)}, bf16[128,128]{1,0:T(8,128)(2,1)S(1)}) custom-call(f32[24,128]{1,0:T(8,128)S(1)} %get-tuple-element.47.own, f32[24,128]{1,0:T(8,128)S(1)} %collective-permute-done.6.first, f32[24,128]{1,0:T(8,128)S(1)} %collective-permute-done.7.second, ...), custom_call_target="tpu_custom_call" | custom-call | flops 1000000 | bytes 1000000 | tf_op jit(solution)/shard_map/pallas_call | solution.py:697
  24.7 0.3 collective-permute-start.8
  25.0 2.9 %collective-permute-done.8.refs_1_.refs_2_ = bf16[256,128]{1,0:T(8,128)(2,1)S(1)} collective-permute-done((bf16[256,128]{1,0:T(8,128)(2,1)S(1)}, bf16[256,128]{1,0:T(8,128)(2,1)S(1)}, u32[]{:S(2)}, u32[]{:S(2)}) %collective-permute-start.8) | collective-permute-done | bytes 65568 | tf_op jit(solution)/shard_map/ppermute | solution.py:198
  27.9 1.2 %collective-permute-start.9 = (bf16[256,128]{1,0:T(8,128)(2,1)S(1)}, bf16[256,128]{1,0:T(8,128)(2,1)S(1)}, u32[]{:S(2)}, u32[]{:S(2)}) collective-permute-start(bf16[256,128]{1,0:T(8,128)(2,1)S(1)} %shard_map.73), channel_id=1, source_target_pairs={{0,16},{4,20},{8,24},{12,28},{16,0},{20,4},{24,8},{28,12},{1,17},{... | collective-permute-start | bytes 196616 | tf_op jit(solution)/shard_map/ppermute | solution.py:198
  29.2 1.9 %collective-permute-done.9.refs_1_ = bf16[256,128]{1,0:T(8,128)(2,1)S(1)} collective-permute-done((bf16[256,128]{1,0:T(8,128)(2,1)S(1)}, bf16[256,128]{1,0:T(8,128)(2,1)S(1)}, u32[]{:S(2)}, u32[]{:S(2)}) %collective-permute-start.9) | collective-permute-done | bytes 65568 | tf_op jit(solution)/shard_map/ppermute | solution.py:198
  31.1 3.9 %collective-permute-start.10 = (bf16[256,128]{1,0:T(8,128)(2,1)S(1)}, bf16[256,128]{1,0:T(8,128)(2,1)S(1)}, u32[]{:S(2)}, u32[]{:S(2)}) collective-permute-start(bf16[256,128]{1,0:T(8,128)(2,1)S(1)} %get-tuple-element.60), channel_id=1, source_target_pairs={{0,4},{4,0},{8,12},{12,8},{16,20},{20,16},{24,28},{28,24},{1,5},{5... | collective-permute-start | bytes 196616 | tf_op jit(solution)/shard_map/ppermute | solution.py:206
  35.0 0.9 %collective-permute-done.10.theirs = bf16[256,128]{1,0:T(8,128)(2,1)S(1)} collective-permute-done((bf16[256,128]{1,0:T(8,128)(2,1)S(1)}, bf16[256,128]{1,0:T(8,128)(2,1)S(1)}, u32[]{:S(2)}, u32[]{:S(2)}) %collective-permute-start.10) | collective-permute-done | bytes 65568 | tf_op jit(solution)/shard_map/ppermute | solution.py:206
  35.9 0.9 %shard_map.76 = f32[2,4,32,256]{3,2,1,0:T(8,128)} custom-call(f32[2,4,32,256]{3,2,1,0:T(8,128)S(1)} %get-tuple-element.37.refs_4_.forecast, bf16[256,128]{1,0:T(8,128)(2,1)S(1)} %get-tuple-element.59.mine, bf16[256,128]{1,0:T(8,128)(2,1)S(1)} %collective-permute-done.10.theirs), custom_call_target="tpu_custom_call" | custom-call | flops 1000000 | bytes 1000000 | tf_op jit(solution)/shard_map/pallas_call | solution.py:705
  (26 shorter events, 0.4 us)
Async XLA Ops:
  0.0 7.1 %copy-start.1 = (f32[2,4,32,256]{3,2,1,0:T(8,128)S(1)}, f32[2,4,32,256]{3,2,1,0:T(8,128)}, u32[]{:S(2)}) copy-start(f32[2,4,32,256]{3,2,1,0:T(8,128)} %courant.5) | copy-start | bytes 786436
  0.0 7.1 %copy-start = (f32[2,4,32,256]{3,2,1,0:T(8,128)S(1)}, f32[2,4,32,256]{3,2,1,0:T(8,128)}, u32[]{:S(2)}) copy-start(f32[2,4,32,256]{3,2,1,0:T(8,128)} %tracer.5) | copy-start | bytes 786436
  1.7 5.3 %copy-start.6 = (f32[40,256]{1,0:T(8,128)S(1)}, f32[40,256]{1,0:T(8,128)}, u32[]{:S(2)}) copy-start(f32[40,256]{1,0:T(8,128)} %get-tuple-element.33._) | copy-start | bytes 122884
  1.7 7.0 %collective-permute-start = (f32[40,256]{1,0:T(8,128)}, f32[40,256]{1,0:T(8,128)S(1)}, u32[]{:S(2)}, u32[]{:S(2)}) collective-permute-start(f32[40,256]{1,0:T(8,128)} %get-tuple-element.36), channel_id=1, source_target_pairs={{0,1},{1,0},{2,3},{3,2},{4,5},{5,4},{6,7},{7,6},{8,9},{9,8},{10,11... | collective-permute-start | bytes 122888 | tf_op jit(solution)/shard_map/ppermute | solution.py:151
  1.8 6.9 %collective-permute-start.1 = (f32[40,256]{1,0:T(8,128)}, f32[40,256]{1,0:T(8,128)S(1)}, u32[]{:S(2)}, u32[]{:S(2)}) collective-permute-start(f32[40,256]{1,0:T(8,128)} %get-tuple-element.33._), channel_id=1, source_target_pairs={{1,2},{2,1},{5,6},{6,5},{9,10},{10,9},{13,14},{14,13},{17,18},{18,... | collective-permute-start | bytes 122888 | tf_op jit(solution)/shard_map/ppermute | solution.py:151
  8.7 3.3 %copy-start.2 = (s32[32768]{0:T(1024)S(1)}, s32[32768]{0:T(1024)}, u32[]{:S(2)}) copy-start(s32[32768]{0:T(1024)} %param.8) | copy-start | bytes 393220
  8.7 3.3 %copy-start.3 = (f32[32768]{0:T(1024)S(1)}, f32[32768]{0:T(1024)}, u32[]{:S(2)}) copy-start(f32[32768]{0:T(1024)} %param.9) | copy-start | bytes 393220
  8.7 3.3 %copy-start.4 = (f32[32768]{0:T(1024)S(1)}, f32[32768]{0:T(1024)}, u32[]{:S(2)}) copy-start(f32[32768]{0:T(1024)} %param.10) | copy-start | bytes 393220
  8.7 3.3 %copy-start.5 = (s32[2,2,1024]{2,1,0:T(2,128)S(1)}, s32[2,2,1024]{2,1,0:T(2,128)}, u32[]{:S(2)}) copy-start(s32[2,2,1024]{2,1,0:T(2,128)} %lists.3) | copy-start | bytes 49156
  9.3 3.9 %collective-permute-start.2 = (bf16[192,128]{1,0:T(8,128)(2,1)S(1)}, bf16[192,128]{1,0:T(8,128)(2,1)S(1)}, u32[]{:S(2)}, u32[]{:S(2)}) collective-permute-start(bf16[192,128]{1,0:T(8,128)(2,1)S(1)} %get-tuple-element.39), channel_id=1, source_target_pairs={{0,24},{4,28},{8,16},{12,20},{16,8},{20,12},{24,0},{28,4},{1,25},{... | collective-permute-start | bytes 147464 | tf_op jit(solution)/shard_map/ppermute | solution.py:164
  11.6 3.2 %collective-permute-start.3 = (bf16[192,128]{1,0:T(8,128)(2,1)S(1)}, bf16[192,128]{1,0:T(8,128)(2,1)S(1)}, u32[]{:S(2)}, u32[]{:S(2)}) collective-permute-start(bf16[192,128]{1,0:T(8,128)(2,1)S(1)} %get-tuple-element.40), channel_id=1, source_target_pairs={{0,16},{4,20},{8,24},{12,28},{16,0},{20,4},{24,8},{28,12},{1,17},{... | collective-permute-start | bytes 147464 | tf_op jit(solution)/shard_map/ppermute | solution.py:164
  11.8 3.4 %collective-permute-start.4 = (bf16[192,128]{1,0:T(8,128)(2,1)S(1)}, bf16[192,128]{1,0:T(8,128)(2,1)S(1)}, u32[]{:S(2)}, u32[]{:S(2)}) collective-permute-start(bf16[192,128]{1,0:T(8,128)(2,1)S(1)} %get-tuple-element.41), channel_id=1, source_target_pairs={{0,8},{4,12},{8,0},{12,4},{16,24},{20,28},{24,16},{28,20},{1,9},{5... | collective-permute-start | bytes 147464 | tf_op jit(solution)/shard_map/ppermute | solution.py:164
  15.3 3.5 %collective-permute-start.5 = (bf16[448,128]{1,0:T(8,128)(2,1)S(1)}, bf16[448,128]{1,0:T(8,128)(2,1)S(1)}, u32[]{:S(2)}, u32[]{:S(2)}) collective-permute-start(bf16[448,128]{1,0:T(8,128)(2,1)S(1)} %get-tuple-element.44), channel_id=1, source_target_pairs={{0,4},{4,0},{8,12},{12,8},{16,20},{20,16},{24,28},{28,24},{1,5},{5... | collective-permute-start | bytes 344072 | tf_op jit(solution)/shard_map/ppermute | solution.py:206
  19.5 3.9 %collective-permute-start.6 = (f32[24,128]{1,0:T(8,128)S(1)}, f32[24,128]{1,0:T(8,128)S(1)}, u32[]{:S(2)}, u32[]{:S(2)}) collective-permute-start(f32[24,128]{1,0:T(8,128)S(1)} %get-tuple-element.48), channel_id=1, source_target_pairs={{0,1},{1,0},{2,3},{3,2},{4,5},{5,4},{6,7},{7,6},{8,9},{9,8},{10,11... | collective-permute-start | bytes 36872 | tf_op jit(solution)/shard_map/ppermute | solution.py:151
  19.6 4.4 %collective-permute-start.7 = (f32[24,128]{1,0:T(8,128)S(1)}, f32[24,128]{1,0:T(8,128)S(1)}, u32[]{:S(2)}, u32[]{:S(2)}) collective-permute-start(f32[24,128]{1,0:T(8,128)S(1)} %get-tuple-element.49), channel_id=1, source_target_pairs={{1,2},{2,1},{5,6},{6,5},{9,10},{10,9},{13,14},{14,13},{17,18},{18,... | collective-permute-start | bytes 36872 | tf_op jit(solution)/shard_map/ppermute | solution.py:151
  24.7 3.2 %collective-permute-start.8 = (bf16[256,128]{1,0:T(8,128)(2,1)S(1)}, bf16[256,128]{1,0:T(8,128)(2,1)S(1)}, u32[]{:S(2)}, u32[]{:S(2)}) collective-permute-start(bf16[256,128]{1,0:T(8,128)(2,1)S(1)} %shard_map.72), channel_id=1, source_target_pairs={{0,8},{4,12},{8,0},{12,4},{16,24},{20,28},{24,16},{28,20},{1,9},{5... | collective-permute-start | bytes 196616 | tf_op jit(solution)/shard_map/ppermute | solution.py:198
  27.9 3.1 %collective-permute-start.9 = (bf16[256,128]{1,0:T(8,128)(2,1)S(1)}, bf16[256,128]{1,0:T(8,128)(2,1)S(1)}, u32[]{:S(2)}, u32[]{:S(2)}) collective-permute-start(bf16[256,128]{1,0:T(8,128)(2,1)S(1)} %shard_map.73), channel_id=1, source_target_pairs={{0,16},{4,20},{8,24},{12,28},{16,0},{20,4},{24,8},{28,12},{1,17},{... | collective-permute-start | bytes 196616 | tf_op jit(solution)/shard_map/ppermute | solution.py:198
  31.1 4.8 %collective-permute-start.10 = (bf16[256,128]{1,0:T(8,128)(2,1)S(1)}, bf16[256,128]{1,0:T(8,128)(2,1)S(1)}, u32[]{:S(2)}, u32[]{:S(2)}) collective-permute-start(bf16[256,128]{1,0:T(8,128)(2,1)S(1)} %get-tuple-element.60), channel_id=1, source_target_pairs={{0,4},{4,0},{8,12},{12,8},{16,20},{20,16},{24,28},{28,24},{1,5},{5... | collective-permute-start | bytes 196616 | tf_op jit(solution)/shard_map/ppermute | solution.py:206

commit v13 on v10

--- a/solution.py
+++ b/solution.py
@@ -152,7 +152,7 @@
 
 
 def turn(s, chips):
-    return (chips - s) % chips
+    return s % (chips - 1) + 1 if s else 0
 
 
 def exchange(chunks):

time: 34.5 us -> 35 us (1.014)
  transfers between devices with their start and end apart: 12 -> 12, of which waited for: 8 -> 7; matrix products, arithmetic and copies ran while one was open for 2% -> 2% of each run, Pallas kernels for 10% -> 10%
where the time goes in v13:
time: 35 us; the launch traced here: 34.6 us
  starting transfers between devices  19.3 us (55%)
  Pallas kernels  8.06 us (23%)
  waiting for transfers between devices  6.28 us (18%)
  local copies, waits for them, and re-layouts  0.8 us (2%)
    ppermute x2, starting transfers between devices, swap(): lax.ppermute(second, 'tile', pairs(1))  7.83 us
    ppermute x2, starting transfers between devices, swap_cores(): lax.ppermute(array, 'member', [(i, i ^ 1) for i in range(lax.axis_size('m...  5.91 us
    ppermute x6, starting transfers between devices, exchange(): lax.ppermute(chunks[s], 'member', swaps(s))  5.43 us
    ppermute x6, waiting for transfers between devices, exchange(): lax.ppermute(chunks[s], 'member', swaps(s))  3.83 us
    ppermute x2, waiting for transfers between devices, swap_cores(): lax.ppermute(array, 'member', [(i, i ^ 1) for i in range(lax.axis_size('m...  1.87 us
    pallas_call x1, Pallas kernels, shards(): call(pack_edges, [((edge_rows, width), f32)] * 2, [pltpu.VMEM(edge_shape,...  1.7 us
    pallas_call x1, Pallas kernels, shards(): call(functools.partial(draft_body, height=height), [(member_concentration...  1.63 us
    pallas_call x1, Pallas kernels, shards(): call(functools.partial(weights_body, tiles=tiles, blocks=blocks, height=h...  1.19 us
  transfers between devices with their start and end apart: 12, of which 7 were waited for; matrix products, arithmetic and copies ran while one was open for 2% of the time, Pallas kernels for 10%

profile of v13, /device:TPU:9, one launch (start us, length us, event | category | flops | bytes accessed | tf_op | source)
XLA Modules:
  0.0 34.6 jit_solution(146342523736437216)
XLA Ops:
  0.0 1.7 %shard_map.64 = (f32[40,256]{1,0:T(8,128)}, f32[40,256]{1,0:T(8,128)}) custom-call(f32[2,4,32,256]{3,2,1,0:T(8,128)} %tracer.5, f32[2,4,32,256]{3,2,1,0:T(8,128)} %courant.5, s32[2,2,1024]{2,1,0:T(2,128)} %lists.3), custom_call_target="tpu_custom_call" | custom-call | flops 1000000 | bytes 1000000 | tf_op jit(solution)/shard_map/pallas_call | solution.py:578
  1.8 4.5 %collective-permute-start.1 = (f32[40,256]{1,0:T(8,128)}, f32[40,256]{1,0:T(8,128)S(1)}, u32[]{:S(2)}, u32[]{:S(2)}) collective-permute-start(f32[40,256]{1,0:T(8,128)} %get-tuple-element.29._), channel_id=1, source_target_pairs={{1,2},{2,1},{5,6},{6,5},{9,10},{10,9},{13,14},{14,13},{17,18},{18,... | collective-permute-start | bytes 122888 | tf_op jit(solution)/shard_map/ppermute | solution.py:151
  6.3 0.8 %dynamic-slice_bitcast_fusion.cell = s32[8,8,128]{2,1,0:T(8,128)S(1)} fusion(s32[8,4,8,128]{3,2,1,0:T(8,128)} %bitcast.6, s32[]{:T(128)S(6)} %select_n.4), kind=kLoop, calls=%fused_computation | loop fusion | bytes 65540 | tf_op jit(solution)/shard_map/jit(dynamic_index_in_dim)/squeeze | solution.py:597
  7.1 1.6 %shard_map.65 = (f32[2,4,32,256]{3,2,1,0:T(8,128)S(1)}, f32[8,2,8,128]{3,2,1,0:T(8,128)S(1)}) custom-call(f32[2,4,32,256]{3,2,1,0:T(8,128)S(1)} %copy-done, f32[2,4,32,256]{3,2,1,0:T(8,128)S(1)} %copy-done.1, s32[8,8,128]{2,1,0:T(8,128)S(1)} %dynamic-slice_bitcast_fusion.cell, f32[40,256]{1,0:T(8,128)S(1)} %copy-done.6), custom_call_target="tpu_custom_call" | custom-call | flops 50000000 | bytes 1000000 | tf_op jit(solution)/shard_map/pallas_call | solution.py:600
  8.8 0.6 %shard_map.66 = (f32[2,4,32,256]{3,2,1,0:T(8,128)S(1)}, bf16[192,128]{1,0:T(8,128)(2,1)S(1)}, bf16[192,128]{1,0:T(8,128)(2,1)S(1)}, bf16[192,128]{1,0:T(8,128)(2,1)S(1)}, bf16[192,128]{1,0:T(8,128)(2,1)S(1)}) custom-call(f32[2,4,32,256]{3,2,1,0:T(8,128)S(1)} %copy-done, f32[2,4,32,256]{3,2,1,0:T(8,128)S(1)} %copy-done.1, ...), custom_call_target="tpu_custom_call" | custom-call | flops 1000000 | bytes 1000000 | tf_op jit(solution)/shard_map/pallas_call | solution.py:607
  9.3 1.3 %collective-permute-start.2 = (bf16[192,128]{1,0:T(8,128)(2,1)S(1)}, bf16[192,128]{1,0:T(8,128)(2,1)S(1)}, u32[]{:S(2)}, u32[]{:S(2)}) collective-permute-start(bf16[192,128]{1,0:T(8,128)(2,1)S(1)} %get-tuple-element.35), channel_id=1, source_target_pairs={{0,16},{4,20},{8,24},{12,28},{16,0},{20,4},{24,8},{28,12},{1,17},{... | collective-permute-start | bytes 147464 | tf_op jit(solution)/shard_map/ppermute | solution.py:164
  10.6 1.2 %collective-permute-start.3 = (bf16[192,128]{1,0:T(8,128)(2,1)S(1)}, bf16[192,128]{1,0:T(8,128)(2,1)S(1)}, u32[]{:S(2)}, u32[]{:S(2)}) collective-permute-start(bf16[192,128]{1,0:T(8,128)(2,1)S(1)} %get-tuple-element.36), channel_id=1, source_target_pairs={{0,24},{4,28},{8,16},{12,20},{16,8},{20,12},{24,0},{28,4},{1,25},{... | collective-permute-start | bytes 147464 | tf_op jit(solution)/shard_map/ppermute | solution.py:164
  11.8 0.3 collective-permute-start.4
  12.1 1.2 %shard_map.67 = (f32[16,3072]{1,0:T(8,128)S(1)}, f32[24,128]{1,0:T(8,128)S(1)}) custom-call(s32[2,2,1024]{2,1,0:T(2,128)S(1)} %copy-done.5, f32[40,256]{1,0:T(8,128)S(1)} %collective-permute-done.first, f32[40,256]{1,0:T(8,128)S(1)} %collective-permute-done.1.second, s32[256,128]{1,0:T(8,128)S(1)} %bitcast.7, f32[256,128]{1,0:T(8,128)S(1)} %bitcast.8, ...), custom_call_target="tpu_custom_call" | custom-call | flops 100000000 | bytes 1000000 | tf_op jit(solution)/shard_map/pallas_call | solution.py:624
  13.3 1.3 %collective-permute-done.3.refs_2_ = bf16[192,128]{1,0:T(8,128)(2,1)S(1)} collective-permute-done((bf16[192,128]{1,0:T(8,128)(2,1)S(1)}, bf16[192,128]{1,0:T(8,128)(2,1)S(1)}, u32[]{:S(2)}, u32[]{:S(2)}) %collective-permute-start.3) | collective-permute-done | bytes 49184 | tf_op jit(solution)/shard_map/ppermute | solution.py:164
  14.8 3.0 %collective-permute-start.5 = (bf16[448,128]{1,0:T(8,128)(2,1)S(1)}, bf16[448,128]{1,0:T(8,128)(2,1)S(1)}, u32[]{:S(2)}, u32[]{:S(2)}) collective-permute-start(bf16[448,128]{1,0:T(8,128)(2,1)S(1)} %get-tuple-element.40), channel_id=1, source_target_pairs={{0,4},{4,0},{8,12},{12,8},{16,20},{20,16},{24,28},{28,24},{1,5},{5... | collective-permute-start | bytes 344072 | tf_op jit(solution)/shard_map/ppermute | solution.py:168
  17.8 1.0 %collective-permute-done.5.theirs = bf16[448,128]{1,0:T(8,128)(2,1)S(1)} collective-permute-done((bf16[448,128]{1,0:T(8,128)(2,1)S(1)}, bf16[448,128]{1,0:T(8,128)(2,1)S(1)}, u32[]{:S(2)}, u32[]{:S(2)}) %collective-permute-start.5) | collective-permute-done | bytes 114720 | tf_op jit(solution)/shard_map/ppermute | solution.py:168
  18.7 0.8 %shard_map.69 = (f32[24,128]{1,0:T(8,128)S(1)}, f32[24,128]{1,0:T(8,128)S(1)}, bf16[48,3072]{1,0:T(8,128)(2,1)S(1)}) custom-call(bf16[448,128]{1,0:T(8,128)(2,1)S(1)} %get-tuple-element.39.mine, bf16[448,128]{1,0:T(8,128)(2,1)S(1)} %collective-permute-done.5.theirs, f32[16,3072]{1,0:T(8,128)S(1)} %get-tuple-element.41.weights, ...), custom_call_target="tpu_custom_call" | custom-call | flops 1000000 | bytes 1000000 | tf_op jit(solution)/shard_map/pallas_call | solution.py:642
  19.6 3.4 %collective-permute-start.7 = (f32[24,128]{1,0:T(8,128)S(1)}, f32[24,128]{1,0:T(8,128)S(1)}, u32[]{:S(2)}, u32[]{:S(2)}) collective-permute-start(f32[24,128]{1,0:T(8,128)S(1)} %get-tuple-element.45), channel_id=1, source_target_pairs={{1,2},{2,1},{5,6},{6,5},{9,10},{10,9},{13,14},{14,13},{17,18},{18,... | collective-permute-start | bytes 36872 | tf_op jit(solution)/shard_map/ppermute | solution.py:151
  22.9 0.5 %shard_map.70 = (f32[24,128]{1,0:T(8,128)S(1)}, f32[16,32,128]{2,1,0:T(8,128)S(1)}) custom-call(bf16[448,128]{1,0:T(8,128)(2,1)S(1)} %get-tuple-element.39.mine, bf16[448,128]{1,0:T(8,128)(2,1)S(1)} %collective-permute-done.5.theirs, f32[16,3072]{1,0:T(8,128)S(1)} %get-tuple-element.41.weights, bf16[48,3072]{1,0:T(8,128)(2,1)S(1)} %get-tuple-element.42.wide), custom_call_target="tpu_custom_call" | custom-call | flops 50000000 | bytes 1000000 | tf_op jit(solution)/shard_map/pallas_call | solution.py:652
  23.4 0.6 %collective-permute-done.7.second = f32[24,128]{1,0:T(8,128)S(1)} collective-permute-done((f32[24,128]{1,0:T(8,128)S(1)}, f32[24,128]{1,0:T(8,128)S(1)}, u32[]{:S(2)}, u32[]{:S(2)}) %collective-permute-start.7) | collective-permute-done | bytes 12320 | tf_op jit(solution)/shard_map/ppermute | solution.py:151
  24.0 0.7 %shard_map.71 = (bf16[128,128]{1,0:T(8,128)(2,1)S(1)}, bf16[128,128]{1,0:T(8,128)(2,1)S(1)}, bf16[128,128]{1,0:T(8,128)(2,1)S(1)}, bf16[128,128]{1,0:T(8,128)(2,1)S(1)}) custom-call(f32[24,128]{1,0:T(8,128)S(1)} %get-tuple-element.43.own, f32[24,128]{1,0:T(8,128)S(1)} %collective-permute-done.6.first, f32[24,128]{1,0:T(8,128)S(1)} %collective-permute-done.7.second, ...), custom_call_target="tpu_custom_call" | custom-call | flops 1000000 | bytes 1000000 | tf_op jit(solution)/shard_map/pallas_call | solution.py:659
  24.7 1.3 %collective-permute-start.8 = (bf16[128,128]{1,0:T(8,128)(2,1)S(1)}, bf16[128,128]{1,0:T(8,128)(2,1)S(1)}, u32[]{:S(2)}, u32[]{:S(2)}) collective-permute-start(bf16[128,128]{1,0:T(8,128)(2,1)S(1)} %get-tuple-element.48), channel_id=1, source_target_pairs={{0,16},{4,20},{8,24},{12,28},{16,0},{20,4},{24,8},{28,12},{1,17},{... | collective-permute-start | bytes 98312 | tf_op jit(solution)/shard_map/ppermute | solution.py:164
  26.0 0.6 %collective-permute-start.9 = (bf16[128,128]{1,0:T(8,128)(2,1)S(1)}, bf16[128,128]{1,0:T(8,128)(2,1)S(1)}, u32[]{:S(2)}, u32[]{:S(2)}) collective-permute-start(bf16[128,128]{1,0:T(8,128)(2,1)S(1)} %get-tuple-element.49), channel_id=1, source_target_pairs={{0,24},{4,28},{8,16},{12,20},{16,8},{20,12},{24,0},{28,4},{1,25},{... | collective-permute-start | bytes 98312 | tf_op jit(solution)/shard_map/ppermute | solution.py:164
  26.6 0.8 %collective-permute-start.10 = (bf16[128,128]{1,0:T(8,128)(2,1)S(1)}, bf16[128,128]{1,0:T(8,128)(2,1)S(1)}, u32[]{:S(2)}, u32[]{:S(2)}) collective-permute-start(bf16[128,128]{1,0:T(8,128)(2,1)S(1)} %get-tuple-element.50), channel_id=1, source_target_pairs={{0,8},{4,12},{8,0},{12,4},{16,24},{20,28},{24,16},{28,20},{1,9},{5... | collective-permute-start | bytes 98312 | tf_op jit(solution)/shard_map/ppermute | solution.py:164
  27.5 2.2 %collective-permute-done.9.refs_2_ = bf16[128,128]{1,0:T(8,128)(2,1)S(1)} collective-permute-done((bf16[128,128]{1,0:T(8,128)(2,1)S(1)}, bf16[128,128]{1,0:T(8,128)(2,1)S(1)}, u32[]{:S(2)}, u32[]{:S(2)}) %collective-permute-start.9) | collective-permute-done | bytes 32800 | tf_op jit(solution)/shard_map/ppermute | solution.py:164
  29.8 2.9 %collective-permute-start.11 = (bf16[256,128]{1,0:T(8,128)(2,1)S(1)}, bf16[256,128]{1,0:T(8,128)(2,1)S(1)}, u32[]{:S(2)}, u32[]{:S(2)}) collective-permute-start(bf16[256,128]{1,0:T(8,128)(2,1)S(1)} %get-tuple-element.52), channel_id=1, source_target_pairs={{0,4},{4,0},{8,12},{12,8},{16,20},{20,16},{24,28},{28,24},{1,5},{5... | collective-permute-start | bytes 196616 | tf_op jit(solution)/shard_map/ppermute | solution.py:168
  32.7 0.9 %collective-permute-done.11.theirs = bf16[256,128]{1,0:T(8,128)(2,1)S(1)} collective-permute-done((bf16[256,128]{1,0:T(8,128)(2,1)S(1)}, bf16[256,128]{1,0:T(8,128)(2,1)S(1)}, u32[]{:S(2)}, u32[]{:S(2)}) %collective-permute-start.11) | collective-permute-done | bytes 65568 | tf_op jit(solution)/shard_map/ppermute | solution.py:168
  33.6 0.9 %shard_map.73 = f32[2,4,32,256]{3,2,1,0:T(8,128)} custom-call(f32[2,4,32,256]{3,2,1,0:T(8,128)S(1)} %get-tuple-element.33.refs_4_.forecast, bf16[256,128]{1,0:T(8,128)(2,1)S(1)} %get-tuple-element.51.mine, bf16[256,128]{1,0:T(8,128)(2,1)S(1)} %collective-permute-done.11.theirs), custom_call_target="tpu_custom_call" | custom-call | flops 1000000 | bytes 1000000 | tf_op jit(solution)/shard_map/pallas_call | solution.py:667
  (25 shorter events, 0.5 us)
Async XLA Ops:
  0.0 7.1 %copy-start.1 = (f32[2,4,32,256]{3,2,1,0:T(8,128)S(1)}, f32[2,4,32,256]{3,2,1,0:T(8,128)}, u32[]{:S(2)}) copy-start(f32[2,4,32,256]{3,2,1,0:T(8,128)} %courant.5) | copy-start | bytes 786436
  0.0 7.1 %copy-start = (f32[2,4,32,256]{3,2,1,0:T(8,128)S(1)}, f32[2,4,32,256]{3,2,1,0:T(8,128)}, u32[]{:S(2)}) copy-start(f32[2,4,32,256]{3,2,1,0:T(8,128)} %tracer.5) | copy-start | bytes 786436
  1.7 5.3 %copy-start.6 = (f32[40,256]{1,0:T(8,128)S(1)}, f32[40,256]{1,0:T(8,128)}, u32[]{:S(2)}) copy-start(f32[40,256]{1,0:T(8,128)} %get-tuple-element.29._) | copy-start | bytes 122884
  1.7 7.0 %collective-permute-start = (f32[40,256]{1,0:T(8,128)}, f32[40,256]{1,0:T(8,128)S(1)}, u32[]{:S(2)}, u32[]{:S(2)}) collective-permute-start(f32[40,256]{1,0:T(8,128)} %get-tuple-element.32), channel_id=1, source_target_pairs={{0,1},{1,0},{2,3},{3,2},{4,5},{5,4},{6,7},{7,6},{8,9},{9,8},{10,11... | collective-permute-start | bytes 122888 | tf_op jit(solution)/shard_map/ppermute | solution.py:151
  1.8 6.9 %collective-permute-start.1 = (f32[40,256]{1,0:T(8,128)}, f32[40,256]{1,0:T(8,128)S(1)}, u32[]{:S(2)}, u32[]{:S(2)}) collective-permute-start(f32[40,256]{1,0:T(8,128)} %get-tuple-element.29._), channel_id=1, source_target_pairs={{1,2},{2,1},{5,6},{6,5},{9,10},{10,9},{13,14},{14,13},{17,18},{18,... | collective-permute-start | bytes 122888 | tf_op jit(solution)/shard_map/ppermute | solution.py:151
  8.7 3.3 %copy-start.2 = (s32[32768]{0:T(1024)S(1)}, s32[32768]{0:T(1024)}, u32[]{:S(2)}) copy-start(s32[32768]{0:T(1024)} %param.8) | copy-start | bytes 393220
  8.7 3.3 %copy-start.3 = (f32[32768]{0:T(1024)S(1)}, f32[32768]{0:T(1024)}, u32[]{:S(2)}) copy-start(f32[32768]{0:T(1024)} %param.9) | copy-start | bytes 393220
  8.7 3.3 %copy-start.4 = (f32[32768]{0:T(1024)S(1)}, f32[32768]{0:T(1024)}, u32[]{:S(2)}) copy-start(f32[32768]{0:T(1024)} %param.10) | copy-start | bytes 393220
  8.7 3.3 %copy-start.5 = (s32[2,2,1024]{2,1,0:T(2,128)S(1)}, s32[2,2,1024]{2,1,0:T(2,128)}, u32[]{:S(2)}) copy-start(s32[2,2,1024]{2,1,0:T(2,128)} %lists.3) | copy-start | bytes 49156
  9.3 3.9 %collective-permute-start.2 = (bf16[192,128]{1,0:T(8,128)(2,1)S(1)}, bf16[192,128]{1,0:T(8,128)(2,1)S(1)}, u32[]{:S(2)}, u32[]{:S(2)}) collective-permute-start(bf16[192,128]{1,0:T(8,128)(2,1)S(1)} %get-tuple-element.35), channel_id=1, source_target_pairs={{0,16},{4,20},{8,24},{12,28},{16,0},{20,4},{24,8},{28,12},{1,17},{... | collective-permute-start | bytes 147464 | tf_op jit(solution)/shard_map/ppermute | solution.py:164
  10.6 3.9 %collective-permute-start.3 = (bf16[192,128]{1,0:T(8,128)(2,1)S(1)}, bf16[192,128]{1,0:T(8,128)(2,1)S(1)}, u32[]{:S(2)}, u32[]{:S(2)}) collective-permute-start(bf16[192,128]{1,0:T(8,128)(2,1)S(1)} %get-tuple-element.36), channel_id=1, source_target_pairs={{0,24},{4,28},{8,16},{12,20},{16,8},{20,12},{24,0},{28,4},{1,25},{... | collective-permute-start | bytes 147464 | tf_op jit(solution)/shard_map/ppermute | solution.py:164
  11.8 2.9 %collective-permute-start.4 = (bf16[192,128]{1,0:T(8,128)(2,1)S(1)}, bf16[192,128]{1,0:T(8,128)(2,1)S(1)}, u32[]{:S(2)}, u32[]{:S(2)}) collective-permute-start(bf16[192,128]{1,0:T(8,128)(2,1)S(1)} %get-tuple-element.37), channel_id=1, source_target_pairs={{0,8},{4,12},{8,0},{12,4},{16,24},{20,28},{24,16},{28,20},{1,9},{5... | collective-permute-start | bytes 147464 | tf_op jit(solution)/shard_map/ppermute | solution.py:164
  14.8 4.0 %collective-permute-start.5 = (bf16[448,128]{1,0:T(8,128)(2,1)S(1)}, bf16[448,128]{1,0:T(8,128)(2,1)S(1)}, u32[]{:S(2)}, u32[]{:S(2)}) collective-permute-start(bf16[448,128]{1,0:T(8,128)(2,1)S(1)} %get-tuple-element.40), channel_id=1, source_target_pairs={{0,4},{4,0},{8,12},{12,8},{16,20},{20,16},{24,28},{28,24},{1,5},{5... | collective-permute-start | bytes 344072 | tf_op jit(solution)/shard_map/ppermute | solution.py:168
  19.5 3.9 %collective-permute-start.6 = (f32[24,128]{1,0:T(8,128)S(1)}, f32[24,128]{1,0:T(8,128)S(1)}, u32[]{:S(2)}, u32[]{:S(2)}) collective-permute-start(f32[24,128]{1,0:T(8,128)S(1)} %get-tuple-element.44), channel_id=1, source_target_pairs={{0,1},{1,0},{2,3},{3,2},{4,5},{5,4},{6,7},{7,6},{8,9},{9,8},{10,11... | collective-permute-start | bytes 36872 | tf_op jit(solution)/shard_map/ppermute | solution.py:151
  19.6 4.4 %collective-permute-start.7 = (f32[24,128]{1,0:T(8,128)S(1)}, f32[24,128]{1,0:T(8,128)S(1)}, u32[]{:S(2)}, u32[]{:S(2)}) collective-permute-start(f32[24,128]{1,0:T(8,128)S(1)} %get-tuple-element.45), channel_id=1, source_target_pairs={{1,2},{2,1},{5,6},{6,5},{9,10},{10,9},{13,14},{14,13},{17,18},{18,... | collective-permute-start | bytes 36872 | tf_op jit(solution)/shard_map/ppermute | solution.py:151
  24.7 2.8 %collective-permute-start.8 = (bf16[128,128]{1,0:T(8,128)(2,1)S(1)}, bf16[128,128]{1,0:T(8,128)(2,1)S(1)}, u32[]{:S(2)}, u32[]{:S(2)}) collective-permute-start(bf16[128,128]{1,0:T(8,128)(2,1)S(1)} %get-tuple-element.48), channel_id=1, source_target_pairs={{0,16},{4,20},{8,24},{12,28},{16,0},{20,4},{24,8},{28,12},{1,17},{... | collective-permute-start | bytes 98312 | tf_op jit(solution)/shard_map/ppermute | solution.py:164
  26.0 3.8 %collective-permute-start.9 = (bf16[128,128]{1,0:T(8,128)(2,1)S(1)}, bf16[128,128]{1,0:T(8,128)(2,1)S(1)}, u32[]{:S(2)}, u32[]{:S(2)}) collective-permute-start(bf16[128,128]{1,0:T(8,128)(2,1)S(1)} %get-tuple-element.49), channel_id=1, source_target_pairs={{0,24},{4,28},{8,16},{12,20},{16,8},{20,12},{24,0},{28,4},{1,25},{... | collective-permute-start | bytes 98312 | tf_op jit(solution)/shard_map/ppermute | solution.py:164
  26.6 3.1 %collective-permute-start.10 = (bf16[128,128]{1,0:T(8,128)(2,1)S(1)}, bf16[128,128]{1,0:T(8,128)(2,1)S(1)}, u32[]{:S(2)}, u32[]{:S(2)}) collective-permute-start(bf16[128,128]{1,0:T(8,128)(2,1)S(1)} %get-tuple-element.50), channel_id=1, source_target_pairs={{0,8},{4,12},{8,0},{12,4},{16,24},{20,28},{24,16},{28,20},{1,9},{5... | collective-permute-start | bytes 98312 | tf_op jit(solution)/shard_map/ppermute | solution.py:164
  29.8 3.8 %collective-permute-start.11 = (bf16[256,128]{1,0:T(8,128)(2,1)S(1)}, bf16[256,128]{1,0:T(8,128)(2,1)S(1)}, u32[]{:S(2)}, u32[]{:S(2)}) collective-permute-start(bf16[256,128]{1,0:T(8,128)(2,1)S(1)} %get-tuple-element.52), channel_id=1, source_target_pairs={{0,4},{4,0},{8,12},{12,8},{16,20},{20,16},{24,28},{28,24},{1,5},{5... | collective-permute-start | bytes 196616 | tf_op jit(solution)/shard_map/ppermute | solution.py:168

commit v14 on v10

--- a/solution.py
+++ b/solution.py
@@ -504,7 +504,7 @@
         pivots = jnp.ones((ensemble, LANES), f32)
         for k in range(ensemble):
             pivot = columns[k][k : k + 1, :]
-            factor = jnp.where(row > k, columns[k], 0.0) / pivot
+            factor = jnp.where(row > k, columns[k], 0.0) * (1.0 / pivot)
             for j in range(k + 1, ensemble):
                 columns[j] = columns[j] - factor * columns[j][k : k + 1, :]
             state = state - factor * state[k : k + 1, :]
@@ -537,22 +537,23 @@
             chunk[at, :] = jnp.concatenate(totals, axis=0).astype(bf16)
 
 
-def output_body(forecast, mine, theirs, analysis, ordered):
+def output_body(forecast, mine, theirs, analysis):
     members, levels, side, width = forecast.shape
     _, chip, core = place()
-    rows = ordered.shape[1]
+    rows = members * levels * BLOCK
     chips = mine.shape[0] // rows
-    for s in range(chips):
-        at = slice(s * rows, (s + 1) * rows)
-        source = 2 * (chip ^ turn(s, chips))
-        ordered[source + core] = mine[at, :].astype(f32)
-        ordered[source + (core ^ 1)] = theirs[at, :].astype(f32)
+
+    def block(device):
+        s = lax.rem(chips - (chip ^ (device // 2)), chips)
+        at = pl.ds(pl.multiple_of(s * rows, rows), rows)
+        return jnp.where(core == device % 2, mine[at, :].astype(f32), theirs[at, :].astype(f32))
+
     for q in range(width // LANES):
-        parts = [ordered[4 * q + c] for c in range(4)]
+        parts = [block(4 * q + c) for c in range(4)]
         at = slice(q * LANES, (q + 1) * LANES)
         for r, part in enumerate(transpose_chunks(parts)):
-            rows = slice(r * BLOCK, (r + 1) * BLOCK)
-            analysis[:, :, rows, at] = forecast[:, :, rows, at] + part.reshape(
+            lines = slice(r * BLOCK, (r + 1) * BLOCK)
+            analysis[:, :, lines, at] = forecast[:, :, lines, at] + part.reshape(
                 members, levels, BLOCK, LANES
             )
 
@@ -664,9 +665,7 @@
     returned = exchange(changes)
     mine, theirs = call(share, [((chips * region_rows, LANES), bf16)] * 2)(*returned, forecast)
     theirs = swap_cores(theirs)
-    (analysis,) = call(
-        output_body, [(forecast.shape, f32)], [pltpu.VMEM((blocks, region_rows, LANES), f32)]
-    )(forecast, mine, theirs)
+    (analysis,) = call(output_body, [(forecast.shape, f32)])(forecast, mine, theirs)
     return analysis
 
 

time: 34.5 us -> 34.5 us (level)
  no operation moved by 1% of the time
where the time goes in v14:
time: 34.5 us; the launch traced here: 34.1 us
  starting transfers between devices  19.1 us (55%)
  Pallas kernels  8 us (23%)
  waiting for transfers between devices  5.97 us (17%)
  local copies, waits for them, and re-layouts  0.8 us (2%)
    ppermute x2, starting transfers between devices, swap(): lax.ppermute(second, 'tile', pairs(1))  7.83 us
    ppermute x2, starting transfers between devices, swap_cores(): lax.ppermute(array, 'member', [(i, i ^ 1) for i in range(lax.axis_size('m...  5.79 us
    ppermute x6, starting transfers between devices, exchange(): lax.ppermute(chunks[s], 'member', swaps(s))  5.43 us
    ppermute x6, waiting for transfers between devices, exchange(): lax.ppermute(chunks[s], 'member', swaps(s))  3.52 us
    ppermute x2, waiting for transfers between devices, swap_cores(): lax.ppermute(array, 'member', [(i, i ^ 1) for i in range(lax.axis_size('m...  1.87 us
    pallas_call x1, Pallas kernels, shards(): call(pack_edges, [((edge_rows, width), f32)] * 2, [pltpu.VMEM(edge_shape,...  1.7 us
    pallas_call x1, Pallas kernels, shards(): call(functools.partial(draft_body, height=height), [(member_concentration...  1.63 us
    pallas_call x1, Pallas kernels, shards(): call(functools.partial(weights_body, tiles=tiles, blocks=blocks, height=h...  1.19 us
  transfers between devices with their start and end apart: 12, of which 8 were waited for; matrix products, arithmetic and copies ran while one was open for 2% of the time, Pallas kernels for 10%

profile of v14, /device:TPU:9, one launch (start us, length us, event | category | flops | bytes accessed | tf_op | source)
XLA Modules:
  0.0 34.1 jit_solution(11304712086077998924)
XLA Ops:
  0.0 1.7 %shard_map.64 = (f32[40,256]{1,0:T(8,128)}, f32[40,256]{1,0:T(8,128)}) custom-call(f32[2,4,32,256]{3,2,1,0:T(8,128)} %tracer.5, f32[2,4,32,256]{3,2,1,0:T(8,128)} %courant.5, s32[2,2,1024]{2,1,0:T(2,128)} %lists.3), custom_call_target="tpu_custom_call" | custom-call | flops 1000000 | bytes 1000000 | tf_op jit(solution)/shard_map/pallas_call | solution.py:579
  1.8 4.5 %collective-permute-start.1 = (f32[40,256]{1,0:T(8,128)}, f32[40,256]{1,0:T(8,128)S(1)}, u32[]{:S(2)}, u32[]{:S(2)}) collective-permute-start(f32[40,256]{1,0:T(8,128)} %get-tuple-element.29._), channel_id=1, source_target_pairs={{1,2},{2,1},{5,6},{6,5},{9,10},{10,9},{13,14},{14,13},{17,18},{18,... | collective-permute-start | bytes 122888 | tf_op jit(solution)/shard_map/ppermute | solution.py:151
  6.3 0.8 %dynamic-slice_bitcast_fusion.cell = s32[8,8,128]{2,1,0:T(8,128)S(1)} fusion(s32[8,4,8,128]{3,2,1,0:T(8,128)} %bitcast.6, s32[]{:T(128)S(6)} %select_n.4), kind=kLoop, calls=%fused_computation | loop fusion | bytes 65540 | tf_op jit(solution)/shard_map/jit(dynamic_index_in_dim)/squeeze | solution.py:598
  7.1 1.6 %shard_map.65 = (f32[2,4,32,256]{3,2,1,0:T(8,128)S(1)}, f32[8,2,8,128]{3,2,1,0:T(8,128)S(1)}) custom-call(f32[2,4,32,256]{3,2,1,0:T(8,128)S(1)} %copy-done, f32[2,4,32,256]{3,2,1,0:T(8,128)S(1)} %copy-done.1, s32[8,8,128]{2,1,0:T(8,128)S(1)} %dynamic-slice_bitcast_fusion.cell, f32[40,256]{1,0:T(8,128)S(1)} %copy-done.6), custom_call_target="tpu_custom_call" | custom-call | flops 50000000 | bytes 1000000 | tf_op jit(solution)/shard_map/pallas_call | solution.py:601
  8.8 0.6 %shard_map.66 = (f32[2,4,32,256]{3,2,1,0:T(8,128)S(1)}, bf16[192,128]{1,0:T(8,128)(2,1)S(1)}, bf16[192,128]{1,0:T(8,128)(2,1)S(1)}, bf16[192,128]{1,0:T(8,128)(2,1)S(1)}, bf16[192,128]{1,0:T(8,128)(2,1)S(1)}) custom-call(f32[2,4,32,256]{3,2,1,0:T(8,128)S(1)} %copy-done, f32[2,4,32,256]{3,2,1,0:T(8,128)S(1)} %copy-done.1, ...), custom_call_target="tpu_custom_call" | custom-call | flops 1000000 | bytes 1000000 | tf_op jit(solution)/shard_map/pallas_call | solution.py:608
  9.3 2.2 %collective-permute-start.2 = (bf16[192,128]{1,0:T(8,128)(2,1)S(1)}, bf16[192,128]{1,0:T(8,128)(2,1)S(1)}, u32[]{:S(2)}, u32[]{:S(2)}) collective-permute-start(bf16[192,128]{1,0:T(8,128)(2,1)S(1)} %get-tuple-element.35), channel_id=1, source_target_pairs={{0,24},{4,28},{8,16},{12,20},{16,8},{20,12},{24,0},{28,4},{1,25},{... | collective-permute-start | bytes 147464 | tf_op jit(solution)/shard_map/ppermute | solution.py:164
  11.8 0.3 collective-permute-start.4
  12.1 1.2 %shard_map.67 = (f32[16,3072]{1,0:T(8,128)S(1)}, f32[24,128]{1,0:T(8,128)S(1)}) custom-call(s32[2,2,1024]{2,1,0:T(2,128)S(1)} %copy-done.5, f32[40,256]{1,0:T(8,128)S(1)} %collective-permute-done.first, f32[40,256]{1,0:T(8,128)S(1)} %collective-permute-done.1.second, s32[256,128]{1,0:T(8,128)S(1)} %bitcast.7, f32[256,128]{1,0:T(8,128)S(1)} %bitcast.8, ...), custom_call_target="tpu_custom_call" | custom-call | flops 100000000 | bytes 1000000 | tf_op jit(solution)/shard_map/pallas_call | solution.py:625
  13.3 1.5 %collective-permute-done.3.refs_2_ = bf16[192,128]{1,0:T(8,128)(2,1)S(1)} collective-permute-done((bf16[192,128]{1,0:T(8,128)(2,1)S(1)}, bf16[192,128]{1,0:T(8,128)(2,1)S(1)}, u32[]{:S(2)}, u32[]{:S(2)}) %collective-permute-start.3) | collective-permute-done | bytes 49184 | tf_op jit(solution)/shard_map/ppermute | solution.py:164
  14.8 0.4 %collective-permute-done.4.refs_3_ = bf16[192,128]{1,0:T(8,128)(2,1)S(1)} collective-permute-done((bf16[192,128]{1,0:T(8,128)(2,1)S(1)}, bf16[192,128]{1,0:T(8,128)(2,1)S(1)}, u32[]{:S(2)}, u32[]{:S(2)}) %collective-permute-start.4) | collective-permute-done | bytes 49184 | tf_op jit(solution)/shard_map/ppermute | solution.py:164
  15.3 2.5 %collective-permute-start.5 = (bf16[448,128]{1,0:T(8,128)(2,1)S(1)}, bf16[448,128]{1,0:T(8,128)(2,1)S(1)}, u32[]{:S(2)}, u32[]{:S(2)}) collective-permute-start(bf16[448,128]{1,0:T(8,128)(2,1)S(1)} %get-tuple-element.40), channel_id=1, source_target_pairs={{0,4},{4,0},{8,12},{12,8},{16,20},{20,16},{24,28},{28,24},{1,5},{5... | collective-permute-start | bytes 344072 | tf_op jit(solution)/shard_map/ppermute | solution.py:168
  17.8 1.0 %collective-permute-done.5.theirs = bf16[448,128]{1,0:T(8,128)(2,1)S(1)} collective-permute-done((bf16[448,128]{1,0:T(8,128)(2,1)S(1)}, bf16[448,128]{1,0:T(8,128)(2,1)S(1)}, u32[]{:S(2)}, u32[]{:S(2)}) %collective-permute-start.5) | collective-permute-done | bytes 114720 | tf_op jit(solution)/shard_map/ppermute | solution.py:168
  18.7 0.8 %shard_map.69 = (f32[24,128]{1,0:T(8,128)S(1)}, f32[24,128]{1,0:T(8,128)S(1)}, bf16[48,3072]{1,0:T(8,128)(2,1)S(1)}) custom-call(bf16[448,128]{1,0:T(8,128)(2,1)S(1)} %get-tuple-element.39.mine, bf16[448,128]{1,0:T(8,128)(2,1)S(1)} %collective-permute-done.5.theirs, f32[16,3072]{1,0:T(8,128)S(1)} %get-tuple-element.41.weights, ...), custom_call_target="tpu_custom_call" | custom-call | flops 1000000 | bytes 1000000 | tf_op jit(solution)/shard_map/pallas_call | solution.py:643
  19.6 3.4 %collective-permute-start.7 = (f32[24,128]{1,0:T(8,128)S(1)}, f32[24,128]{1,0:T(8,128)S(1)}, u32[]{:S(2)}, u32[]{:S(2)}) collective-permute-start(f32[24,128]{1,0:T(8,128)S(1)} %get-tuple-element.45), channel_id=1, source_target_pairs={{1,2},{2,1},{5,6},{6,5},{9,10},{10,9},{13,14},{14,13},{17,18},{18,... | collective-permute-start | bytes 36872 | tf_op jit(solution)/shard_map/ppermute | solution.py:151
  22.9 0.5 %shard_map.70 = (f32[24,128]{1,0:T(8,128)S(1)}, f32[16,32,128]{2,1,0:T(8,128)S(1)}) custom-call(bf16[448,128]{1,0:T(8,128)(2,1)S(1)} %get-tuple-element.39.mine, bf16[448,128]{1,0:T(8,128)(2,1)S(1)} %collective-permute-done.5.theirs, f32[16,3072]{1,0:T(8,128)S(1)} %get-tuple-element.41.weights, bf16[48,3072]{1,0:T(8,128)(2,1)S(1)} %get-tuple-element.42.wide), custom_call_target="tpu_custom_call" | custom-call | flops 50000000 | bytes 1000000 | tf_op jit(solution)/shard_map/pallas_call | solution.py:653
  23.4 0.6 %collective-permute-done.7.second = f32[24,128]{1,0:T(8,128)S(1)} collective-permute-done((f32[24,128]{1,0:T(8,128)S(1)}, f32[24,128]{1,0:T(8,128)S(1)}, u32[]{:S(2)}, u32[]{:S(2)}) %collective-permute-start.7) | collective-permute-done | bytes 12320 | tf_op jit(solution)/shard_map/ppermute | solution.py:151
  24.0 0.7 %shard_map.71 = (bf16[128,128]{1,0:T(8,128)(2,1)S(1)}, bf16[128,128]{1,0:T(8,128)(2,1)S(1)}, bf16[128,128]{1,0:T(8,128)(2,1)S(1)}, bf16[128,128]{1,0:T(8,128)(2,1)S(1)}) custom-call(f32[24,128]{1,0:T(8,128)S(1)} %get-tuple-element.43.own, f32[24,128]{1,0:T(8,128)S(1)} %collective-permute-done.6.first, f32[24,128]{1,0:T(8,128)S(1)} %collective-permute-done.7.second, ...), custom_call_target="tpu_custom_call" | custom-call | flops 1000000 | bytes 1000000 | tf_op jit(solution)/shard_map/pallas_call | solution.py:660
  24.7 1.3 %collective-permute-start.8 = (bf16[128,128]{1,0:T(8,128)(2,1)S(1)}, bf16[128,128]{1,0:T(8,128)(2,1)S(1)}, u32[]{:S(2)}, u32[]{:S(2)}) collective-permute-start(bf16[128,128]{1,0:T(8,128)(2,1)S(1)} %get-tuple-element.48), channel_id=1, source_target_pairs={{0,24},{4,28},{8,16},{12,20},{16,8},{20,12},{24,0},{28,4},{1,25},{... | collective-permute-start | bytes 98312 | tf_op jit(solution)/shard_map/ppermute | solution.py:164
  26.2 1.2 %collective-permute-start.10 = (bf16[128,128]{1,0:T(8,128)(2,1)S(1)}, bf16[128,128]{1,0:T(8,128)(2,1)S(1)}, u32[]{:S(2)}, u32[]{:S(2)}) collective-permute-start(bf16[128,128]{1,0:T(8,128)(2,1)S(1)} %get-tuple-element.50), channel_id=1, source_target_pairs={{0,8},{4,12},{8,0},{12,4},{16,24},{20,28},{24,16},{28,20},{1,9},{5... | collective-permute-start | bytes 98312 | tf_op jit(solution)/shard_map/ppermute | solution.py:164
  27.4 1.0 %collective-permute-done.8.refs_1_ = bf16[128,128]{1,0:T(8,128)(2,1)S(1)} collective-permute-done((bf16[128,128]{1,0:T(8,128)(2,1)S(1)}, bf16[128,128]{1,0:T(8,128)(2,1)S(1)}, u32[]{:S(2)}, u32[]{:S(2)}) %collective-permute-start.8) | collective-permute-done | bytes 32800 | tf_op jit(solution)/shard_map/ppermute | solution.py:164
  28.4 0.4 %collective-permute-done.9.refs_2_ = bf16[128,128]{1,0:T(8,128)(2,1)S(1)} collective-permute-done((bf16[128,128]{1,0:T(8,128)(2,1)S(1)}, bf16[128,128]{1,0:T(8,128)(2,1)S(1)}, u32[]{:S(2)}, u32[]{:S(2)}) %collective-permute-start.9) | collective-permute-done | bytes 32800 | tf_op jit(solution)/shard_map/ppermute | solution.py:164
  29.0 3.3 %collective-permute-start.11 = (bf16[256,128]{1,0:T(8,128)(2,1)S(1)}, bf16[256,128]{1,0:T(8,128)(2,1)S(1)}, u32[]{:S(2)}, u32[]{:S(2)}) collective-permute-start(bf16[256,128]{1,0:T(8,128)(2,1)S(1)} %get-tuple-element.52), channel_id=1, source_target_pairs={{0,4},{4,0},{8,12},{12,8},{16,20},{20,16},{24,28},{28,24},{1,5},{5... | collective-permute-start | bytes 196616 | tf_op jit(solution)/shard_map/ppermute | solution.py:168
  32.3 0.9 %collective-permute-done.11.theirs = bf16[256,128]{1,0:T(8,128)(2,1)S(1)} collective-permute-done((bf16[256,128]{1,0:T(8,128)(2,1)S(1)}, bf16[256,128]{1,0:T(8,128)(2,1)S(1)}, u32[]{:S(2)}, u32[]{:S(2)}) %collective-permute-start.11) | collective-permute-done | bytes 65568 | tf_op jit(solution)/shard_map/ppermute | solution.py:168
  33.2 0.9 %shard_map.73 = f32[2,4,32,256]{3,2,1,0:T(8,128)} custom-call(f32[2,4,32,256]{3,2,1,0:T(8,128)S(1)} %get-tuple-element.33.refs_4_.forecast, bf16[256,128]{1,0:T(8,128)(2,1)S(1)} %get-tuple-element.51.mine, bf16[256,128]{1,0:T(8,128)(2,1)S(1)} %collective-permute-done.11.theirs), custom_call_target="tpu_custom_call" | custom-call | flops 1000000 | bytes 1000000 | tf_op jit(solution)/shard_map/pallas_call | solution.py:668
  (25 shorter events, 0.8 us)
Async XLA Ops:
  0.0 7.1 %copy-start.1 = (f32[2,4,32,256]{3,2,1,0:T(8,128)S(1)}, f32[2,4,32,256]{3,2,1,0:T(8,128)}, u32[]{:S(2)}) copy-start(f32[2,4,32,256]{3,2,1,0:T(8,128)} %courant.5) | copy-start | bytes 786436
  0.0 7.1 %copy-start = (f32[2,4,32,256]{3,2,1,0:T(8,128)S(1)}, f32[2,4,32,256]{3,2,1,0:T(8,128)}, u32[]{:S(2)}) copy-start(f32[2,4,32,256]{3,2,1,0:T(8,128)} %tracer.5) | copy-start | bytes 786436
  1.7 5.3 %copy-start.6 = (f32[40,256]{1,0:T(8,128)S(1)}, f32[40,256]{1,0:T(8,128)}, u32[]{:S(2)}) copy-start(f32[40,256]{1,0:T(8,128)} %get-tuple-element.29._) | copy-start | bytes 122884
  1.7 7.0 %collective-permute-start = (f32[40,256]{1,0:T(8,128)}, f32[40,256]{1,0:T(8,128)S(1)}, u32[]{:S(2)}, u32[]{:S(2)}) collective-permute-start(f32[40,256]{1,0:T(8,128)} %get-tuple-element.32), channel_id=1, source_target_pairs={{0,1},{1,0},{2,3},{3,2},{4,5},{5,4},{6,7},{7,6},{8,9},{9,8},{10,11... | collective-permute-start | bytes 122888 | tf_op jit(solution)/shard_map/ppermute | solution.py:151
  1.8 6.9 %collective-permute-start.1 = (f32[40,256]{1,0:T(8,128)}, f32[40,256]{1,0:T(8,128)S(1)}, u32[]{:S(2)}, u32[]{:S(2)}) collective-permute-start(f32[40,256]{1,0:T(8,128)} %get-tuple-element.29._), channel_id=1, source_target_pairs={{1,2},{2,1},{5,6},{6,5},{9,10},{10,9},{13,14},{14,13},{17,18},{18,... | collective-permute-start | bytes 122888 | tf_op jit(solution)/shard_map/ppermute | solution.py:151
  8.7 3.3 %copy-start.2 = (s32[32768]{0:T(1024)S(1)}, s32[32768]{0:T(1024)}, u32[]{:S(2)}) copy-start(s32[32768]{0:T(1024)} %param.8) | copy-start | bytes 393220
  8.7 3.3 %copy-start.3 = (f32[32768]{0:T(1024)S(1)}, f32[32768]{0:T(1024)}, u32[]{:S(2)}) copy-start(f32[32768]{0:T(1024)} %param.9) | copy-start | bytes 393220
  8.7 3.3 %copy-start.4 = (f32[32768]{0:T(1024)S(1)}, f32[32768]{0:T(1024)}, u32[]{:S(2)}) copy-start(f32[32768]{0:T(1024)} %param.10) | copy-start | bytes 393220
  8.7 3.3 %copy-start.5 = (s32[2,2,1024]{2,1,0:T(2,128)S(1)}, s32[2,2,1024]{2,1,0:T(2,128)}, u32[]{:S(2)}) copy-start(s32[2,2,1024]{2,1,0:T(2,128)} %lists.3) | copy-start | bytes 49156
  9.3 3.9 %collective-permute-start.2 = (bf16[192,128]{1,0:T(8,128)(2,1)S(1)}, bf16[192,128]{1,0:T(8,128)(2,1)S(1)}, u32[]{:S(2)}, u32[]{:S(2)}) collective-permute-start(bf16[192,128]{1,0:T(8,128)(2,1)S(1)} %get-tuple-element.35), channel_id=1, source_target_pairs={{0,24},{4,28},{8,16},{12,20},{16,8},{20,12},{24,0},{28,4},{1,25},{... | collective-permute-start | bytes 147464 | tf_op jit(solution)/shard_map/ppermute | solution.py:164
  11.6 3.2 %collective-permute-start.3 = (bf16[192,128]{1,0:T(8,128)(2,1)S(1)}, bf16[192,128]{1,0:T(8,128)(2,1)S(1)}, u32[]{:S(2)}, u32[]{:S(2)}) collective-permute-start(bf16[192,128]{1,0:T(8,128)(2,1)S(1)} %get-tuple-element.36), channel_id=1, source_target_pairs={{0,16},{4,20},{8,24},{12,28},{16,0},{20,4},{24,8},{28,12},{1,17},{... | collective-permute-start | bytes 147464 | tf_op jit(solution)/shard_map/ppermute | solution.py:164
  11.8 3.4 %collective-permute-start.4 = (bf16[192,128]{1,0:T(8,128)(2,1)S(1)}, bf16[192,128]{1,0:T(8,128)(2,1)S(1)}, u32[]{:S(2)}, u32[]{:S(2)}) collective-permute-start(bf16[192,128]{1,0:T(8,128)(2,1)S(1)} %get-tuple-element.37), channel_id=1, source_target_pairs={{0,8},{4,12},{8,0},{12,4},{16,24},{20,28},{24,16},{28,20},{1,9},{5... | collective-permute-start | bytes 147464 | tf_op jit(solution)/shard_map/ppermute | solution.py:164
  15.3 3.5 %collective-permute-start.5 = (bf16[448,128]{1,0:T(8,128)(2,1)S(1)}, bf16[448,128]{1,0:T(8,128)(2,1)S(1)}, u32[]{:S(2)}, u32[]{:S(2)}) collective-permute-start(bf16[448,128]{1,0:T(8,128)(2,1)S(1)} %get-tuple-element.40), channel_id=1, source_target_pairs={{0,4},{4,0},{8,12},{12,8},{16,20},{20,16},{24,28},{28,24},{1,5},{5... | collective-permute-start | bytes 344072 | tf_op jit(solution)/shard_map/ppermute | solution.py:168
  19.5 3.9 %collective-permute-start.6 = (f32[24,128]{1,0:T(8,128)S(1)}, f32[24,128]{1,0:T(8,128)S(1)}, u32[]{:S(2)}, u32[]{:S(2)}) collective-permute-start(f32[24,128]{1,0:T(8,128)S(1)} %get-tuple-element.44), channel_id=1, source_target_pairs={{0,1},{1,0},{2,3},{3,2},{4,5},{5,4},{6,7},{7,6},{8,9},{9,8},{10,11... | collective-permute-start | bytes 36872 | tf_op jit(solution)/shard_map/ppermute | solution.py:151
  19.6 4.4 %collective-permute-start.7 = (f32[24,128]{1,0:T(8,128)S(1)}, f32[24,128]{1,0:T(8,128)S(1)}, u32[]{:S(2)}, u32[]{:S(2)}) collective-permute-start(f32[24,128]{1,0:T(8,128)S(1)} %get-tuple-element.45), channel_id=1, source_target_pairs={{1,2},{2,1},{5,6},{6,5},{9,10},{10,9},{13,14},{14,13},{17,18},{18,... | collective-permute-start | bytes 36872 | tf_op jit(solution)/shard_map/ppermute | solution.py:151
  24.7 3.7 %collective-permute-start.8 = (bf16[128,128]{1,0:T(8,128)(2,1)S(1)}, bf16[128,128]{1,0:T(8,128)(2,1)S(1)}, u32[]{:S(2)}, u32[]{:S(2)}) collective-permute-start(bf16[128,128]{1,0:T(8,128)(2,1)S(1)} %get-tuple-element.48), channel_id=1, source_target_pairs={{0,24},{4,28},{8,16},{12,20},{16,8},{20,12},{24,0},{28,4},{1,25},{... | collective-permute-start | bytes 98312 | tf_op jit(solution)/shard_map/ppermute | solution.py:164
  26.0 2.8 %collective-permute-start.9 = (bf16[128,128]{1,0:T(8,128)(2,1)S(1)}, bf16[128,128]{1,0:T(8,128)(2,1)S(1)}, u32[]{:S(2)}, u32[]{:S(2)}) collective-permute-start(bf16[128,128]{1,0:T(8,128)(2,1)S(1)} %get-tuple-element.49), channel_id=1, source_target_pairs={{0,16},{4,20},{8,24},{12,28},{16,0},{20,4},{24,8},{28,12},{1,17},{... | collective-permute-start | bytes 98312 | tf_op jit(solution)/shard_map/ppermute | solution.py:164
  26.2 2.8 %collective-permute-start.10 = (bf16[128,128]{1,0:T(8,128)(2,1)S(1)}, bf16[128,128]{1,0:T(8,128)(2,1)S(1)}, u32[]{:S(2)}, u32[]{:S(2)}) collective-permute-start(bf16[128,128]{1,0:T(8,128)(2,1)S(1)} %get-tuple-element.50), channel_id=1, source_target_pairs={{0,8},{4,12},{8,0},{12,4},{16,24},{20,28},{24,16},{28,20},{1,9},{5... | collective-permute-start | bytes 98312 | tf_op jit(solution)/shard_map/ppermute | solution.py:164
  29.0 4.2 %collective-permute-start.11 = (bf16[256,128]{1,0:T(8,128)(2,1)S(1)}, bf16[256,128]{1,0:T(8,128)(2,1)S(1)}, u32[]{:S(2)}, u32[]{:S(2)}) collective-permute-start(bf16[256,128]{1,0:T(8,128)(2,1)S(1)} %get-tuple-element.52), channel_id=1, source_target_pairs={{0,4},{4,0},{8,12},{12,8},{16,20},{20,16},{24,28},{28,24},{1,5},{5... | collective-permute-start | bytes 196616 | tf_op jit(solution)/shard_map/ppermute | solution.py:168
